TPU v7x, 32 devices: a whole 2x2x4 slice. The times are simulated.
32 devices in a mesh: ens: 2 (over x), gy: 16 (over z, y, core).
Axes of the slice: x: 2, y: 2, z: 4, core: 2. Of those that a mesh axis runs over, the one named last changes fastest.
Arguments:
- flow_state: float32 [5, 32, 128, 128], P(None, 'ens', 'gy'), parts along dimension 1, may hold values from -0.05 to 1.1, as said below
- section_cotangent: float32 [5, 32, 128, 128], P(None, 'ens', 'gy'), parts along dimension 1, may hold values from -6 to 6
- face_flags: int32 [3, 32, 128, 128], P(None, 'ens', 'gy'), parts along dimension 1, may hold values from 0 to 15
- conv_kernel: float32 [16, 135], replicated, may hold values from -0.5 to 0.5
- head_weights: float32 [5, 16], replicated, may hold values from -1.5 to 1.5
Outputs:
- flow_adjoint: float32 [5, 32, 128, 128], P(None, 'ens', 'gy'), parts along dimension 1
- kernel_adjoint: float32 [32, 135], P('ens'), parts along dimension 0
- head_adjoint: float32 [10, 16], P('ens'), parts along dimension 0
There are 2 independent parts, one for each index of `ens`. A program takes and returns all parts, laid end to end along the dimension named above; an argument that names none is the same for every part. Nothing has to cross between parts.
Inputs may be any that keep to these rules, and one draw needn't show every extreme that they name: `flow_state`: components 0 and 4 (density, pressure) lie within 0.9 to 1.1, components 1 to 3 (velocities) within -0.05 to 0.05. `face_flags`: entry [d, i] belongs to the face between cell i and cell i+1 along direction d; its value mod 4 is the HLLC region, its value div 4 the reconstruction choice.
All inputs are finite; a program needn't handle non-finite values.
Results may differ from a plain program's by a relative error of at most 0.0003.
Values sent between devices are 32-bit elements; how exact they have to be, the bound alone decides.
No kernel may reach another device: no remote copies, remote signals or barrier semaphores. Data moves between devices by JAX's collectives and lax.ppermute only.
A program may use at most 128 MiB of HBM per device.

v0:
```python
import functools

import jax
import jax.numpy as jnp
import numpy as np
from jax import lax
from jax.experimental import pallas as pl
from jax.experimental.pallas import tpu as pltpu
from jax.sharding import PartitionSpec as P

STEP = 0.3
FLOOR = 0.01
BELOW, ABOVE = 2, 3
SLABS = 2
VMEM = 48 * 1024 * 1024
F32 = jnp.float32
BF16 = jnp.bfloat16


def rcp(x):
    return pl.reciprocal(x, approx=True)


def shared_terms(v):
    p = [v[i + 1] - v[i] for i in range(5)]
    d = [p[i + 1] - p[i] for i in range(4)]
    h = [(4.0 / 3.0) * x for x in d]
    k = [h[i] * d[i] + FLOOR for i in range(4)]
    g = [x + x for x in h]
    t = [d[i + 1] - d[i] for i in range(3)]
    return p, d, k, g, t


def side_value(pa, pm, pm2, ka, kb, kc, m0, m2, td, t1, smooth, c0, c2):
    i0 = rcp(ka + pa * m0)
    i1 = rcp(kb + pa * pm)
    i2 = rcp(kc + pm * m2)
    w0 = i0 * i0
    w1 = 6.0 * (i1 * i1)
    w2 = 3.0 * (i2 * i2)
    r = rcp(w0 + w1 + w2)
    o0 = jnp.where(smooth, w0 * r, c0)
    o2 = jnp.where(smooth, w2 * r, c2)
    u = o0 * td + o2 * t1
    return (pa + pm2) - u, (i0, i1, i2, w0, w1, w2, r, o0, o2, u)


def side_pull(mu, pa, pm, m0, m2, td, t1, smooth, saved):
    i0, i1, i2, w0, w1, w2, r, o0, o2, u = saved
    mu2 = mu + mu
    rm = jnp.where(smooth, mu2, 0.0) * r
    s0 = (w0 * i0) * rm * (td - u)
    s1 = (w1 * i1) * rm * u
    s2 = (w2 * i2) * rm * (t1 - u)
    pa_bar = s0 * (m0 + pa) - s1 * pm + mu
    pm_bar = s2 * (m2 + pm) - s1 * pa + mu2
    return s0, s1, s2, pa_bar, pm_bar, o0 * mu2, o2 * mu


def hllc_pull(left, right, normal, flags, cot):
    region = flags & 3
    is_right = region >= 2
    star = ((region + 1) & 2) != 0
    n_at = 1 + normal
    tang = [1 + i for i in range(3) if i != normal]
    rl, rr_, pl_, pr_, nl, nr = left[0], right[0], left[4], right[4], left[n_at], right[n_at]

    def sound(r, p):
        inv = rcp(r)
        t = 1.4 * p * inv
        inv_c = lax.rsqrt(t)
        return inv, inv_c, t * inv_c

    inv_rl, inv_cl, cl = sound(rl, pl_)
    inv_rr, inv_cr, cr = sound(rr_, pr_)
    c = 0.5 * (cl + cr)
    r2 = rl + rr_
    inv = rcp(r2 * c)
    nm = 0.5 * (nl + nr)
    gap = (pl_ - pr_) * inv
    sm = nm + gap
    sc = jnp.where(is_right, c, -c)
    s = nm + sc
    pick = [jnp.where(is_right, right[i], left[i]) for i in range(5)]
    r, un, u1, u2, p = pick[0], pick[n_at], pick[tang[0]], pick[tang[1]], pick[4]
    a = s - un
    dl = sm - un
    si = jnp.where(star, rcp(sc - gap), 0.0)
    j = s * si
    kap = j * dl
    g0, gn, g1, g2, ge = cot[0], cot[n_at], cot[tang[0]], cot[tang[1]], cot[4]
    w = un + kap
    half_q = 0.5 * (un * un + u1 * u1 + u2 * u2)
    enthalpy = 3.5 * p + r * half_q
    b = g0 + u1 * g1 + u2 * g2 + un * gn
    m = r * b + enthalpy * ge
    n = gn + sm * ge
    rkap = r * kap
    f_kap = m + r * a * n
    f_a = rkap * n
    si2 = si * si
    s_bar = f_a - f_kap * (dl * sm * si2)
    sm_bar = f_kap * (s * a * si2) + rkap * a * ge
    wr = w * r
    k_bar = [None] * 5
    k_bar[0] = w * (b + half_q * ge) + kap * a * n
    k_bar[n_at] = m + wr * (gn + un * ge) - f_kap * j - f_a
    k_bar[tang[0]] = wr * (g1 + u1 * ge)
    k_bar[tang[1]] = wr * (g2 + u2 * ge)
    k_bar[4] = 3.5 * (w * ge) + gn
    e = sm_bar * inv
    eg = e * gap
    c_half = 0.5 * (jnp.where(is_right, s_bar, -s_bar) - eg * r2)
    n_half = 0.5 * (s_bar + sm_bar)
    r_both = -(eg * c)
    xl = c_half * inv_rl
    xr = c_half * inv_rr
    base_l = {0: r_both - 0.5 * (xl * cl), n_at: n_half, 4: 0.7 * (xl * inv_cl) + e}
    base_r = {0: r_both - 0.5 * (xr * cr), n_at: n_half, 4: 0.7 * (xr * inv_cr) - e}
    l_bar, r_bar = [], []
    for i in range(5):
        kr = jnp.where(is_right, k_bar[i], 0.0)
        kl = k_bar[i] - kr
        l_bar.append(base_l[i] + kl if i in base_l else kl)
        r_bar.append(base_r[i] + kr if i in base_r else kr)
    return l_bar, r_bar


def face_pull(cells, cot, flags, normal):
    stencil = flags >> 2
    smooth = stencil == 0
    c0 = jnp.where(stencil == 1, 1.0, 0.0)
    c2 = jnp.where(stencil == 3, 1.0, 0.0)
    left, right, kept = [], [], []
    for v in cells:
        p, d, k, g, t = shared_terms(v)
        pm2 = p[2] + p[2]
        args_l = (p[1], p[2], p[1] + d[0], p[2] - d[2], t[0] + t[0], t[1])
        args_r = (p[3], p[2], p[3] - d[3], p[2] + d[1], t[2] + t[2], t[1])
        hl, saved_l = side_value(
            p[1], p[2], pm2, k[0], k[1], k[2], *args_l[2:], smooth, c0, c2
        )
        hr, saved_r = side_value(
            p[3], p[2], pm2, k[3], k[2], k[1], *args_r[2:], smooth, c0, c2
        )
        left.append(v[2] + hl * (1.0 / 6.0))
        right.append(v[3] - hr * (1.0 / 6.0))
        kept.append((p, g, args_l, args_r, saved_l, saved_r))
    l_bar, r_bar = hllc_pull(left, right, normal, flags, cot)
    out = []
    for i in range(5):
        p, g, args_l, args_r, saved_l, saved_r = kept[i]
        a0, a1, a2, pa_l, pm_l, x0, x2 = side_pull(
            l_bar[i] * (1.0 / 6.0), *args_l, smooth, saved_l
        )
        b0, b1, b2, pa_r, pm_r, y0, y2 = side_pull(
            r_bar[i] * (-1.0 / 6.0), *args_r, smooth, saved_r
        )
        d0 = a0 * (g[0] + p[1]) + x0
        d1 = (b2 * (g[1] + p[2]) - a1 * g[1]) + (x2 - x0) + y2
        d2 = (a2 * (g[2] - p[2]) - b1 * g[2]) + (y0 - y2) - x2
        d3 = b0 * (g[3] - p[3]) - y0
        p2 = pa_l + (d0 - d1)
        p3 = pm_l + pm_r + (d1 - d2)
        p4 = pa_r + (d2 - d3)
        out.append([d0, -d0 - p2, l_bar[i] + (p2 - p3), r_bar[i] + (p3 - p4), p4 - d3, d3])
    return out


def conserved_pull(s, g):
    half_q = 0.5 * (s[1] * s[1] + s[2] * s[2] + s[3] * s[3])
    return [
        g[0] + s[1] * g[1] + s[2] * g[2] + s[3] * g[3] + half_q * g[4],
        s[0] * (g[1] + s[1] * g[4]),
        s[0] * (g[2] + s[2] * g[4]),
        s[0] * (g[3] + s[3] * g[4]),
        2.5 * g[4],
    ]


def x_kernel(state, cot, flags, kernel, pick, mass, out, w_rows, w_cols, bias, pad, gpad, acc, wide):
    nx = state.shape[1]
    for v in range(5):
        pad[v, pl.ds(2, nx)] = state[v]
        pad[v, pl.ds(0, 2)] = state[v, pl.ds(nx - 2, 2)]
        pad[v, pl.ds(nx + 2, 3)] = state[v, pl.ds(0, 3)]
        gpad[v, pl.ds(0, nx)] = cot[v]
        gpad[v, pl.ds(nx, 1)] = cot[v, pl.ds(0, 1)]
    acc[...] = jnp.zeros_like(acc)

    def step(i, carry):
        x = i * SLABS
        cells = [[pad[v, pl.ds(x + k, SLABS)] for k in range(6)] for v in range(5)]
        g = [gpad[v, pl.ds(x, SLABS)] for v in range(5)]
        face = [STEP * (gpad[v, pl.ds(x + 1, SLABS)] - g[v]) for v in range(5)]
        terms = face_pull(cells, face, flags[0, pl.ds(x, SLABS)], 0)
        own = conserved_pull([cells[v][2] for v in range(5)], g)
        for v in range(5):
            terms[v][2] = terms[v][2] + own[v]
            for s in range(SLABS + 5):
                total = None
                for k in range(6):
                    if 0 <= s - k < SLABS:
                        part = terms[v][k][s - k]
                        total = part if total is None else total + part
                acc[v, x + s] = acc[v, x + s] + total
        return carry

    lax.fori_loop(0, nx // SLABS, step, 0)
    for v in range(5):
        acc[v, pl.ds(nx, 2)] = acc[v, pl.ds(nx, 2)] + acc[v, pl.ds(0, 2)]
        acc[v, pl.ds(2, 3)] = acc[v, pl.ds(2, 3)] + acc[v, pl.ds(nx + 2, 3)]
        out[v] = acc[v, pl.ds(2, nx)]

    ch, taps = kernel.shape
    rows = pick.shape[1] // 512
    w = kernel[...]
    hi = w.astype(BF16)
    lo = (w - hi.astype(F32)).astype(BF16)
    wide[...] = jnp.zeros_like(wide)
    wide[pl.ds(0, ch), pl.ds(0, taps)] = hi.astype(F32)
    wide[pl.ds(ch, ch), pl.ds(0, taps)] = lo.astype(F32)
    both = wide[...].astype(BF16)
    band = jnp.dot(both, pick[...], preferred_element_type=F32)
    top = [band[:ch, y * 512 : (y + 1) * 512] for y in range(rows)]
    low = [band[ch:, y * 512 : (y + 1) * 512] for y in range(rows)]
    full = jnp.concatenate(top + low, axis=0)
    w_rows[...] = full.astype(BF16)
    w_cols[...] = full.T.astype(BF16)
    total = jnp.sum(w * mass[...], axis=1, keepdims=True)
    total = jnp.broadcast_to(total, (ch, 128))
    bias[...] = jnp.concatenate([total] * rows, axis=0)


def y_kernel(state, cot, flags, above, below, own, rim, out, up, down, halo, ghalo, back):
    nx = state.shape[1]
    for v in range(5):
        base = v * nx * 8
        for r in range(BELOW):
            halo[pl.ds(base + 8 - BELOW + r, nx, stride=8), :] = below[r, v]
        for r in range(ABOVE):
            halo[pl.ds(base + r, nx, stride=8), :] = above[r, v]
        ghalo[pl.ds(base, nx, stride=8), :] = above[ABOVE, v]
    row = lax.broadcasted_iota(jnp.int32, (SLABS, 8, 128), 1)
    inside = {}
    for k in (-2, -1, 1, 2, 3):
        inside[k] = (row < 8 + k) if k < 0 else (row >= k)

    def step(i, carry):
        x = i * SLABS
        cells, face = [], []
        for v in range(5):
            at = pl.multiple_of((v * nx + x) * 8, 8)
            rim_rows = halo[pl.ds(at, 8 * SLABS), :].reshape(SLABS, 8, 128)
            mid = state[v, pl.ds(x, SLABS)]
            line = []
            for k in range(-2, 4):
                if k == 0:
                    line.append(mid)
                else:
                    line.append(pltpu.roll(jnp.where(inside[k], mid, rim_rows), (-k) % 8, 1))
            cells.append(line)
            g = cot[v, pl.ds(x, SLABS)]
            g_rim = ghalo[pl.ds(at, 8 * SLABS), :].reshape(SLABS, 8, 128)
            face.append(STEP * (pltpu.roll(jnp.where(inside[1], g, g_rim), 7, 1) - g))
        terms = face_pull(cells, face, flags[1, pl.ds(x, SLABS)], 1)
        for v in range(5):
            at = pl.multiple_of((v * nx + x) * 8, 8)
            mine = own[v, pl.ds(x, SLABS)] + terms[v][2]
            outer = None
            for k in (-2, -1, 1, 2, 3):
                moved = pltpu.roll(terms[v][k + 2], k % 8, 1)
                kept = jnp.where(inside[k], moved, 0.0)
                mine = mine + kept
                left = moved - kept
                outer = left if outer is None else outer + left
            out[v, pl.ds(x, SLABS)] = mine
            back[pl.ds(at, 8 * SLABS), :] = outer.reshape(8 * SLABS, 128)
        return carry

    lax.fori_loop(0, nx // SLABS, step, 0)
    for v in range(5):
        base = v * nx * 8
        for r in range(BELOW):
            rows = back[pl.ds(base + 8 - BELOW + r, nx, stride=8), :]
            if r == BELOW - 1:
                rows = rows + rim[pl.ds(v, nx, stride=16), :]
            down[r, v] = rows
        for r in range(ABOVE):
            rows = back[pl.ds(base + r, nx, stride=8), :]
            if r == 0:
                rows = rows + rim[pl.ds(5 + v, nx, stride=16), :]
            up[r, v] = rows


def z_faces(state, cot, flags, x):
    cells, face = [], []
    for v in range(5):
        mid = state[v, pl.ds(x, SLABS)]
        cells.append([mid if k == 0 else pltpu.roll(mid, (-k) % 128, 2) for k in range(-2, 4)])
        g = cot[v, pl.ds(x, SLABS)]
        face.append(STEP * (pltpu.roll(g, 127, 2) - g))
    terms = face_pull(cells, face, flags[2, pl.ds(x, SLABS)], 2)
    total = []
    for v in range(5):
        t = terms[v][2]
        for k in (-2, -1, 1, 2, 3):
            t = t + pltpu.roll(terms[v][k + 2], k % 128, 2)
        total.append(t)
    return total


def z_kernel(state, cot, flags, first, out):
    half = out.shape[1]

    def step(i, carry):
        x = i * SLABS
        total = z_faces(state, cot, flags, x)
        for v in range(5):
            out[v, pl.ds(x, SLABS)] = first[v, pl.ds(x, SLABS)] + total[v]
        return carry

    lax.fori_loop(0, half // SLABS, step, 0)


def last_kernel(scale, state, cot, flags, first, second, done, from_below, from_above, parts, out, k_out, h_out, halo):
    nx = state.shape[1]
    half = done.shape[1]
    for v in range(5):
        base = v * nx * 8
        for r in range(8):
            if r < ABOVE:
                rows = from_below[r, v]
            elif r >= 8 - BELOW:
                rows = from_above[r - (8 - BELOW), v]
            else:
                rows = jnp.zeros((nx, 128), F32)
            halo[pl.ds(base + r, nx, stride=8), :] = rows

    def put(x, v, value):
        at = pl.multiple_of((v * nx + x) * 8, 8)
        rim = halo[pl.ds(at, 8 * SLABS), :].reshape(SLABS, 8, 128)
        out[v, pl.ds(x, SLABS)] = value + second[v, pl.ds(x, SLABS)] + rim

    def step(i, carry):
        x = i * SLABS
        total = z_faces(state, cot, flags, half + x)
        for v in range(5):
            put(half + x, v, first[v, pl.ds(half + x, SLABS)] + total[v])
            put(x, v, done[v, pl.ds(x, SLABS)])
        return carry

    lax.fori_loop(0, half // SLABS, step, 0)
    total = parts[0]
    for i in range(1, parts.shape[0]):
        total = total + parts[i]
    total = total * scale
    k_out[...] = total[:, : k_out.shape[1]]
    ch = total.shape[0]
    pick = (
        lax.broadcasted_iota(jnp.int32, (8, 128), 1)
        == lax.broadcasted_iota(jnp.int32, (8, 128), 0) + 16
    ).astype(F32)
    heads = lax.dot_general(
        pick,
        total[:, 128:],
        (((1,), (1,)), ((), ())),
        precision=lax.Precision.HIGHEST,
        preferred_element_type=F32,
    )
    h_out[...] = heads[: h_out.shape[0], :ch]


def split(x):
    hi = x.astype(BF16)
    return hi, (x - hi.astype(F32)).astype(BF16)


def over_lanes(a, b):
    return lax.dot_general(a, b, (((1,), (1,)), ((), ())), preferred_element_type=F32)


def c_kernel(
    state, cot, above, below, heads, pick, mass, w_rows, w_cols, bias,
    own, rim, parts,
    t, acc, edge, kg, hg, dsum,
):
    nx = state.shape[1]
    ch = heads.shape[1]
    block, slot = 56, 168

    edge[...] = jnp.zeros_like(edge)
    for v in range(5):
        level = 1.0 if v in (0, 4) else 0.0
        edge[pl.ds(v, nx, stride=16), :] = below[BELOW - 1, v] - level
        edge[pl.ds(5 + v, nx, stride=16), :] = above[0, v] - level

    def fill(x, carry):
        rows = [state[v, x] - (1.0 if v in (0, 4) else 0.0) for v in range(5)]
        rows.append(edge[pl.ds(pl.multiple_of(x * 16, 16), 16), :])
        mid = jnp.concatenate(rows, axis=0)
        at = pl.multiple_of((x + 1) * slot, 8)
        t[pl.ds(at, block), :] = pltpu.roll(mid, 1, 1)
        t[pl.ds(at + block, block), :] = mid
        t[pl.ds(at + 2 * block, block), :] = pltpu.roll(mid, 127, 1)
        return carry

    lax.fori_loop(0, nx, fill, 0)
    t[pl.ds(0, slot), :] = t[pl.ds(nx * slot, slot), :]
    t[pl.ds((nx + 1) * slot, slot), :] = t[pl.ds(slot, slot), :]
    t[pl.ds((nx + 2) * slot, 8), :] = jnp.zeros((8, 128), F32)
    acc[...] = jnp.zeros_like(acc)
    kg[...] = jnp.zeros_like(kg)
    hg[...] = jnp.zeros_like(hg)
    dsum[...] = jnp.zeros_like(dsum)

    r = lax.broadcasted_iota(jnp.int32, (8 * ch, ch), 0)
    q = lax.broadcasted_iota(jnp.int32, (8 * ch, ch), 1)
    spread = ((r & (ch - 1)) == q).astype(F32)
    high = dict(precision=lax.Precision.HIGHEST, preferred_element_type=F32)
    h5 = lax.dot_general(spread, heads[...], (((1,), (1,)), ((), ())), **high)
    e_of = lax.broadcasted_iota(jnp.int32, (5, 40), 0)
    c_of = lax.broadcasted_iota(jnp.int32, (5, 40), 1)
    h40 = jnp.dot(h5, ((c_of >> 3) == e_of).astype(F32), **high)
    y_row = lax.broadcasted_iota(jnp.int32, (8 * ch, 40), 0)
    y_col = lax.broadcasted_iota(jnp.int32, (8 * ch, 40), 1) & 7
    same_y = (y_row >= y_col * ch) & (y_row < (y_col + 1) * ch)
    h_hi, h_lo = split(jnp.where(same_y, STEP * h40, 0.0))
    wide_head = jnp.concatenate(
        [h_hi.astype(F32), h_lo.astype(F32), h_hi.astype(F32)], axis=1
    ).astype(BF16)

    def step(i, carry):
        x = i * 2
        at0 = pl.multiple_of(x * slot, 8)
        at1 = pl.multiple_of((x + 1) * slot, 8)
        s = jnp.concatenate([t[pl.ds(at0, 512), :], t[pl.ds(at1, 512), :]], axis=1).astype(BF16)
        z2 = jnp.dot(w_rows[...], s, preferred_element_type=F32)
        b = bias[...]
        z = z2[: 8 * ch] + z2[8 * ch :] + jnp.concatenate([b, b], axis=1)
        hidden = jnp.tanh(z)
        g = jnp.concatenate(
            [jnp.concatenate([cot[v, x + j] for v in range(5)], axis=0) for j in range(2)], axis=1
        )
        g_hi, g_lo = split(g)
        g_hi32, g_lo32 = g_hi.astype(F32), g_lo.astype(F32)
        g3 = jnp.concatenate([g_hi32, g_hi32, g_lo32], axis=0).astype(BF16)
        d = (1.0 - hidden * hidden) * jnp.dot(wide_head, g3, preferred_element_type=F32)
        hid_hi, hid_lo = split(hidden)
        hid2 = jnp.concatenate([hid_hi, hid_lo], axis=0)
        g2 = jnp.concatenate([g_hi32, g_lo32], axis=0).astype(BF16)
        hg[...] = hg[...] + over_lanes(hid2, g2)
        d_hi, d_lo = split(d)
        d2 = jnp.concatenate([d_hi, d_lo], axis=0)
        k2 = over_lanes(d2, s)
        kg[...] = kg[...] + (k2[: 8 * ch] + k2[8 * ch :])
        dsum[...] = dsum[...] + (d[:, :128] + d[:, 128:])
        wc_hi = w_cols[:, : 8 * ch]
        wc2 = jnp.concatenate([wc_hi, wc_hi], axis=1)
        back = jnp.dot(wc2, d2, preferred_element_type=F32) + jnp.dot(
            w_cols[:, 8 * ch :], d_hi, preferred_element_type=F32
        )
        acc[pl.ds(at0, 504), :] = acc[pl.ds(at0, 504), :] + back[:504, :128]
        acc[pl.ds(at1, 504), :] = acc[pl.ds(at1, 504), :] + back[:504, 128:]
        return carry

    lax.fori_loop(0, nx // 2, step, 0)
    acc[pl.ds(nx * slot, slot), :] = acc[pl.ds(nx * slot, slot), :] + acc[pl.ds(0, slot), :]
    acc[pl.ds(slot, slot), :] = acc[pl.ds(slot, slot), :] + acc[pl.ds((nx + 1) * slot, slot), :]

    def drain(x, carry):
        at = pl.multiple_of((x + 1) * slot, 8)
        total = (
            acc[pl.ds(at + block, block), :]
            + pltpu.roll(acc[pl.ds(at, block), :], 127, 1)
            + pltpu.roll(acc[pl.ds(at + 2 * block, block), :], 1, 1)
        )
        for v in range(5):
            own[v, x] = total[8 * v : 8 * v + 8]
        rim[pl.ds(pl.multiple_of(x * 16, 16), 16), :] = total[40:56]
        return carry

    lax.fori_loop(0, nx, drain, 0)

    grads = jnp.zeros((2 * ch, pick.shape[0]), F32)
    level_sum = jnp.zeros((ch, 1), F32)
    head_sum = jnp.zeros((ch, 40), F32)
    sums = jnp.sum(dsum[...], axis=1, keepdims=True)
    h2 = hg[...]
    h_all = (h2[: 8 * ch, :40] + h2[8 * ch :, :40]) + (h2[: 8 * ch, 40:80] + h2[8 * ch :, 40:80])
    h_all = jnp.where(same_y, h_all, 0.0)
    for y in range(8):
        rows = kg[pl.ds(y * ch, ch), :]
        hi, lo = split(rows)
        pair = jnp.concatenate([hi, lo], axis=0)
        grads = grads + over_lanes(pair, pick[:, y * 512 : (y + 1) * 512])
        level_sum = level_sum + sums[y * ch : (y + 1) * ch]
        head_sum = head_sum + h_all[y * ch : (y + 1) * ch]
    taps = mass.shape[1]
    n_pick = pick.shape[0]
    parts[...] = jnp.zeros_like(parts)
    parts[:, pl.ds(0, n_pick)] = grads[:ch] + grads[ch:]
    parts[:, pl.ds(0, taps)] = parts[:, pl.ds(0, taps)] + level_sum * mass[...]
    e_row = lax.broadcasted_iota(jnp.int32, (40, 128), 0) >> 3
    e_col = lax.broadcasted_iota(jnp.int32, (40, 128), 1) - 16
    head_out = jnp.dot(head_sum * STEP, (e_row == e_col).astype(F32), **high)
    parts[:, pl.ds(128, 128)] = parts[:, pl.ds(128, 128)] + head_out


def band_pick():
    pick = np.zeros((144, 8, 512), np.float32)
    for ox in range(3):
        for oz in range(3):
            for v in range(5):
                for y in range(8):
                    for oy in range(3):
                        row = y + oy - 1
                        if row < 0:
                            at = 40 + v
                        elif row > 7:
                            at = 45 + v
                        else:
                            at = v * 8 + row
                        pick[(oy * 9 + ox * 3 + oz) * 5 + v, y, (ox * 3 + oz) * 56 + at] = 1.0
    return pick.reshape(144, 8 * 512)


def call(kernel, outs, scratch, flops, moved):
    return pl.pallas_call(
        kernel,
        out_shape=outs,
        scratch_shapes=scratch,
        compiler_params=pltpu.CompilerParams(vmem_limit_bytes=VMEM),
        cost_estimate=pl.CostEstimate(flops=flops, bytes_accessed=moved, transcendentals=0),
    )


def body(pick, mass, state, cot, flags, kernel, heads):
    _, nx, ny, nz = state.shape
    ch, taps = kernel.shape
    count = lax.axis_size("gy")
    cells = nx * ny * nz
    shape = lambda *dims: jax.ShapeDtypeStruct(dims, F32)
    full = shape(5, nx, ny, nz)
    up = [(i, (i + 1) % count) for i in range(count)]
    down = [((i + 1) % count, i) for i in range(count)]
    pick = jnp.asarray(pick, BF16)
    mass = jnp.asarray(mass)

    rows = lambda a, lo, hi: jnp.transpose(a[:, :, lo:hi], (2, 0, 1, 3))
    head = jnp.concatenate([rows(state, 0, ABOVE), rows(cot, 0, 1)], axis=0)
    above = lax.ppermute(head, "gy", down)
    below = lax.ppermute(rows(state, ny - BELOW, ny), "gy", up)

    vm = pltpu.VMEM
    first, w_rows, w_cols, bias = call(
        x_kernel,
        (
            full,
            jax.ShapeDtypeStruct((16 * ch, 512), BF16),
            jax.ShapeDtypeStruct((512, 16 * ch), BF16),
            shape(8 * ch, 128),
        ),
        [
            vm((5, nx + 5, ny, nz), F32),
            vm((5, nx + 1, ny, nz), F32),
            vm((5, nx + 5, ny, nz), F32),
            vm((2 * ch, pick.shape[0]), F32),
        ],
        1000 * cells,
        1 << 22,
    )(state, cot, flags, kernel, pick, mass)
    own, rim, parts = call(
        c_kernel,
        (full, shape(16 * nx, nz), shape(ch, 256)),
        [
            vm(((nx + 2) * 168 + 8, nz), F32),
            vm(((nx + 2) * 168 + 8, nz), F32),
            vm((16 * nx, nz), F32),
            vm((8 * ch, 512), F32),
            vm((16 * ch, 80), F32),
            vm((8 * ch, 128), F32),
        ],
        1000 * cells,
        1 << 22,
    )(state, cot, above, below, heads, pick, mass, w_rows, w_cols, bias)
    gathered = lax.all_gather(parts, "gy")
    second, give_up, give_down = call(
        y_kernel,
        (full, shape(ABOVE, 5, nx, nz), shape(BELOW, 5, nx, nz)),
        [vm((5 * nx * 8, nz), F32)] * 3,
        1000 * cells,
        1 << 22,
    )(state, cot, flags, above, below, own, rim)
    from_below = lax.ppermute(give_up, "gy", up)
    from_above = lax.ppermute(give_down, "gy", down)
    done = call(z_kernel, shape(5, nx // 2, ny, nz), [], 500 * cells, 1 << 22)(
        state, cot, flags, first
    )
    scale = float(cells * count) ** (-0.5)
    return call(
        functools.partial(last_kernel, scale),
        (full, shape(ch, taps), shape(5, ch)),
        [vm((5 * nx * 8, nz), F32)],
        500 * cells,
        1 << 22,
    )(state, cot, flags, first, second, done, from_below, from_above, gathered)


def solution(mesh):
    pick = band_pick()
    mass = np.zeros((16, 135), np.float32)
    mass[:, 0::5] = 1.0
    mass[:, 4::5] = 1.0
    split_y = P(None, "ens", "gy", None)
    return jax.shard_map(
        functools.partial(body, pick, mass),
        mesh=mesh,
        in_specs=(split_y, split_y, split_y, P(), P()),
        out_specs=(split_y, P("ens", None), P("ens", None)),
        check_vma=False,
    )
```

profile of v0, /device:TPU:0, one launch (start us, length us, event | category | flops | bytes accessed | tf_op | source)
XLA Modules:
  0.0 54.2 jit_solution(6412023208880218724)
XLA Ops:
  0.6 0.0 copy-start.5
  0.6 0.0 copy-start.1
  0.7 0.0 copy-start
  0.7 0.0 copy-start.4
  0.7 0.0 copy-start.6
  0.7 1.1 %slice.10 = f32[5,16,1,128]{3,2,1,0:T(1,128)S(1)} slice(f32[5,16,8,128]{3,2,1,0:T(8,128)} %cot.9), slice={[0:5], [0:16], [0:1], [0:128]} | slice | bytes 81920 | tf_op jit(solution)/shard_map/slice | solution.py:550
  1.8 1.0 %slice.9 = f32[5,16,3,128]{3,2,1,0:T(4,128)S(1)} slice(f32[5,16,8,128]{3,2,1,0:T(8,128)} %state.9), slice={[0:5], [0:16], [0:3], [0:128]} | slice | bytes 245760 | tf_op jit(solution)/shard_map/slice | solution.py:550
  2.8 5.5 %collective-permute-start = (f32[4,5,16,128]{3,2,1,0:T(8,128)S(1)}, f32[4,5,16,128]{3,2,1,0:T(8,128)S(1)}, u32[]{:S(2)}, u32[]{:S(2)}) collective-permute-start(f32[4,5,16,128]{3,2,1,0:T(8,128)S(1)} %pad_maximum_fusion), channel_id=1, source_target_pairs={{1,0},{2,1},{3,2},{4,3},{5,4},{6,5},{7,6},{8,7},{9,8},{10,9},{11,1... | collective-permute-start | bytes 491528 | tf_op jit(solution)/shard_map/ppermute | solution.py:552
  8.3 1.0 %slice.11 = f32[5,16,2,128]{3,2,1,0:T(2,128)S(1)} slice(f32[5,16,8,128]{3,2,1,0:T(8,128)} %state.9), slice={[0:5], [0:16], [6:8], [0:128]} | slice | bytes 163840 | tf_op jit(solution)/shard_map/slice | solution.py:550
  9.3 0.1 collective-permute-start.1
  9.4 0.0 copy-done.5
  9.4 0.0 copy-done.1
  9.4 0.0 copy-done
  9.4 0.0 copy-done.4
  9.4 0.0 copy-done.6
  9.4 0.0 copy-start.2
  9.4 1.3 %copy-done.2 = bf16[144,4096]{1,0:T(8,128)(2,1)S(1)} copy-done((bf16[144,4096]{1,0:T(8,128)(2,1)S(1)}, bf16[144,4096]{1,0:T(8,128)(2,1)}, u32[]{:S(2)}) %copy-start.2) | copy-done | bytes 1179672
  10.7 3.2 %shard_map.94 = (f32[5,16,8,128]{3,2,1,0:T(8,128)S(1)}, bf16[256,512]{1,0:T(8,128)(2,1)S(1)}, bf16[512,256]{1,0:T(8,128)(2,1)S(1)}, f32[128,128]{1,0:T(8,128)S(1)}) custom-call(f32[5,16,8,128]{3,2,1,0:T(8,128)S(1)} %copy-done, f32[5,16,8,128]{3,2,1,0:T(8,128)S(1)} %copy-done.1, s32[3,16,8,128]{3,2,1,0:T(8,128)S(1)} %copy-done.4, f32[16,135]{1,0:T(8,128)S(1)} %copy-done.6, ...), custom_call_target="tpu_custom_call" | custom-call | flops 16384000 | bytes 4194304 | tf_op jit(solution)/shard_map/pallas_call | solution.py:556
  13.9 0.0 copy-start.3
  13.9 1.8 %shard_map.97.done = f32[5,8,8,128]{3,2,1,0:T(8,128)S(1)} custom-call(f32[5,16,8,128]{3,2,1,0:T(8,128)S(1)} %copy-done, f32[5,16,8,128]{3,2,1,0:T(8,128)S(1)} %copy-done.1, s32[3,16,8,128]{3,2,1,0:T(8,128)S(1)} %copy-done.4, f32[5,16,8,128]{3,2,1,0:T(8,128)S(1)} %get-tuple-element.13.first), custom_call_target="tpu_custom_call" | custom-call | flops 8192000 | bytes 4194304 | tf_op jit(solution)/shard_map/pallas_call | solution.py:597
  15.8 0.2 collective-permute-done.1.below
  15.9 0.0 collective-permute-done.above
  15.9 0.0 copy-done.3
  15.9 0.0 copy-done.7
  15.9 9.4 %shard_map.95 = (f32[5,16,8,128]{3,2,1,0:T(8,128)S(1)}, f32[256,128]{1,0:T(8,128)S(1)}, f32[16,256]{1,0:T(8,128)S(1)}) custom-call(f32[5,16,8,128]{3,2,1,0:T(8,128)S(1)} %copy-done, f32[5,16,8,128]{3,2,1,0:T(8,128)S(1)} %copy-done.1, f32[4,5,16,128]{3,2,1,0:T(8,128)S(1)} %collective-permute-done.above, f32[2,5,16,128]{3,2,1,0:T(8,128)S(1)} %collective-permute-done.1.below, ...), custom_call_target="tpu_custom_call" | custom-call | flops 16384000 | bytes 4194304 | tf_op jit(solution)/shard_map/pallas_call | solution.py:573
  25.3 3.1 %shard_map.96 = (f32[5,16,8,128]{3,2,1,0:T(8,128)S(1)}, f32[3,5,16,128]{3,2,1,0:T(8,128)S(1)}, f32[2,5,16,128]{3,2,1,0:T(8,128)S(1)}) custom-call(f32[5,16,8,128]{3,2,1,0:T(8,128)S(1)} %copy-done, f32[5,16,8,128]{3,2,1,0:T(8,128)S(1)} %copy-done.1, s32[3,16,8,128]{3,2,1,0:T(8,128)S(1)} %copy-done.4, f32[4,5,16,128]{3,2,1,0:T(8,128)S(1)} %collective-permute-done.above, ...), custom_call_target="tpu_custom_call" | custom-call | flops 16384000 | bytes 4194304 | tf_op jit(solution)/shard_map/pallas_call | solution.py:588
  28.5 4.3 %collective-permute-start.3 = (f32[2,5,16,128]{3,2,1,0:T(8,128)S(1)}, f32[2,5,16,128]{3,2,1,0:T(8,128)S(1)}, u32[]{:S(2)}, u32[]{:S(2)}) collective-permute-start(f32[2,5,16,128]{3,2,1,0:T(8,128)S(1)} %get-tuple-element.21), channel_id=1, source_target_pairs={{1,0},{2,1},{3,2},{4,3},{5,4},{6,5},{7,6},{8,7},{9,8},{10,9},{11,1... | collective-permute-start | bytes 245768 | tf_op jit(solution)/shard_map/ppermute | solution.py:596
  32.8 0.0 collective-permute-start.2
  32.8 18.8 %all-gather = f32[256,256]{1,0:T(8,128)S(1)} all-gather(f32[16,256]{1,0:T(8,128)S(1)} %get-tuple-element.22), channel_id=2, replica_groups=mesh['ens'=2,'gy'=16] {'gy'}, dimensions={0}, use_global_device_ids=true | all-gather | bytes 278528 | tf_op jit(solution)/shard_map/all_gather | solution.py:587
  51.6 0.0 collective-permute-done.3.from_above
  51.6 0.0 collective-permute-done.2.from_below
  51.6 2.7 %shard_map.98 = (f32[5,16,8,128]{3,2,1,0:T(8,128)}, f32[16,135]{1,0:T(8,128)}, f32[5,16]{1,0:T(8,128)}) custom-call(f32[5,16,8,128]{3,2,1,0:T(8,128)S(1)} %copy-done, f32[5,16,8,128]{3,2,1,0:T(8,128)S(1)} %copy-done.1, s32[3,16,8,128]{3,2,1,0:T(8,128)S(1)} %copy-done.4, f32[5,16,8,128]{3,2,1,0:T(8,128)S(1)} %get-tuple-element.13.first, ...), custom_call_target="tpu_custom_call" | custom-call | flops 8192000 | bytes 4194304 | tf_op jit(solution)/shard_map/pallas_call | solution.py:601
  (4 shorter events, 0.0 us)
Async XLA Ops:
  0.6 8.8 %copy-start.5 = (f32[16,135]{1,0:T(8,128)S(1)}, f32[16,135]{1,0:T(8,128)}, u32[]{:S(2)}) copy-start(f32[16,135]{1,0:T(8,128)} %constant.5.clone.mass) | copy-start | bytes 25924
  0.6 8.8 %copy-start.1 = (f32[5,16,8,128]{3,2,1,0:T(8,128)S(1)}, f32[5,16,8,128]{3,2,1,0:T(8,128)}, u32[]{:S(2)}) copy-start(f32[5,16,8,128]{3,2,1,0:T(8,128)} %cot.9) | copy-start | bytes 983044
  0.7 8.8 %copy-start = (f32[5,16,8,128]{3,2,1,0:T(8,128)S(1)}, f32[5,16,8,128]{3,2,1,0:T(8,128)}, u32[]{:S(2)}) copy-start(f32[5,16,8,128]{3,2,1,0:T(8,128)} %state.9) | copy-start | bytes 983044
  0.7 8.8 %copy-start.4 = (s32[3,16,8,128]{3,2,1,0:T(8,128)S(1)}, s32[3,16,8,128]{3,2,1,0:T(8,128)}, u32[]{:S(2)}) copy-start(s32[3,16,8,128]{3,2,1,0:T(8,128)} %flags.7) | copy-start | bytes 589828
  0.7 8.8 %copy-start.6 = (f32[16,135]{1,0:T(8,128)S(1)}, f32[16,135]{1,0:T(8,128)}, u32[]{:S(2)}) copy-start(f32[16,135]{1,0:T(8,128)} %kernel.1) | copy-start | bytes 25924
  2.8 13.1 %collective-permute-start = (f32[4,5,16,128]{3,2,1,0:T(8,128)S(1)}, f32[4,5,16,128]{3,2,1,0:T(8,128)S(1)}, u32[]{:S(2)}, u32[]{:S(2)}) collective-permute-start(f32[4,5,16,128]{3,2,1,0:T(8,128)S(1)} %pad_maximum_fusion), channel_id=1, source_target_pairs={{1,0},{2,1},{3,2},{4,3},{5,4},{6,5},{7,6},{8,7},{9,8},{10,9},{11,1... | collective-permute-start | bytes 491528 | tf_op jit(solution)/shard_map/ppermute | solution.py:552
  9.3 6.6 %collective-permute-start.1 = (f32[2,5,16,128]{3,2,1,0:T(8,128)S(1)}, f32[2,5,16,128]{3,2,1,0:T(8,128)S(1)}, u32[]{:S(2)}, u32[]{:S(2)}) collective-permute-start(f32[2,5,16,128]{3,2,1,0:T(8,128)S(1)} %bitcast.13), channel_id=1, source_target_pairs={{0,1},{1,2},{2,3},{3,4},{4,5},{5,6},{6,7},{7,8},{8,9},{9,10},{10,1... | collective-permute-start | bytes 245768 | tf_op jit(solution)/shard_map/ppermute | solution.py:553
  9.4 1.3 %copy-start.2 = (bf16[144,4096]{1,0:T(8,128)(2,1)S(1)}, bf16[144,4096]{1,0:T(8,128)(2,1)}, u32[]{:S(2)}) copy-start(bf16[144,4096]{1,0:T(8,128)(2,1)} %constant.4.clone.pick) | copy-start | bytes 3538948
  13.9 2.0 %copy-start.3 = (bf16[144,4096]{1,0:T(8,128)(2,1)S(1)}, bf16[144,4096]{1,0:T(8,128)(2,1)}, u32[]{:S(2)}) copy-start(bf16[144,4096]{1,0:T(8,128)(2,1)} %constant.4.clone.pick) | copy-start | bytes 3538948
  13.9 2.0 %copy-start.7 = (f32[5,16]{1,0:T(8,128)S(1)}, f32[5,16]{1,0:T(8,128)}, u32[]{:S(2)}) copy-start(f32[5,16]{1,0:T(8,128)} %heads.1) | copy-start | bytes 964
  28.5 23.1 %collective-permute-start.3 = (f32[2,5,16,128]{3,2,1,0:T(8,128)S(1)}, f32[2,5,16,128]{3,2,1,0:T(8,128)S(1)}, u32[]{:S(2)}, u32[]{:S(2)}) collective-permute-start(f32[2,5,16,128]{3,2,1,0:T(8,128)S(1)} %get-tuple-element.21), channel_id=1, source_target_pairs={{1,0},{2,1},{3,2},{4,3},{5,4},{6,5},{7,6},{8,7},{9,8},{10,9},{11,1... | collective-permute-start | bytes 245768 | tf_op jit(solution)/shard_map/ppermute | solution.py:596
  32.8 18.8 %collective-permute-start.2 = (f32[3,5,16,128]{3,2,1,0:T(8,128)S(1)}, f32[3,5,16,128]{3,2,1,0:T(8,128)S(1)}, u32[]{:S(2)}, u32[]{:S(2)}) collective-permute-start(f32[3,5,16,128]{3,2,1,0:T(8,128)S(1)} %get-tuple-element.20), channel_id=1, source_target_pairs={{0,1},{1,2},{2,3},{3,4},{4,5},{5,6},{6,7},{7,8},{8,9},{9,10},{10,1... | collective-permute-start | bytes 368648 | tf_op jit(solution)/shard_map/ppermute | solution.py:595
where the time goes:
time: 54.5 us; the launch traced here: 54.2 us
  Pallas kernels  20.2 us (37%)
  blocking collectives  18.8 us (34%)
  starting transfers between devices  9.87 us (18%)
  local copies, waits for them, and re-layouts  4.39 us (8%)
  between operations  0.78 us (1%)
    all_gather x1, blocking collectives, body(): gathered = lax.all_gather(parts, 'gy')  18.8 us
    pallas_call x1, Pallas kernels, body(): call(c_kernel, (full, shape(16 * nx, nz), shape(ch, 256)), [vm(((nx + 2)...  9.38 us
    ppermute x1, starting transfers between devices, body(): above = lax.ppermute(head, 'gy', down)  5.5 us
    ppermute x1, starting transfers between devices, body(): from_above = lax.ppermute(give_down, 'gy', down)  4.31 us
    pallas_call x1, Pallas kernels, body(): call(x_kernel, (full, jax.ShapeDtypeStruct((16 * ch, 512), BF16), jax.Sha...  3.21 us
    pallas_call x1, Pallas kernels, body(): call(y_kernel, (full, shape(ABOVE, 5, nx, nz), shape(BELOW, 5, nx, nz)),...  3.12 us
    slice x3, local copies, waits for them, and re-layouts, body(): rows = lambda a, lo, hi: jnp.transpose(a[:, :, lo:hi], (2, 0, 1, 3))  3.07 us
    pallas_call x1, Pallas kernels, body(): call(functools.partial(last_kernel, scale), (full, shape(ch, taps), shape...  2.66 us
  transfers between devices with their start and end apart: 4, of which 1 were waited for; matrix products, arithmetic and copies ran while one was open for 2% of the time, Pallas kernels for 9%

commit v1 on v0

--- a/solution.py
+++ b/solution.py
@@ -12,6 +12,7 @@
 FLOOR = 0.01
 BELOW, ABOVE = 2, 3
 SLABS = 2
+WIDE = 4
 VMEM = 48 * 1024 * 1024
 F32 = jnp.float32
 BF16 = jnp.bfloat16
@@ -178,7 +179,29 @@
     ]
 
 
-def x_kernel(state, cot, flags, kernel, pick, mass, out, w_rows, w_cols, bias, pad, gpad, acc, wide):
+def is_even():
+    return lax.rem(lax.axis_index("gy"), 2) == 0
+
+
+def pack_kernel(state, cot, twin, other):
+    even = is_even()
+    nx = twin.shape[2]
+    for v in range(5):
+        base = v * nx * 8
+        for r in range(ABOVE + 1):
+            if r < ABOVE:
+                low = state[pl.ds(base + r, nx, stride=8), :]
+            else:
+                low = cot[pl.ds(base, nx, stride=8), :]
+            if r < BELOW:
+                top = state[pl.ds(base + 8 - BELOW + r, nx, stride=8), :]
+            else:
+                top = low
+            twin[r, v] = jnp.where(even, top, low)
+            other[r, v] = jnp.where(even, low, top)
+
+
+def x_kernel(state, cot, flags, kernel, pick, code, mass, out, w_rows, w_cols, bias, pad, gpad, acc, wide):
     nx = state.shape[1]
     for v in range(5):
         pad[v, pl.ds(2, nx)] = state[v]
@@ -213,34 +236,51 @@
         out[v] = acc[v, pl.ds(2, nx)]
 
     ch, taps = kernel.shape
-    rows = pick.shape[1] // 512
     w = kernel[...]
-    hi = w.astype(BF16)
-    lo = (w - hi.astype(F32)).astype(BF16)
+    hi, lo = split(w)
     wide[...] = jnp.zeros_like(wide)
     wide[pl.ds(0, ch), pl.ds(0, taps)] = hi.astype(F32)
     wide[pl.ds(ch, ch), pl.ds(0, taps)] = lo.astype(F32)
-    both = wide[...].astype(BF16)
-    band = jnp.dot(both, pick[...], preferred_element_type=F32)
-    top = [band[:ch, y * 512 : (y + 1) * 512] for y in range(rows)]
-    low = [band[ch:, y * 512 : (y + 1) * 512] for y in range(rows)]
-    full = jnp.concatenate(top + low, axis=0)
+    base = jnp.dot(wide[...].astype(BF16), pick[...], preferred_element_type=F32)
+    kind = jnp.broadcast_to(code[0:1], base.shape)
+    main = jnp.where(kind < 3, base, 0.0)
+    bands = []
+    for y in range(8):
+        rows = main
+        if y == 0:
+            rows = jnp.where(kind == 0, 0.0, rows)
+        if y == 7:
+            rows = jnp.where(kind == 2, 0.0, rows)
+        if y != 1:
+            rows = pltpu.roll(rows, (y - 1) % 512, 1)
+        if y == 0:
+            rows = rows + jnp.where(kind == 8, base, 0.0)
+        if y == 7:
+            rows = rows + jnp.where(kind == 9, base, 0.0)
+        bands.append(rows)
+    full = jnp.concatenate([b[:ch] for b in bands] + [b[ch:] for b in bands], axis=0)
     w_rows[...] = full.astype(BF16)
-    w_cols[...] = full.T.astype(BF16)
+    cols = full.T.astype(BF16)
+    w_cols[...] = jnp.concatenate([cols[:, : 8 * ch], cols], axis=1)
     total = jnp.sum(w * mass[...], axis=1, keepdims=True)
     total = jnp.broadcast_to(total, (ch, 128))
-    bias[...] = jnp.concatenate([total] * rows, axis=0)
-
-
-def y_kernel(state, cot, flags, above, below, own, rim, out, up, down, halo, ghalo, back):
-    nx = state.shape[1]
-    for v in range(5):
-        base = v * nx * 8
-        for r in range(BELOW):
-            halo[pl.ds(base + 8 - BELOW + r, nx, stride=8), :] = below[r, v]
-        for r in range(ABOVE):
-            halo[pl.ds(base + r, nx, stride=8), :] = above[r, v]
-        ghalo[pl.ds(base, nx, stride=8), :] = above[ABOVE, v]
+    bias[...] = jnp.concatenate([total] * 8, axis=0)
+
+
+def y_faces(x0, state, cot, flags, twin, other, own, first, out, halo, ghalo, back):
+    part = out.shape[1]
+    even = is_even()
+    for v in range(5):
+        base = v * part * 8
+        for r in range(ABOVE + 1):
+            a, b = twin[r, v, pl.ds(x0, part)], other[r, v, pl.ds(x0, part)]
+            above = jnp.where(even, a, b)
+            if r < ABOVE:
+                halo[pl.ds(base + r, part, stride=8), :] = above
+            else:
+                ghalo[pl.ds(base, part, stride=8), :] = above
+            if r < BELOW:
+                halo[pl.ds(base + 8 - BELOW + r, part, stride=8), :] = jnp.where(even, b, a)
     row = lax.broadcasted_iota(jnp.int32, (SLABS, 8, 128), 1)
     inside = {}
     for k in (-2, -1, 1, 2, 3):
@@ -250,9 +290,9 @@
         x = i * SLABS
         cells, face = [], []
         for v in range(5):
-            at = pl.multiple_of((v * nx + x) * 8, 8)
+            at = pl.multiple_of((v * part + x) * 8, 8)
             rim_rows = halo[pl.ds(at, 8 * SLABS), :].reshape(SLABS, 8, 128)
-            mid = state[v, pl.ds(x, SLABS)]
+            mid = state[v, pl.ds(x0 + x, SLABS)]
             line = []
             for k in range(-2, 4):
                 if k == 0:
@@ -260,13 +300,13 @@
                 else:
                     line.append(pltpu.roll(jnp.where(inside[k], mid, rim_rows), (-k) % 8, 1))
             cells.append(line)
-            g = cot[v, pl.ds(x, SLABS)]
+            g = cot[v, pl.ds(x0 + x, SLABS)]
             g_rim = ghalo[pl.ds(at, 8 * SLABS), :].reshape(SLABS, 8, 128)
             face.append(STEP * (pltpu.roll(jnp.where(inside[1], g, g_rim), 7, 1) - g))
-        terms = face_pull(cells, face, flags[1, pl.ds(x, SLABS)], 1)
+        terms = face_pull(cells, face, flags[1, pl.ds(x0 + x, SLABS)], 1)
         for v in range(5):
-            at = pl.multiple_of((v * nx + x) * 8, 8)
-            mine = own[v, pl.ds(x, SLABS)] + terms[v][2]
+            at = pl.multiple_of((v * part + x) * 8, 8)
+            mine = own[v, pl.ds(x0 + x, SLABS)] + first[v, pl.ds(x0 + x, SLABS)] + terms[v][2]
             outer = None
             for k in (-2, -1, 1, 2, 3):
                 moved = pltpu.roll(terms[v][k + 2], k % 8, 1)
@@ -278,19 +318,33 @@
             back[pl.ds(at, 8 * SLABS), :] = outer.reshape(8 * SLABS, 128)
         return carry
 
-    lax.fori_loop(0, nx // SLABS, step, 0)
-    for v in range(5):
-        base = v * nx * 8
-        for r in range(BELOW):
-            rows = back[pl.ds(base + 8 - BELOW + r, nx, stride=8), :]
-            if r == BELOW - 1:
-                rows = rows + rim[pl.ds(v, nx, stride=16), :]
-            down[r, v] = rows
+    lax.fori_loop(0, part // SLABS, step, 0)
+
+
+def y_kernel(state, cot, flags, twin, other, own, first, out, back, halo, ghalo):
+    y_faces(0, state, cot, flags, twin, other, own, first, out, halo, ghalo, back)
+
+
+def y_last_kernel(state, cot, flags, twin, other, own, first, back0, rim, order, out, give_twin, give_other, halo, ghalo, back1):
+    del order
+    nx = state.shape[1]
+    part = out.shape[1]
+    y_faces(nx - part, state, cot, flags, twin, other, own, first, out, halo, ghalo, back1)
+    even = is_even()
+    for v in range(5):
+        base = v * part * 8
         for r in range(ABOVE):
-            rows = back[pl.ds(base + r, nx, stride=8), :]
-            if r == 0:
-                rows = rows + rim[pl.ds(5 + v, nx, stride=16), :]
-            up[r, v] = rows
+            for h, back in ((0, back0), (1, back1)):
+                rows = back[pl.ds(base + r, part, stride=8), :]
+                if r == 0:
+                    rows = rows + rim[pl.ds(h * part * 16 + 5 + v, part, stride=16), :]
+                up = rows
+                if r < BELOW:
+                    rows = back[pl.ds(base + 8 - BELOW + r, part, stride=8), :]
+                    if r == BELOW - 1:
+                        rows = rows + rim[pl.ds(h * part * 16 + v, part, stride=16), :]
+                give_twin[r, v, pl.ds(h * part, part)] = jnp.where(even, up, rows)
+                give_other[r, v, pl.ds(h * part, part)] = jnp.where(even, rows, up)
 
 
 def z_faces(state, cot, flags, x):
@@ -310,51 +364,54 @@
     return total
 
 
-def z_kernel(state, cot, flags, first, out):
+def z_kernel(state, cot, flags, before, order, order2, out):
+    del order, order2
     half = out.shape[1]
 
     def step(i, carry):
         x = i * SLABS
         total = z_faces(state, cot, flags, x)
         for v in range(5):
-            out[v, pl.ds(x, SLABS)] = first[v, pl.ds(x, SLABS)] + total[v]
+            out[v, pl.ds(x, SLABS)] = before[v, pl.ds(x, SLABS)] + total[v]
         return carry
 
     lax.fori_loop(0, half // SLABS, step, 0)
 
 
-def last_kernel(scale, state, cot, flags, first, second, done, from_below, from_above, parts, out, k_out, h_out, halo):
+def z_last_kernel(state, cot, flags, done, before, twin, other, order, out, halo):
+    del order
     nx = state.shape[1]
     half = done.shape[1]
+    even = is_even()
     for v in range(5):
         base = v * nx * 8
         for r in range(8):
             if r < ABOVE:
-                rows = from_below[r, v]
+                rows = jnp.where(even, other[r, v], twin[r, v])
             elif r >= 8 - BELOW:
-                rows = from_above[r - (8 - BELOW), v]
+                q = r - (8 - BELOW)
+                rows = jnp.where(even, twin[q, v], other[q, v])
             else:
                 rows = jnp.zeros((nx, 128), F32)
             halo[pl.ds(base + r, nx, stride=8), :] = rows
 
     def put(x, v, value):
         at = pl.multiple_of((v * nx + x) * 8, 8)
-        rim = halo[pl.ds(at, 8 * SLABS), :].reshape(SLABS, 8, 128)
-        out[v, pl.ds(x, SLABS)] = value + second[v, pl.ds(x, SLABS)] + rim
+        out[v, pl.ds(x, SLABS)] = value + halo[pl.ds(at, 8 * SLABS), :].reshape(SLABS, 8, 128)
 
     def step(i, carry):
         x = i * SLABS
         total = z_faces(state, cot, flags, half + x)
         for v in range(5):
-            put(half + x, v, first[v, pl.ds(half + x, SLABS)] + total[v])
+            put(half + x, v, before[v, pl.ds(x, SLABS)] + total[v])
             put(x, v, done[v, pl.ds(x, SLABS)])
         return carry
 
     lax.fori_loop(0, half // SLABS, step, 0)
-    total = parts[0]
-    for i in range(1, parts.shape[0]):
-        total = total + parts[i]
-    total = total * scale
+
+
+def sum_kernel(scale, mine, theirs, k_out, h_out):
+    total = (mine[...] + theirs[...]) * scale
     k_out[...] = total[:, : k_out.shape[1]]
     ch = total.shape[0]
     pick = (
@@ -381,7 +438,7 @@
 
 
 def c_kernel(
-    state, cot, above, below, heads, pick, mass, w_rows, w_cols, bias,
+    state, cot, twin, other, heads, pick, code, mass, w_rows, w_cols, bias,
     own, rim, parts,
     t, acc, edge, kg, hg, dsum,
 ):
@@ -389,11 +446,14 @@
     ch = heads.shape[1]
     block, slot = 56, 168
 
+    even = is_even()
     edge[...] = jnp.zeros_like(edge)
     for v in range(5):
         level = 1.0 if v in (0, 4) else 0.0
-        edge[pl.ds(v, nx, stride=16), :] = below[BELOW - 1, v] - level
-        edge[pl.ds(5 + v, nx, stride=16), :] = above[0, v] - level
+        below = jnp.where(even, other[BELOW - 1, v], twin[BELOW - 1, v])
+        above = jnp.where(even, twin[0, v], other[0, v])
+        edge[pl.ds(v, nx, stride=16), :] = below - level
+        edge[pl.ds(5 + v, nx, stride=16), :] = above - level
 
     def fill(x, carry):
         rows = [state[v, x] - (1.0 if v in (0, 4) else 0.0) for v in range(5)]
@@ -431,40 +491,44 @@
     ).astype(BF16)
 
     def step(i, carry):
-        x = i * 2
-        at0 = pl.multiple_of(x * slot, 8)
-        at1 = pl.multiple_of((x + 1) * slot, 8)
-        s = jnp.concatenate([t[pl.ds(at0, 512), :], t[pl.ds(at1, 512), :]], axis=1).astype(BF16)
+        x = i * WIDE
+        at = [pl.multiple_of((x + j) * slot, 8) for j in range(WIDE)]
+        s = jnp.concatenate([t[pl.ds(a, 512), :] for a in at], axis=1).astype(BF16)
         z2 = jnp.dot(w_rows[...], s, preferred_element_type=F32)
-        b = bias[...]
-        z = z2[: 8 * ch] + z2[8 * ch :] + jnp.concatenate([b, b], axis=1)
+        z = z2[: 8 * ch] + z2[8 * ch :] + jnp.concatenate([bias[...]] * WIDE, axis=1)
         hidden = jnp.tanh(z)
         g = jnp.concatenate(
-            [jnp.concatenate([cot[v, x + j] for v in range(5)], axis=0) for j in range(2)], axis=1
+            [jnp.concatenate([cot[v, x + j] for v in range(5)], axis=0) for j in range(WIDE)], axis=1
         )
         g_hi, g_lo = split(g)
         g_hi32, g_lo32 = g_hi.astype(F32), g_lo.astype(F32)
         g3 = jnp.concatenate([g_hi32, g_hi32, g_lo32], axis=0).astype(BF16)
         d = (1.0 - hidden * hidden) * jnp.dot(wide_head, g3, preferred_element_type=F32)
-        hid_hi, hid_lo = split(hidden)
-        hid2 = jnp.concatenate([hid_hi, hid_lo], axis=0)
+        d_hi, d_lo = split(d)
+        back = jnp.dot(
+            w_cols[...], jnp.concatenate([d_hi, d_lo, d_hi], axis=0), preferred_element_type=F32
+        )
+        k2 = over_lanes(jnp.concatenate([d_hi, d_lo], axis=0), s)
+        hid2 = jnp.concatenate(split(hidden), axis=0)
         g2 = jnp.concatenate([g_hi32, g_lo32], axis=0).astype(BF16)
         hg[...] = hg[...] + over_lanes(hid2, g2)
-        d_hi, d_lo = split(d)
-        d2 = jnp.concatenate([d_hi, d_lo], axis=0)
-        k2 = over_lanes(d2, s)
         kg[...] = kg[...] + (k2[: 8 * ch] + k2[8 * ch :])
-        dsum[...] = dsum[...] + (d[:, :128] + d[:, 128:])
-        wc_hi = w_cols[:, : 8 * ch]
-        wc2 = jnp.concatenate([wc_hi, wc_hi], axis=1)
-        back = jnp.dot(wc2, d2, preferred_element_type=F32) + jnp.dot(
-            w_cols[:, 8 * ch :], d_hi, preferred_element_type=F32
-        )
-        acc[pl.ds(at0, 504), :] = acc[pl.ds(at0, 504), :] + back[:504, :128]
-        acc[pl.ds(at1, 504), :] = acc[pl.ds(at1, 504), :] + back[:504, 128:]
+        level = d[:, :128]
+        for j in range(1, WIDE):
+            level = level + d[:, 128 * j : 128 * (j + 1)]
+        dsum[...] = dsum[...] + level
+        for m in range(WIDE + 2):
+            total = None
+            for j in range(WIDE):
+                if 0 <= m - j < 3:
+                    q = m - j
+                    piece = back[q * slot : (q + 1) * slot, 128 * j : 128 * (j + 1)]
+                    total = piece if total is None else total + piece
+            here = pl.multiple_of((x + m) * slot, 8)
+            acc[pl.ds(here, slot), :] = acc[pl.ds(here, slot), :] + total
         return carry
 
-    lax.fori_loop(0, nx // 2, step, 0)
+    lax.fori_loop(0, nx // WIDE, step, 0)
     acc[pl.ds(nx * slot, slot), :] = acc[pl.ds(nx * slot, slot), :] + acc[pl.ds(0, slot), :]
     acc[pl.ds(slot, slot), :] = acc[pl.ds(slot, slot), :] + acc[pl.ds((nx + 1) * slot, slot), :]
 
@@ -482,20 +546,28 @@
 
     lax.fori_loop(0, nx, drain, 0)
 
-    grads = jnp.zeros((2 * ch, pick.shape[0]), F32)
-    level_sum = jnp.zeros((ch, 1), F32)
-    head_sum = jnp.zeros((ch, 40), F32)
     sums = jnp.sum(dsum[...], axis=1, keepdims=True)
     h2 = hg[...]
     h_all = (h2[: 8 * ch, :40] + h2[8 * ch :, :40]) + (h2[: 8 * ch, 40:80] + h2[8 * ch :, 40:80])
     h_all = jnp.where(same_y, h_all, 0.0)
+    level_sum = jnp.zeros((ch, 1), F32)
+    head_sum = jnp.zeros((ch, 40), F32)
+    kind = jnp.broadcast_to(code[0:1], (ch, 512))
+    total = jnp.zeros((ch, 512), F32)
     for y in range(8):
         rows = kg[pl.ds(y * ch, ch), :]
-        hi, lo = split(rows)
-        pair = jnp.concatenate([hi, lo], axis=0)
-        grads = grads + over_lanes(pair, pick[:, y * 512 : (y + 1) * 512])
+        moved = rows if y == 1 else pltpu.roll(rows, (1 - y) % 512, 1)
+        keep = kind < 3
+        if y == 0:
+            keep = (kind == 1) | (kind == 2)
+            total = total + jnp.where(kind == 8, rows, 0.0)
+        if y == 7:
+            keep = kind < 2
+            total = total + jnp.where(kind == 9, rows, 0.0)
+        total = total + jnp.where(keep, moved, 0.0)
         level_sum = level_sum + sums[y * ch : (y + 1) * ch]
         head_sum = head_sum + h_all[y * ch : (y + 1) * ch]
+    grads = over_lanes(jnp.concatenate(split(total), axis=0), pick[...])
     taps = mass.shape[1]
     n_pick = pick.shape[0]
     parts[...] = jnp.zeros_like(parts)
@@ -508,57 +580,66 @@
 
 
 def band_pick():
-    pick = np.zeros((144, 8, 512), np.float32)
+    pick = np.zeros((144, 512), np.float32)
+    code = np.full((8, 512), 10, np.int32)
     for ox in range(3):
         for oz in range(3):
             for v in range(5):
-                for y in range(8):
-                    for oy in range(3):
-                        row = y + oy - 1
-                        if row < 0:
-                            at = 40 + v
-                        elif row > 7:
-                            at = 45 + v
-                        else:
-                            at = v * 8 + row
-                        pick[(oy * 9 + ox * 3 + oz) * 5 + v, y, (ox * 3 + oz) * 56 + at] = 1.0
-    return pick.reshape(144, 8 * 512)
-
-
-def call(kernel, outs, scratch, flops, moved):
+                at = (ox * 3 + oz) * 56
+                tap = [(oy * 9 + ox * 3 + oz) * 5 + v for oy in range(3)]
+                for k in range(8):
+                    code[:, at + v * 8 + k] = k if k < 3 else 7
+                for oy in range(3):
+                    pick[tap[oy], at + v * 8 + oy] = 1.0
+                pick[tap[0], at + 40 + v] = 1.0
+                pick[tap[2], at + 45 + v] = 1.0
+                code[:, at + 40 + v] = 8
+                code[:, at + 45 + v] = 9
+    return pick, code
+
+
+def call(kernel, outs, scratch, us, n_in, order=0):
+    spec = pl.BlockSpec(memory_space=pltpu.VMEM)
     return pl.pallas_call(
         kernel,
         out_shape=outs,
+        in_specs=[spec] * n_in + [pl.BlockSpec(memory_space=pl.ANY)] * order,
         scratch_shapes=scratch,
         compiler_params=pltpu.CompilerParams(vmem_limit_bytes=VMEM),
-        cost_estimate=pl.CostEstimate(flops=flops, bytes_accessed=moved, transcendentals=0),
+        cost_estimate=pl.CostEstimate(
+            flops=0, bytes_accessed=int(us * 3.69e6), transcendentals=0
+        ),
     )
 
 
-def body(pick, mass, state, cot, flags, kernel, heads):
+def body(pick, code, mass, state, cot, flags, kernel, heads):
     _, nx, ny, nz = state.shape
     ch, taps = kernel.shape
     count = lax.axis_size("gy")
     cells = nx * ny * nz
+    half = nx // 2
     shape = lambda *dims: jax.ShapeDtypeStruct(dims, F32)
-    full = shape(5, nx, ny, nz)
-    up = [(i, (i + 1) % count) for i in range(count)]
-    down = [((i + 1) % count, i) for i in range(count)]
+    full, part = shape(5, nx, ny, nz), shape(5, half, ny, nz)
+    with_twin = [(i, i ^ 1) for i in range(count)]
+    with_other = [(i, (i + 1) % count if i % 2 else (i - 1) % count) for i in range(count)]
     pick = jnp.asarray(pick, BF16)
+    code = jnp.asarray(code)
     mass = jnp.asarray(mass)
-
-    rows = lambda a, lo, hi: jnp.transpose(a[:, :, lo:hi], (2, 0, 1, 3))
-    head = jnp.concatenate([rows(state, 0, ABOVE), rows(cot, 0, 1)], axis=0)
-    above = lax.ppermute(head, "gy", down)
-    below = lax.ppermute(rows(state, ny - BELOW, ny), "gy", up)
-
     vm = pltpu.VMEM
+
+    rows = shape(ABOVE + 1, 5, nx, nz)
+    to_twin, to_other = call(pack_kernel, (rows, rows), [], 1.0, 2)(
+        state.reshape(5 * nx * ny, nz), cot.reshape(5 * nx * ny, nz)
+    )
+    twin = lax.ppermute(to_twin, "gy", with_twin)
+    other = lax.ppermute(to_other, "gy", with_other)
+
     first, w_rows, w_cols, bias = call(
         x_kernel,
         (
             full,
             jax.ShapeDtypeStruct((16 * ch, 512), BF16),
-            jax.ShapeDtypeStruct((512, 16 * ch), BF16),
+            jax.ShapeDtypeStruct((512, 24 * ch), BF16),
             shape(8 * ch, 128),
         ),
         [
@@ -567,9 +648,9 @@
             vm((5, nx + 5, ny, nz), F32),
             vm((2 * ch, pick.shape[0]), F32),
         ],
-        1000 * cells,
-        1 << 22,
-    )(state, cot, flags, kernel, pick, mass)
+        3.2,
+        7,
+    )(state, cot, flags, kernel, pick, code, mass)
     own, rim, parts = call(
         c_kernel,
         (full, shape(16 * nx, nz), shape(ch, 256)),
@@ -581,40 +662,58 @@
             vm((16 * ch, 80), F32),
             vm((8 * ch, 128), F32),
         ],
-        1000 * cells,
-        1 << 22,
-    )(state, cot, above, below, heads, pick, mass, w_rows, w_cols, bias)
-    gathered = lax.all_gather(parts, "gy")
-    second, give_up, give_down = call(
-        y_kernel,
-        (full, shape(ABOVE, 5, nx, nz), shape(BELOW, 5, nx, nz)),
-        [vm((5 * nx * 8, nz), F32)] * 3,
-        1000 * cells,
-        1 << 22,
-    )(state, cot, flags, above, below, own, rim)
-    from_below = lax.ppermute(give_up, "gy", up)
-    from_above = lax.ppermute(give_down, "gy", down)
-    done = call(z_kernel, shape(5, nx // 2, ny, nz), [], 500 * cells, 1 << 22)(
-        state, cot, flags, first
+        5.0,
+        11,
+    )(state, cot, twin, other, heads, pick, code, mass, w_rows, w_cols, bias)
+
+    def exchanged(value, bit):
+        return lax.ppermute(value, "gy", [(i, i ^ bit) for i in range(count)])
+
+    bits = [1 << b for b in range(count.bit_length() - 1)]
+    late = bits[3:]
+    sums = parts
+    got = exchanged(sums, bits[0])
+    halos = [vm((5 * half * ny, nz), F32)] * 2
+    y0, back0 = call(
+        y_kernel, (part, shape(5 * half * ny, nz)), halos, 1.6, 7
+    )(state, cot, flags, twin, other, own, first)
+    sums = sums + got
+    got = exchanged(sums, bits[1])
+    y1, give_twin, give_other = call(
+        y_last_kernel,
+        (part, shape(ABOVE, 5, nx, nz), shape(ABOVE, 5, nx, nz)),
+        [*halos, halos[0]],
+        1.8,
+        9,
+        1,
+    )(state, cot, flags, twin, other, own, first, back0, rim, sums)
+    sums = sums + got
+    back_twin = lax.ppermute(give_twin, "gy", with_twin)
+    back_other = lax.ppermute(give_other, "gy", with_other)
+    got = exchanged(sums, bits[2])
+    z0 = call(z_kernel, part, [], 1.8, 4, 2)(state, cot, flags, y0, give_twin, sums)
+    sums = sums + got
+    for bit in late[:-1]:
+        sums = sums + exchanged(sums, bit)
+    got = exchanged(sums, late[-1])
+    flow = call(z_last_kernel, full, [vm((5 * nx * ny, nz), F32)], 2.6, 7, 1)(
+        state, cot, flags, z0, y1, back_twin, back_other, sums
     )
     scale = float(cells * count) ** (-0.5)
-    return call(
-        functools.partial(last_kernel, scale),
-        (full, shape(ch, taps), shape(5, ch)),
-        [vm((5 * nx * 8, nz), F32)],
-        500 * cells,
-        1 << 22,
-    )(state, cot, flags, first, second, done, from_below, from_above, gathered)
+    k_out, h_out = call(
+        functools.partial(sum_kernel, scale), (shape(ch, taps), shape(5, ch)), [], 0.5, 2
+    )(sums, got)
+    return flow, k_out, h_out
 
 
 def solution(mesh):
-    pick = band_pick()
+    pick, code = band_pick()
     mass = np.zeros((16, 135), np.float32)
     mass[:, 0::5] = 1.0
     mass[:, 4::5] = 1.0
     split_y = P(None, "ens", "gy", None)
     return jax.shard_map(
-        functools.partial(body, pick, mass),
+        functools.partial(body, pick, code, mass),
         mesh=mesh,
         in_specs=(split_y, split_y, split_y, P(), P()),
         out_specs=(split_y, P("ens", None), P("ens", None)),

time: 54.5 us -> 43.3 us (0.79)
  blocking collectives: 18.8 us -> 0 us
  waiting for transfers between devices: 0.18 us -> 10.3 us
  local copies, waits for them, and re-layouts: 4.39 us -> 2.64 us
  Pallas kernels: 20.2 us -> 19 us
    all_gather x1 -> x0, blocking collectives: 18.8 us -> none  [body(): gathered = lax.all_gather(parts, 'gy')]
    ppermute x4 -> x8, waiting for transfers between devices: 0.18 us -> 10.3 us  [the longest x4 10.3 us: exchanged(): return lax.ppermute(value, 'gy', [(i, i ^ bit) for i in range(count)])]
    slice x3 -> x0, local copies, waits for them, and re-layouts: 3.07 us -> none  [body(): rows = lambda a, lo, hi: jnp.transpose(a[:, :, lo:hi], (2, 0, 1, 3))]
    pallas_call x1, Pallas kernels: 9.38 us -> 7.49 us  [body(): call(c_kernel, (full, shape(16 * nx, nz), shape(ch, 256)), [vm(((nx + 2)...]
    unnamed x18, local copies, waits for them, and re-layouts: 1.32 us -> 2.64 us
    pallas_call x3 -> x6, Pallas kernels: 7.61 us -> 8.37 us  [the longest x1 2.64 us: body(): call(z_last_kernel, full, [vm((5 * nx * ny, nz), F32)], 2.6, 7, 1)]
    ppermute x4 -> x8, starting transfers between devices: 9.87 us -> 10.3 us  [the longest x1 5.67 us: body(): other = lax.ppermute(to_other, 'gy', with_other)]
  transfers between devices with their start and end apart: 4 -> 8, of which waited for: 1 -> 3; matrix products, arithmetic and copies ran while one was open for 2% -> 0% of each run, Pallas kernels for 9% -> 17%
where the time goes in v1:
time: 43.3 us; the launch traced here: 43.1 us
  Pallas kernels  19 us (44%)
  starting transfers between devices  10.3 us (24%)
  waiting for transfers between devices  10.3 us (24%)
  local copies, waits for them, and re-layouts  2.64 us (6%)
  between operations  0.76 us (2%)
    ppermute x4, waiting for transfers between devices, exchanged(): return lax.ppermute(value, 'gy', [(i, i ^ bit) for i in range(count)])  10.3 us
    pallas_call x1, Pallas kernels, body(): call(c_kernel, (full, shape(16 * nx, nz), shape(ch, 256)), [vm(((nx + 2)...  7.49 us
    ppermute x1, starting transfers between devices, body(): other = lax.ppermute(to_other, 'gy', with_other)  5.67 us
    ppermute x1, starting transfers between devices, body(): back_other = lax.ppermute(give_other, 'gy', with_other)  3.53 us
    pallas_call x1, Pallas kernels, body(): call(x_kernel, (full, jax.ShapeDtypeStruct((16 * ch, 512), BF16), jax.Sha...  3.19 us
    pallas_call x1, Pallas kernels, body(): call(z_last_kernel, full, [vm((5 * nx * ny, nz), F32)], 2.6, 7, 1)  2.64 us
    unnamed x18, local copies, waits for them, and re-layouts  2.64 us
    pallas_call x1, Pallas kernels, body(): call(z_kernel, part, [], 1.8, 4, 2)(state, cot, flags, y0, give_twin, sums)  1.83 us
  transfers between devices with their start and end apart: 8, of which 3 were waited for; matrix products, arithmetic and copies ran while one was open for 0% of the time, Pallas kernels for 17%

profile of v1, /device:TPU:0, one launch (start us, length us, event | category | flops | bytes accessed | tf_op | source)
XLA Modules:
  0.0 43.1 jit_solution(1977354671853014493)
XLA Ops:
  0.6 0.0 copy-start
  0.6 1.0 %copy-done = f32[5,16,8,128]{3,2,1,0:T(8,128)S(1)} copy-done((f32[5,16,8,128]{3,2,1,0:T(8,128)S(1)}, f32[5,16,8,128]{3,2,1,0:T(8,128)}, u32[]{:S(2)}) %copy-start) | copy-done | bytes 327704
  1.6 1.0 %copy-done.2 = f32[5,16,8,128]{3,2,1,0:T(8,128)S(1)} copy-done((f32[5,16,8,128]{3,2,1,0:T(8,128)S(1)}, f32[5,16,8,128]{3,2,1,0:T(8,128)}, u32[]{:S(2)}) %copy-start.2) | copy-done | bytes 327704
  2.6 0.0 copy-start.7
  2.7 0.5 %collective-permute-start = (f32[4,5,16,128]{3,2,1,0:T(8,128)S(1)}, f32[4,5,16,128]{3,2,1,0:T(8,128)S(1)}, u32[]{:S(2)}, u32[]{:S(2)}) collective-permute-start(f32[4,5,16,128]{3,2,1,0:T(8,128)S(1)} %get-tuple-element.19), channel_id=1, source_target_pairs={{0,1},{1,0},{2,3},{3,2},{4,5},{5,4},{6,7},{7,6},{8,9},{9,8},{10,11... | collective-permute-start | bytes 491528 | tf_op jit(solution)/shard_map/ppermute | solution.py:634
  3.2 5.7 %collective-permute-start.1 = (f32[4,5,16,128]{3,2,1,0:T(8,128)S(1)}, f32[4,5,16,128]{3,2,1,0:T(8,128)S(1)}, u32[]{:S(2)}, u32[]{:S(2)}) collective-permute-start(f32[4,5,16,128]{3,2,1,0:T(8,128)S(1)} %get-tuple-element.20), channel_id=1, source_target_pairs={{0,15},{1,2},{2,1},{3,4},{4,3},{5,6},{6,5},{7,8},{8,7},{9,10},{10,... | collective-permute-start | bytes 491528 | tf_op jit(solution)/shard_map/ppermute | solution.py:635
  8.8 0.0 copy-done.3
  8.8 0.0 copy-done.4
  8.8 0.0 copy-done.5
  8.9 3.2 %shard_map.104 = (f32[5,16,8,128]{3,2,1,0:T(8,128)S(1)}, bf16[256,512]{1,0:T(8,128)(2,1)S(1)}, bf16[512,384]{1,0:T(8,128)(2,1)S(1)}, f32[128,128]{1,0:T(8,128)S(1)}) custom-call(f32[5,16,8,128]{3,2,1,0:T(8,128)S(1)} %copy-done, f32[5,16,8,128]{3,2,1,0:T(8,128)S(1)} %copy-done.2, s32[3,16,8,128]{3,2,1,0:T(8,128)S(1)} %copy-done.3, f32[16,135]{1,0:T(8,128)S(1)} %copy-done.7, ...), custom_call_target="tpu_custom_call" | custom-call | bytes 11808000 | tf_op jit(solution)/shard_map/pallas_call | solution.py:637
  12.1 0.0 collective-permute-done.twin
  12.1 0.0 collective-permute-done.1.other
  12.1 0.7 %copy-done.8 = f32[5,16]{1,0:T(8,128)S(1)} copy-done((f32[5,16]{1,0:T(8,128)S(1)}, f32[5,16]{1,0:T(8,128)}, u32[]{:S(2)}) %copy-start.8) | copy-done | bytes 344
  12.8 7.5 %shard_map.105 = (f32[5,16,8,128]{3,2,1,0:T(8,128)S(1)}, f32[256,128]{1,0:T(8,128)S(1)}, f32[16,256]{1,0:T(8,128)S(1)}) custom-call(f32[5,16,8,128]{3,2,1,0:T(8,128)S(1)} %copy-done, f32[5,16,8,128]{3,2,1,0:T(8,128)S(1)} %copy-done.2, f32[4,5,16,128]{3,2,1,0:T(8,128)S(1)} %collective-permute-done.twin, f32[4,5,16,128]{3,2,1,0:T(8,128)S(1)} %collective-permute-done.1.other, ...), custom_call_target="tpu_custom_call" | custom-call | bytes 18450000 | tf_op jit(solution)/shard_map/pallas_call | solution.py:654
  20.2 0.1 collective-permute-start.2
  20.3 1.5 %shard_map.106 = (f32[5,8,8,128]{3,2,1,0:T(8,128)S(1)}, f32[320,128]{1,0:T(8,128)S(1)}) custom-call(f32[5,16,8,128]{3,2,1,0:T(8,128)S(1)} %copy-done, f32[5,16,8,128]{3,2,1,0:T(8,128)S(1)} %copy-done.2, s32[3,16,8,128]{3,2,1,0:T(8,128)S(1)} %copy-done.3, f32[4,5,16,128]{3,2,1,0:T(8,128)S(1)} %collective-permute-done.twin, ...), custom_call_target="tpu_custom_call" | custom-call | bytes 5904000 | tf_op jit(solution)/shard_map/pallas_call | solution.py:677
  21.8 0.0 collective-permute-done.2
  21.9 1.6 %shard_map.107 = (f32[5,8,8,128]{3,2,1,0:T(8,128)S(1)}, f32[3,5,16,128]{3,2,1,0:T(8,128)S(1)}, f32[3,5,16,128]{3,2,1,0:T(8,128)S(1)}) custom-call(f32[5,16,8,128]{3,2,1,0:T(8,128)S(1)} %copy-done, f32[5,16,8,128]{3,2,1,0:T(8,128)S(1)} %copy-done.2, s32[3,16,8,128]{3,2,1,0:T(8,128)S(1)} %copy-done.3, f32[4,5,16,128]{3,2,1,0:T(8,128)S(1)} %collective-permute-done.twin, ...), custom_call_target="tpu_custom_call" | custom-call | bytes 6642000 | tf_op jit(solution)/shard_map/pallas_call | solution.py:682
  23.5 0.6 %collective-permute-start.4 = (f32[3,5,16,128]{3,2,1,0:T(8,128)S(1)}, f32[3,5,16,128]{3,2,1,0:T(8,128)S(1)}, u32[]{:S(2)}, u32[]{:S(2)}) collective-permute-start(f32[3,5,16,128]{3,2,1,0:T(8,128)S(1)} %get-tuple-element.30.order), channel_id=1, source_target_pairs={{0,1},{1,0},{2,3},{3,2},{4,5},{5,4},{6,7},{7,6},{8,9},{9,8},{10,11... | collective-permute-start | bytes 368648 | tf_op jit(solution)/shard_map/ppermute | solution.py:691
  24.0 3.5 %collective-permute-start.5 = (f32[3,5,16,128]{3,2,1,0:T(8,128)S(1)}, f32[3,5,16,128]{3,2,1,0:T(8,128)S(1)}, u32[]{:S(2)}, u32[]{:S(2)}) collective-permute-start(f32[3,5,16,128]{3,2,1,0:T(8,128)S(1)} %get-tuple-element.32), channel_id=1, source_target_pairs={{0,15},{1,2},{2,1},{3,4},{4,3},{5,6},{6,5},{7,8},{8,7},{9,10},{10,... | collective-permute-start | bytes 368648 | tf_op jit(solution)/shard_map/ppermute | solution.py:692
  27.6 0.0 collective-permute-start.3
  27.6 3.7 %collective-permute-done.3 = f32[16,256]{1,0:T(8,128)S(1)} collective-permute-done((f32[16,256]{1,0:T(8,128)S(1)}, f32[16,256]{1,0:T(8,128)S(1)}, u32[]{:S(2)}, u32[]{:S(2)}) %collective-permute-start.3) | collective-permute-done | bytes 16416 | tf_op jit(solution)/shard_map/ppermute | solution.py:670
  31.3 0.0 collective-permute-start.6
  31.3 3.7 %collective-permute-done.6 = f32[16,256]{1,0:T(8,128)S(1)} collective-permute-done((f32[16,256]{1,0:T(8,128)S(1)}, f32[16,256]{1,0:T(8,128)S(1)}, u32[]{:S(2)}, u32[]{:S(2)}) %collective-permute-start.6) | collective-permute-done | bytes 16416 | tf_op jit(solution)/shard_map/ppermute | solution.py:670
  35.0 0.0 collective-permute-start.7
  35.0 0.0 copy-start.1
  35.1 1.8 %shard_map.108.done = f32[5,8,8,128]{3,2,1,0:T(8,128)S(1)} custom-call(f32[5,16,8,128]{3,2,1,0:T(8,128)S(1)} %copy-done, f32[5,16,8,128]{3,2,1,0:T(8,128)S(1)} %copy-done.2, s32[3,16,8,128]{3,2,1,0:T(8,128)S(1)} %copy-done.3, f32[5,8,8,128]{3,2,1,0:T(8,128)S(1)} %get-tuple-element.26.before, f32[3,5,16,128]{3,2,1,0:T(8,128)S(1)} %get-tuple-element.30.order, ...), custom_call_target="tpu_custom_call" | custom-call | bytes 6642000 | tf_op jit(solution)/shard_map/pallas_call | solution.py:694
  36.9 2.8 %collective-permute-done.7.theirs = f32[16,256]{1,0:T(8,128)S(1)} collective-permute-done((f32[16,256]{1,0:T(8,128)S(1)}, f32[16,256]{1,0:T(8,128)S(1)}, u32[]{:S(2)}, u32[]{:S(2)}) %collective-permute-start.7) | collective-permute-done | bytes 16416 | tf_op jit(solution)/shard_map/ppermute | solution.py:670
  39.7 0.7 %shard_map.110 = (f32[16,135]{1,0:T(8,128)}, f32[5,16]{1,0:T(8,128)}) custom-call(f32[16,256]{1,0:T(8,128)S(1)} %add.11.order.mine, f32[16,256]{1,0:T(8,128)S(1)} %collective-permute-done.7.theirs), custom_call_target="tpu_custom_call" | custom-call | bytes 1845000 | tf_op jit(solution)/shard_map/pallas_call | solution.py:703
  40.4 0.0 collective-permute-done.4.twin
  40.4 0.0 collective-permute-done.5.other
  40.4 2.6 %shard_map.109 = f32[5,16,8,128]{3,2,1,0:T(8,128)} custom-call(f32[5,16,8,128]{3,2,1,0:T(8,128)S(1)} %copy-done.1, f32[5,16,8,128]{3,2,1,0:T(8,128)S(1)} %copy-done.2, s32[3,16,8,128]{3,2,1,0:T(8,128)S(1)} %copy-done.3, f32[5,8,8,128]{3,2,1,0:T(8,128)S(1)} %shard_map.108.done, f32[5,8,8,128]{3,2,1,0:T(8,128)S(1)} %get-tuple-element.31.before, ...), custom_call_target="tpu_custom_call" | custom-call | bytes 9594000 | tf_op jit(solution)/shard_map/pallas_call | solution.py:699
  (13 shorter events, 0.1 us)
Async XLA Ops:
  0.6 1.0 %copy-start = (f32[5,16,8,128]{3,2,1,0:T(8,128)S(1)}, f32[5,16,8,128]{3,2,1,0:T(8,128)}, u32[]{:S(2)}) copy-start(f32[5,16,8,128]{3,2,1,0:T(8,128)} %state.11) | copy-start | bytes 983044
  1.6 1.0 %copy-start.2 = (f32[5,16,8,128]{3,2,1,0:T(8,128)S(1)}, f32[5,16,8,128]{3,2,1,0:T(8,128)}, u32[]{:S(2)}) copy-start(f32[5,16,8,128]{3,2,1,0:T(8,128)} %cot.11) | copy-start | bytes 983044
  2.6 6.3 %copy-start.3 = (s32[3,16,8,128]{3,2,1,0:T(8,128)S(1)}, s32[3,16,8,128]{3,2,1,0:T(8,128)}, u32[]{:S(2)}) copy-start(s32[3,16,8,128]{3,2,1,0:T(8,128)} %flags.9) | copy-start | bytes 589828
  2.6 6.3 %copy-start.4 = (bf16[144,512]{1,0:T(8,128)(2,1)S(1)}, bf16[144,512]{1,0:T(8,128)(2,1)}, u32[]{:S(2)}) copy-start(bf16[144,512]{1,0:T(8,128)(2,1)} %constant.6.clone.pick) | copy-start | bytes 442372
  2.6 6.3 %copy-start.5 = (s32[8,512]{1,0:T(8,128)S(1)}, s32[8,512]{1,0:T(8,128)}, u32[]{:S(2)}) copy-start(s32[8,512]{1,0:T(8,128)} %constant.7.clone.code) | copy-start | bytes 49156
  2.6 6.3 %copy-start.6 = (f32[16,135]{1,0:T(8,128)S(1)}, f32[16,135]{1,0:T(8,128)}, u32[]{:S(2)}) copy-start(f32[16,135]{1,0:T(8,128)} %constant.8.clone.mass) | copy-start | bytes 25924
  2.6 6.3 %copy-start.7 = (f32[16,135]{1,0:T(8,128)S(1)}, f32[16,135]{1,0:T(8,128)}, u32[]{:S(2)}) copy-start(f32[16,135]{1,0:T(8,128)} %kernel.1) | copy-start | bytes 25924
  2.7 9.4 %collective-permute-start = (f32[4,5,16,128]{3,2,1,0:T(8,128)S(1)}, f32[4,5,16,128]{3,2,1,0:T(8,128)S(1)}, u32[]{:S(2)}, u32[]{:S(2)}) collective-permute-start(f32[4,5,16,128]{3,2,1,0:T(8,128)S(1)} %get-tuple-element.19), channel_id=1, source_target_pairs={{0,1},{1,0},{2,3},{3,2},{4,5},{5,4},{6,7},{7,6},{8,9},{9,8},{10,11... | collective-permute-start | bytes 491528 | tf_op jit(solution)/shard_map/ppermute | solution.py:634
  3.2 8.9 %collective-permute-start.1 = (f32[4,5,16,128]{3,2,1,0:T(8,128)S(1)}, f32[4,5,16,128]{3,2,1,0:T(8,128)S(1)}, u32[]{:S(2)}, u32[]{:S(2)}) collective-permute-start(f32[4,5,16,128]{3,2,1,0:T(8,128)S(1)} %get-tuple-element.20), channel_id=1, source_target_pairs={{0,15},{1,2},{2,1},{3,4},{4,3},{5,6},{6,5},{7,8},{8,7},{9,10},{10,... | collective-permute-start | bytes 491528 | tf_op jit(solution)/shard_map/ppermute | solution.py:635
  12.1 0.7 %copy-start.8 = (f32[5,16]{1,0:T(8,128)S(1)}, f32[5,16]{1,0:T(8,128)}, u32[]{:S(2)}) copy-start(f32[5,16]{1,0:T(8,128)} %heads.1) | copy-start | bytes 964
  20.2 1.6 %collective-permute-start.2 = (f32[16,256]{1,0:T(8,128)S(1)}, f32[16,256]{1,0:T(8,128)S(1)}, u32[]{:S(2)}, u32[]{:S(2)}) collective-permute-start(f32[16,256]{1,0:T(8,128)S(1)} %get-tuple-element.29), channel_id=1, source_target_pairs={{0,1},{1,0},{2,3},{3,2},{4,5},{5,4},{6,7},{7,6},{8,9},{9,8},{10,11... | collective-permute-start | bytes 49160 | tf_op jit(solution)/shard_map/ppermute | solution.py:670
  23.5 16.9 %collective-permute-start.4 = (f32[3,5,16,128]{3,2,1,0:T(8,128)S(1)}, f32[3,5,16,128]{3,2,1,0:T(8,128)S(1)}, u32[]{:S(2)}, u32[]{:S(2)}) collective-permute-start(f32[3,5,16,128]{3,2,1,0:T(8,128)S(1)} %get-tuple-element.30.order), channel_id=1, source_target_pairs={{0,1},{1,0},{2,3},{3,2},{4,5},{5,4},{6,7},{7,6},{8,9},{9,8},{10,11... | collective-permute-start | bytes 368648 | tf_op jit(solution)/shard_map/ppermute | solution.py:691
  24.0 16.4 %collective-permute-start.5 = (f32[3,5,16,128]{3,2,1,0:T(8,128)S(1)}, f32[3,5,16,128]{3,2,1,0:T(8,128)S(1)}, u32[]{:S(2)}, u32[]{:S(2)}) collective-permute-start(f32[3,5,16,128]{3,2,1,0:T(8,128)S(1)} %get-tuple-element.32), channel_id=1, source_target_pairs={{0,15},{1,2},{2,1},{3,4},{4,3},{5,6},{6,5},{7,8},{8,7},{9,10},{10,... | collective-permute-start | bytes 368648 | tf_op jit(solution)/shard_map/ppermute | solution.py:692
  27.6 3.7 %collective-permute-start.3 = (f32[16,256]{1,0:T(8,128)S(1)}, f32[16,256]{1,0:T(8,128)S(1)}, u32[]{:S(2)}, u32[]{:S(2)}) collective-permute-start(f32[16,256]{1,0:T(8,128)S(1)} %add.9.order), channel_id=1, source_target_pairs={{0,2},{1,3},{2,0},{3,1},{4,6},{5,7},{6,4},{7,5},{8,10},{9,11},{10,... | collective-permute-start | bytes 49160 | tf_op jit(solution)/shard_map/ppermute | solution.py:670
  31.3 3.7 %collective-permute-start.6 = (f32[16,256]{1,0:T(8,128)S(1)}, f32[16,256]{1,0:T(8,128)S(1)}, u32[]{:S(2)}, u32[]{:S(2)}) collective-permute-start(f32[16,256]{1,0:T(8,128)S(1)} %add.10.order2), channel_id=1, source_target_pairs={{0,4},{1,5},{2,6},{3,7},{4,0},{5,1},{6,2},{7,3},{8,12},{9,13},{10,... | collective-permute-start | bytes 49160 | tf_op jit(solution)/shard_map/ppermute | solution.py:670
  35.0 4.6 %collective-permute-start.7 = (f32[16,256]{1,0:T(8,128)S(1)}, f32[16,256]{1,0:T(8,128)S(1)}, u32[]{:S(2)}, u32[]{:S(2)}) collective-permute-start(f32[16,256]{1,0:T(8,128)S(1)} %add.11.order.mine), channel_id=1, source_target_pairs={{0,8},{1,9},{2,10},{3,11},{4,12},{5,13},{6,14},{7,15},{8,0},{9,1},... | collective-permute-start | bytes 49160 | tf_op jit(solution)/shard_map/ppermute | solution.py:670
  35.0 5.4 %copy-start.1 = (f32[5,16,8,128]{3,2,1,0:T(8,128)S(1)}, f32[5,16,8,128]{3,2,1,0:T(8,128)}, u32[]{:S(2)}) copy-start(f32[5,16,8,128]{3,2,1,0:T(8,128)} %state.11) | copy-start | bytes 983044

commit v2 on v1

v2 whole, which is shorter than its diff:
```python
import functools

import jax
import jax.numpy as jnp
import numpy as np
from jax import lax
from jax.experimental import pallas as pl
from jax.experimental.pallas import tpu as pltpu
from jax.sharding import PartitionSpec as P

STEP = 0.3
FLOOR = 0.01
BELOW, ABOVE = 2, 3
SLABS = 2
WIDE = 4
VMEM = 48 * 1024 * 1024
F32 = jnp.float32
BF16 = jnp.bfloat16


def rcp(x):
    return pl.reciprocal(x, approx=True)


def shared_terms(v):
    p = [v[i + 1] - v[i] for i in range(5)]
    d = [p[i + 1] - p[i] for i in range(4)]
    h = [(4.0 / 3.0) * x for x in d]
    k = [h[i] * d[i] + FLOOR for i in range(4)]
    g = [x + x for x in h]
    t = [d[i + 1] - d[i] for i in range(3)]
    return p, d, k, g, t


def side_value(pa, pm, pm2, ka, kb, kc, m0, m2, td, t1, smooth, c0, c2):
    i0 = rcp(ka + pa * m0)
    i1 = rcp(kb + pa * pm)
    i2 = rcp(kc + pm * m2)
    w0 = i0 * i0
    w1 = 6.0 * (i1 * i1)
    w2 = 3.0 * (i2 * i2)
    r = rcp(w0 + w1 + w2)
    o0 = jnp.where(smooth, w0 * r, c0)
    o2 = jnp.where(smooth, w2 * r, c2)
    u = o0 * td + o2 * t1
    return (pa + pm2) - u, (i0, i1, i2, w0, w1, w2, r, o0, o2, u)


def side_pull(mu, pa, pm, m0, m2, td, t1, smooth, saved):
    i0, i1, i2, w0, w1, w2, r, o0, o2, u = saved
    mu2 = mu + mu
    rm = jnp.where(smooth, mu2, 0.0) * r
    s0 = (w0 * i0) * rm * (td - u)
    s1 = (w1 * i1) * rm * u
    s2 = (w2 * i2) * rm * (t1 - u)
    pa_bar = s0 * (m0 + pa) - s1 * pm + mu
    pm_bar = s2 * (m2 + pm) - s1 * pa + mu2
    return s0, s1, s2, pa_bar, pm_bar, o0 * mu2, o2 * mu


def hllc_pull(left, right, normal, flags, cot):
    region = flags & 3
    is_right = region >= 2
    star = ((region + 1) & 2) != 0
    n_at = 1 + normal
    tang = [1 + i for i in range(3) if i != normal]
    rl, rr_, pl_, pr_, nl, nr = left[0], right[0], left[4], right[4], left[n_at], right[n_at]

    def sound(r, p):
        inv = rcp(r)
        t = 1.4 * p * inv
        inv_c = lax.rsqrt(t)
        return inv, inv_c, t * inv_c

    inv_rl, inv_cl, cl = sound(rl, pl_)
    inv_rr, inv_cr, cr = sound(rr_, pr_)
    c = 0.5 * (cl + cr)
    r2 = rl + rr_
    inv = rcp(r2 * c)
    nm = 0.5 * (nl + nr)
    gap = (pl_ - pr_) * inv
    sm = nm + gap
    sc = jnp.where(is_right, c, -c)
    s = nm + sc
    pick = [jnp.where(is_right, right[i], left[i]) for i in range(5)]
    r, un, u1, u2, p = pick[0], pick[n_at], pick[tang[0]], pick[tang[1]], pick[4]
    a = s - un
    dl = sm - un
    si = jnp.where(star, rcp(sc - gap), 0.0)
    j = s * si
    kap = j * dl
    g0, gn, g1, g2, ge = cot[0], cot[n_at], cot[tang[0]], cot[tang[1]], cot[4]
    w = un + kap
    half_q = 0.5 * (un * un + u1 * u1 + u2 * u2)
    enthalpy = 3.5 * p + r * half_q
    b = g0 + u1 * g1 + u2 * g2 + un * gn
    m = r * b + enthalpy * ge
    n = gn + sm * ge
    rkap = r * kap
    f_kap = m + r * a * n
    f_a = rkap * n
    si2 = si * si
    s_bar = f_a - f_kap * (dl * sm * si2)
    sm_bar = f_kap * (s * a * si2) + rkap * a * ge
    wr = w * r
    k_bar = [None] * 5
    k_bar[0] = w * (b + half_q * ge) + kap * a * n
    k_bar[n_at] = m + wr * (gn + un * ge) - f_kap * j - f_a
    k_bar[tang[0]] = wr * (g1 + u1 * ge)
    k_bar[tang[1]] = wr * (g2 + u2 * ge)
    k_bar[4] = 3.5 * (w * ge) + gn
    e = sm_bar * inv
    eg = e * gap
    c_half = 0.5 * (jnp.where(is_right, s_bar, -s_bar) - eg * r2)
    n_half = 0.5 * (s_bar + sm_bar)
    r_both = -(eg * c)
    xl = c_half * inv_rl
    xr = c_half * inv_rr
    base_l = {0: r_both - 0.5 * (xl * cl), n_at: n_half, 4: 0.7 * (xl * inv_cl) + e}
    base_r = {0: r_both - 0.5 * (xr * cr), n_at: n_half, 4: 0.7 * (xr * inv_cr) - e}
    l_bar, r_bar = [], []
    for i in range(5):
        kr = jnp.where(is_right, k_bar[i], 0.0)
        kl = k_bar[i] - kr
        l_bar.append(base_l[i] + kl if i in base_l else kl)
        r_bar.append(base_r[i] + kr if i in base_r else kr)
    return l_bar, r_bar


def face_pull(cells, cot, flags, normal):
    stencil = flags >> 2
    smooth = stencil == 0
    c0 = jnp.where(stencil == 1, 1.0, 0.0)
    c2 = jnp.where(stencil == 3, 1.0, 0.0)
    left, right, kept = [], [], []
    for v in cells:
        p, d, k, g, t = shared_terms(v)
        pm2 = p[2] + p[2]
        args_l = (p[1], p[2], p[1] + d[0], p[2] - d[2], t[0] + t[0], t[1])
        args_r = (p[3], p[2], p[3] - d[3], p[2] + d[1], t[2] + t[2], t[1])
        hl, saved_l = side_value(
            p[1], p[2], pm2, k[0], k[1], k[2], *args_l[2:], smooth, c0, c2
        )
        hr, saved_r = side_value(
            p[3], p[2], pm2, k[3], k[2], k[1], *args_r[2:], smooth, c0, c2
        )
        left.append(v[2] + hl * (1.0 / 6.0))
        right.append(v[3] - hr * (1.0 / 6.0))
        kept.append((p, g, args_l, args_r, saved_l, saved_r))
    l_bar, r_bar = hllc_pull(left, right, normal, flags, cot)
    out = []
    for i in range(5):
        p, g, args_l, args_r, saved_l, saved_r = kept[i]
        a0, a1, a2, pa_l, pm_l, x0, x2 = side_pull(
            l_bar[i] * (1.0 / 6.0), *args_l, smooth, saved_l
        )
        b0, b1, b2, pa_r, pm_r, y0, y2 = side_pull(
            r_bar[i] * (-1.0 / 6.0), *args_r, smooth, saved_r
        )
        d0 = a0 * (g[0] + p[1]) + x0
        d1 = (b2 * (g[1] + p[2]) - a1 * g[1]) + (x2 - x0) + y2
        d2 = (a2 * (g[2] - p[2]) - b1 * g[2]) + (y0 - y2) - x2
        d3 = b0 * (g[3] - p[3]) - y0
        p2 = pa_l + (d0 - d1)
        p3 = pm_l + pm_r + (d1 - d2)
        p4 = pa_r + (d2 - d3)
        out.append([d0, -d0 - p2, l_bar[i] + (p2 - p3), r_bar[i] + (p3 - p4), p4 - d3, d3])
    return out


def conserved_pull(s, g):
    half_q = 0.5 * (s[1] * s[1] + s[2] * s[2] + s[3] * s[3])
    return [
        g[0] + s[1] * g[1] + s[2] * g[2] + s[3] * g[3] + half_q * g[4],
        s[0] * (g[1] + s[1] * g[4]),
        s[0] * (g[2] + s[2] * g[4]),
        s[0] * (g[3] + s[3] * g[4]),
        2.5 * g[4],
    ]


REACH_STATE, REACH_COT, REACH_FLAGS = 5, 3, 3
COT_AT = 5 * REACH_STATE
FLAGS_AT = COT_AT + 5 * REACH_COT
SENT = FLAGS_AT + REACH_FLAGS


def pack_kernel(state, cot, flags, twin, other, s, g, f, sem):
    rows_in = f.shape[0]
    copies = [
        pltpu.make_async_copy(state, s, sem.at[0]),
        pltpu.make_async_copy(cot, g, sem.at[1]),
        pltpu.make_async_copy(flags.at[pl.ds(rows_in, rows_in)], f, sem.at[2]),
    ]
    for copy in copies:
        copy.start()
    for copy in copies:
        copy.wait()
    even = is_even()
    nx = twin.shape[1]

    def put(at, low, top):
        twin[at] = jnp.where(even, top, low)
        other[at] = jnp.where(even, low, top)

    for v in range(5):
        base = v * nx * 8
        for ref, reach, at in ((s, REACH_STATE, 0), (g, REACH_COT, COT_AT)):
            for r in range(reach):
                put(
                    at + r * 5 + v,
                    ref[pl.ds(base + r, nx, stride=8), :],
                    ref[pl.ds(base + 8 - reach + r, nx, stride=8), :],
                )
    for r in range(REACH_FLAGS):
        low = f[pl.ds(r, nx, stride=8), :]
        top = f[pl.ds(8 - REACH_FLAGS + r, nx, stride=8), :]
        put(FLAGS_AT + r, low.astype(F32), top.astype(F32))


def from_rims(twin, other):
    even = is_even()

    def read(row, reach, at, v):
        if row < 0:
            i = at + (reach + row) * 5 + v
            return jnp.where(even, other[i], twin[i])
        i = at + (row - 8) * 5 + v
        return jnp.where(even, twin[i], other[i])

    def state(row, v):
        return read(row, REACH_STATE, 0, v)

    def cot(row, v):
        return read(row, REACH_COT, COT_AT, v)

    def flags(row):
        if row < 0:
            i = FLAGS_AT + REACH_FLAGS + row
            return jnp.where(even, other[i], twin[i])
        i = FLAGS_AT + row - 8
        return jnp.where(even, twin[i], other[i])

    return state, cot, flags


def xz_kernel(state, cot, flags, kernel, heads, pick, pick2, code, mass, out, w_rows, w_cols, w_head, bias, pad, gpad, acc, wide):
    nx = state.shape[1]
    for v in range(5):
        pad[v, pl.ds(2, nx)] = state[v]
        pad[v, pl.ds(0, 2)] = state[v, pl.ds(nx - 2, 2)]
        pad[v, pl.ds(nx + 2, 3)] = state[v, pl.ds(0, 3)]
        gpad[v, pl.ds(0, nx)] = cot[v]
        gpad[v, pl.ds(nx, 1)] = cot[v, pl.ds(0, 1)]
    acc[...] = jnp.zeros_like(acc)

    def step(i, carry):
        x = i * SLABS
        cells = [[pad[v, pl.ds(x + k, SLABS)] for k in range(6)] for v in range(5)]
        g = [gpad[v, pl.ds(x, SLABS)] for v in range(5)]
        face = [STEP * (gpad[v, pl.ds(x + 1, SLABS)] - g[v]) for v in range(5)]
        terms = face_pull(cells, face, flags[0, pl.ds(x, SLABS)], 0)
        own = conserved_pull([cells[v][2] for v in range(5)], g)
        for v in range(5):
            terms[v][2] = terms[v][2] + own[v]
            for s in range(SLABS + 5):
                total = None
                for k in range(6):
                    if 0 <= s - k < SLABS:
                        part = terms[v][k][s - k]
                        total = part if total is None else total + part
                acc[v, x + s] = acc[v, x + s] + total
        return carry

    lax.fori_loop(0, nx // SLABS, step, 0)
    for v in range(5):
        acc[v, pl.ds(nx, 2)] = acc[v, pl.ds(nx, 2)] + acc[v, pl.ds(0, 2)]
        acc[v, pl.ds(2, 3)] = acc[v, pl.ds(2, 3)] + acc[v, pl.ds(nx + 2, 3)]

    def z_step(i, carry):
        x = i * SLABS
        cells, face = [], []
        for v in range(5):
            mid = state[v, pl.ds(x, SLABS)]
            cells.append([mid if k == 0 else pltpu.roll(mid, (-k) % 128, 2) for k in range(-2, 4)])
            g = cot[v, pl.ds(x, SLABS)]
            face.append(STEP * (pltpu.roll(g, 127, 2) - g))
        terms = face_pull(cells, face, flags[2, pl.ds(x, SLABS)], 2)
        for v in range(5):
            t = acc[v, pl.ds(x + 2, SLABS)] + terms[v][2]
            for k in (-2, -1, 1, 2, 3):
                t = t + pltpu.roll(terms[v][k + 2], k % 128, 2)
            out[v, pl.ds(x, SLABS)] = t
        return carry

    lax.fori_loop(0, nx // SLABS, z_step, 0)

    ch, taps = kernel.shape
    w = kernel[...]
    hi, lo = split(w)
    wide[...] = jnp.zeros_like(wide)
    wide[pl.ds(0, ch), pl.ds(0, taps)] = hi.astype(F32)
    wide[pl.ds(ch, ch), pl.ds(0, taps)] = lo.astype(F32)
    both = wide[...].astype(BF16)
    base = jnp.dot(both, pick[...], preferred_element_type=F32)
    rim = jnp.dot(both, pick2[...], preferred_element_type=F32)
    n = base.shape[1]
    kind = jnp.broadcast_to(code[0:1], base.shape)
    main = jnp.where(kind < 3, base, 0.0)
    bands = []
    for y in range(8):
        rows = main
        if y == 0:
            rows = jnp.where(kind == 0, 0.0, rows)
        if y == 7:
            rows = jnp.where(kind == 2, 0.0, rows)
        if y != 1:
            rows = pltpu.roll(rows, (y - 1) % n, 1)
        if y == 0:
            rows = rows + jnp.where(kind == 9, base, 0.0)
        if y == 7:
            rows = rows + jnp.where(kind == 10, base, 0.0)
        bands.append(rows)
    bands.append(jnp.where((kind == 0) | (kind == 8) | (kind == 9), rim, 0.0))
    bands.append(jnp.where((kind == 7) | (kind == 10) | (kind == 11), rim, 0.0))
    full = jnp.concatenate([b[:ch] for b in bands] + [b[ch:] for b in bands], axis=0)
    w_rows[...] = full.astype(BF16)
    kept = full.shape[0] // 2
    cols = jnp.concatenate([full[:kept], full[:kept], full[kept:]], axis=0)
    cols = jnp.concatenate([cols, jnp.zeros((512 - 3 * kept, n), F32)], axis=0)
    own_cols = []
    for q in range(3):
        own_cols += [cols[:, (3 * q + o) * BLOCK : (3 * q + o) * BLOCK + 40] for o in range(3)]
        own_cols.append(jnp.zeros((512, 8), F32))
    w_cols[...] = jnp.concatenate(own_cols, axis=1).T.astype(BF16)
    total = jnp.sum(w * mass[...], axis=1, keepdims=True)
    total = jnp.broadcast_to(total, (ch, 128))
    bias[...] = jnp.concatenate([total] * 10, axis=0)

    h_hi, h_lo = split(STEP * heads[...])
    none = jnp.zeros((3, ch), F32)
    pair = jnp.concatenate([h_hi.astype(F32), none, h_lo.astype(F32), none], axis=0).astype(BF16)
    r = lax.broadcasted_iota(jnp.int32, (kept, ch), 0)
    q = lax.broadcasted_iota(jnp.int32, (kept, ch), 1)
    spread = jnp.where((r & (ch - 1)) == q, 1.0, 0.0).astype(BF16)
    picked = over_lanes(pair, spread)
    y_of = lax.broadcasted_iota(jnp.int32, (8, kept), 0)
    col = lax.broadcasted_iota(jnp.int32, (8, kept), 1)
    same = (col >= y_of * ch) & (col < (y_of + 1) * ch)
    split_heads = []
    for at in (0, 8):
        rows = [
            jnp.where(same, jnp.broadcast_to(picked[at + e : at + e + 1], (8, kept)), 0.0)
            for e in range(5)
        ]
        five = picked[at : at + 8]
        rows.append(jnp.where((col >= 8 * ch) & (col < 9 * ch), five, 0.0))
        rows.append(jnp.where(col >= 9 * ch, five, 0.0))
        rows.append(jnp.zeros((8, kept), F32))
        split_heads.append(jnp.concatenate(rows, axis=0))
    three = jnp.concatenate([split_heads[0], split_heads[1], split_heads[0]], axis=0)
    w_head[...] = three.T.astype(BF16)


def e_kernel(state, cot, twin, other, order, out):
    del order
    nx = twin.shape[1]
    rim_state, rim_cot, rim_flags = from_rims(twin, other)

    def own(ref, row, v):
        return ref[pl.ds(v * nx * 8 + row, nx, stride=8), :]

    state_rows, cot_rows = {}, {}
    for v in range(5):
        for row in (*range(-5, 3), *range(6, 13)):
            inside = 0 <= row < 8
            state_rows[row, v] = own(state, row, v) if inside else rim_state(row, v)
        for row in (-3, -2, -1, 0, 8, 9, 10):
            inside = 0 <= row < 8
            cot_rows[row, v] = own(cot, row, v) if inside else rim_cot(row, v)
    sums = {}
    for j in (-3, -2, -1, 8, 9):
        cells = [[state_rows[j + k, v] for k in range(-2, 4)] for v in range(5)]
        face = [STEP * (cot_rows[j + 1, v] - cot_rows[j, v]) for v in range(5)]
        terms = face_pull(cells, face, rim_flags(j).astype(jnp.int32), 1)
        for v in range(5):
            for k in range(-2, 4):
                if 0 <= j + k < 8:
                    t = terms[v][k + 2]
                    sums[j + k, v] = sums[j + k, v] + t if (j + k, v) in sums else t
    for v in range(5):
        for row in range(8):
            value = sums[row, v] if (row, v) in sums else jnp.zeros((nx, 128), F32)
            out[pl.ds(v * nx * 8 + row, nx, stride=8), :] = value


def y_faces(x0, state, cot, flags, twin, other, own, first, rim, put, part, halo, ghalo):
    rim_state, rim_cot, _ = from_rims(twin, other)
    nx = state.shape[1]
    for v in range(5):
        base = v * nx * 8
        for r in range(ABOVE):
            halo[pl.ds(base + r, nx, stride=8), :] = rim_state(8 + r, v)
        for r in range(BELOW):
            halo[pl.ds(base + 8 - BELOW + r, nx, stride=8), :] = rim_state(r - BELOW, v)
        ghalo[pl.ds(base, nx, stride=8), :] = rim_cot(8, v)
    row = lax.broadcasted_iota(jnp.int32, (SLABS, 8, 128), 1)
    inside = {}
    for k in (-2, -1, 1, 2, 3):
        inside[k] = (row < 8 + k) if k < 0 else (row >= k)

    def step(i, carry):
        x = x0 + i * SLABS
        cells, face = [], []
        for v in range(5):
            at = pl.multiple_of((v * nx + x) * 8, 8)
            rim_rows = halo[pl.ds(at, 8 * SLABS), :].reshape(SLABS, 8, 128)
            mid = state[v, pl.ds(x, SLABS)]
            line = []
            for k in range(-2, 4):
                if k == 0:
                    line.append(mid)
                else:
                    line.append(pltpu.roll(jnp.where(inside[k], mid, rim_rows), (-k) % 8, 1))
            cells.append(line)
            g = cot[v, pl.ds(x, SLABS)]
            g_rim = ghalo[pl.ds(at, 8 * SLABS), :].reshape(SLABS, 8, 128)
            face.append(STEP * (pltpu.roll(jnp.where(inside[1], g, g_rim), 7, 1) - g))
        terms = face_pull(cells, face, flags[1, pl.ds(x, SLABS)], 1)
        for v in range(5):
            at = pl.multiple_of((v * nx + x) * 8, 8)
            total = own[v, pl.ds(x, SLABS)] + first[v, pl.ds(x, SLABS)] + terms[v][2]
            total = total + rim[pl.ds(at, 8 * SLABS), :].reshape(SLABS, 8, 128)
            for k in (-2, -1, 1, 2, 3):
                moved = pltpu.roll(terms[v][k + 2], k % 8, 1)
                total = total + jnp.where(inside[k], moved, 0.0)
            put(i, x, v, total)
        return carry

    lax.fori_loop(0, part // SLABS, step, 0)


def y_kernel(state, cot, flags, twin, other, own, first, rim, order, out, halo, ghalo):
    del order
    part = out.shape[1]

    def put(i, x, v, total):
        out[v, pl.ds(x, SLABS)] = total

    y_faces(0, state, cot, flags, twin, other, own, first, rim, put, part, halo, ghalo)


def y_last_kernel(state, cot, flags, twin, other, own, first, rim, done, order, out, halo, ghalo):
    del order
    part = done.shape[1]
    half = out.shape[1] - part

    def put(i, x, v, total):
        out[v, pl.ds(x, SLABS)] = total
        out[v, pl.ds(i * SLABS, SLABS)] = done[v, pl.ds(i * SLABS, SLABS)]

    y_faces(half, state, cot, flags, twin, other, own, first, rim, put, part, halo, ghalo)


def sum_kernel(scale, mine, theirs, k_out, h_out):
    total = (mine[...] + theirs[...]) * scale
    k_out[...] = total[:, : k_out.shape[1]]
    ch = total.shape[0]
    pick = (
        lax.broadcasted_iota(jnp.int32, (8, 128), 1)
        == lax.broadcasted_iota(jnp.int32, (8, 128), 0) + 16
    ).astype(F32)
    heads = lax.dot_general(
        pick,
        total[:, 128:],
        (((1,), (1,)), ((), ())),
        precision=lax.Precision.HIGHEST,
        preferred_element_type=F32,
    )
    h_out[...] = heads[: h_out.shape[0], :ch]


BLOCK = 64
SLOT = 3 * BLOCK


def split(x):
    hi = x.astype(BF16)
    return hi, (x - hi.astype(F32)).astype(BF16)


def over_lanes(a, b):
    return lax.dot_general(a, b, (((1,), (1,)), ((), ())), preferred_element_type=F32)


def is_even():
    return lax.rem(lax.axis_index("gy"), 2) == 0


def c_kernel(
    state, cot, twin, other, pick, code, mass, w_rows, w_cols, w_head, bias,
    own, parts,
    t, acc, edge, gedge,
):
    nx = state.shape[1]
    ch, taps = mass.shape
    rim_state, rim_cot, _ = from_rims(twin, other)

    for v in range(5):
        level = 1.0 if v in (0, 4) else 0.0
        for q, row in enumerate((-2, -1, 8, 9)):
            edge[pl.ds(5 * q + v, nx, stride=24), :] = rim_state(row, v) - level
        gedge[pl.ds(v, nx, stride=16), :] = rim_cot(-1, v)
        gedge[pl.ds(8 + v, nx, stride=16), :] = rim_cot(8, v)
    for q in range(20, 24):
        edge[pl.ds(q, nx, stride=24), :] = jnp.zeros((nx, 128), F32)
    for q in (5, 6, 7):
        gedge[pl.ds(q, nx, stride=16), :] = jnp.zeros((nx, 128), F32)
        gedge[pl.ds(8 + q, nx, stride=16), :] = jnp.zeros((nx, 128), F32)
    for x in range(nx):
        rows = [state[v, x] - (1.0 if v in (0, 4) else 0.0) for v in range(5)]
        rows.append(edge[pl.ds(x * 24, 24), :])
        mid = jnp.concatenate(rows, axis=0)
        at = (x + 1) * SLOT
        t[pl.ds(at, BLOCK), :] = pltpu.roll(mid, 1, 1).astype(BF16)
        t[pl.ds(at + BLOCK, BLOCK), :] = mid.astype(BF16)
        t[pl.ds(at + 2 * BLOCK, BLOCK), :] = pltpu.roll(mid, 127, 1).astype(BF16)
    t[pl.ds(0, SLOT), :] = t[pl.ds(nx * SLOT, SLOT), :]
    t[pl.ds((nx + 1) * SLOT, SLOT), :] = t[pl.ds(SLOT, SLOT), :]

    kept = 8 * ch
    kg = hg = dsum = None
    zeros8 = jnp.zeros((8, 128 * WIDE), F32)
    written = set()
    for x in range(0, nx, WIDE):
        s = jnp.concatenate([t[pl.ds((x + j) * SLOT, 3 * SLOT), :] for j in range(WIDE)], axis=1)
        z2 = jnp.dot(w_rows[...], s, preferred_element_type=F32)
        rows = z2.shape[0] // 2
        z = z2[:rows] + z2[rows:] + jnp.concatenate([bias[...]] * WIDE, axis=1)
        hidden = jnp.tanh(z)
        g = jnp.concatenate(
            [
                jnp.concatenate(
                    [cot[v, x + j] for v in range(5)] + [gedge[pl.ds((x + j) * 16, 16), :]], axis=0
                )
                for j in range(WIDE)
            ],
            axis=1,
        )
        g_hi, g_lo = split(g)
        g_hi32, g_lo32 = g_hi.astype(F32), g_lo.astype(F32)
        g3 = jnp.concatenate(
            [g_hi32, zeros8, g_hi32, zeros8, g_lo32, zeros8], axis=0
        ).astype(BF16)
        d = (1.0 - hidden * hidden) * jnp.dot(w_head[...], g3, preferred_element_type=F32)
        d_hi, d_lo = split(d)
        zeros = jnp.zeros((512 - 3 * rows, 128 * WIDE), BF16)
        back = jnp.dot(
            w_cols[...],
            jnp.concatenate([d_hi, d_lo, d_hi, zeros], axis=0),
            preferred_element_type=F32,
        )
        k2 = over_lanes(jnp.concatenate([d_hi[:kept], d_lo[:kept]], axis=0), s)
        k2 = k2[:kept] + k2[kept:]
        kg = k2 if kg is None else kg + k2
        hid2 = jnp.concatenate(split(hidden[:kept]), axis=0)
        g2 = jnp.concatenate([g_hi32[:40], g_lo32[:40]], axis=0).astype(BF16)
        h2 = over_lanes(hid2, g2)
        hg = h2 if hg is None else hg + h2
        for j in range(WIDE):
            level = d[:kept, 128 * j : 128 * (j + 1)]
            dsum = level if dsum is None else dsum + level
        for m in range(WIDE + 2):
            total = None
            for j in range(WIDE):
                if 0 <= m - j < 3:
                    q = m - j
                    piece = back[q * 128 : q * 128 + 120, 128 * j : 128 * (j + 1)]
                    total = piece if total is None else total + piece
            here = (x + m - 1) % nx
            if here in written:
                total = total + acc[pl.ds(here * 120, 120), :]
            written.add(here)
            acc[pl.ds(here * 120, 120), :] = total
    for x in range(nx):
        at = x * 120
        total = (
            acc[pl.ds(at + 40, 40), :]
            + pltpu.roll(acc[pl.ds(at, 40), :], 127, 1)
            + pltpu.roll(acc[pl.ds(at + 80, 40), :], 1, 1)
        )
        for v in range(5):
            own[v, x] = total[8 * v : 8 * v + 8]

    sums = jnp.sum(dsum, axis=1, keepdims=True)
    y_row = lax.broadcasted_iota(jnp.int32, (kept, 40), 0)
    y_col = lax.broadcasted_iota(jnp.int32, (kept, 40), 1) & 7
    same_y = (y_row >= y_col * ch) & (y_row < (y_col + 1) * ch)
    h_all = (hg[:kept, :40] + hg[kept:, :40]) + (hg[:kept, 40:80] + hg[kept:, 40:80])
    h_all = jnp.where(same_y, h_all, 0.0)
    level_sum = jnp.zeros((ch, 1), F32)
    head_sum = jnp.zeros((ch, 40), F32)
    n = kg.shape[1]
    kind = jnp.broadcast_to(code[0:1], (ch, n))
    total = jnp.zeros((ch, n), F32)
    for y in range(8):
        rows = kg[y * ch : (y + 1) * ch]
        moved = rows if y == 1 else pltpu.roll(rows, (1 - y) % n, 1)
        keep = kind < 3
        if y == 0:
            keep = (kind == 1) | (kind == 2)
            total = total + jnp.where(kind == 9, rows, 0.0)
        if y == 7:
            keep = kind < 2
            total = total + jnp.where(kind == 10, rows, 0.0)
        total = total + jnp.where(keep, moved, 0.0)
        level_sum = level_sum + sums[y * ch : (y + 1) * ch]
        head_sum = head_sum + h_all[y * ch : (y + 1) * ch]
    grads = over_lanes(jnp.concatenate(split(total), axis=0), pick[...])
    n_pick = pick.shape[0]
    parts[...] = jnp.zeros_like(parts)
    parts[:, pl.ds(0, n_pick)] = grads[:ch] + grads[ch:]
    parts[:, pl.ds(0, taps)] = parts[:, pl.ds(0, taps)] + level_sum * mass[...]
    e_row = lax.broadcasted_iota(jnp.int32, (40, 128), 0) >> 3
    e_col = lax.broadcasted_iota(jnp.int32, (40, 128), 1) - 16
    to_col = jnp.where(e_row == e_col, 1.0, 0.0).astype(BF16)
    head_out = jnp.dot(
        jnp.concatenate(split(head_sum * STEP), axis=0), to_col, preferred_element_type=F32
    )
    parts[:, pl.ds(128, 128)] = parts[:, pl.ds(128, 128)] + (head_out[:ch] + head_out[ch:])


def band_pick():
    n = 9 * BLOCK
    pick = np.zeros((144, n), np.float32)
    pick2 = np.zeros((144, n), np.float32)
    code = np.full((8, n), 12, np.int32)
    for o in range(9):
        for v in range(5):
            at = o * BLOCK
            tap = [(oy * 9 + o) * 5 + v for oy in range(3)]
            for k in range(8):
                code[:, at + v * 8 + k] = k
            for q in range(4):
                code[:, at + 40 + 5 * q + v] = 8 + q
            for oy in range(3):
                pick[tap[oy], at + v * 8 + oy] = 1.0
            pick[tap[0], at + 45 + v] = 1.0
            pick[tap[2], at + 50 + v] = 1.0
            pick2[tap[0], at + 40 + v] = 1.0
            pick2[tap[1], at + 45 + v] = 1.0
            pick2[tap[2], at + v * 8] = 1.0
            pick2[tap[0], at + v * 8 + 7] = 1.0
            pick2[tap[1], at + 50 + v] = 1.0
            pick2[tap[2], at + 55 + v] = 1.0
    return pick, pick2, code


def call(kernel, outs, scratch, us, n_in, order=0, space=pl.ANY, limit=VMEM):
    spec = pl.BlockSpec(memory_space=pltpu.VMEM)
    return pl.pallas_call(
        kernel,
        out_shape=outs,
        in_specs=[spec] * n_in + [pl.BlockSpec(memory_space=space)] * order,
        scratch_shapes=scratch,
        compiler_params=pltpu.CompilerParams(vmem_limit_bytes=limit),
        cost_estimate=pl.CostEstimate(
            flops=0, bytes_accessed=int(us * 3.69e6), transcendentals=0
        ),
    )


def body(pick, pick2, code, mass, state, cot, flags, kernel, heads):
    _, nx, ny, nz = state.shape
    ch, taps = kernel.shape
    count = lax.axis_size("gy")
    cells = nx * ny * nz
    half = nx // 2
    shape = lambda *dims: jax.ShapeDtypeStruct(dims, F32)
    half_shape = lambda *dims: jax.ShapeDtypeStruct(dims, BF16)
    full, part = shape(5, nx, ny, nz), shape(5, half, ny, nz)
    with_twin = [(i, i ^ 1) for i in range(count)]
    with_other = [(i, (i + 1) % count if i % 2 else (i - 1) % count) for i in range(count)]
    pick, pick2 = jnp.asarray(pick, BF16), jnp.asarray(pick2, BF16)
    code = jnp.asarray(code)
    mass = jnp.asarray(mass)
    vm = pltpu.VMEM
    lines = 5 * nx * ny
    flat_state, flat_cot = state.reshape(lines, nz), cot.reshape(lines, nz)

    sent = shape(SENT, nx, nz)
    to_twin, to_other = call(
        pack_kernel,
        (sent, sent),
        [
            vm((lines, nz), F32),
            vm((lines, nz), F32),
            vm((nx * ny, nz), jnp.int32),
            pltpu.SemaphoreType.DMA((3,)),
        ],
        1.0,
        0,
        3,
        pltpu.HBM,
        64 * 1024 * 1024 - 256 * 1024,
    )(flat_state, flat_cot, flags.reshape(3 * nx * ny, nz))
    twin = lax.ppermute(to_twin, "gy", with_twin)
    other = lax.ppermute(to_other, "gy", with_other)

    first, w_rows, w_cols, w_head, bias = call(
        xz_kernel,
        (
            full,
            half_shape(20 * ch, 9 * BLOCK),
            half_shape(384, 512),
            half_shape(10 * ch, SLOT),
            shape(10 * ch, 128),
        ),
        [
            vm((5, nx + 5, ny, nz), F32),
            vm((5, nx + 1, ny, nz), F32),
            vm((5, nx + 5, ny, nz), F32),
            vm((2 * ch, pick.shape[0]), F32),
        ],
        6.6,
        9,
    )(state, cot, flags, kernel, heads, pick, pick2, code, mass)
    own, parts = call(
        c_kernel,
        (full, shape(ch, 256)),
        [
            vm(((nx + 2) * SLOT, nz), BF16),
            vm((nx * 120, nz), F32),
            vm((24 * nx, nz), F32),
            vm((16 * nx, nz), F32),
        ],
        5.0,
        11,
    )(state, cot, twin, other, pick, code, mass, w_rows, w_cols, w_head, bias)

    def exchanged(value, bit):
        return lax.ppermute(value, "gy", [(i, i ^ bit) for i in range(count)])

    bits = [1 << b for b in range(count.bit_length() - 1)]
    sums = parts
    for bit in bits[:-3]:
        sums = sums + exchanged(sums, bit)
    halos = [vm((lines, nz), F32)] * 2
    got = exchanged(sums, bits[-3])
    rim = call(e_kernel, shape(lines, nz), [], 2.0, 4, 1)(
        flat_state, flat_cot, twin, other, sums
    )
    got, rim = lax.optimization_barrier((got, rim))
    sums = sums + got
    got = exchanged(sums, bits[-2])
    y0 = call(y_kernel, part, halos, 1.6, 8, 1)(
        state, cot, flags, twin, other, own, first, rim, sums
    )
    got, y0 = lax.optimization_barrier((got, y0))
    sums = sums + got
    got = exchanged(sums, bits[-1])
    flow = call(y_last_kernel, full, halos, 2.0, 9, 1)(
        state, cot, flags, twin, other, own, first, rim, y0, sums
    )
    scale = float(cells * count) ** (-0.5)
    k_out, h_out = call(
        functools.partial(sum_kernel, scale), (shape(ch, taps), shape(5, ch)), [], 0.5, 2
    )(sums, got)
    return flow, k_out, h_out


def solution(mesh):
    picks = band_pick()
    mass = np.zeros((16, 135), np.float32)
    mass[:, 0::5] = 1.0
    mass[:, 4::5] = 1.0
    split_y = P(None, "ens", "gy", None)
    return jax.shard_map(
        functools.partial(body, *picks, mass),
        mesh=mesh,
        in_specs=(split_y, split_y, split_y, P(), P()),
        out_specs=(split_y, P("ens", None), P("ens", None)),
        check_vma=False,
    )
```

time: 43.3 us -> 41.9 us (0.968)
  starting transfers between devices: 10.3 us -> 6.26 us
  local copies, waits for them, and re-layouts: 2.64 us -> 6.64 us
  waiting for transfers between devices: 10.3 us -> 8.37 us
    ppermute x2 -> x0, starting transfers between devices: 4.09 us -> none  [the longest x1 3.53 us: body(): back_other = lax.ppermute(give_other, 'gy', with_other)]
    unnamed x18 -> x20, local copies, waits for them, and re-layouts: 2.64 us -> 6.64 us
    ppermute x4, waiting for transfers between devices: 10.3 us -> 8.36 us  [exchanged(): return lax.ppermute(value, 'gy', [(i, i ^ bit) for i in range(count)])]
    pallas_call x7 -> x6, Pallas kernels: 18.3 us -> 18.7 us  [the longest x1 7.5 us: body(): call(xz_kernel, (full, half_shape(20 * ch, 9 * BLOCK), half_shape(384, 51...]
  transfers between devices with their start and end apart: 8 -> 6, of which waited for: 3 -> 4; matrix products, arithmetic and copies ran while one was open for 0% -> 0% of each run, Pallas kernels for 17% -> 30%
where the time goes in v2:
time: 41.9 us; the launch traced here: 41.5 us
  Pallas kernels  19.4 us (46%)
  waiting for transfers between devices  8.37 us (20%)
  local copies, waits for them, and re-layouts  6.64 us (16%)
  starting transfers between devices  6.26 us (15%)
  between operations  0.71 us (2%)
    ppermute x4, waiting for transfers between devices, exchanged(): return lax.ppermute(value, 'gy', [(i, i ^ bit) for i in range(count)])  8.36 us
    pallas_call x1, Pallas kernels, body(): call(xz_kernel, (full, half_shape(20 * ch, 9 * BLOCK), half_shape(384, 51...  7.5 us
    unnamed x20, local copies, waits for them, and re-layouts  6.64 us
    ppermute x1, starting transfers between devices, body(): other = lax.ppermute(to_other, 'gy', with_other)  5.67 us
    pallas_call x1, Pallas kernels, body(): call(c_kernel, (full, shape(ch, 256)), [vm(((nx + 2) * SLOT, nz), BF16),...  4.19 us
    pallas_call x1, Pallas kernels, body(): call(y_last_kernel, full, halos, 2.0, 9, 1)  2.26 us
    pallas_call x1, Pallas kernels, body(): call(pack_kernel, (sent, sent), [vm((lines, nz), F32), vm((lines, nz), F3...  2.14 us
    pallas_call x1, Pallas kernels, body(): call(y_kernel, part, halos, 1.6, 8, 1)  1.53 us
  transfers between devices with their start and end apart: 6, of which 4 were waited for; matrix products, arithmetic and copies ran while one was open for 0% of the time, Pallas kernels for 30%

profile of v2, /device:TPU:0, one launch (start us, length us, event | category | flops | bytes accessed | tf_op | source)
XLA Modules:
  0.0 41.5 jit_solution(9820762036739393805)
XLA Ops:
  0.6 0.0 copy-start.2
  0.6 2.1 %shard_map.112 = (f32[43,16,128]{2,1,0:T(8,128)}, f32[43,16,128]{2,1,0:T(8,128)}) custom-call(f32[640,128]{1,0:T(8,128)} %bitcast.3, f32[640,128]{1,0:T(8,128)} %bitcast.5, s32[384,128]{1,0:T(8,128)} %bitcast.7), custom_call_target="tpu_custom_call" | custom-call | bytes 3690000 | tf_op jit(solution)/shard_map/pallas_call | solution.py:692
  2.8 0.5 %collective-permute-start = (f32[43,16,128]{2,1,0:T(8,128)}, f32[43,16,128]{2,1,0:T(8,128)S(1)}, u32[]{:S(2)}, u32[]{:S(2)}) collective-permute-start(f32[43,16,128]{2,1,0:T(8,128)} %get-tuple-element.18), channel_id=1, source_target_pairs={{0,1},{1,0},{2,3},{3,2},{4,5},{5,4},{6,7},{7,6},{8,9},{9,8},{10,11... | collective-permute-start | bytes 1056776 | tf_op jit(solution)/shard_map/ppermute | solution.py:707
  3.3 5.7 %collective-permute-start.1 = (f32[43,16,128]{2,1,0:T(8,128)}, f32[43,16,128]{2,1,0:T(8,128)S(1)}, u32[]{:S(2)}, u32[]{:S(2)}) collective-permute-start(f32[43,16,128]{2,1,0:T(8,128)} %get-tuple-element.19), channel_id=1, source_target_pairs={{0,15},{1,2},{2,1},{3,4},{4,3},{5,6},{6,5},{7,8},{8,7},{9,10},{10,... | collective-permute-start | bytes 1056776 | tf_op jit(solution)/shard_map/ppermute | solution.py:708
  9.0 0.0 copy-done.2
  9.0 0.0 copy-start
  9.0 1.0 %copy-done = f32[5,16,8,128]{3,2,1,0:T(8,128)S(1)} copy-done((f32[5,16,8,128]{3,2,1,0:T(8,128)S(1)}, f32[5,16,8,128]{3,2,1,0:T(8,128)}, u32[]{:S(2)}) %copy-start) | copy-done | bytes 327704
  9.9 0.0 copy-start.1
  9.9 1.0 %copy-done.1 = f32[5,16,8,128]{3,2,1,0:T(8,128)S(1)} copy-done((f32[5,16,8,128]{3,2,1,0:T(8,128)S(1)}, f32[5,16,8,128]{3,2,1,0:T(8,128)}, u32[]{:S(2)}) %copy-start.1) | copy-done | bytes 327704
  10.9 0.9 %copy-done.3 = bf16[144,576]{1,0:T(8,128)(2,1)S(1)} copy-done((bf16[144,576]{1,0:T(8,128)(2,1)S(1)}, bf16[144,576]{1,0:T(8,128)(2,1)}, u32[]{:S(2)}) %copy-start.3) | copy-done | bytes 165912
  11.8 0.9 %copy-done.5 = bf16[144,576]{1,0:T(8,128)(2,1)S(1)} copy-done((bf16[144,576]{1,0:T(8,128)(2,1)S(1)}, bf16[144,576]{1,0:T(8,128)(2,1)}, u32[]{:S(2)}) %copy-start.5) | copy-done | bytes 165912
  12.8 0.7 %copy-done.6 = s32[8,576]{1,0:T(8,128)S(1)} copy-done((s32[8,576]{1,0:T(8,128)S(1)}, s32[8,576]{1,0:T(8,128)}, u32[]{:S(2)}) %copy-start.6) | copy-done | bytes 18456
  13.5 0.7 %copy-done.7 = f32[16,135]{1,0:T(8,128)S(1)} copy-done((f32[16,135]{1,0:T(8,128)S(1)}, f32[16,135]{1,0:T(8,128)}, u32[]{:S(2)}) %copy-start.7) | copy-done | bytes 8664
  14.2 0.7 %copy-done.8 = f32[16,135]{1,0:T(8,128)S(1)} copy-done((f32[16,135]{1,0:T(8,128)S(1)}, f32[16,135]{1,0:T(8,128)}, u32[]{:S(2)}) %copy-start.8) | copy-done | bytes 8664
  14.9 0.7 %copy-done.9 = f32[5,16]{1,0:T(8,128)S(1)} copy-done((f32[5,16]{1,0:T(8,128)S(1)}, f32[5,16]{1,0:T(8,128)}, u32[]{:S(2)}) %copy-start.9) | copy-done | bytes 344
  15.6 7.5 %shard_map.113 = (f32[5,16,8,128]{3,2,1,0:T(8,128)S(1)}, bf16[320,576]{1,0:T(8,128)(2,1)S(1)}, bf16[384,512]{1,0:T(8,128)(2,1)S(1)}, bf16[160,192]{1,0:T(8,128)(2,1)S(1)}, f32[160,128]{1,0:T(8,128)S(1)}) custom-call(f32[5,16,8,128]{3,2,1,0:T(8,128)S(1)} %copy-done, f32[5,16,8,128]{3,2,1,0:T(8,128)S(1)} %copy-done.1, s32[3,16,8,128]{3,2,1,0:T(8,128)S(1)} %copy-done.2, ...), custom_call_target="tpu_custom_call" | custom-call | bytes 24354000 | tf_op jit(solution)/shard_map/pallas_call | solution.py:710
  23.1 0.0 collective-permute-done.twin
  23.1 0.0 collective-permute-done.1.other
  23.1 0.0 copy-done.4
  23.1 4.2 %shard_map.114 = (f32[5,16,8,128]{3,2,1,0:T(8,128)S(1)}, f32[16,256]{1,0:T(8,128)S(1)}) custom-call(f32[5,16,8,128]{3,2,1,0:T(8,128)S(1)} %copy-done, f32[5,16,8,128]{3,2,1,0:T(8,128)S(1)} %copy-done.1, f32[43,16,128]{2,1,0:T(8,128)S(1)} %collective-permute-done.twin, f32[43,16,128]{2,1,0:T(8,128)S(1)} %collective-permute-done.1.other, ...), custom_call_target="tpu_custom_call" | custom-call | bytes 18450000 | tf_op jit(solution)/shard_map/pallas_call | solution.py:728
  27.3 0.1 collective-permute-start.2
  27.4 1.2 %collective-permute-done.2 = f32[16,256]{1,0:T(8,128)S(1)} collective-permute-done((f32[16,256]{1,0:T(8,128)S(1)}, f32[16,256]{1,0:T(8,128)S(1)}, u32[]{:S(2)}, u32[]{:S(2)}) %collective-permute-start.2) | collective-permute-done | bytes 16416 | tf_op jit(solution)/shard_map/ppermute | solution.py:742
  28.6 0.0 collective-permute-start.3
  28.6 1.1 %shard_map.115.rim = f32[640,128]{1,0:T(8,128)S(1)} custom-call(f32[640,128]{1,0:T(8,128)S(1)} %bitcast.4, f32[640,128]{1,0:T(8,128)S(1)} %bitcast.6, f32[43,16,128]{2,1,0:T(8,128)S(1)} %collective-permute-done.twin, f32[43,16,128]{2,1,0:T(8,128)S(1)} %collective-permute-done.1.other, f32[16,256]{1,0:T(8,128)S(1)} %add.9.order), custom_call_target="tpu_custom_call" | custom-call | bytes 7380000 | tf_op jit(solution)/shard_map/pallas_call | solution.py:750
  29.7 2.6 %collective-permute-done.3 = f32[16,256]{1,0:T(8,128)S(1)} collective-permute-done((f32[16,256]{1,0:T(8,128)S(1)}, f32[16,256]{1,0:T(8,128)S(1)}, u32[]{:S(2)}, u32[]{:S(2)}) %collective-permute-start.3) | collective-permute-done | bytes 16416 | tf_op jit(solution)/shard_map/ppermute | solution.py:742
  32.3 0.0 collective-permute-start.4
  32.3 1.5 %shard_map.116.done = f32[5,8,8,128]{3,2,1,0:T(8,128)S(1)} custom-call(f32[5,16,8,128]{3,2,1,0:T(8,128)S(1)} %copy-done, f32[5,16,8,128]{3,2,1,0:T(8,128)S(1)} %copy-done.1, s32[3,16,8,128]{3,2,1,0:T(8,128)S(1)} %copy-done.2, f32[43,16,128]{2,1,0:T(8,128)S(1)} %collective-permute-done.twin, f32[43,16,128]{2,1,0:T(8,128)S(1)} %collective-permute-done.1.other, ...), custom_call_target="tpu_custom_call" | custom-call | bytes 5904000 | tf_op jit(solution)/shard_map/pallas_call | solution.py:756
  33.9 2.2 %collective-permute-done.4 = f32[16,256]{1,0:T(8,128)S(1)} collective-permute-done((f32[16,256]{1,0:T(8,128)S(1)}, f32[16,256]{1,0:T(8,128)S(1)}, u32[]{:S(2)}, u32[]{:S(2)}) %collective-permute-start.4) | collective-permute-done | bytes 16416 | tf_op jit(solution)/shard_map/ppermute | solution.py:742
  36.1 0.0 collective-permute-start.5
  36.1 2.3 %shard_map.117 = f32[5,16,8,128]{3,2,1,0:T(8,128)} custom-call(f32[5,16,8,128]{3,2,1,0:T(8,128)S(1)} %copy-done, f32[5,16,8,128]{3,2,1,0:T(8,128)S(1)} %copy-done.1, s32[3,16,8,128]{3,2,1,0:T(8,128)S(1)} %copy-done.2, f32[43,16,128]{2,1,0:T(8,128)S(1)} %collective-permute-done.twin, f32[43,16,128]{2,1,0:T(8,128)S(1)} %collective-permute-done.1.other, ...), custom_call_target="tpu_custom_call" | custom-call | bytes 7380000 | tf_op jit(solution)/shard_map/pallas_call | solution.py:762
  38.4 2.4 %collective-permute-done.5.theirs = f32[16,256]{1,0:T(8,128)S(1)} collective-permute-done((f32[16,256]{1,0:T(8,128)S(1)}, f32[16,256]{1,0:T(8,128)S(1)}, u32[]{:S(2)}, u32[]{:S(2)}) %collective-permute-start.5) | collective-permute-done | bytes 16416 | tf_op jit(solution)/shard_map/ppermute | solution.py:742
  40.7 0.7 %shard_map.118 = (f32[16,135]{1,0:T(8,128)}, f32[5,16]{1,0:T(8,128)}) custom-call(f32[16,256]{1,0:T(8,128)S(1)} %add.11.order.mine, f32[16,256]{1,0:T(8,128)S(1)} %collective-permute-done.5.theirs), custom_call_target="tpu_custom_call" | custom-call | bytes 1845000 | tf_op jit(solution)/shard_map/pallas_call | solution.py:766
  (10 shorter events, 0.0 us)
Async XLA Ops:
  0.6 8.3 %copy-start.2 = (s32[3,16,8,128]{3,2,1,0:T(8,128)S(1)}, s32[3,16,8,128]{3,2,1,0:T(8,128)}, u32[]{:S(2)}) copy-start(s32[3,16,8,128]{3,2,1,0:T(8,128)} %flags.5) | copy-start | bytes 589828
  2.8 20.3 %collective-permute-start = (f32[43,16,128]{2,1,0:T(8,128)}, f32[43,16,128]{2,1,0:T(8,128)S(1)}, u32[]{:S(2)}, u32[]{:S(2)}) collective-permute-start(f32[43,16,128]{2,1,0:T(8,128)} %get-tuple-element.18), channel_id=1, source_target_pairs={{0,1},{1,0},{2,3},{3,2},{4,5},{5,4},{6,7},{7,6},{8,9},{9,8},{10,11... | collective-permute-start | bytes 1056776 | tf_op jit(solution)/shard_map/ppermute | solution.py:707
  3.3 19.8 %collective-permute-start.1 = (f32[43,16,128]{2,1,0:T(8,128)}, f32[43,16,128]{2,1,0:T(8,128)S(1)}, u32[]{:S(2)}, u32[]{:S(2)}) collective-permute-start(f32[43,16,128]{2,1,0:T(8,128)} %get-tuple-element.19), channel_id=1, source_target_pairs={{0,15},{1,2},{2,1},{3,4},{4,3},{5,6},{6,5},{7,8},{8,7},{9,10},{10,... | collective-permute-start | bytes 1056776 | tf_op jit(solution)/shard_map/ppermute | solution.py:708
  9.0 1.0 %copy-start = (f32[5,16,8,128]{3,2,1,0:T(8,128)S(1)}, f32[5,16,8,128]{3,2,1,0:T(8,128)}, u32[]{:S(2)}) copy-start(f32[5,16,8,128]{3,2,1,0:T(8,128)} %state.7) | copy-start | bytes 983044
  9.9 1.0 %copy-start.1 = (f32[5,16,8,128]{3,2,1,0:T(8,128)S(1)}, f32[5,16,8,128]{3,2,1,0:T(8,128)}, u32[]{:S(2)}) copy-start(f32[5,16,8,128]{3,2,1,0:T(8,128)} %cot.7) | copy-start | bytes 983044
  10.9 0.9 %copy-start.3 = (bf16[144,576]{1,0:T(8,128)(2,1)S(1)}, bf16[144,576]{1,0:T(8,128)(2,1)}, u32[]{:S(2)}) copy-start(bf16[144,576]{1,0:T(8,128)(2,1)} %constant.8.clone.pick) | copy-start | bytes 497668
  11.8 0.9 %copy-start.5 = (bf16[144,576]{1,0:T(8,128)(2,1)S(1)}, bf16[144,576]{1,0:T(8,128)(2,1)}, u32[]{:S(2)}) copy-start(bf16[144,576]{1,0:T(8,128)(2,1)} %constant.9.clone.pick2) | copy-start | bytes 497668
  12.8 0.7 %copy-start.6 = (s32[8,576]{1,0:T(8,128)S(1)}, s32[8,576]{1,0:T(8,128)}, u32[]{:S(2)}) copy-start(s32[8,576]{1,0:T(8,128)} %constant.10.clone.code) | copy-start | bytes 55300
  13.5 0.7 %copy-start.7 = (f32[16,135]{1,0:T(8,128)S(1)}, f32[16,135]{1,0:T(8,128)}, u32[]{:S(2)}) copy-start(f32[16,135]{1,0:T(8,128)} %constant.11.clone.mass) | copy-start | bytes 25924
  14.2 0.7 %copy-start.8 = (f32[16,135]{1,0:T(8,128)S(1)}, f32[16,135]{1,0:T(8,128)}, u32[]{:S(2)}) copy-start(f32[16,135]{1,0:T(8,128)} %kernel.1) | copy-start | bytes 25924
  14.9 0.7 %copy-start.9 = (f32[5,16]{1,0:T(8,128)S(1)}, f32[5,16]{1,0:T(8,128)}, u32[]{:S(2)}) copy-start(f32[5,16]{1,0:T(8,128)} %heads.1) | copy-start | bytes 964
  15.6 7.5 %copy-start.4 = (bf16[144,576]{1,0:T(8,128)(2,1)S(1)}, bf16[144,576]{1,0:T(8,128)(2,1)}, u32[]{:S(2)}) copy-start(bf16[144,576]{1,0:T(8,128)(2,1)} %constant.8.clone.pick) | copy-start | bytes 497668
  27.3 1.2 %collective-permute-start.2 = (f32[16,256]{1,0:T(8,128)S(1)}, f32[16,256]{1,0:T(8,128)S(1)}, u32[]{:S(2)}, u32[]{:S(2)}) collective-permute-start(f32[16,256]{1,0:T(8,128)S(1)} %get-tuple-element.26), channel_id=1, source_target_pairs={{0,1},{1,0},{2,3},{3,2},{4,5},{5,4},{6,7},{7,6},{8,9},{9,8},{10,11... | collective-permute-start | bytes 49160 | tf_op jit(solution)/shard_map/ppermute | solution.py:742
  28.6 3.7 %collective-permute-start.3 = (f32[16,256]{1,0:T(8,128)S(1)}, f32[16,256]{1,0:T(8,128)S(1)}, u32[]{:S(2)}, u32[]{:S(2)}) collective-permute-start(f32[16,256]{1,0:T(8,128)S(1)} %add.9.order), channel_id=1, source_target_pairs={{0,2},{1,3},{2,0},{3,1},{4,6},{5,7},{6,4},{7,5},{8,10},{9,11},{10,... | collective-permute-start | bytes 49160 | tf_op jit(solution)/shard_map/ppermute | solution.py:742
  32.3 3.7 %collective-permute-start.4 = (f32[16,256]{1,0:T(8,128)S(1)}, f32[16,256]{1,0:T(8,128)S(1)}, u32[]{:S(2)}, u32[]{:S(2)}) collective-permute-start(f32[16,256]{1,0:T(8,128)S(1)} %add.10.order), channel_id=1, source_target_pairs={{0,4},{1,5},{2,6},{3,7},{4,0},{5,1},{6,2},{7,3},{8,12},{9,13},{10,... | collective-permute-start | bytes 49160 | tf_op jit(solution)/shard_map/ppermute | solution.py:742
  36.1 4.6 %collective-permute-start.5 = (f32[16,256]{1,0:T(8,128)S(1)}, f32[16,256]{1,0:T(8,128)S(1)}, u32[]{:S(2)}, u32[]{:S(2)}) collective-permute-start(f32[16,256]{1,0:T(8,128)S(1)} %add.11.order.mine), channel_id=1, source_target_pairs={{0,8},{1,9},{2,10},{3,11},{4,12},{5,13},{6,14},{7,15},{8,0},{9,1},... | collective-permute-start | bytes 49160 | tf_op jit(solution)/shard_map/ppermute | solution.py:742

commit v3 on v2

--- a/solution.py
+++ b/solution.py
@@ -2,7 +2,6 @@
 
 import jax
 import jax.numpy as jnp
-import numpy as np
 from jax import lax
 from jax.experimental import pallas as pl
 from jax.experimental.pallas import tpu as pltpu
@@ -185,17 +184,18 @@
 SENT = FLAGS_AT + REACH_FLAGS
 
 
-def pack_kernel(state, cot, flags, twin, other, s, g, f, sem):
-    rows_in = f.shape[0]
-    copies = [
-        pltpu.make_async_copy(state, s, sem.at[0]),
-        pltpu.make_async_copy(cot, g, sem.at[1]),
-        pltpu.make_async_copy(flags.at[pl.ds(rows_in, rows_in)], f, sem.at[2]),
-    ]
-    for copy in copies:
-        copy.start()
-    for copy in copies:
-        copy.wait()
+def views(fields):
+    n = fields.shape[0] // 13
+    return (
+        fields.at[pl.ds(0, 5 * n)],
+        fields.at[pl.ds(5 * n, 5 * n)],
+        fields.at[pl.ds(10 * n, 3 * n)],
+    )
+
+
+def pack_kernel(fields, twin, other):
+    s, g, f = views(fields)
+    rows_in = f.shape[0] // 3
     even = is_even()
     nx = twin.shape[1]
 
@@ -213,9 +213,9 @@
                     ref[pl.ds(base + 8 - reach + r, nx, stride=8), :],
                 )
     for r in range(REACH_FLAGS):
-        low = f[pl.ds(r, nx, stride=8), :]
-        top = f[pl.ds(8 - REACH_FLAGS + r, nx, stride=8), :]
-        put(FLAGS_AT + r, low.astype(F32), top.astype(F32))
+        low = f[pl.ds(rows_in + r, nx, stride=8), :]
+        top = f[pl.ds(rows_in + 8 - REACH_FLAGS + r, nx, stride=8), :]
+        put(FLAGS_AT + r, low, top)
 
 
 def from_rims(twin, other):
@@ -244,7 +244,8 @@
     return state, cot, flags
 
 
-def xz_kernel(state, cot, flags, kernel, heads, pick, pick2, code, mass, out, w_rows, w_cols, w_head, bias, pad, gpad, acc, wide):
+def x_kernel(fields, out, pad, gpad, acc):
+    state, cot, flags = views(fields)
     nx = state.shape[1]
     for v in range(5):
         pad[v, pl.ds(2, nx)] = state[v]
@@ -259,7 +260,7 @@
         cells = [[pad[v, pl.ds(x + k, SLABS)] for k in range(6)] for v in range(5)]
         g = [gpad[v, pl.ds(x, SLABS)] for v in range(5)]
         face = [STEP * (gpad[v, pl.ds(x + 1, SLABS)] - g[v]) for v in range(5)]
-        terms = face_pull(cells, face, flags[0, pl.ds(x, SLABS)], 0)
+        terms = face_pull(cells, face, flags[0, pl.ds(x, SLABS)].astype(jnp.int32), 0)
         own = conserved_pull([cells[v][2] for v in range(5)], g)
         for v in range(5):
             terms[v][2] = terms[v][2] + own[v]
@@ -277,6 +278,15 @@
         acc[v, pl.ds(nx, 2)] = acc[v, pl.ds(nx, 2)] + acc[v, pl.ds(0, 2)]
         acc[v, pl.ds(2, 3)] = acc[v, pl.ds(2, 3)] + acc[v, pl.ds(nx + 2, 3)]
 
+    for v in range(5):
+        out[v] = acc[v, pl.ds(2, nx)]
+
+
+def z_kernel(fields, first, order, out):
+    del order
+    state, cot, flags = views(fields)
+    nx = state.shape[1]
+
     def z_step(i, carry):
         x = i * SLABS
         cells, face = [], []
@@ -285,9 +295,9 @@
             cells.append([mid if k == 0 else pltpu.roll(mid, (-k) % 128, 2) for k in range(-2, 4)])
             g = cot[v, pl.ds(x, SLABS)]
             face.append(STEP * (pltpu.roll(g, 127, 2) - g))
-        terms = face_pull(cells, face, flags[2, pl.ds(x, SLABS)], 2)
+        terms = face_pull(cells, face, flags[2, pl.ds(x, SLABS)].astype(jnp.int32), 2)
         for v in range(5):
-            t = acc[v, pl.ds(x + 2, SLABS)] + terms[v][2]
+            t = first[v, pl.ds(x, SLABS)] + terms[v][2]
             for k in (-2, -1, 1, 2, 3):
                 t = t + pltpu.roll(terms[v][k + 2], k % 128, 2)
             out[v, pl.ds(x, SLABS)] = t
@@ -295,6 +305,145 @@
 
     lax.fori_loop(0, nx // SLABS, z_step, 0)
 
+
+def e_kernel(fields, twin, other, order, out):
+    del order
+    state, cot, _ = views(fields)
+    nx = twin.shape[1]
+    rim_state, rim_cot, rim_flags = from_rims(twin, other)
+
+    def own(ref, row, v):
+        return ref[pl.ds(v * nx * 8 + row, nx, stride=8), :]
+
+    state_rows, cot_rows = {}, {}
+    for v in range(5):
+        for row in (*range(-5, 3), *range(6, 13)):
+            inside = 0 <= row < 8
+            state_rows[row, v] = own(state, row, v) if inside else rim_state(row, v)
+        for row in (-3, -2, -1, 0, 8, 9, 10):
+            inside = 0 <= row < 8
+            cot_rows[row, v] = own(cot, row, v) if inside else rim_cot(row, v)
+    sums = {}
+    for j in (-3, -2, -1, 8, 9):
+        cells = [[state_rows[j + k, v] for k in range(-2, 4)] for v in range(5)]
+        face = [STEP * (cot_rows[j + 1, v] - cot_rows[j, v]) for v in range(5)]
+        terms = face_pull(cells, face, rim_flags(j).astype(jnp.int32), 1)
+        for v in range(5):
+            for k in range(-2, 4):
+                if 0 <= j + k < 8:
+                    t = terms[v][k + 2]
+                    sums[j + k, v] = sums[j + k, v] + t if (j + k, v) in sums else t
+    for v in range(5):
+        for row in range(8):
+            value = sums[row, v] if (row, v) in sums else jnp.zeros((nx, 128), F32)
+            out[pl.ds(v * nx * 8 + row, nx, stride=8), :] = value
+
+
+def y_faces(x0, fields, twin, other, own, first, rim, put, part, halo, ghalo):
+    rim_state, rim_cot, _ = from_rims(twin, other)
+    state, cot, flags = views(fields)
+    nx = state.shape[1]
+    for v in range(5):
+        base = v * nx * 8
+        for r in range(ABOVE):
+            halo[pl.ds(base + r, nx, stride=8), :] = rim_state(8 + r, v)
+        for r in range(BELOW):
+            halo[pl.ds(base + 8 - BELOW + r, nx, stride=8), :] = rim_state(r - BELOW, v)
+        ghalo[pl.ds(base, nx, stride=8), :] = rim_cot(8, v)
+    row = lax.broadcasted_iota(jnp.int32, (SLABS, 8, 128), 1)
+    inside = {}
+    for k in (-2, -1, 1, 2, 3):
+        inside[k] = (row < 8 + k) if k < 0 else (row >= k)
+
+    def step(i, carry):
+        x = x0 + i * SLABS
+        cells, face = [], []
+        for v in range(5):
+            at = pl.multiple_of((v * nx + x) * 8, 8)
+            rim_rows = halo[pl.ds(at, 8 * SLABS), :].reshape(SLABS, 8, 128)
+            mid = state[v, pl.ds(x, SLABS)]
+            line = []
+            for k in range(-2, 4):
+                if k == 0:
+                    line.append(mid)
+                else:
+                    line.append(pltpu.roll(jnp.where(inside[k], mid, rim_rows), (-k) % 8, 1))
+            cells.append(line)
+            g = cot[v, pl.ds(x, SLABS)]
+            g_rim = ghalo[pl.ds(at, 8 * SLABS), :].reshape(SLABS, 8, 128)
+            face.append(STEP * (pltpu.roll(jnp.where(inside[1], g, g_rim), 7, 1) - g))
+        terms = face_pull(cells, face, flags[1, pl.ds(x, SLABS)].astype(jnp.int32), 1)
+        for v in range(5):
+            at = pl.multiple_of((v * nx + x) * 8, 8)
+            total = own[v, pl.ds(x, SLABS)] + first[v, pl.ds(x, SLABS)] + terms[v][2]
+            total = total + rim[pl.ds(at, 8 * SLABS), :].reshape(SLABS, 8, 128)
+            for k in (-2, -1, 1, 2, 3):
+                moved = pltpu.roll(terms[v][k + 2], k % 8, 1)
+                total = total + jnp.where(inside[k], moved, 0.0)
+            put(i, x, v, total)
+        return carry
+
+    lax.fori_loop(0, part // SLABS, step, 0)
+
+
+def y_kernel(fields, twin, other, own, first, rim, order, out, halo, ghalo):
+    del order
+    part = out.shape[1]
+
+    def put(i, x, v, total):
+        out[v, pl.ds(x, SLABS)] = total
+
+    y_faces(0, fields, twin, other, own, first, rim, put, part, halo, ghalo)
+
+
+def y_last_kernel(fields, twin, other, own, first, rim, done, order, out, halo, ghalo):
+    del order
+    part = done.shape[1]
+    half = out.shape[1] - part
+
+    def put(i, x, v, total):
+        out[v, pl.ds(x, SLABS)] = total
+        out[v, pl.ds(i * SLABS, SLABS)] = done[v, pl.ds(i * SLABS, SLABS)]
+
+    y_faces(half, fields, twin, other, own, first, rim, put, part, halo, ghalo)
+
+
+def sum_kernel(scale, mine, theirs, k_out, h_out):
+    total = (mine[...] + theirs[...]) * scale
+    k_out[...] = total[:, : k_out.shape[1]]
+    ch = total.shape[0]
+    pick = (
+        lax.broadcasted_iota(jnp.int32, (8, 128), 1)
+        == lax.broadcasted_iota(jnp.int32, (8, 128), 0) + 16
+    ).astype(F32)
+    heads = lax.dot_general(
+        pick,
+        total[:, 128:],
+        (((1,), (1,)), ((), ())),
+        precision=lax.Precision.HIGHEST,
+        preferred_element_type=F32,
+    )
+    h_out[...] = heads[: h_out.shape[0], :ch]
+
+
+BLOCK = 64
+SLOT = 3 * BLOCK
+
+
+def split(x):
+    hi = x.astype(BF16)
+    return hi, (x - hi.astype(F32)).astype(BF16)
+
+
+def over_lanes(a, b):
+    return lax.dot_general(a, b, (((1,), (1,)), ((), ())), preferred_element_type=F32)
+
+
+def is_even():
+    return lax.rem(lax.axis_index("gy"), 2) == 0
+
+
+def band_matrices(kernel, heads, wide):
     ch, taps = kernel.shape
     w = kernel[...]
     hi, lo = split(w)
@@ -302,10 +451,11 @@
     wide[pl.ds(0, ch), pl.ds(0, taps)] = hi.astype(F32)
     wide[pl.ds(ch, ch), pl.ds(0, taps)] = lo.astype(F32)
     both = wide[...].astype(BF16)
-    base = jnp.dot(both, pick[...], preferred_element_type=F32)
-    rim = jnp.dot(both, pick2[...], preferred_element_type=F32)
+    kind, tap = columns()
+    base = jnp.dot(both, own_taps(kind, tap), preferred_element_type=F32)
+    rim = jnp.dot(both, rim_taps(kind, tap), preferred_element_type=F32)
     n = base.shape[1]
-    kind = jnp.broadcast_to(code[0:1], base.shape)
+    kind = jnp.broadcast_to(kind[0:1], base.shape)
     main = jnp.where(kind < 3, base, 0.0)
     bands = []
     for y in range(8):
@@ -324,7 +474,7 @@
     bands.append(jnp.where((kind == 0) | (kind == 8) | (kind == 9), rim, 0.0))
     bands.append(jnp.where((kind == 7) | (kind == 10) | (kind == 11), rim, 0.0))
     full = jnp.concatenate([b[:ch] for b in bands] + [b[ch:] for b in bands], axis=0)
-    w_rows[...] = full.astype(BF16)
+    w_rows = full.astype(BF16)
     kept = full.shape[0] // 2
     cols = jnp.concatenate([full[:kept], full[:kept], full[kept:]], axis=0)
     cols = jnp.concatenate([cols, jnp.zeros((512 - 3 * kept, n), F32)], axis=0)
@@ -332,10 +482,10 @@
     for q in range(3):
         own_cols += [cols[:, (3 * q + o) * BLOCK : (3 * q + o) * BLOCK + 40] for o in range(3)]
         own_cols.append(jnp.zeros((512, 8), F32))
-    w_cols[...] = jnp.concatenate(own_cols, axis=1).T.astype(BF16)
-    total = jnp.sum(w * mass[...], axis=1, keepdims=True)
+    w_cols = jnp.concatenate(own_cols, axis=1).T.astype(BF16)
+    total = jnp.sum(w * level_taps(w.shape), axis=1, keepdims=True)
     total = jnp.broadcast_to(total, (ch, 128))
-    bias[...] = jnp.concatenate([total] * 10, axis=0)
+    bias = jnp.concatenate([total] * 10, axis=0)
 
     h_hi, h_lo = split(STEP * heads[...])
     none = jnp.zeros((3, ch), F32)
@@ -359,151 +509,19 @@
         rows.append(jnp.zeros((8, kept), F32))
         split_heads.append(jnp.concatenate(rows, axis=0))
     three = jnp.concatenate([split_heads[0], split_heads[1], split_heads[0]], axis=0)
-    w_head[...] = three.T.astype(BF16)
-
-
-def e_kernel(state, cot, twin, other, order, out):
-    del order
-    nx = twin.shape[1]
-    rim_state, rim_cot, rim_flags = from_rims(twin, other)
-
-    def own(ref, row, v):
-        return ref[pl.ds(v * nx * 8 + row, nx, stride=8), :]
-
-    state_rows, cot_rows = {}, {}
-    for v in range(5):
-        for row in (*range(-5, 3), *range(6, 13)):
-            inside = 0 <= row < 8
-            state_rows[row, v] = own(state, row, v) if inside else rim_state(row, v)
-        for row in (-3, -2, -1, 0, 8, 9, 10):
-            inside = 0 <= row < 8
-            cot_rows[row, v] = own(cot, row, v) if inside else rim_cot(row, v)
-    sums = {}
-    for j in (-3, -2, -1, 8, 9):
-        cells = [[state_rows[j + k, v] for k in range(-2, 4)] for v in range(5)]
-        face = [STEP * (cot_rows[j + 1, v] - cot_rows[j, v]) for v in range(5)]
-        terms = face_pull(cells, face, rim_flags(j).astype(jnp.int32), 1)
-        for v in range(5):
-            for k in range(-2, 4):
-                if 0 <= j + k < 8:
-                    t = terms[v][k + 2]
-                    sums[j + k, v] = sums[j + k, v] + t if (j + k, v) in sums else t
-    for v in range(5):
-        for row in range(8):
-            value = sums[row, v] if (row, v) in sums else jnp.zeros((nx, 128), F32)
-            out[pl.ds(v * nx * 8 + row, nx, stride=8), :] = value
-
-
-def y_faces(x0, state, cot, flags, twin, other, own, first, rim, put, part, halo, ghalo):
-    rim_state, rim_cot, _ = from_rims(twin, other)
+    w_head = three.T.astype(BF16)
+    return w_rows, w_cols, w_head, bias
+
+
+def c_kernel(
+    fields, twin, other, kernel, heads,
+    own, parts,
+    t, acc, edge, gedge, wide,
+):
+    state, cot, _ = views(fields)
     nx = state.shape[1]
-    for v in range(5):
-        base = v * nx * 8
-        for r in range(ABOVE):
-            halo[pl.ds(base + r, nx, stride=8), :] = rim_state(8 + r, v)
-        for r in range(BELOW):
-            halo[pl.ds(base + 8 - BELOW + r, nx, stride=8), :] = rim_state(r - BELOW, v)
-        ghalo[pl.ds(base, nx, stride=8), :] = rim_cot(8, v)
-    row = lax.broadcasted_iota(jnp.int32, (SLABS, 8, 128), 1)
-    inside = {}
-    for k in (-2, -1, 1, 2, 3):
-        inside[k] = (row < 8 + k) if k < 0 else (row >= k)
-
-    def step(i, carry):
-        x = x0 + i * SLABS
-        cells, face = [], []
-        for v in range(5):
-            at = pl.multiple_of((v * nx + x) * 8, 8)
-            rim_rows = halo[pl.ds(at, 8 * SLABS), :].reshape(SLABS, 8, 128)
-            mid = state[v, pl.ds(x, SLABS)]
-            line = []
-            for k in range(-2, 4):
-                if k == 0:
-                    line.append(mid)
-                else:
-                    line.append(pltpu.roll(jnp.where(inside[k], mid, rim_rows), (-k) % 8, 1))
-            cells.append(line)
-            g = cot[v, pl.ds(x, SLABS)]
-            g_rim = ghalo[pl.ds(at, 8 * SLABS), :].reshape(SLABS, 8, 128)
-            face.append(STEP * (pltpu.roll(jnp.where(inside[1], g, g_rim), 7, 1) - g))
-        terms = face_pull(cells, face, flags[1, pl.ds(x, SLABS)], 1)
-        for v in range(5):
-            at = pl.multiple_of((v * nx + x) * 8, 8)
-            total = own[v, pl.ds(x, SLABS)] + first[v, pl.ds(x, SLABS)] + terms[v][2]
-            total = total + rim[pl.ds(at, 8 * SLABS), :].reshape(SLABS, 8, 128)
-            for k in (-2, -1, 1, 2, 3):
-                moved = pltpu.roll(terms[v][k + 2], k % 8, 1)
-                total = total + jnp.where(inside[k], moved, 0.0)
-            put(i, x, v, total)
-        return carry
-
-    lax.fori_loop(0, part // SLABS, step, 0)
-
-
-def y_kernel(state, cot, flags, twin, other, own, first, rim, order, out, halo, ghalo):
-    del order
-    part = out.shape[1]
-
-    def put(i, x, v, total):
-        out[v, pl.ds(x, SLABS)] = total
-
-    y_faces(0, state, cot, flags, twin, other, own, first, rim, put, part, halo, ghalo)
-
-
-def y_last_kernel(state, cot, flags, twin, other, own, first, rim, done, order, out, halo, ghalo):
-    del order
-    part = done.shape[1]
-    half = out.shape[1] - part
-
-    def put(i, x, v, total):
-        out[v, pl.ds(x, SLABS)] = total
-        out[v, pl.ds(i * SLABS, SLABS)] = done[v, pl.ds(i * SLABS, SLABS)]
-
-    y_faces(half, state, cot, flags, twin, other, own, first, rim, put, part, halo, ghalo)
-
-
-def sum_kernel(scale, mine, theirs, k_out, h_out):
-    total = (mine[...] + theirs[...]) * scale
-    k_out[...] = total[:, : k_out.shape[1]]
-    ch = total.shape[0]
-    pick = (
-        lax.broadcasted_iota(jnp.int32, (8, 128), 1)
-        == lax.broadcasted_iota(jnp.int32, (8, 128), 0) + 16
-    ).astype(F32)
-    heads = lax.dot_general(
-        pick,
-        total[:, 128:],
-        (((1,), (1,)), ((), ())),
-        precision=lax.Precision.HIGHEST,
-        preferred_element_type=F32,
-    )
-    h_out[...] = heads[: h_out.shape[0], :ch]
-
-
-BLOCK = 64
-SLOT = 3 * BLOCK
-
-
-def split(x):
-    hi = x.astype(BF16)
-    return hi, (x - hi.astype(F32)).astype(BF16)
-
-
-def over_lanes(a, b):
-    return lax.dot_general(a, b, (((1,), (1,)), ((), ())), preferred_element_type=F32)
-
-
-def is_even():
-    return lax.rem(lax.axis_index("gy"), 2) == 0
-
-
-def c_kernel(
-    state, cot, twin, other, pick, code, mass, w_rows, w_cols, w_head, bias,
-    own, parts,
-    t, acc, edge, gedge,
-):
-    nx = state.shape[1]
-    ch, taps = mass.shape
+    ch, taps = kernel.shape
+    w_rows, w_cols, w_head, bias = band_matrices(kernel, heads, wide)
     rim_state, rim_cot, _ = from_rims(twin, other)
 
     for v in range(5):
@@ -534,9 +552,9 @@
     written = set()
     for x in range(0, nx, WIDE):
         s = jnp.concatenate([t[pl.ds((x + j) * SLOT, 3 * SLOT), :] for j in range(WIDE)], axis=1)
-        z2 = jnp.dot(w_rows[...], s, preferred_element_type=F32)
+        z2 = jnp.dot(w_rows, s, preferred_element_type=F32)
         rows = z2.shape[0] // 2
-        z = z2[:rows] + z2[rows:] + jnp.concatenate([bias[...]] * WIDE, axis=1)
+        z = z2[:rows] + z2[rows:] + jnp.concatenate([bias] * WIDE, axis=1)
         hidden = jnp.tanh(z)
         g = jnp.concatenate(
             [
@@ -552,11 +570,11 @@
         g3 = jnp.concatenate(
             [g_hi32, zeros8, g_hi32, zeros8, g_lo32, zeros8], axis=0
         ).astype(BF16)
-        d = (1.0 - hidden * hidden) * jnp.dot(w_head[...], g3, preferred_element_type=F32)
+        d = (1.0 - hidden * hidden) * jnp.dot(w_head, g3, preferred_element_type=F32)
         d_hi, d_lo = split(d)
         zeros = jnp.zeros((512 - 3 * rows, 128 * WIDE), BF16)
         back = jnp.dot(
-            w_cols[...],
+            w_cols,
             jnp.concatenate([d_hi, d_lo, d_hi, zeros], axis=0),
             preferred_element_type=F32,
         )
@@ -601,7 +619,8 @@
     level_sum = jnp.zeros((ch, 1), F32)
     head_sum = jnp.zeros((ch, 40), F32)
     n = kg.shape[1]
-    kind = jnp.broadcast_to(code[0:1], (ch, n))
+    columns_at, tap = columns()
+    kind = jnp.broadcast_to(columns_at[0:1], (ch, n))
     total = jnp.zeros((ch, n), F32)
     for y in range(8):
         rows = kg[y * ch : (y + 1) * ch]
@@ -616,11 +635,11 @@
         total = total + jnp.where(keep, moved, 0.0)
         level_sum = level_sum + sums[y * ch : (y + 1) * ch]
         head_sum = head_sum + h_all[y * ch : (y + 1) * ch]
-    grads = over_lanes(jnp.concatenate(split(total), axis=0), pick[...])
-    n_pick = pick.shape[0]
+    grads = over_lanes(jnp.concatenate(split(total), axis=0), own_taps(columns_at, tap))
+    n_pick = grads.shape[1]
     parts[...] = jnp.zeros_like(parts)
     parts[:, pl.ds(0, n_pick)] = grads[:ch] + grads[ch:]
-    parts[:, pl.ds(0, taps)] = parts[:, pl.ds(0, taps)] + level_sum * mass[...]
+    parts[:, pl.ds(0, taps)] = parts[:, pl.ds(0, taps)] + level_sum * level_taps((ch, taps))
     e_row = lax.broadcasted_iota(jnp.int32, (40, 128), 0) >> 3
     e_col = lax.broadcasted_iota(jnp.int32, (40, 128), 1) - 16
     to_col = jnp.where(e_row == e_col, 1.0, 0.0).astype(BF16)
@@ -630,101 +649,97 @@
     parts[:, pl.ds(128, 128)] = parts[:, pl.ds(128, 128)] + (head_out[:ch] + head_out[ch:])
 
 
-def band_pick():
-    n = 9 * BLOCK
-    pick = np.zeros((144, n), np.float32)
-    pick2 = np.zeros((144, n), np.float32)
-    code = np.full((8, n), 12, np.int32)
-    for o in range(9):
-        for v in range(5):
-            at = o * BLOCK
-            tap = [(oy * 9 + o) * 5 + v for oy in range(3)]
-            for k in range(8):
-                code[:, at + v * 8 + k] = k
-            for q in range(4):
-                code[:, at + 40 + 5 * q + v] = 8 + q
-            for oy in range(3):
-                pick[tap[oy], at + v * 8 + oy] = 1.0
-            pick[tap[0], at + 45 + v] = 1.0
-            pick[tap[2], at + 50 + v] = 1.0
-            pick2[tap[0], at + 40 + v] = 1.0
-            pick2[tap[1], at + 45 + v] = 1.0
-            pick2[tap[2], at + v * 8] = 1.0
-            pick2[tap[0], at + v * 8 + 7] = 1.0
-            pick2[tap[1], at + 50 + v] = 1.0
-            pick2[tap[2], at + 55 + v] = 1.0
-    return pick, pick2, code
-
-
-def call(kernel, outs, scratch, us, n_in, order=0, space=pl.ANY, limit=VMEM):
+def columns():
+    lane = lax.broadcasted_iota(jnp.int32, (8, 9 * BLOCK), 1)
+    o = lane >> 6
+    r = lane & (BLOCK - 1)
+    q = r - 40
+    which = sum((q >= 5 * i).astype(jnp.int32) for i in (1, 2, 3, 4))
+    main = r < 40
+    kind = jnp.where(main, r & 7, 8 + which)
+    v = jnp.where(main, r >> 3, q - 5 * which)
+    return kind, o * 5 + v
+
+
+def taps_of(columns_at):
+    n = columns_at.shape[1]
+    row = lax.broadcasted_iota(jnp.int32, (144, n), 0)
+    return jnp.where(row == jnp.broadcast_to(columns_at[0:1], (144, n)), 1.0, 0.0).astype(BF16)
+
+
+def own_taps(kind, tap):
+    at = jnp.where(kind < 3, tap + 45 * kind, 1000)
+    at = jnp.where(kind == 9, tap, at)
+    return taps_of(jnp.where(kind == 10, tap + 90, at))
+
+
+def rim_taps(kind, tap):
+    first = (kind == 8) | (kind == 7)
+    middle = (kind == 9) | (kind == 10)
+    last = (kind == 0) | (kind == 11)
+    at = jnp.where(first, tap, jnp.where(middle, tap + 45, 1000))
+    return taps_of(jnp.where(last, tap + 90, at))
+
+
+def level_taps(shape):
+    t = lax.broadcasted_iota(jnp.int32, shape, 1).astype(F32)
+    v = t - 5.0 * jnp.floor((t + 0.5) * 0.2)
+    return jnp.where((v < 0.5) | (v > 3.5), 1.0, 0.0)
+
+
+def call(kernel, outs, scratch, us, n_in, order=0):
     spec = pl.BlockSpec(memory_space=pltpu.VMEM)
     return pl.pallas_call(
         kernel,
         out_shape=outs,
-        in_specs=[spec] * n_in + [pl.BlockSpec(memory_space=space)] * order,
+        in_specs=[spec] * n_in + [pl.BlockSpec(memory_space=pl.ANY)] * order,
         scratch_shapes=scratch,
-        compiler_params=pltpu.CompilerParams(vmem_limit_bytes=limit),
+        compiler_params=pltpu.CompilerParams(vmem_limit_bytes=VMEM),
         cost_estimate=pl.CostEstimate(
             flops=0, bytes_accessed=int(us * 3.69e6), transcendentals=0
         ),
     )
 
 
-def body(pick, pick2, code, mass, state, cot, flags, kernel, heads):
+def body(state, cot, flags, kernel, heads):
     _, nx, ny, nz = state.shape
     ch, taps = kernel.shape
     count = lax.axis_size("gy")
     cells = nx * ny * nz
     half = nx // 2
     shape = lambda *dims: jax.ShapeDtypeStruct(dims, F32)
-    half_shape = lambda *dims: jax.ShapeDtypeStruct(dims, BF16)
     full, part = shape(5, nx, ny, nz), shape(5, half, ny, nz)
     with_twin = [(i, i ^ 1) for i in range(count)]
     with_other = [(i, (i + 1) % count if i % 2 else (i - 1) % count) for i in range(count)]
-    pick, pick2 = jnp.asarray(pick, BF16), jnp.asarray(pick2, BF16)
-    code = jnp.asarray(code)
-    mass = jnp.asarray(mass)
     vm = pltpu.VMEM
     lines = 5 * nx * ny
-    flat_state, flat_cot = state.reshape(lines, nz), cot.reshape(lines, nz)
+
+    flat = jnp.concatenate(
+        [
+            state.reshape(lines, nz),
+            cot.reshape(lines, nz),
+            flags.reshape(3 * nx * ny, nz).astype(F32),
+        ]
+    )
+    fields = flat.reshape(13, nx, ny, nz)
 
     sent = shape(SENT, nx, nz)
-    to_twin, to_other = call(
-        pack_kernel,
-        (sent, sent),
-        [
-            vm((lines, nz), F32),
-            vm((lines, nz), F32),
-            vm((nx * ny, nz), jnp.int32),
-            pltpu.SemaphoreType.DMA((3,)),
-        ],
-        1.0,
-        0,
-        3,
-        pltpu.HBM,
-        64 * 1024 * 1024 - 256 * 1024,
-    )(flat_state, flat_cot, flags.reshape(3 * nx * ny, nz))
+    to_twin, to_other = call(pack_kernel, (sent, sent), [], 0.2, 1)(flat)
     twin = lax.ppermute(to_twin, "gy", with_twin)
     other = lax.ppermute(to_other, "gy", with_other)
 
-    first, w_rows, w_cols, w_head, bias = call(
-        xz_kernel,
-        (
-            full,
-            half_shape(20 * ch, 9 * BLOCK),
-            half_shape(384, 512),
-            half_shape(10 * ch, SLOT),
-            shape(10 * ch, 128),
-        ),
+    first = call(
+        x_kernel,
+        full,
         [
             vm((5, nx + 5, ny, nz), F32),
             vm((5, nx + 1, ny, nz), F32),
             vm((5, nx + 5, ny, nz), F32),
-            vm((2 * ch, pick.shape[0]), F32),
         ],
-        6.6,
-        9,
-    )(state, cot, flags, kernel, heads, pick, pick2, code, mass)
+        3.3,
+        1,
+    )(fields)
+    first, twin, other = lax.optimization_barrier((first, twin, other))
     own, parts = call(
         c_kernel,
         (full, shape(ch, 256)),
@@ -733,34 +748,35 @@
             vm((nx * 120, nz), F32),
             vm((24 * nx, nz), F32),
             vm((16 * nx, nz), F32),
+            vm((2 * ch, 144), F32),
         ],
         5.0,
-        11,
-    )(state, cot, twin, other, pick, code, mass, w_rows, w_cols, w_head, bias)
+        5,
+    )(fields, twin, other, kernel, heads)
 
     def exchanged(value, bit):
         return lax.ppermute(value, "gy", [(i, i ^ bit) for i in range(count)])
 
     bits = [1 << b for b in range(count.bit_length() - 1)]
     sums = parts
-    for bit in bits[:-3]:
+    for bit in bits[:-4]:
         sums = sums + exchanged(sums, bit)
     halos = [vm((lines, nz), F32)] * 2
-    got = exchanged(sums, bits[-3])
-    rim = call(e_kernel, shape(lines, nz), [], 2.0, 4, 1)(
-        flat_state, flat_cot, twin, other, sums
-    )
+    got = exchanged(sums, bits[-4])
+    rim = call(e_kernel, shape(lines, nz), [], 1.1, 3, 1)(flat, twin, other, sums)
     got, rim = lax.optimization_barrier((got, rim))
     sums = sums + got
+    got = exchanged(sums, bits[-3])
+    first = call(z_kernel, full, [], 3.3, 2, 1)(fields, first, sums)
+    got, first = lax.optimization_barrier((got, first))
+    sums = sums + got
     got = exchanged(sums, bits[-2])
-    y0 = call(y_kernel, part, halos, 1.6, 8, 1)(
-        state, cot, flags, twin, other, own, first, rim, sums
-    )
+    y0 = call(y_kernel, part, halos, 1.6, 6, 1)(fields, twin, other, own, first, rim, sums)
     got, y0 = lax.optimization_barrier((got, y0))
     sums = sums + got
     got = exchanged(sums, bits[-1])
-    flow = call(y_last_kernel, full, halos, 2.0, 9, 1)(
-        state, cot, flags, twin, other, own, first, rim, y0, sums
+    flow = call(y_last_kernel, full, halos, 2.0, 7, 1)(
+        fields, twin, other, own, first, rim, y0, sums
     )
     scale = float(cells * count) ** (-0.5)
     k_out, h_out = call(
@@ -770,13 +786,9 @@
 
 
 def solution(mesh):
-    picks = band_pick()
-    mass = np.zeros((16, 135), np.float32)
-    mass[:, 0::5] = 1.0
-    mass[:, 4::5] = 1.0
     split_y = P(None, "ens", "gy", None)
     return jax.shard_map(
-        functools.partial(body, *picks, mass),
+        body,
         mesh=mesh,
         in_specs=(split_y, split_y, split_y, P(), P()),
         out_specs=(split_y, P("ens", None), P("ens", None)),

time: 41.9 us -> 35.9 us (0.86)
  starting transfers between devices: 6.26 us -> 12.9 us
  local copies, waits for them, and re-layouts: 6.64 us -> 0.08 us
  waiting for transfers between devices: 8.37 us -> 2.94 us
  Pallas kernels: 19.4 us -> 17 us
  other arithmetic: 0.01 us -> 2.03 us
    ppermute x4, waiting for transfers between devices: 8.36 us -> 0.64 us  [exchanged(): return lax.ppermute(value, 'gy', [(i, i ^ bit) for i in range(count)])]
    ppermute x4, starting transfers between devices: 0.08 us -> 6.73 us  [exchanged(): return lax.ppermute(value, 'gy', [(i, i ^ bit) for i in range(count)])]
    unnamed x20 -> x6, local copies, waits for them, and re-layouts: 6.64 us -> 0.08 us
    pallas_call x5 -> x6, Pallas kernels: 14.5 us -> 11.4 us  [the longest x1 3.65 us: body(): first = call(z_kernel, full, [], 3.3, 2, 1)(fields, first, sums)]
    ppermute x1, waiting for transfers between devices: 0.01 us -> 2.3 us  [body(): other = lax.ppermute(to_other, 'gy', with_other)]
    concatenate x0 -> x1, other arithmetic: none -> 1.03 us  [body(): jnp.concatenate([state.reshape(lines, nz), cot.reshape(lines, nz), flags....]
    convert_element_type x0 -> x1, other arithmetic: none -> 0.99 us  [body(): flags.reshape(3 * nx * ny, nz).astype(F32)]
    pallas_call x1, Pallas kernels: 4.19 us -> 4.86 us  [body(): call(c_kernel, (full, shape(ch, 256)), [vm(((nx + 2) * SLOT, nz), BF16),...]
  transfers between devices with their start and end apart: 6 -> 6, of which waited for: 4 -> 2; matrix products, arithmetic and copies ran while one was open for 0% -> 0% of each run, Pallas kernels for 30% -> 32%
where the time goes in v3:
time: 35.9 us; the launch traced here: 35.7 us
  Pallas kernels  17 us (47%)
  starting transfers between devices  12.9 us (36%)
  waiting for transfers between devices  2.94 us (8%)
  other arithmetic  2.03 us (6%)
  between operations  0.72 us (2%)
    ppermute x4, starting transfers between devices, exchanged(): return lax.ppermute(value, 'gy', [(i, i ^ bit) for i in range(count)])  6.73 us
    ppermute x1, starting transfers between devices, body(): other = lax.ppermute(to_other, 'gy', with_other)  5.67 us
    pallas_call x1, Pallas kernels, body(): call(c_kernel, (full, shape(ch, 256)), [vm(((nx + 2) * SLOT, nz), BF16),...  4.86 us
    pallas_call x1, Pallas kernels, body(): first = call(z_kernel, full, [], 3.3, 2, 1)(fields, first, sums)  3.65 us
    pallas_call x1, Pallas kernels, body(): call(x_kernel, full, [vm((5, nx + 5, ny, nz), F32), vm((5, nx + 1, ny, nz...  2.81 us
    ppermute x1, waiting for transfers between devices, body(): other = lax.ppermute(to_other, 'gy', with_other)  2.3 us
    pallas_call x1, Pallas kernels, body(): call(y_last_kernel, full, halos, 2.0, 7, 1)  2.24 us
    pallas_call x1, Pallas kernels, body(): call(y_kernel, part, halos, 1.6, 6, 1)  1.52 us
  transfers between devices with their start and end apart: 6, of which 2 were waited for; matrix products, arithmetic and copies ran while one was open for 0% of the time, Pallas kernels for 32%

profile of v3, /device:TPU:0, one launch (start us, length us, event | category | flops | bytes accessed | tf_op | source)
XLA Modules:
  0.0 35.7 jit_solution(8416954354017586764)
XLA Ops:
  0.6 0.0 copy-start.2
  0.6 1.0 %convert_element_type.6 = f32[3,16,8,128]{3,2,1,0:T(8,128)S(1)} convert(s32[3,16,8,128]{3,2,1,0:T(8,128)} %param.7) | non-fusion elementwise | flops 49152 | bytes 393216 | tf_op jit(solution)/shard_map/convert_element_type | solution.py:721
  1.6 0.1 copy-done.2
  1.7 1.0 %pad_maximum_fusion.fields = f32[1664,128]{1,0:T(8,128)S(1)} fusion(f32[384,128]{1,0:T(8,128)S(1)} %bitcast.9, f32[640,128]{1,0:T(8,128)S(1)} %bitcast.10, f32[640,128]{1,0:T(8,128)} %bitcast.11), kind=kLoop, calls=%fused_computation | loop fusion | flops 425984 | bytes 1703936 | tf_op jit(solution)/shard_map/concatenate | solution.py:717
  2.7 0.1 shard_map.77
  2.8 0.5 %collective-permute-start = (f32[43,16,128]{2,1,0:T(8,128)S(1)}, f32[43,16,128]{2,1,0:T(8,128)S(1)}, u32[]{:S(2)}, u32[]{:S(2)}) collective-permute-start(f32[43,16,128]{2,1,0:T(8,128)S(1)} %get-tuple-element.18), channel_id=1, source_target_pairs={{0,1},{1,0},{2,3},{3,2},{4,5},{5,4},{6,7},{7,6},{8,9},{9,8},{10,11... | collective-permute-start | bytes 1056776 | tf_op jit(solution)/shard_map/ppermute | solution.py:728
  3.4 5.7 %collective-permute-start.1 = (f32[43,16,128]{2,1,0:T(8,128)S(1)}, f32[43,16,128]{2,1,0:T(8,128)S(1)}, u32[]{:S(2)}, u32[]{:S(2)}) collective-permute-start(f32[43,16,128]{2,1,0:T(8,128)S(1)} %get-tuple-element.19), channel_id=1, source_target_pairs={{0,15},{1,2},{2,1},{3,4},{4,3},{5,6},{6,5},{7,8},{8,7},{9,10},{10,... | collective-permute-start | bytes 1056776 | tf_op jit(solution)/shard_map/ppermute | solution.py:729
  9.0 0.0 copy-start
  9.0 0.0 copy-start.1
  9.0 2.8 %shard_map.76.first = f32[5,16,8,128]{3,2,1,0:T(8,128)S(1)} custom-call(f32[13,16,8,128]{3,2,1,0:T(8,128)S(1)} %bitcast.4), custom_call_target="tpu_custom_call" | custom-call | bytes 12177000 | tf_op jit(solution)/shard_map/pallas_call | solution.py:731
  11.9 0.0 collective-permute-done.twin
  11.9 2.3 %collective-permute-done.1.other = f32[43,16,128]{2,1,0:T(8,128)S(1)} collective-permute-done((f32[43,16,128]{2,1,0:T(8,128)S(1)}, f32[43,16,128]{2,1,0:T(8,128)S(1)}, u32[]{:S(2)}, u32[]{:S(2)}) %collective-permute-start.1) | collective-permute-done | bytes 352288 | tf_op jit(solution)/shard_map/ppermute | solution.py:729
  14.2 0.0 copy-done
  14.2 0.0 copy-done.1
  14.2 4.9 %shard_map.78 = (f32[5,16,8,128]{3,2,1,0:T(8,128)S(1)}, f32[16,256]{1,0:T(8,128)S(1)}) custom-call(f32[13,16,8,128]{3,2,1,0:T(8,128)S(1)} %bitcast.5, f32[43,16,128]{2,1,0:T(8,128)S(1)} %collective-permute-done.twin, f32[43,16,128]{2,1,0:T(8,128)S(1)} %collective-permute-done.1.other, f32[16,135]{1,0:T(8,128)S(1)} %copy-done, f32[5,16]{1,0:T(8,128)S(1)} %copy-done.1), custom_call_target="tpu_custom_call" | custom-call | bytes 18450000 | tf_op jit(solution)/shard_map/pallas_call | solution.py:743
  19.0 0.8 %collective-permute-start.2 = (f32[16,256]{1,0:T(8,128)S(1)}, f32[16,256]{1,0:T(8,128)S(1)}, u32[]{:S(2)}, u32[]{:S(2)}) collective-permute-start(f32[16,256]{1,0:T(8,128)S(1)} %get-tuple-element.23.order), channel_id=1, source_target_pairs={{0,1},{1,0},{2,3},{3,2},{4,5},{5,4},{6,7},{7,6},{8,9},{9,8},{10,11... | collective-permute-start | bytes 49160 | tf_op jit(solution)/shard_map/ppermute | solution.py:758
  19.8 1.1 %shard_map.79.rim = f32[640,128]{1,0:T(8,128)S(1)} custom-call(f32[1664,128]{1,0:T(8,128)S(1)} %pad_maximum_fusion.fields, f32[43,16,128]{2,1,0:T(8,128)S(1)} %collective-permute-done.twin, f32[43,16,128]{2,1,0:T(8,128)S(1)} %collective-permute-done.1.other, f32[16,256]{1,0:T(8,128)S(1)} %get-tuple-element.23.order), custom_call_target="tpu_custom_call" | custom-call | bytes 4059000 | tf_op jit(solution)/shard_map/pallas_call | solution.py:766
  20.9 0.0 collective-permute-done.2
  20.9 1.7 %collective-permute-start.3 = (f32[16,256]{1,0:T(8,128)S(1)}, f32[16,256]{1,0:T(8,128)S(1)}, u32[]{:S(2)}, u32[]{:S(2)}) collective-permute-start(f32[16,256]{1,0:T(8,128)S(1)} %add.9.order), channel_id=1, source_target_pairs={{0,2},{1,3},{2,0},{3,1},{4,6},{5,7},{6,4},{7,5},{8,10},{9,11},{10,... | collective-permute-start | bytes 49160 | tf_op jit(solution)/shard_map/ppermute | solution.py:758
  22.6 3.7 %shard_map.80.first = f32[5,16,8,128]{3,2,1,0:T(8,128)S(1)} custom-call(f32[13,16,8,128]{3,2,1,0:T(8,128)S(1)} %bitcast.6, f32[5,16,8,128]{3,2,1,0:T(8,128)S(1)} %shard_map.76.first, f32[16,256]{1,0:T(8,128)S(1)} %add.9.order), custom_call_target="tpu_custom_call" | custom-call | bytes 12177000 | tf_op jit(solution)/shard_map/pallas_call | solution.py:770
  26.3 0.0 collective-permute-done.3
  26.3 1.6 %collective-permute-start.4 = (f32[16,256]{1,0:T(8,128)S(1)}, f32[16,256]{1,0:T(8,128)S(1)}, u32[]{:S(2)}, u32[]{:S(2)}) collective-permute-start(f32[16,256]{1,0:T(8,128)S(1)} %add.10.order), channel_id=1, source_target_pairs={{0,4},{1,5},{2,6},{3,7},{4,0},{5,1},{6,2},{7,3},{8,12},{9,13},{10,... | collective-permute-start | bytes 49160 | tf_op jit(solution)/shard_map/ppermute | solution.py:758
  28.0 1.5 %shard_map.81.done = f32[5,8,8,128]{3,2,1,0:T(8,128)S(1)} custom-call(f32[13,16,8,128]{3,2,1,0:T(8,128)S(1)} %bitcast.7, f32[43,16,128]{2,1,0:T(8,128)S(1)} %collective-permute-done.twin, f32[43,16,128]{2,1,0:T(8,128)S(1)} %collective-permute-done.1.other, f32[5,16,8,128]{3,2,1,0:T(8,128)S(1)} %get-tuple-element.22.own, ...), custom_call_target="tpu_custom_call" | custom-call | bytes 5904000 | tf_op jit(solution)/shard_map/pallas_call | solution.py:774
  29.5 0.6 %collective-permute-done.4 = f32[16,256]{1,0:T(8,128)S(1)} collective-permute-done((f32[16,256]{1,0:T(8,128)S(1)}, f32[16,256]{1,0:T(8,128)S(1)}, u32[]{:S(2)}, u32[]{:S(2)}) %collective-permute-start.4) | collective-permute-done | bytes 16416 | tf_op jit(solution)/shard_map/ppermute | solution.py:758
  30.1 2.6 %collective-permute-start.5 = (f32[16,256]{1,0:T(8,128)S(1)}, f32[16,256]{1,0:T(8,128)S(1)}, u32[]{:S(2)}, u32[]{:S(2)}) collective-permute-start(f32[16,256]{1,0:T(8,128)S(1)} %add.11.order.mine), channel_id=1, source_target_pairs={{0,8},{1,9},{2,10},{3,11},{4,12},{5,13},{6,14},{7,15},{8,0},{9,1},... | collective-permute-start | bytes 49160 | tf_op jit(solution)/shard_map/ppermute | solution.py:758
  32.7 2.2 %shard_map.82 = f32[5,16,8,128]{3,2,1,0:T(8,128)} custom-call(f32[13,16,8,128]{3,2,1,0:T(8,128)S(1)} %bitcast.8, f32[43,16,128]{2,1,0:T(8,128)S(1)} %collective-permute-done.twin, f32[43,16,128]{2,1,0:T(8,128)S(1)} %collective-permute-done.1.other, f32[5,16,8,128]{3,2,1,0:T(8,128)S(1)} %get-tuple-element.22.own, f32[5,16,8,128]{3,2,1,0:T(8,128)S(1)} %shard_map.80.first, ...), custom_call_target="tpu_custom_call" | custom-call | bytes 7380000 | tf_op jit(solution)/shard_map/pallas_call | solution.py:778
  35.0 0.0 collective-permute-done.5.theirs
  35.0 0.7 %shard_map.83 = (f32[16,135]{1,0:T(8,128)}, f32[5,16]{1,0:T(8,128)}) custom-call(f32[16,256]{1,0:T(8,128)S(1)} %add.11.order.mine, f32[16,256]{1,0:T(8,128)S(1)} %collective-permute-done.5.theirs), custom_call_target="tpu_custom_call" | custom-call | bytes 1845000 | tf_op jit(solution)/shard_map/pallas_call | solution.py:782
  (3 shorter events, 0.0 us)
Async XLA Ops:
  0.6 1.1 %copy-start.2 = (f32[5,16,8,128]{3,2,1,0:T(8,128)S(1)}, f32[5,16,8,128]{3,2,1,0:T(8,128)}, u32[]{:S(2)}) copy-start(f32[5,16,8,128]{3,2,1,0:T(8,128)} %param.6) | copy-start | bytes 983044
  2.8 9.0 %collective-permute-start = (f32[43,16,128]{2,1,0:T(8,128)S(1)}, f32[43,16,128]{2,1,0:T(8,128)S(1)}, u32[]{:S(2)}, u32[]{:S(2)}) collective-permute-start(f32[43,16,128]{2,1,0:T(8,128)S(1)} %get-tuple-element.18), channel_id=1, source_target_pairs={{0,1},{1,0},{2,3},{3,2},{4,5},{5,4},{6,7},{7,6},{8,9},{9,8},{10,11... | collective-permute-start | bytes 1056776 | tf_op jit(solution)/shard_map/ppermute | solution.py:728
  3.4 10.8 %collective-permute-start.1 = (f32[43,16,128]{2,1,0:T(8,128)S(1)}, f32[43,16,128]{2,1,0:T(8,128)S(1)}, u32[]{:S(2)}, u32[]{:S(2)}) collective-permute-start(f32[43,16,128]{2,1,0:T(8,128)S(1)} %get-tuple-element.19), channel_id=1, source_target_pairs={{0,15},{1,2},{2,1},{3,4},{4,3},{5,6},{6,5},{7,8},{8,7},{9,10},{10,... | collective-permute-start | bytes 1056776 | tf_op jit(solution)/shard_map/ppermute | solution.py:729
  9.0 5.1 %copy-start = (f32[16,135]{1,0:T(8,128)S(1)}, f32[16,135]{1,0:T(8,128)}, u32[]{:S(2)}) copy-start(f32[16,135]{1,0:T(8,128)} %kernel.1) | copy-start | bytes 25924
  9.0 5.1 %copy-start.1 = (f32[5,16]{1,0:T(8,128)S(1)}, f32[5,16]{1,0:T(8,128)}, u32[]{:S(2)}) copy-start(f32[5,16]{1,0:T(8,128)} %heads.1) | copy-start | bytes 964
  19.0 1.9 %collective-permute-start.2 = (f32[16,256]{1,0:T(8,128)S(1)}, f32[16,256]{1,0:T(8,128)S(1)}, u32[]{:S(2)}, u32[]{:S(2)}) collective-permute-start(f32[16,256]{1,0:T(8,128)S(1)} %get-tuple-element.23.order), channel_id=1, source_target_pairs={{0,1},{1,0},{2,3},{3,2},{4,5},{5,4},{6,7},{7,6},{8,9},{9,8},{10,11... | collective-permute-start | bytes 49160 | tf_op jit(solution)/shard_map/ppermute | solution.py:758
  20.9 5.4 %collective-permute-start.3 = (f32[16,256]{1,0:T(8,128)S(1)}, f32[16,256]{1,0:T(8,128)S(1)}, u32[]{:S(2)}, u32[]{:S(2)}) collective-permute-start(f32[16,256]{1,0:T(8,128)S(1)} %add.9.order), channel_id=1, source_target_pairs={{0,2},{1,3},{2,0},{3,1},{4,6},{5,7},{6,4},{7,5},{8,10},{9,11},{10,... | collective-permute-start | bytes 49160 | tf_op jit(solution)/shard_map/ppermute | solution.py:758
  26.3 3.8 %collective-permute-start.4 = (f32[16,256]{1,0:T(8,128)S(1)}, f32[16,256]{1,0:T(8,128)S(1)}, u32[]{:S(2)}, u32[]{:S(2)}) collective-permute-start(f32[16,256]{1,0:T(8,128)S(1)} %add.10.order), channel_id=1, source_target_pairs={{0,4},{1,5},{2,6},{3,7},{4,0},{5,1},{6,2},{7,3},{8,12},{9,13},{10,... | collective-permute-start | bytes 49160 | tf_op jit(solution)/shard_map/ppermute | solution.py:758
  30.1 4.8 %collective-permute-start.5 = (f32[16,256]{1,0:T(8,128)S(1)}, f32[16,256]{1,0:T(8,128)S(1)}, u32[]{:S(2)}, u32[]{:S(2)}) collective-permute-start(f32[16,256]{1,0:T(8,128)S(1)} %add.11.order.mine), channel_id=1, source_target_pairs={{0,8},{1,9},{2,10},{3,11},{4,12},{5,13},{6,14},{7,15},{8,0},{9,1},... | collective-permute-start | bytes 49160 | tf_op jit(solution)/shard_map/ppermute | solution.py:758

commit v4 on v3

--- a/solution.py
+++ b/solution.py
@@ -178,74 +178,76 @@
     ]
 
 
-REACH_STATE, REACH_COT, REACH_FLAGS = 5, 3, 3
-COT_AT = 5 * REACH_STATE
-FLAGS_AT = COT_AT + 5 * REACH_COT
-SENT = FLAGS_AT + REACH_FLAGS
+NEAR_STATE, FAR_STATE = 2, 3
+NEAR_COT, FAR_COT = 1, 2
+FLAG_ROWS = 3
+NEAR = 5 * (NEAR_STATE + NEAR_COT)
+FAR = 5 * (FAR_STATE + FAR_COT) + FLAG_ROWS
 
 
 def views(fields):
-    n = fields.shape[0] // 13
-    return (
-        fields.at[pl.ds(0, 5 * n)],
-        fields.at[pl.ds(5 * n, 5 * n)],
-        fields.at[pl.ds(10 * n, 3 * n)],
-    )
-
-
-def pack_kernel(fields, twin, other):
-    s, g, f = views(fields)
-    rows_in = f.shape[0] // 3
+    n = fields.shape[0] // 2
+    return fields.at[pl.ds(0, n)], fields.at[pl.ds(n, n)]
+
+
+def pack(ref, rows, first, twin, other, at):
     even = is_even()
     nx = twin.shape[1]
-
-    def put(at, low, top):
-        twin[at] = jnp.where(even, top, low)
-        other[at] = jnp.where(even, low, top)
-
-    for v in range(5):
-        base = v * nx * 8
-        for ref, reach, at in ((s, REACH_STATE, 0), (g, REACH_COT, COT_AT)):
-            for r in range(reach):
-                put(
-                    at + r * 5 + v,
-                    ref[pl.ds(base + r, nx, stride=8), :],
-                    ref[pl.ds(base + 8 - reach + r, nx, stride=8), :],
-                )
-    for r in range(REACH_FLAGS):
-        low = f[pl.ds(rows_in + r, nx, stride=8), :]
-        top = f[pl.ds(rows_in + 8 - REACH_FLAGS + r, nx, stride=8), :]
-        put(FLAGS_AT + r, low, top)
-
-
-def from_rims(twin, other):
+    count = ref.shape[0] // (8 * nx)
+    for r in rows:
+        for v in range(count):
+            low = ref[pl.ds(v * nx * 8 + r, nx, stride=8), :].astype(F32)
+            top = ref[pl.ds(v * nx * 8 + 7 - r, nx, stride=8), :].astype(F32)
+            i = at + (r - first) * count + v
+            twin[i] = jnp.where(even, top, low)
+            other[i] = jnp.where(even, low, top)
+
+
+def near_kernel(flat, twin, other):
+    s, g = views(flat)
+    pack(s, range(NEAR_STATE), 0, twin, other, 0)
+    pack(g, range(NEAR_COT), 0, twin, other, 5 * NEAR_STATE)
+
+
+def far_rows(flat, flags, twin, other):
+    s, g = views(flat)
+    n = flags.shape[0] // 3
+    pack(s, range(NEAR_STATE, NEAR_STATE + FAR_STATE), NEAR_STATE, twin, other, 0)
+    pack(g, range(NEAR_COT, NEAR_COT + FAR_COT), NEAR_COT, twin, other, 5 * FAR_STATE)
+    pack(flags.at[pl.ds(n, n)], range(FLAG_ROWS), 0, twin, other, FAR - FLAG_ROWS)
+
+
+def from_rims(near_twin, near_other, far_twin=None, far_other=None):
     even = is_even()
 
-    def read(row, reach, at, v):
-        if row < 0:
-            i = at + (reach + row) * 5 + v
+    def pick(twin, other, i, below):
+        if below:
             return jnp.where(even, other[i], twin[i])
-        i = at + (row - 8) * 5 + v
         return jnp.where(even, twin[i], other[i])
 
+    def read(row, near, near_at, far_at, v):
+        below = row < 0
+        r = -1 - row if below else row - 8
+        if r < near:
+            return pick(near_twin, near_other, near_at + r * 5 + v, below)
+        return pick(far_twin, far_other, far_at + (r - near) * 5 + v, below)
+
     def state(row, v):
-        return read(row, REACH_STATE, 0, v)
+        return read(row, NEAR_STATE, 0, 0, v)
 
     def cot(row, v):
-        return read(row, REACH_COT, COT_AT, v)
+        return read(row, NEAR_COT, 5 * NEAR_STATE, 5 * FAR_STATE, v)
 
     def flags(row):
-        if row < 0:
-            i = FLAGS_AT + REACH_FLAGS + row
-            return jnp.where(even, other[i], twin[i])
-        i = FLAGS_AT + row - 8
-        return jnp.where(even, twin[i], other[i])
+        below = row < 0
+        r = -1 - row if below else row - 8
+        return pick(far_twin, far_other, FAR - FLAG_ROWS + r, below).astype(jnp.int32)
 
     return state, cot, flags
 
 
-def x_kernel(fields, out, pad, gpad, acc):
-    state, cot, flags = views(fields)
+def x_kernel(fields, flags, before, out, pad, gpad, acc):
+    state, cot = views(fields)
     nx = state.shape[1]
     for v in range(5):
         pad[v, pl.ds(2, nx)] = state[v]
@@ -260,7 +262,7 @@
         cells = [[pad[v, pl.ds(x + k, SLABS)] for k in range(6)] for v in range(5)]
         g = [gpad[v, pl.ds(x, SLABS)] for v in range(5)]
         face = [STEP * (gpad[v, pl.ds(x + 1, SLABS)] - g[v]) for v in range(5)]
-        terms = face_pull(cells, face, flags[0, pl.ds(x, SLABS)].astype(jnp.int32), 0)
+        terms = face_pull(cells, face, flags[0, pl.ds(x, SLABS)], 0)
         own = conserved_pull([cells[v][2] for v in range(5)], g)
         for v in range(5):
             terms[v][2] = terms[v][2] + own[v]
@@ -279,12 +281,12 @@
         acc[v, pl.ds(2, 3)] = acc[v, pl.ds(2, 3)] + acc[v, pl.ds(nx + 2, 3)]
 
     for v in range(5):
-        out[v] = acc[v, pl.ds(2, nx)]
-
-
-def z_kernel(fields, first, order, out):
+        out[v] = acc[v, pl.ds(2, nx)] + before[v]
+
+
+def z_kernel(fields, flags, before, order, out):
     del order
-    state, cot, flags = views(fields)
+    state, cot = views(fields)
     nx = state.shape[1]
 
     def z_step(i, carry):
@@ -295,9 +297,9 @@
             cells.append([mid if k == 0 else pltpu.roll(mid, (-k) % 128, 2) for k in range(-2, 4)])
             g = cot[v, pl.ds(x, SLABS)]
             face.append(STEP * (pltpu.roll(g, 127, 2) - g))
-        terms = face_pull(cells, face, flags[2, pl.ds(x, SLABS)].astype(jnp.int32), 2)
+        terms = face_pull(cells, face, flags[2, pl.ds(x, SLABS)], 2)
         for v in range(5):
-            t = first[v, pl.ds(x, SLABS)] + terms[v][2]
+            t = before[v, pl.ds(x, SLABS)] + terms[v][2]
             for k in (-2, -1, 1, 2, 3):
                 t = t + pltpu.roll(terms[v][k + 2], k % 128, 2)
             out[v, pl.ds(x, SLABS)] = t
@@ -306,11 +308,9 @@
     lax.fori_loop(0, nx // SLABS, z_step, 0)
 
 
-def e_kernel(fields, twin, other, order, out):
-    del order
-    state, cot, _ = views(fields)
-    nx = twin.shape[1]
-    rim_state, rim_cot, rim_flags = from_rims(twin, other)
+def e_faces(state, cot, rims, out):
+    nx = out.shape[0] // 40
+    rim_state, rim_cot, rim_flags = rims
 
     def own(ref, row, v):
         return ref[pl.ds(v * nx * 8 + row, nx, stride=8), :]
@@ -327,7 +327,7 @@
     for j in (-3, -2, -1, 8, 9):
         cells = [[state_rows[j + k, v] for k in range(-2, 4)] for v in range(5)]
         face = [STEP * (cot_rows[j + 1, v] - cot_rows[j, v]) for v in range(5)]
-        terms = face_pull(cells, face, rim_flags(j).astype(jnp.int32), 1)
+        terms = face_pull(cells, face, rim_flags(j), 1)
         for v in range(5):
             for k in range(-2, 4):
                 if 0 <= j + k < 8:
@@ -339,10 +339,13 @@
             out[pl.ds(v * nx * 8 + row, nx, stride=8), :] = value
 
 
-def y_faces(x0, fields, twin, other, own, first, rim, put, part, halo, ghalo):
-    rim_state, rim_cot, _ = from_rims(twin, other)
-    state, cot, flags = views(fields)
-    nx = state.shape[1]
+def y_kernel(fields, flat, flags, near_twin, near_other, far_twin, far_other, before, order, out, rim, halo, ghalo):
+    del order
+    state, cot = views(fields)
+    rims = from_rims(near_twin, near_other, far_twin, far_other)
+    e_faces(*views(flat), rims, rim)
+    rim_state, rim_cot, _ = rims
+    nx = out.shape[1]
     for v in range(5):
         base = v * nx * 8
         for r in range(ABOVE):
@@ -356,7 +359,7 @@
         inside[k] = (row < 8 + k) if k < 0 else (row >= k)
 
     def step(i, carry):
-        x = x0 + i * SLABS
+        x = i * SLABS
         cells, face = [], []
         for v in range(5):
             at = pl.multiple_of((v * nx + x) * 8, 8)
@@ -372,40 +375,18 @@
             g = cot[v, pl.ds(x, SLABS)]
             g_rim = ghalo[pl.ds(at, 8 * SLABS), :].reshape(SLABS, 8, 128)
             face.append(STEP * (pltpu.roll(jnp.where(inside[1], g, g_rim), 7, 1) - g))
-        terms = face_pull(cells, face, flags[1, pl.ds(x, SLABS)].astype(jnp.int32), 1)
+        terms = face_pull(cells, face, flags[1, pl.ds(x, SLABS)], 1)
         for v in range(5):
             at = pl.multiple_of((v * nx + x) * 8, 8)
-            total = own[v, pl.ds(x, SLABS)] + first[v, pl.ds(x, SLABS)] + terms[v][2]
+            total = before[v, pl.ds(x, SLABS)] + terms[v][2]
             total = total + rim[pl.ds(at, 8 * SLABS), :].reshape(SLABS, 8, 128)
             for k in (-2, -1, 1, 2, 3):
                 moved = pltpu.roll(terms[v][k + 2], k % 8, 1)
                 total = total + jnp.where(inside[k], moved, 0.0)
-            put(i, x, v, total)
+            out[v, pl.ds(x, SLABS)] = total
         return carry
 
-    lax.fori_loop(0, part // SLABS, step, 0)
-
-
-def y_kernel(fields, twin, other, own, first, rim, order, out, halo, ghalo):
-    del order
-    part = out.shape[1]
-
-    def put(i, x, v, total):
-        out[v, pl.ds(x, SLABS)] = total
-
-    y_faces(0, fields, twin, other, own, first, rim, put, part, halo, ghalo)
-
-
-def y_last_kernel(fields, twin, other, own, first, rim, done, order, out, halo, ghalo):
-    del order
-    part = done.shape[1]
-    half = out.shape[1] - part
-
-    def put(i, x, v, total):
-        out[v, pl.ds(x, SLABS)] = total
-        out[v, pl.ds(i * SLABS, SLABS)] = done[v, pl.ds(i * SLABS, SLABS)]
-
-    y_faces(half, fields, twin, other, own, first, rim, put, part, halo, ghalo)
+    lax.fori_loop(0, nx // SLABS, step, 0)
 
 
 def sum_kernel(scale, mine, theirs, k_out, h_out):
@@ -426,8 +407,8 @@
     h_out[...] = heads[: h_out.shape[0], :ch]
 
 
-BLOCK = 64
-SLOT = 3 * BLOCK
+MAIN, RIM = 48, 32
+COLUMNS = 9 * (MAIN + RIM)
 
 
 def split(x):
@@ -443,7 +424,20 @@
     return lax.rem(lax.axis_index("gy"), 2) == 0
 
 
-def band_matrices(kernel, heads, wide):
+def prepare_kernel(fields, flat, flags, kernel, heads, twin, other, w_rows, w_cols, w_head, bias, t, wide):
+    far_rows(flat, flags, twin, other)
+    state, _ = views(fields)
+    nx = state.shape[1]
+    for x in range(nx):
+        rows = [state[v, x] - (1.0 if v in (0, 4) else 0.0) for v in range(5)]
+        mid = jnp.concatenate([*rows, jnp.zeros((8, 128), F32)], axis=0)
+        at = (x + 1) * 3 * MAIN
+        t[pl.ds(at, MAIN), :] = pltpu.roll(mid, 1, 1).astype(BF16)
+        t[pl.ds(at + MAIN, MAIN), :] = mid.astype(BF16)
+        t[pl.ds(at + 2 * MAIN, MAIN), :] = pltpu.roll(mid, 127, 1).astype(BF16)
+    t[pl.ds(0, 3 * MAIN), :] = t[pl.ds(nx * 3 * MAIN, 3 * MAIN), :]
+    t[pl.ds((nx + 1) * 3 * MAIN, 3 * MAIN), :] = t[pl.ds(3 * MAIN, 3 * MAIN), :]
+
     ch, taps = kernel.shape
     w = kernel[...]
     hi, lo = split(w)
@@ -467,25 +461,25 @@
         if y != 1:
             rows = pltpu.roll(rows, (y - 1) % n, 1)
         if y == 0:
-            rows = rows + jnp.where(kind == 9, base, 0.0)
+            rows = rows + jnp.where(kind == 8, base, 0.0)
         if y == 7:
             rows = rows + jnp.where(kind == 10, base, 0.0)
         bands.append(rows)
     bands.append(jnp.where((kind == 0) | (kind == 8) | (kind == 9), rim, 0.0))
     bands.append(jnp.where((kind == 7) | (kind == 10) | (kind == 11), rim, 0.0))
     full = jnp.concatenate([b[:ch] for b in bands] + [b[ch:] for b in bands], axis=0)
-    w_rows = full.astype(BF16)
+    w_rows[...] = full.astype(BF16)
     kept = full.shape[0] // 2
     cols = jnp.concatenate([full[:kept], full[:kept], full[kept:]], axis=0)
     cols = jnp.concatenate([cols, jnp.zeros((512 - 3 * kept, n), F32)], axis=0)
     own_cols = []
     for q in range(3):
-        own_cols += [cols[:, (3 * q + o) * BLOCK : (3 * q + o) * BLOCK + 40] for o in range(3)]
+        own_cols += [cols[:, (3 * q + o) * MAIN : (3 * q + o) * MAIN + 40] for o in range(3)]
         own_cols.append(jnp.zeros((512, 8), F32))
-    w_cols = jnp.concatenate(own_cols, axis=1).T.astype(BF16)
+    w_cols[...] = jnp.concatenate(own_cols, axis=1).T.astype(BF16)
     total = jnp.sum(w * level_taps(w.shape), axis=1, keepdims=True)
     total = jnp.broadcast_to(total, (ch, 128))
-    bias = jnp.concatenate([total] * 10, axis=0)
+    bias[...] = jnp.concatenate([total] * 10, axis=0)
 
     h_hi, h_lo = split(STEP * heads[...])
     none = jnp.zeros((3, ch), F32)
@@ -509,52 +503,61 @@
         rows.append(jnp.zeros((8, kept), F32))
         split_heads.append(jnp.concatenate(rows, axis=0))
     three = jnp.concatenate([split_heads[0], split_heads[1], split_heads[0]], axis=0)
-    w_head = three.T.astype(BF16)
-    return w_rows, w_cols, w_head, bias
+    w_head[...] = three.T.astype(BF16)
 
 
 def c_kernel(
-    fields, twin, other, kernel, heads,
+    fields, near_twin, near_other, kernel, w_rows, w_cols, w_head, bias, t,
     own, parts,
-    t, acc, edge, gedge, wide,
+    t_rim, acc, edge, gedge,
 ):
-    state, cot, _ = views(fields)
-    nx = state.shape[1]
+    _, cot = views(fields)
+    nx = cot.shape[1]
     ch, taps = kernel.shape
-    w_rows, w_cols, w_head, bias = band_matrices(kernel, heads, wide)
-    rim_state, rim_cot, _ = from_rims(twin, other)
+    rim_state, rim_cot, _ = from_rims(near_twin, near_other)
 
     for v in range(5):
         level = 1.0 if v in (0, 4) else 0.0
-        for q, row in enumerate((-2, -1, 8, 9)):
-            edge[pl.ds(5 * q + v, nx, stride=24), :] = rim_state(row, v) - level
+        for q, row in enumerate((-1, -2, 8, 9)):
+            edge[pl.ds(5 * q + v, nx, stride=RIM), :] = rim_state(row, v) - level
         gedge[pl.ds(v, nx, stride=16), :] = rim_cot(-1, v)
         gedge[pl.ds(8 + v, nx, stride=16), :] = rim_cot(8, v)
-    for q in range(20, 24):
-        edge[pl.ds(q, nx, stride=24), :] = jnp.zeros((nx, 128), F32)
+    none = jnp.zeros((nx, 128), F32)
+    for q in range(20, RIM):
+        edge[pl.ds(q, nx, stride=RIM), :] = none
     for q in (5, 6, 7):
-        gedge[pl.ds(q, nx, stride=16), :] = jnp.zeros((nx, 128), F32)
-        gedge[pl.ds(8 + q, nx, stride=16), :] = jnp.zeros((nx, 128), F32)
+        gedge[pl.ds(q, nx, stride=16), :] = none
+        gedge[pl.ds(8 + q, nx, stride=16), :] = none
     for x in range(nx):
-        rows = [state[v, x] - (1.0 if v in (0, 4) else 0.0) for v in range(5)]
-        rows.append(edge[pl.ds(x * 24, 24), :])
-        mid = jnp.concatenate(rows, axis=0)
-        at = (x + 1) * SLOT
-        t[pl.ds(at, BLOCK), :] = pltpu.roll(mid, 1, 1).astype(BF16)
-        t[pl.ds(at + BLOCK, BLOCK), :] = mid.astype(BF16)
-        t[pl.ds(at + 2 * BLOCK, BLOCK), :] = pltpu.roll(mid, 127, 1).astype(BF16)
-    t[pl.ds(0, SLOT), :] = t[pl.ds(nx * SLOT, SLOT), :]
-    t[pl.ds((nx + 1) * SLOT, SLOT), :] = t[pl.ds(SLOT, SLOT), :]
+        mid = edge[pl.ds(x * RIM, RIM), :]
+        at = (x + 1) * 3 * RIM
+        t_rim[pl.ds(at, RIM), :] = pltpu.roll(mid, 1, 1).astype(BF16)
+        t_rim[pl.ds(at + RIM, RIM), :] = mid.astype(BF16)
+        t_rim[pl.ds(at + 2 * RIM, RIM), :] = pltpu.roll(mid, 127, 1).astype(BF16)
+    t_rim[pl.ds(0, 3 * RIM), :] = t_rim[pl.ds(nx * 3 * RIM, 3 * RIM), :]
+    t_rim[pl.ds((nx + 1) * 3 * RIM, 3 * RIM), :] = t_rim[pl.ds(3 * RIM, 3 * RIM), :]
 
     kept = 8 * ch
     kg = hg = dsum = None
     zeros8 = jnp.zeros((8, 128 * WIDE), F32)
     written = set()
     for x in range(0, nx, WIDE):
-        s = jnp.concatenate([t[pl.ds((x + j) * SLOT, 3 * SLOT), :] for j in range(WIDE)], axis=1)
-        z2 = jnp.dot(w_rows, s, preferred_element_type=F32)
+        s = jnp.concatenate(
+            [
+                jnp.concatenate(
+                    [
+                        t[pl.ds((x + j) * 3 * MAIN, 9 * MAIN), :],
+                        t_rim[pl.ds((x + j) * 3 * RIM, 9 * RIM), :],
+                    ],
+                    axis=0,
+                )
+                for j in range(WIDE)
+            ],
+            axis=1,
+        )
+        z2 = jnp.dot(w_rows[...], s, preferred_element_type=F32)
         rows = z2.shape[0] // 2
-        z = z2[:rows] + z2[rows:] + jnp.concatenate([bias] * WIDE, axis=1)
+        z = z2[:rows] + z2[rows:] + jnp.concatenate([bias[...]] * WIDE, axis=1)
         hidden = jnp.tanh(z)
         g = jnp.concatenate(
             [
@@ -570,11 +573,11 @@
         g3 = jnp.concatenate(
             [g_hi32, zeros8, g_hi32, zeros8, g_lo32, zeros8], axis=0
         ).astype(BF16)
-        d = (1.0 - hidden * hidden) * jnp.dot(w_head, g3, preferred_element_type=F32)
+        d = (1.0 - hidden * hidden) * jnp.dot(w_head[...], g3, preferred_element_type=F32)
         d_hi, d_lo = split(d)
         zeros = jnp.zeros((512 - 3 * rows, 128 * WIDE), BF16)
         back = jnp.dot(
-            w_cols,
+            w_cols[...],
             jnp.concatenate([d_hi, d_lo, d_hi, zeros], axis=0),
             preferred_element_type=F32,
         )
@@ -628,7 +631,7 @@
         keep = kind < 3
         if y == 0:
             keep = (kind == 1) | (kind == 2)
-            total = total + jnp.where(kind == 9, rows, 0.0)
+            total = total + jnp.where(kind == 8, rows, 0.0)
         if y == 7:
             keep = kind < 2
             total = total + jnp.where(kind == 10, rows, 0.0)
@@ -650,14 +653,15 @@
 
 
 def columns():
-    lane = lax.broadcasted_iota(jnp.int32, (8, 9 * BLOCK), 1)
-    o = lane >> 6
-    r = lane & (BLOCK - 1)
-    q = r - 40
-    which = sum((q >= 5 * i).astype(jnp.int32) for i in (1, 2, 3, 4))
-    main = r < 40
-    kind = jnp.where(main, r & 7, 8 + which)
-    v = jnp.where(main, r >> 3, q - 5 * which)
+    lane = lax.broadcasted_iota(jnp.int32, (8, COLUMNS), 1)
+    main = lane < 9 * MAIN
+    past = lane - 9 * MAIN
+    block = sum((lane >= MAIN * i).astype(jnp.int32) for i in range(1, 9))
+    o = jnp.where(main, block, past >> 5)
+    r = jnp.where(main, lane - MAIN * block, past & (RIM - 1))
+    which = sum((r >= 5 * i).astype(jnp.int32) for i in (1, 2, 3, 4))
+    kind = jnp.where(main, jnp.where(r < 40, r & 7, 12), 8 + which)
+    v = jnp.where(main, r >> 3, r - 5 * which)
     return kind, o * 5 + v
 
 
@@ -669,13 +673,13 @@
 
 def own_taps(kind, tap):
     at = jnp.where(kind < 3, tap + 45 * kind, 1000)
-    at = jnp.where(kind == 9, tap, at)
+    at = jnp.where(kind == 8, tap, at)
     return taps_of(jnp.where(kind == 10, tap + 90, at))
 
 
 def rim_taps(kind, tap):
-    first = (kind == 8) | (kind == 7)
-    middle = (kind == 9) | (kind == 10)
+    first = (kind == 9) | (kind == 7)
+    middle = (kind == 8) | (kind == 10)
     last = (kind == 0) | (kind == 11)
     at = jnp.where(first, tap, jnp.where(middle, tap + 45, 1000))
     return taps_of(jnp.where(last, tap + 90, at))
@@ -706,29 +710,68 @@
     ch, taps = kernel.shape
     count = lax.axis_size("gy")
     cells = nx * ny * nz
-    half = nx // 2
     shape = lambda *dims: jax.ShapeDtypeStruct(dims, F32)
-    full, part = shape(5, nx, ny, nz), shape(5, half, ny, nz)
+    half_shape = lambda *dims: jax.ShapeDtypeStruct(dims, BF16)
+    full = shape(5, nx, ny, nz)
     with_twin = [(i, i ^ 1) for i in range(count)]
     with_other = [(i, (i + 1) % count if i % 2 else (i - 1) % count) for i in range(count)]
     vm = pltpu.VMEM
     lines = 5 * nx * ny
 
-    flat = jnp.concatenate(
+    flat = jnp.concatenate([state.reshape(lines, nz), cot.reshape(lines, nz)])
+    fields = flat.reshape(10, nx, ny, nz)
+    near, far = shape(NEAR, nx, nz), shape(FAR, nx, nz)
+    near_twin, near_other = call(near_kernel, (near, near), [], 0.2, 1)(flat)
+    near_rims = (
+        lax.ppermute(near_twin, "gy", with_twin),
+        lax.ppermute(near_other, "gy", with_other),
+    )
+    far_twin, far_other, *prepared, patches = call(
+        prepare_kernel,
+        (
+            far,
+            far,
+            half_shape(20 * ch, COLUMNS),
+            half_shape(384, 512),
+            half_shape(10 * ch, 192),
+            shape(10 * ch, 128),
+            half_shape((nx + 2) * 3 * MAIN, nz),
+        ),
+        [vm((2 * ch, 144), F32)],
+        1.5,
+        5,
+    )(fields, flat, flags.reshape(3 * nx * ny, nz), kernel, heads)
+    far_rims = (
+        lax.ppermute(far_twin, "gy", with_twin),
+        lax.ppermute(far_other, "gy", with_other),
+    )
+    near_rims, patches = lax.optimization_barrier((near_rims, patches))
+    own, parts = call(
+        c_kernel,
+        (full, shape(ch, 256)),
         [
-            state.reshape(lines, nz),
-            cot.reshape(lines, nz),
-            flags.reshape(3 * nx * ny, nz).astype(F32),
-        ]
-    )
-    fields = flat.reshape(13, nx, ny, nz)
-
-    sent = shape(SENT, nx, nz)
-    to_twin, to_other = call(pack_kernel, (sent, sent), [], 0.2, 1)(flat)
-    twin = lax.ppermute(to_twin, "gy", with_twin)
-    other = lax.ppermute(to_other, "gy", with_other)
-
-    first = call(
+            vm(((nx + 2) * 3 * RIM, nz), BF16),
+            vm((nx * 120, nz), F32),
+            vm((RIM * nx, nz), F32),
+            vm((16 * nx, nz), F32),
+        ],
+        3.5,
+        9,
+    )(fields, *near_rims, kernel, *prepared, patches)
+
+    def exchanged(value, bit):
+        return lax.ppermute(value, "gy", [(i, i ^ bit) for i in range(count)])
+
+    bits = [1 << b for b in range(count.bit_length() - 1)]
+    sums = parts
+    for bit in bits[:-3]:
+        sums = sums + exchanged(sums, bit)
+    got = exchanged(sums, bits[-3])
+    total = call(z_kernel, full, [], 3.5, 3, 1)(fields, flags, own, sums)
+    got, total = lax.optimization_barrier((got, total))
+    sums = sums + got
+    got = exchanged(sums, bits[-2])
+    total = call(
         x_kernel,
         full,
         [
@@ -736,48 +779,16 @@
             vm((5, nx + 1, ny, nz), F32),
             vm((5, nx + 5, ny, nz), F32),
         ],
-        3.3,
-        1,
-    )(fields)
-    first, twin, other = lax.optimization_barrier((first, twin, other))
-    own, parts = call(
-        c_kernel,
-        (full, shape(ch, 256)),
-        [
-            vm(((nx + 2) * SLOT, nz), BF16),
-            vm((nx * 120, nz), F32),
-            vm((24 * nx, nz), F32),
-            vm((16 * nx, nz), F32),
-            vm((2 * ch, 144), F32),
-        ],
-        5.0,
-        5,
-    )(fields, twin, other, kernel, heads)
-
-    def exchanged(value, bit):
-        return lax.ppermute(value, "gy", [(i, i ^ bit) for i in range(count)])
-
-    bits = [1 << b for b in range(count.bit_length() - 1)]
-    sums = parts
-    for bit in bits[:-4]:
-        sums = sums + exchanged(sums, bit)
-    halos = [vm((lines, nz), F32)] * 2
-    got = exchanged(sums, bits[-4])
-    rim = call(e_kernel, shape(lines, nz), [], 1.1, 3, 1)(flat, twin, other, sums)
-    got, rim = lax.optimization_barrier((got, rim))
-    sums = sums + got
-    got = exchanged(sums, bits[-3])
-    first = call(z_kernel, full, [], 3.3, 2, 1)(fields, first, sums)
-    got, first = lax.optimization_barrier((got, first))
-    sums = sums + got
-    got = exchanged(sums, bits[-2])
-    y0 = call(y_kernel, part, halos, 1.6, 6, 1)(fields, twin, other, own, first, rim, sums)
-    got, y0 = lax.optimization_barrier((got, y0))
+        2.8,
+        3,
+    )(fields, flags, total)
+    got, total = lax.optimization_barrier((got, total))
     sums = sums + got
     got = exchanged(sums, bits[-1])
-    flow = call(y_last_kernel, full, halos, 2.0, 7, 1)(
-        fields, twin, other, own, first, rim, y0, sums
+    flow = call(y_kernel, full, [vm((lines, nz), F32)] * 3, 4.5, 8, 1)(
+        fields, flat, flags, *near_rims, *far_rims, total, sums
     )
+    got, flow = lax.optimization_barrier((got, flow))
     scale = float(cells * count) ** (-0.5)
     k_out, h_out = call(
         functools.partial(sum_kernel, scale), (shape(ch, taps), shape(5, ch)), [], 0.5, 2

time: 35.9 us -> 38.8 us (1.081)
  waiting for transfers between devices: 2.94 us -> 7.64 us
  starting transfers between devices: 12.9 us -> 11.5 us
  other arithmetic: 2.03 us -> 1.18 us
  Pallas kernels: 17 us -> 17.6 us
    ppermute x2 -> x4, waiting for transfers between devices: 2.3 us -> 6.46 us  [the longest x1 5.74 us: body(): lax.ppermute(near_other, 'gy', with_other)]
    ppermute x4, starting transfers between devices: 6.73 us -> 4.64 us  [exchanged(): return lax.ppermute(value, 'gy', [(i, i ^ bit) for i in range(count)])]
    convert_element_type x1 -> x0, other arithmetic: 0.99 us -> none  [body(): flags.reshape(3 * nx * ny, nz).astype(F32)]
    ppermute x2 -> x4, starting transfers between devices: 6.18 us -> 6.86 us  [the longest x1 5.67 us: body(): lax.ppermute(far_other, 'gy', with_other)]
    pallas_call x6 -> x5, Pallas kernels: 13.5 us -> 14.1 us  [the longest x1 4.83 us: body(): call(y_kernel, full, [vm((lines, nz), F32)] * 3, 4.5, 8, 1)]
    ppermute x4, waiting for transfers between devices: 0.64 us -> 1.18 us  [exchanged(): return lax.ppermute(value, 'gy', [(i, i ^ bit) for i in range(count)])]
  transfers between devices with their start and end apart: 6 -> 8, of which waited for: 2 -> 3; matrix products, arithmetic and copies ran while one was open for 0% -> 0% of each run, Pallas kernels for 32% -> 41%
where the time goes in v4:
time: 38.8 us; the launch traced here: 38.7 us
  Pallas kernels  17.6 us (45%)
  starting transfers between devices  11.5 us (30%)
  waiting for transfers between devices  7.64 us (20%)
  other arithmetic  1.18 us (3%)
  between operations  0.76 us (2%)
    ppermute x1, waiting for transfers between devices, body(): lax.ppermute(near_other, 'gy', with_other)  5.74 us
    ppermute x1, starting transfers between devices, body(): lax.ppermute(far_other, 'gy', with_other)  5.67 us
    pallas_call x1, Pallas kernels, body(): call(y_kernel, full, [vm((lines, nz), F32)] * 3, 4.5, 8, 1)  4.83 us
    ppermute x4, starting transfers between devices, exchanged(): return lax.ppermute(value, 'gy', [(i, i ^ bit) for i in range(count)])  4.64 us
    pallas_call x1, Pallas kernels, body(): call(c_kernel, (full, shape(ch, 256)), [vm(((nx + 2) * 3 * RIM, nz), BF16...  4.4 us
    pallas_call x1, Pallas kernels, body(): total = call(z_kernel, full, [], 3.5, 3, 1)(fields, flags, own, sums)  3.67 us
    pallas_call x1, Pallas kernels, body(): call(x_kernel, full, [vm((5, nx + 5, ny, nz), F32), vm((5, nx + 1, ny, nz...  2.79 us
    ppermute x4, waiting for transfers between devices, exchanged(): return lax.ppermute(value, 'gy', [(i, i ^ bit) for i in range(count)])  1.18 us
  transfers between devices with their start and end apart: 8, of which 3 were waited for; matrix products, arithmetic and copies ran while one was open for 0% of the time, Pallas kernels for 41%

profile of v4, /device:TPU:0, one launch (start us, length us, event | category | flops | bytes accessed | tf_op | source)
XLA Modules:
  0.0 38.7 jit_solution(7763214642763409711)
XLA Ops:
  0.6 0.0 copy-start
  0.6 0.0 copy-start.1
  0.7 0.0 copy-start.2
  0.7 1.2 %pad_maximum_fusion.flat = f32[1280,128]{1,0:T(8,128)S(1)} fusion(f32[640,128]{1,0:T(8,128)} %bitcast.10, f32[640,128]{1,0:T(8,128)} %bitcast.11), kind=kLoop, calls=%fused_computation | loop fusion | flops 163840 | bytes 1310720 | tf_op jit(solution)/shard_map/concatenate | solution.py:721
  1.8 0.0 copy-done
  1.8 0.0 copy-done.1
  1.8 0.0 copy-done.2
  1.9 1.1 %shard_map.77 = (f32[28,16,128]{2,1,0:T(8,128)S(1)}, f32[28,16,128]{2,1,0:T(8,128)S(1)}, bf16[320,720]{1,0:T(8,128)(2,1)S(1)}, bf16[384,512]{1,0:T(8,128)(2,1)S(...) custom-call(f32[10,16,8,128]{3,2,1,0:T(8,128)S(1)} %bitcast.4, ...), custom_call_target="tpu_custom_call" | custom-call | bytes 5535000 | tf_op jit(solution)/shard_map/pallas_call | solution.py:729
  3.0 0.5 %collective-permute-start.6 = (f32[28,16,128]{2,1,0:T(8,128)S(1)}, f32[28,16,128]{2,1,0:T(8,128)S(1)}, u32[]{:S(2)}, u32[]{:S(2)}) collective-permute-start(f32[28,16,128]{2,1,0:T(8,128)S(1)} %get-tuple-element.40), channel_id=1, source_target_pairs={{0,1},{1,0},{2,3},{3,2},{4,5},{5,4},{6,7},{7,6},{8,9},{9,8},{10,11... | collective-permute-start | bytes 688136 | tf_op jit(solution)/shard_map/ppermute | solution.py:745
  3.5 5.7 %collective-permute-start.7 = (f32[28,16,128]{2,1,0:T(8,128)S(1)}, f32[28,16,128]{2,1,0:T(8,128)S(1)}, u32[]{:S(2)}, u32[]{:S(2)}) collective-permute-start(f32[28,16,128]{2,1,0:T(8,128)S(1)} %get-tuple-element.41), channel_id=1, source_target_pairs={{0,15},{1,2},{2,1},{3,4},{4,3},{5,6},{6,5},{7,8},{8,7},{9,10},{10,... | collective-permute-start | bytes 688136 | tf_op jit(solution)/shard_map/ppermute | solution.py:746
  9.2 0.1 collective-permute-start
  9.3 0.6 %collective-permute-start.1 = (f32[15,16,128]{2,1,0:T(8,128)S(1)}, f32[15,16,128]{2,1,0:T(8,128)S(1)}, u32[]{:S(2)}, u32[]{:S(2)}) collective-permute-start(f32[15,16,128]{2,1,0:T(8,128)S(1)} %get-tuple-element.26), channel_id=1, source_target_pairs={{0,15},{1,2},{2,1},{3,4},{4,3},{5,6},{6,5},{7,8},{8,7},{9,10},{10,... | collective-permute-start | bytes 368648 | tf_op jit(solution)/shard_map/ppermute | solution.py:727
  9.9 0.7 %collective-permute-done.near_twin = f32[15,16,128]{2,1,0:T(8,128)S(1)} collective-permute-done((f32[15,16,128]{2,1,0:T(8,128)S(1)}, f32[15,16,128]{2,1,0:T(8,128)S(1)}, u32[]{:S(2)}, u32[]{:S(2)}) %collective-permute-start) | collective-permute-done | bytes 122912 | tf_op jit(solution)/shard_map/ppermute | solution.py:726
  10.6 5.7 %collective-permute-done.1.near_other = f32[15,16,128]{2,1,0:T(8,128)S(1)} collective-permute-done((f32[15,16,128]{2,1,0:T(8,128)S(1)}, f32[15,16,128]{2,1,0:T(8,128)S(1)}, u32[]{:S(2)}, u32[]{:S(2)}) %collective-permute-start.1) | collective-permute-done | bytes 122912 | tf_op jit(solution)/shard_map/ppermute | solution.py:727
  16.4 4.4 %shard_map.78 = (f32[5,16,8,128]{3,2,1,0:T(8,128)S(1)}, f32[16,256]{1,0:T(8,128)S(1)}) custom-call(f32[10,16,8,128]{3,2,1,0:T(8,128)S(1)} %bitcast.5, f32[15,16,128]{2,1,0:T(8,128)S(1)} %collective-permute-done.near_twin, f32[15,16,128]{2,1,0:T(8,128)S(1)} %collective-permute-done.1.near_other, f32[16,135]{1,0:T(8,128)S(1)} %copy-done.1, ...), custom_call_target="tpu_custom_call" | custom-call | bytes 12915000 | tf_op jit(solution)/shard_map/pallas_call | solution.py:749
  20.8 0.1 collective-permute-start.2
  20.8 1.2 %collective-permute-done.2 = f32[16,256]{1,0:T(8,128)S(1)} collective-permute-done((f32[16,256]{1,0:T(8,128)S(1)}, f32[16,256]{1,0:T(8,128)S(1)}, u32[]{:S(2)}, u32[]{:S(2)}) %collective-permute-start.2) | collective-permute-done | bytes 16416 | tf_op jit(solution)/shard_map/ppermute | solution.py:763
  22.0 0.3 collective-permute-start.3
  22.3 3.7 %shard_map.79.before = f32[5,16,8,128]{3,2,1,0:T(8,128)S(1)} custom-call(f32[10,16,8,128]{3,2,1,0:T(8,128)S(1)} %bitcast.6, s32[3,16,8,128]{3,2,1,0:T(8,128)S(1)} %copy-done, f32[5,16,8,128]{3,2,1,0:T(8,128)S(1)} %get-tuple-element.36.before, f32[16,256]{1,0:T(8,128)S(1)} %add.9.order), custom_call_target="tpu_custom_call" | custom-call | bytes 12915000 | tf_op jit(solution)/shard_map/pallas_call | solution.py:770
  26.0 0.0 collective-permute-done.3
  26.0 1.6 %collective-permute-start.4 = (f32[16,256]{1,0:T(8,128)S(1)}, f32[16,256]{1,0:T(8,128)S(1)}, u32[]{:S(2)}, u32[]{:S(2)}) collective-permute-start(f32[16,256]{1,0:T(8,128)S(1)} %add.10), channel_id=1, source_target_pairs={{0,4},{1,5},{2,6},{3,7},{4,0},{5,1},{6,2},{7,3},{8,12},{9,13},{10,... | collective-permute-start | bytes 49160 | tf_op jit(solution)/shard_map/ppermute | solution.py:763
  27.6 2.8 %shard_map.80.before = f32[5,16,8,128]{3,2,1,0:T(8,128)S(1)} custom-call(f32[10,16,8,128]{3,2,1,0:T(8,128)S(1)} %bitcast.7, s32[3,16,8,128]{3,2,1,0:T(8,128)S(1)} %copy-done, f32[5,16,8,128]{3,2,1,0:T(8,128)S(1)} %shard_map.79.before), custom_call_target="tpu_custom_call" | custom-call | bytes 10332000 | tf_op jit(solution)/shard_map/pallas_call | solution.py:774
  30.4 0.0 collective-permute-done.4
  30.5 2.7 %collective-permute-start.5 = (f32[16,256]{1,0:T(8,128)S(1)}, f32[16,256]{1,0:T(8,128)S(1)}, u32[]{:S(2)}, u32[]{:S(2)}) collective-permute-start(f32[16,256]{1,0:T(8,128)S(1)} %add.11.order.mine), channel_id=1, source_target_pairs={{0,8},{1,9},{2,10},{3,11},{4,12},{5,13},{6,14},{7,15},{8,0},{9,1},... | collective-permute-start | bytes 49160 | tf_op jit(solution)/shard_map/ppermute | solution.py:763
  33.1 0.0 collective-permute-done.6.far_twin
  33.1 0.0 collective-permute-done.7.far_other
  33.1 4.8 %shard_map.81 = f32[5,16,8,128]{3,2,1,0:T(8,128)} custom-call(f32[10,16,8,128]{3,2,1,0:T(8,128)S(1)} %bitcast.8, f32[1280,128]{1,0:T(8,128)S(1)} %pad_maximum_fusion.flat, s32[3,16,8,128]{3,2,1,0:T(8,128)S(1)} %copy-done, f32[15,16,128]{2,1,0:T(8,128)S(1)} %collective-permute-done.near_twin, f32[15,16,128]{2,1,0:T(8,128)S(1)} %collective-permute-done.1.near_other, ...), custom_call_target="tpu_custom_call" | custom-call | bytes 16605000 | tf_op jit(solution)/shard_map/pallas_call | solution.py:788
  37.9 0.0 collective-permute-done.5.theirs
  37.9 0.7 %shard_map.82 = (f32[16,135]{1,0:T(8,128)}, f32[5,16]{1,0:T(8,128)}) custom-call(f32[16,256]{1,0:T(8,128)S(1)} %add.11.order.mine, f32[16,256]{1,0:T(8,128)S(1)} %collective-permute-done.5.theirs), custom_call_target="tpu_custom_call" | custom-call | bytes 1845000 | tf_op jit(solution)/shard_map/pallas_call | solution.py:793
  (4 shorter events, 0.1 us)
Async XLA Ops:
  0.6 1.2 %copy-start = (s32[3,16,8,128]{3,2,1,0:T(8,128)S(1)}, s32[3,16,8,128]{3,2,1,0:T(8,128)}, u32[]{:S(2)}) copy-start(s32[3,16,8,128]{3,2,1,0:T(8,128)} %flags.5) | copy-start | bytes 589828
  0.6 1.2 %copy-start.1 = (f32[16,135]{1,0:T(8,128)S(1)}, f32[16,135]{1,0:T(8,128)}, u32[]{:S(2)}) copy-start(f32[16,135]{1,0:T(8,128)} %kernel.3) | copy-start | bytes 25924
  0.7 1.2 %copy-start.2 = (f32[5,16]{1,0:T(8,128)S(1)}, f32[5,16]{1,0:T(8,128)}, u32[]{:S(2)}) copy-start(f32[5,16]{1,0:T(8,128)} %heads.1) | copy-start | bytes 964
  3.0 30.1 %collective-permute-start.6 = (f32[28,16,128]{2,1,0:T(8,128)S(1)}, f32[28,16,128]{2,1,0:T(8,128)S(1)}, u32[]{:S(2)}, u32[]{:S(2)}) collective-permute-start(f32[28,16,128]{2,1,0:T(8,128)S(1)} %get-tuple-element.40), channel_id=1, source_target_pairs={{0,1},{1,0},{2,3},{3,2},{4,5},{5,4},{6,7},{7,6},{8,9},{9,8},{10,11... | collective-permute-start | bytes 688136 | tf_op jit(solution)/shard_map/ppermute | solution.py:745
  3.5 29.6 %collective-permute-start.7 = (f32[28,16,128]{2,1,0:T(8,128)S(1)}, f32[28,16,128]{2,1,0:T(8,128)S(1)}, u32[]{:S(2)}, u32[]{:S(2)}) collective-permute-start(f32[28,16,128]{2,1,0:T(8,128)S(1)} %get-tuple-element.41), channel_id=1, source_target_pairs={{0,15},{1,2},{2,1},{3,4},{4,3},{5,6},{6,5},{7,8},{8,7},{9,10},{10,... | collective-permute-start | bytes 688136 | tf_op jit(solution)/shard_map/ppermute | solution.py:746
  9.2 1.4 %collective-permute-start = (f32[15,16,128]{2,1,0:T(8,128)S(1)}, f32[15,16,128]{2,1,0:T(8,128)S(1)}, u32[]{:S(2)}, u32[]{:S(2)}) collective-permute-start(f32[15,16,128]{2,1,0:T(8,128)S(1)} %get-tuple-element.25), channel_id=1, source_target_pairs={{0,1},{1,0},{2,3},{3,2},{4,5},{5,4},{6,7},{7,6},{8,9},{9,8},{10,11... | collective-permute-start | bytes 368648 | tf_op jit(solution)/shard_map/ppermute | solution.py:726
  9.3 7.1 %collective-permute-start.1 = (f32[15,16,128]{2,1,0:T(8,128)S(1)}, f32[15,16,128]{2,1,0:T(8,128)S(1)}, u32[]{:S(2)}, u32[]{:S(2)}) collective-permute-start(f32[15,16,128]{2,1,0:T(8,128)S(1)} %get-tuple-element.26), channel_id=1, source_target_pairs={{0,15},{1,2},{2,1},{3,4},{4,3},{5,6},{6,5},{7,8},{8,7},{9,10},{10,... | collective-permute-start | bytes 368648 | tf_op jit(solution)/shard_map/ppermute | solution.py:727
  20.8 1.2 %collective-permute-start.2 = (f32[16,256]{1,0:T(8,128)S(1)}, f32[16,256]{1,0:T(8,128)S(1)}, u32[]{:S(2)}, u32[]{:S(2)}) collective-permute-start(f32[16,256]{1,0:T(8,128)S(1)} %get-tuple-element.35), channel_id=1, source_target_pairs={{0,1},{1,0},{2,3},{3,2},{4,5},{5,4},{6,7},{7,6},{8,9},{9,8},{10,11... | collective-permute-start | bytes 49160 | tf_op jit(solution)/shard_map/ppermute | solution.py:763
  22.0 4.0 %collective-permute-start.3 = (f32[16,256]{1,0:T(8,128)S(1)}, f32[16,256]{1,0:T(8,128)S(1)}, u32[]{:S(2)}, u32[]{:S(2)}) collective-permute-start(f32[16,256]{1,0:T(8,128)S(1)} %add.9.order), channel_id=1, source_target_pairs={{0,2},{1,3},{2,0},{3,1},{4,6},{5,7},{6,4},{7,5},{8,10},{9,11},{10,... | collective-permute-start | bytes 49160 | tf_op jit(solution)/shard_map/ppermute | solution.py:763
  26.0 4.4 %collective-permute-start.4 = (f32[16,256]{1,0:T(8,128)S(1)}, f32[16,256]{1,0:T(8,128)S(1)}, u32[]{:S(2)}, u32[]{:S(2)}) collective-permute-start(f32[16,256]{1,0:T(8,128)S(1)} %add.10), channel_id=1, source_target_pairs={{0,4},{1,5},{2,6},{3,7},{4,0},{5,1},{6,2},{7,3},{8,12},{9,13},{10,... | collective-permute-start | bytes 49160 | tf_op jit(solution)/shard_map/ppermute | solution.py:763
  30.5 7.5 %collective-permute-start.5 = (f32[16,256]{1,0:T(8,128)S(1)}, f32[16,256]{1,0:T(8,128)S(1)}, u32[]{:S(2)}, u32[]{:S(2)}) collective-permute-start(f32[16,256]{1,0:T(8,128)S(1)} %add.11.order.mine), channel_id=1, source_target_pairs={{0,8},{1,9},{2,10},{3,11},{4,12},{5,13},{6,14},{7,15},{8,0},{9,1},... | collective-permute-start | bytes 49160 | tf_op jit(solution)/shard_map/ppermute | solution.py:763

commit v5 on v4

--- a/solution.py
+++ b/solution.py
@@ -209,7 +209,8 @@
     pack(g, range(NEAR_COT), 0, twin, other, 5 * NEAR_STATE)
 
 
-def far_rows(flat, flags, twin, other):
+def far_kernel(flat, flags, order, order2, twin, other):
+    del order, order2
     s, g = views(flat)
     n = flags.shape[0] // 3
     pack(s, range(NEAR_STATE, NEAR_STATE + FAR_STATE), NEAR_STATE, twin, other, 0)
@@ -246,7 +247,8 @@
     return state, cot, flags
 
 
-def x_kernel(fields, flags, before, out, pad, gpad, acc):
+def x_kernel(fields, flags, before, order, out, pad, gpad, acc):
+    del order
     state, cot = views(fields)
     nx = state.shape[1]
     for v in range(5):
@@ -284,13 +286,15 @@
         out[v] = acc[v, pl.ds(2, nx)] + before[v]
 
 
-def z_kernel(fields, flags, before, order, out):
+def z_kernel(half, fields, flags, before, order, out):
     del order
     state, cot = views(fields)
-    nx = state.shape[1]
+    nx = state.shape[1] // 2
+    for v in range(5):
+        out[v, pl.ds((1 - half) * nx, nx)] = before[v, pl.ds((1 - half) * nx, nx)]
 
     def z_step(i, carry):
-        x = i * SLABS
+        x = half * nx + i * SLABS
         cells, face = [], []
         for v in range(5):
             mid = state[v, pl.ds(x, SLABS)]
@@ -424,8 +428,8 @@
     return lax.rem(lax.axis_index("gy"), 2) == 0
 
 
-def prepare_kernel(fields, flat, flags, kernel, heads, twin, other, w_rows, w_cols, w_head, bias, t, wide):
-    far_rows(flat, flags, twin, other)
+def prepare_kernel(fields, kernel, heads, order, order2, w_rows, w_cols, w_head, bias, t, wide):
+    del order, order2
     state, _ = views(fields)
     nx = state.shape[1]
     for x in range(nx):
@@ -581,12 +585,12 @@
             jnp.concatenate([d_hi, d_lo, d_hi, zeros], axis=0),
             preferred_element_type=F32,
         )
-        k2 = over_lanes(jnp.concatenate([d_hi[:kept], d_lo[:kept]], axis=0), s)
-        k2 = k2[:kept] + k2[kept:]
+        k2 = over_lanes(s, jnp.concatenate([d_hi[:kept], d_lo[:kept]], axis=0))
+        k2 = k2[:, :kept] + k2[:, kept:]
         kg = k2 if kg is None else kg + k2
         hid2 = jnp.concatenate(split(hidden[:kept]), axis=0)
         g2 = jnp.concatenate([g_hi32[:40], g_lo32[:40]], axis=0).astype(BF16)
-        h2 = over_lanes(hid2, g2)
+        h2 = over_lanes(g2, hid2)
         hg = h2 if hg is None else hg + h2
         for j in range(WIDE):
             level = d[:kept, 128 * j : 128 * (j + 1)]
@@ -614,13 +618,19 @@
             own[v, x] = total[8 * v : 8 * v + 8]
 
     sums = jnp.sum(dsum, axis=1, keepdims=True)
-    y_row = lax.broadcasted_iota(jnp.int32, (kept, 40), 0)
-    y_col = lax.broadcasted_iota(jnp.int32, (kept, 40), 1) & 7
-    same_y = (y_row >= y_col * ch) & (y_row < (y_col + 1) * ch)
-    h_all = (hg[:kept, :40] + hg[kept:, :40]) + (hg[:kept, 40:80] + hg[kept:, 40:80])
-    h_all = jnp.where(same_y, h_all, 0.0)
+    kg = kg.T
+    hg = (hg[:40, :kept] + hg[40:, :kept]) + (hg[:40, kept:] + hg[40:, kept:])
+    y_row = lax.broadcasted_iota(jnp.int32, (40, kept), 0) & 7
+    y_col = lax.broadcasted_iota(jnp.int32, (40, kept), 1)
+    same_y = (y_col >= y_row * ch) & (y_col < (y_row + 1) * ch)
+    hg = jnp.where(same_y, hg, 0.0)
+    by_eq = jnp.concatenate(
+        [jnp.sum(hg[8 * e : 8 * e + 8], axis=0, keepdims=True) for e in range(5)]
+        + [jnp.zeros((123, kept), F32)],
+        axis=0,
+    ).T
     level_sum = jnp.zeros((ch, 1), F32)
-    head_sum = jnp.zeros((ch, 40), F32)
+    head_sum = jnp.zeros((ch, 128), F32)
     n = kg.shape[1]
     columns_at, tap = columns()
     kind = jnp.broadcast_to(columns_at[0:1], (ch, n))
@@ -637,19 +647,13 @@
             total = total + jnp.where(kind == 10, rows, 0.0)
         total = total + jnp.where(keep, moved, 0.0)
         level_sum = level_sum + sums[y * ch : (y + 1) * ch]
-        head_sum = head_sum + h_all[y * ch : (y + 1) * ch]
+        head_sum = head_sum + by_eq[y * ch : (y + 1) * ch]
     grads = over_lanes(jnp.concatenate(split(total), axis=0), own_taps(columns_at, tap))
     n_pick = grads.shape[1]
     parts[...] = jnp.zeros_like(parts)
     parts[:, pl.ds(0, n_pick)] = grads[:ch] + grads[ch:]
     parts[:, pl.ds(0, taps)] = parts[:, pl.ds(0, taps)] + level_sum * level_taps((ch, taps))
-    e_row = lax.broadcasted_iota(jnp.int32, (40, 128), 0) >> 3
-    e_col = lax.broadcasted_iota(jnp.int32, (40, 128), 1) - 16
-    to_col = jnp.where(e_row == e_col, 1.0, 0.0).astype(BF16)
-    head_out = jnp.dot(
-        jnp.concatenate(split(head_sum * STEP), axis=0), to_col, preferred_element_type=F32
-    )
-    parts[:, pl.ds(128, 128)] = parts[:, pl.ds(128, 128)] + (head_out[:ch] + head_out[ch:])
+    parts[:, pl.ds(128, 128)] = parts[:, pl.ds(128, 128)] + pltpu.roll(head_sum * STEP, 16, 1)
 
 
 def columns():
@@ -700,7 +704,7 @@
         scratch_shapes=scratch,
         compiler_params=pltpu.CompilerParams(vmem_limit_bytes=VMEM),
         cost_estimate=pl.CostEstimate(
-            flops=0, bytes_accessed=int(us * 3.69e6), transcendentals=0
+            flops=int(us * 1.15e9), bytes_accessed=int(us * 3.69e6), transcendentals=0
         ),
     )
 
@@ -726,11 +730,12 @@
         lax.ppermute(near_twin, "gy", with_twin),
         lax.ppermute(near_other, "gy", with_other),
     )
-    far_twin, far_other, *prepared, patches = call(
+    far_twin, far_other = call(far_kernel, (far, far), [], 0.2, 2, 2)(
+        flat, flags.reshape(3 * nx * ny, nz), near_twin, near_other
+    )
+    *prepared, patches = call(
         prepare_kernel,
         (
-            far,
-            far,
             half_shape(20 * ch, COLUMNS),
             half_shape(384, 512),
             half_shape(10 * ch, 192),
@@ -739,8 +744,9 @@
         ),
         [vm((2 * ch, 144), F32)],
         1.5,
-        5,
-    )(fields, flat, flags.reshape(3 * nx * ny, nz), kernel, heads)
+        3,
+        2,
+    )(fields, kernel, heads, near_twin, near_other)
     far_rims = (
         lax.ppermute(far_twin, "gy", with_twin),
         lax.ppermute(far_other, "gy", with_other),
@@ -764,13 +770,16 @@
 
     bits = [1 << b for b in range(count.bit_length() - 1)]
     sums = parts
-    for bit in bits[:-3]:
+    for bit in bits[:-4]:
         sums = sums + exchanged(sums, bit)
-    got = exchanged(sums, bits[-3])
-    total = call(z_kernel, full, [], 3.5, 3, 1)(fields, flags, own, sums)
+    z_half = lambda half, before, order: call(
+        functools.partial(z_kernel, half), full, [], 1.9, 3, 1
+    )(fields, flags, before, order)
+    got = exchanged(sums, bits[-4])
+    total = z_half(0, own, sums)
     got, total = lax.optimization_barrier((got, total))
     sums = sums + got
-    got = exchanged(sums, bits[-2])
+    got = exchanged(sums, bits[-3])
     total = call(
         x_kernel,
         full,
@@ -781,7 +790,12 @@
         ],
         2.8,
         3,
-    )(fields, flags, total)
+        1,
+    )(fields, flags, total, sums)
+    got, total = lax.optimization_barrier((got, total))
+    sums = sums + got
+    got = exchanged(sums, bits[-2])
+    total = z_half(1, total, sums)
     got, total = lax.optimization_barrier((got, total))
     sums = sums + got
     got = exchanged(sums, bits[-1])

time: 38.8 us -> 34.4 us (0.89)
  waiting for transfers between devices: 7.64 us -> 0.68 us
  starting transfers between devices: 11.5 us -> 13.8 us
    ppermute x1, waiting for transfers between devices: 5.74 us -> 0.54 us  [body(): lax.ppermute(near_other, 'gy', with_other)]
    ppermute x1, starting transfers between devices: 0.61 us -> 5.67 us  [body(): lax.ppermute(near_other, 'gy', with_other)]
    ppermute x1, starting transfers between devices: 5.67 us -> 0.78 us  [body(): lax.ppermute(far_other, 'gy', with_other)]
    ppermute x4, starting transfers between devices: 4.64 us -> 6.75 us  [exchanged(): return lax.ppermute(value, 'gy', [(i, i ^ bit) for i in range(count)])]
    ppermute x4, waiting for transfers between devices: 1.18 us -> 0.13 us  [exchanged(): return lax.ppermute(value, 'gy', [(i, i ^ bit) for i in range(count)])]
    ppermute x1, waiting for transfers between devices: 0.71 us -> 0.01 us  [body(): lax.ppermute(near_twin, 'gy', with_twin)]
    ppermute x1, starting transfers between devices: 0.07 us -> 0.52 us  [body(): lax.ppermute(near_twin, 'gy', with_twin)]
    ppermute x1, starting transfers between devices: 0.52 us -> 0.07 us  [body(): lax.ppermute(far_twin, 'gy', with_twin)]
  transfers between devices with their start and end apart: 8 -> 8, of which waited for: 3 -> 2; matrix products, arithmetic and copies ran while one was open for 0% -> 0% of each run, Pallas kernels for 41% -> 50%
where the time goes in v5:
time: 34.4 us; the launch traced here: 34.3 us
  Pallas kernels  17.9 us (52%)
  starting transfers between devices  13.8 us (40%)
  other arithmetic  1.13 us (3%)
  between operations  0.76 us (2%)
  waiting for transfers between devices  0.68 us (2%)
    ppermute x4, starting transfers between devices, exchanged(): return lax.ppermute(value, 'gy', [(i, i ^ bit) for i in range(count)])  6.75 us
    ppermute x1, starting transfers between devices, body(): lax.ppermute(near_other, 'gy', with_other)  5.67 us
    pallas_call x1, Pallas kernels, body(): call(y_kernel, full, [vm((lines, nz), F32)] * 3, 4.5, 8, 1)  4.82 us
    pallas_call x1, Pallas kernels, body(): call(c_kernel, (full, shape(ch, 256)), [vm(((nx + 2) * 3 * RIM, nz), BF16...  4.7 us
    pallas_call x2, Pallas kernels, body(): call(functools.partial(z_kernel, half), full, [], 1.9, 3, 1)  3.7 us
    pallas_call x1, Pallas kernels, body(): call(x_kernel, full, [vm((5, nx + 5, ny, nz), F32), vm((5, nx + 1, ny, nz...  2.79 us
    concatenate x1, other arithmetic, body(): flat = jnp.concatenate([state.reshape(lines, nz), cot.reshape(lines, nz)])  1.12 us
    pallas_call x1, Pallas kernels, body(): call(prepare_kernel, (half_shape(20 * ch, COLUMNS), half_shape(384, 512),...  1.05 us
  transfers between devices with their start and end apart: 8, of which 2 were waited for; matrix products, arithmetic and copies ran while one was open for 0% of the time, Pallas kernels for 50%

profile of v5, /device:TPU:0, one launch (start us, length us, event | category | flops | bytes accessed | tf_op | source)
XLA Modules:
  0.0 34.3 jit_solution(9571021508890947773)
XLA Ops:
  0.6 1.1 %pad_maximum_fusion.flat = f32[1280,128]{1,0:T(8,128)S(1)} fusion(f32[640,128]{1,0:T(8,128)} %bitcast.11, f32[640,128]{1,0:T(8,128)} %bitcast.12), kind=kLoop, calls=%fused_computation | loop fusion | flops 163840 | bytes 1310720 | tf_op jit(solution)/shard_map/concatenate | solution.py:725
  1.7 0.0 copy-start
  1.8 0.5 %collective-permute-start = (f32[15,16,128]{2,1,0:T(8,128)S(1)}, f32[15,16,128]{2,1,0:T(8,128)S(1)}, u32[]{:S(2)}, u32[]{:S(2)}) collective-permute-start(f32[15,16,128]{2,1,0:T(8,128)S(1)} %get-tuple-element.27.order), channel_id=1, source_target_pairs={{0,1},{1,0},{2,3},{3,2},{4,5},{5,4},{6,7},{7,6},{8,9},{9,8},{10,11... | collective-permute-start | bytes 368648 | tf_op jit(solution)/shard_map/ppermute | solution.py:730
  2.3 5.7 %collective-permute-start.1 = (f32[15,16,128]{2,1,0:T(8,128)S(1)}, f32[15,16,128]{2,1,0:T(8,128)S(1)}, u32[]{:S(2)}, u32[]{:S(2)}) collective-permute-start(f32[15,16,128]{2,1,0:T(8,128)S(1)} %get-tuple-element.28.order2), channel_id=1, source_target_pairs={{0,15},{1,2},{2,1},{3,4},{4,3},{5,6},{6,5},{7,8},{8,7},{9,10},{10,... | collective-permute-start | bytes 368648 | tf_op jit(solution)/shard_map/ppermute | solution.py:731
  8.0 0.0 copy-done
  8.0 0.0 copy-start.1
  8.0 0.1 shard_map.82
  8.1 0.0 copy-start.2
  8.1 0.1 collective-permute-start.6
  8.2 0.8 %collective-permute-start.7 = (f32[28,16,128]{2,1,0:T(8,128)S(1)}, f32[28,16,128]{2,1,0:T(8,128)S(1)}, u32[]{:S(2)}, u32[]{:S(2)}) collective-permute-start(f32[28,16,128]{2,1,0:T(8,128)S(1)} %get-tuple-element.45), channel_id=1, source_target_pairs={{0,15},{1,2},{2,1},{3,4},{4,3},{5,6},{6,5},{7,8},{8,7},{9,10},{10,... | collective-permute-start | bytes 688136 | tf_op jit(solution)/shard_map/ppermute | solution.py:752
  9.0 0.0 copy-done.1
  9.0 0.0 copy-done.2
  9.0 1.1 %shard_map.77 = (bf16[320,720]{1,0:T(8,128)(2,1)S(1)}, bf16[384,512]{1,0:T(8,128)(2,1)S(1)}, bf16[160,192]{1,0:T(8,128)(2,1)S(1)}, f32[160,128]{1,0:T(8,128)S(1)}, bf16[2592,128]{1,0:T(8,128)(2,1)S(1)}) custom-call(f32[10,16,8,128]{3,2,1,0:T(8,128)S(1)} %bitcast.4, f32[16,135]{1,0:T(8,128)S(1)} %copy-done.1, f32[5,16]{1,0:T(8,128)S(1)} %copy-done.2, ...), custom_call_target="tpu_custom_call" | custom-call | flops 1724999936 | bytes 5535000 | tf_op jit(solution)/shard_map/pallas_call | solution.py:736
  10.0 0.0 collective-permute-done.near_twin
  10.0 0.5 %collective-permute-done.1.near_other = f32[15,16,128]{2,1,0:T(8,128)S(1)} collective-permute-done((f32[15,16,128]{2,1,0:T(8,128)S(1)}, f32[15,16,128]{2,1,0:T(8,128)S(1)}, u32[]{:S(2)}, u32[]{:S(2)}) %collective-permute-start.1) | collective-permute-done | bytes 122912 | tf_op jit(solution)/shard_map/ppermute | solution.py:731
  10.6 4.7 %shard_map.78 = (f32[5,16,8,128]{3,2,1,0:T(8,128)S(1)}, f32[16,256]{1,0:T(8,128)S(1)}) custom-call(f32[10,16,8,128]{3,2,1,0:T(8,128)S(1)} %bitcast.5, f32[15,16,128]{2,1,0:T(8,128)S(1)} %collective-permute-done.near_twin, f32[15,16,128]{2,1,0:T(8,128)S(1)} %collective-permute-done.1.near_other, f32[16,135]{1,0:T(8,128)S(1)} %copy-done.1, ...), custom_call_target="tpu_custom_call" | custom-call | flops 4024999936 | bytes 12915000 | tf_op jit(solution)/shard_map/pallas_call | solution.py:755
  15.3 0.1 collective-permute-start.2
  15.4 1.9 %shard_map.79.before = f32[5,16,8,128]{3,2,1,0:T(8,128)S(1)} custom-call(f32[10,16,8,128]{3,2,1,0:T(8,128)S(1)} %bitcast.6, s32[3,16,8,128]{3,2,1,0:T(8,128)S(1)} %copy-done, f32[5,16,8,128]{3,2,1,0:T(8,128)S(1)} %get-tuple-element.38.before, f32[16,256]{1,0:T(8,128)S(1)} %get-tuple-element.37.order), custom_call_target="tpu_custom_call" | custom-call | flops 2184999936 | bytes 7011000 | tf_op jit(solution)/shard_map/pallas_call | solution.py:775
  17.2 0.0 collective-permute-done.2
  17.2 0.9 %collective-permute-start.3 = (f32[16,256]{1,0:T(8,128)S(1)}, f32[16,256]{1,0:T(8,128)S(1)}, u32[]{:S(2)}, u32[]{:S(2)}) collective-permute-start(f32[16,256]{1,0:T(8,128)S(1)} %add.9.order), channel_id=1, source_target_pairs={{0,2},{1,3},{2,0},{3,1},{4,6},{5,7},{6,4},{7,5},{8,10},{9,11},{10,... | collective-permute-start | bytes 49160 | tf_op jit(solution)/shard_map/ppermute | solution.py:769
  18.1 2.8 %shard_map.80.before = f32[5,16,8,128]{3,2,1,0:T(8,128)S(1)} custom-call(f32[10,16,8,128]{3,2,1,0:T(8,128)S(1)} %bitcast.7, s32[3,16,8,128]{3,2,1,0:T(8,128)S(1)} %copy-done, f32[5,16,8,128]{3,2,1,0:T(8,128)S(1)} %shard_map.79.before, f32[16,256]{1,0:T(8,128)S(1)} %add.9.order), custom_call_target="tpu_custom_call" | custom-call | flops 3220000000 | bytes 10332000 | tf_op jit(solution)/shard_map/pallas_call | solution.py:783
  20.9 0.1 collective-permute-done.3
  21.0 2.9 %collective-permute-start.4 = (f32[16,256]{1,0:T(8,128)S(1)}, f32[16,256]{1,0:T(8,128)S(1)}, u32[]{:S(2)}, u32[]{:S(2)}) collective-permute-start(f32[16,256]{1,0:T(8,128)S(1)} %add.10.order), channel_id=1, source_target_pairs={{0,4},{1,5},{2,6},{3,7},{4,0},{5,1},{6,2},{7,3},{8,12},{9,13},{10,... | collective-permute-start | bytes 49160 | tf_op jit(solution)/shard_map/ppermute | solution.py:769
  24.0 1.8 %shard_map.81.before = f32[5,16,8,128]{3,2,1,0:T(8,128)S(1)} custom-call(f32[10,16,8,128]{3,2,1,0:T(8,128)S(1)} %bitcast.8, s32[3,16,8,128]{3,2,1,0:T(8,128)S(1)} %copy-done, f32[5,16,8,128]{3,2,1,0:T(8,128)S(1)} %shard_map.80.before, f32[16,256]{1,0:T(8,128)S(1)} %add.10.order), custom_call_target="tpu_custom_call" | custom-call | flops 2184999936 | bytes 7011000 | tf_op jit(solution)/shard_map/pallas_call | solution.py:775
  25.8 0.0 collective-permute-done.4
  25.8 2.9 %collective-permute-start.5 = (f32[16,256]{1,0:T(8,128)S(1)}, f32[16,256]{1,0:T(8,128)S(1)}, u32[]{:S(2)}, u32[]{:S(2)}) collective-permute-start(f32[16,256]{1,0:T(8,128)S(1)} %add.11.order.mine), channel_id=1, source_target_pairs={{0,8},{1,9},{2,10},{3,11},{4,12},{5,13},{6,14},{7,15},{8,0},{9,1},... | collective-permute-start | bytes 49160 | tf_op jit(solution)/shard_map/ppermute | solution.py:769
  28.7 0.0 collective-permute-done.6.far_twin
  28.7 0.0 collective-permute-done.7.far_other
  28.7 4.8 %shard_map.83 = f32[5,16,8,128]{3,2,1,0:T(8,128)} custom-call(f32[10,16,8,128]{3,2,1,0:T(8,128)S(1)} %bitcast.9, f32[1280,128]{1,0:T(8,128)S(1)} %pad_maximum_fusion.flat, s32[3,16,8,128]{3,2,1,0:T(8,128)S(1)} %copy-done, f32[15,16,128]{2,1,0:T(8,128)S(1)} %collective-permute-done.near_twin, f32[15,16,128]{2,1,0:T(8,128)S(1)} %collective-permute-done.1.near_other, ...), custom_call_target="tpu_custom_call" | custom-call | flops 5175000064 | bytes 16605000 | tf_op jit(solution)/shard_map/pallas_call | solution.py:802
  33.5 0.0 collective-permute-done.5.theirs
  33.5 0.7 %shard_map.84 = (f32[16,135]{1,0:T(8,128)}, f32[5,16]{1,0:T(8,128)}) custom-call(f32[16,256]{1,0:T(8,128)S(1)} %add.11.order.mine, f32[16,256]{1,0:T(8,128)S(1)} %collective-permute-done.5.theirs), custom_call_target="tpu_custom_call" | custom-call | flops 575000000 | bytes 1845000 | tf_op jit(solution)/shard_map/pallas_call | solution.py:807
  (4 shorter events, 0.1 us)
Async XLA Ops:
  1.7 6.3 %copy-start = (s32[3,16,8,128]{3,2,1,0:T(8,128)S(1)}, s32[3,16,8,128]{3,2,1,0:T(8,128)}, u32[]{:S(2)}) copy-start(s32[3,16,8,128]{3,2,1,0:T(8,128)} %flags.7) | copy-start | bytes 589828
  1.8 8.2 %collective-permute-start = (f32[15,16,128]{2,1,0:T(8,128)S(1)}, f32[15,16,128]{2,1,0:T(8,128)S(1)}, u32[]{:S(2)}, u32[]{:S(2)}) collective-permute-start(f32[15,16,128]{2,1,0:T(8,128)S(1)} %get-tuple-element.27.order), channel_id=1, source_target_pairs={{0,1},{1,0},{2,3},{3,2},{4,5},{5,4},{6,7},{7,6},{8,9},{9,8},{10,11... | collective-permute-start | bytes 368648 | tf_op jit(solution)/shard_map/ppermute | solution.py:730
  2.3 8.2 %collective-permute-start.1 = (f32[15,16,128]{2,1,0:T(8,128)S(1)}, f32[15,16,128]{2,1,0:T(8,128)S(1)}, u32[]{:S(2)}, u32[]{:S(2)}) collective-permute-start(f32[15,16,128]{2,1,0:T(8,128)S(1)} %get-tuple-element.28.order2), channel_id=1, source_target_pairs={{0,15},{1,2},{2,1},{3,4},{4,3},{5,6},{6,5},{7,8},{8,7},{9,10},{10,... | collective-permute-start | bytes 368648 | tf_op jit(solution)/shard_map/ppermute | solution.py:731
  8.0 0.9 %copy-start.1 = (f32[16,135]{1,0:T(8,128)S(1)}, f32[16,135]{1,0:T(8,128)}, u32[]{:S(2)}) copy-start(f32[16,135]{1,0:T(8,128)} %kernel.3) | copy-start | bytes 25924
  8.1 0.9 %copy-start.2 = (f32[5,16]{1,0:T(8,128)S(1)}, f32[5,16]{1,0:T(8,128)}, u32[]{:S(2)}) copy-start(f32[5,16]{1,0:T(8,128)} %heads.1) | copy-start | bytes 964
  8.1 20.6 %collective-permute-start.6 = (f32[28,16,128]{2,1,0:T(8,128)S(1)}, f32[28,16,128]{2,1,0:T(8,128)S(1)}, u32[]{:S(2)}, u32[]{:S(2)}) collective-permute-start(f32[28,16,128]{2,1,0:T(8,128)S(1)} %get-tuple-element.44), channel_id=1, source_target_pairs={{0,1},{1,0},{2,3},{3,2},{4,5},{5,4},{6,7},{7,6},{8,9},{9,8},{10,11... | collective-permute-start | bytes 688136 | tf_op jit(solution)/shard_map/ppermute | solution.py:751
  8.2 20.6 %collective-permute-start.7 = (f32[28,16,128]{2,1,0:T(8,128)S(1)}, f32[28,16,128]{2,1,0:T(8,128)S(1)}, u32[]{:S(2)}, u32[]{:S(2)}) collective-permute-start(f32[28,16,128]{2,1,0:T(8,128)S(1)} %get-tuple-element.45), channel_id=1, source_target_pairs={{0,15},{1,2},{2,1},{3,4},{4,3},{5,6},{6,5},{7,8},{8,7},{9,10},{10,... | collective-permute-start | bytes 688136 | tf_op jit(solution)/shard_map/ppermute | solution.py:752
  15.3 1.9 %collective-permute-start.2 = (f32[16,256]{1,0:T(8,128)S(1)}, f32[16,256]{1,0:T(8,128)S(1)}, u32[]{:S(2)}, u32[]{:S(2)}) collective-permute-start(f32[16,256]{1,0:T(8,128)S(1)} %get-tuple-element.37.order), channel_id=1, source_target_pairs={{0,1},{1,0},{2,3},{3,2},{4,5},{5,4},{6,7},{7,6},{8,9},{9,8},{10,11... | collective-permute-start | bytes 49160 | tf_op jit(solution)/shard_map/ppermute | solution.py:769
  17.2 3.8 %collective-permute-start.3 = (f32[16,256]{1,0:T(8,128)S(1)}, f32[16,256]{1,0:T(8,128)S(1)}, u32[]{:S(2)}, u32[]{:S(2)}) collective-permute-start(f32[16,256]{1,0:T(8,128)S(1)} %add.9.order), channel_id=1, source_target_pairs={{0,2},{1,3},{2,0},{3,1},{4,6},{5,7},{6,4},{7,5},{8,10},{9,11},{10,... | collective-permute-start | bytes 49160 | tf_op jit(solution)/shard_map/ppermute | solution.py:769
  21.0 4.8 %collective-permute-start.4 = (f32[16,256]{1,0:T(8,128)S(1)}, f32[16,256]{1,0:T(8,128)S(1)}, u32[]{:S(2)}, u32[]{:S(2)}) collective-permute-start(f32[16,256]{1,0:T(8,128)S(1)} %add.10.order), channel_id=1, source_target_pairs={{0,4},{1,5},{2,6},{3,7},{4,0},{5,1},{6,2},{7,3},{8,12},{9,13},{10,... | collective-permute-start | bytes 49160 | tf_op jit(solution)/shard_map/ppermute | solution.py:769
  25.8 7.7 %collective-permute-start.5 = (f32[16,256]{1,0:T(8,128)S(1)}, f32[16,256]{1,0:T(8,128)S(1)}, u32[]{:S(2)}, u32[]{:S(2)}) collective-permute-start(f32[16,256]{1,0:T(8,128)S(1)} %add.11.order.mine), channel_id=1, source_target_pairs={{0,8},{1,9},{2,10},{3,11},{4,12},{5,13},{6,14},{7,15},{8,0},{9,1},... | collective-permute-start | bytes 49160 | tf_op jit(solution)/shard_map/ppermute | solution.py:769

commit v6 on v5

--- a/solution.py
+++ b/solution.py
@@ -209,8 +209,8 @@
     pack(g, range(NEAR_COT), 0, twin, other, 5 * NEAR_STATE)
 
 
-def far_kernel(flat, flags, order, order2, twin, other):
-    del order, order2
+def far_kernel(flat, flags, order, twin, other):
+    del order
     s, g = views(flat)
     n = flags.shape[0] // 3
     pack(s, range(NEAR_STATE, NEAR_STATE + FAR_STATE), NEAR_STATE, twin, other, 0)
@@ -247,8 +247,8 @@
     return state, cot, flags
 
 
-def x_kernel(fields, flags, before, order, out, pad, gpad, acc):
-    del order
+def x_kernel(fields, flags, order, order2, out, pad, gpad, acc):
+    del order, order2
     state, cot = views(fields)
     nx = state.shape[1]
     for v in range(5):
@@ -283,15 +283,16 @@
         acc[v, pl.ds(2, 3)] = acc[v, pl.ds(2, 3)] + acc[v, pl.ds(nx + 2, 3)]
 
     for v in range(5):
-        out[v] = acc[v, pl.ds(2, nx)] + before[v]
-
-
-def z_kernel(half, fields, flags, before, order, out):
+        out[v] = acc[v, pl.ds(2, nx)]
+
+
+def z_kernel(half, fields, flags, before, more, order, out):
     del order
     state, cot = views(fields)
     nx = state.shape[1] // 2
     for v in range(5):
-        out[v, pl.ds((1 - half) * nx, nx)] = before[v, pl.ds((1 - half) * nx, nx)]
+        kept = pl.ds((1 - half) * nx, nx)
+        out[v, kept] = before[v, kept]
 
     def z_step(i, carry):
         x = half * nx + i * SLABS
@@ -303,7 +304,7 @@
             face.append(STEP * (pltpu.roll(g, 127, 2) - g))
         terms = face_pull(cells, face, flags[2, pl.ds(x, SLABS)], 2)
         for v in range(5):
-            t = before[v, pl.ds(x, SLABS)] + terms[v][2]
+            t = before[v, pl.ds(x, SLABS)] + more[v, pl.ds(x, SLABS)] + terms[v][2]
             for k in (-2, -1, 1, 2, 3):
                 t = t + pltpu.roll(terms[v][k + 2], k % 128, 2)
             out[v, pl.ds(x, SLABS)] = t
@@ -730,9 +731,6 @@
         lax.ppermute(near_twin, "gy", with_twin),
         lax.ppermute(near_other, "gy", with_other),
     )
-    far_twin, far_other = call(far_kernel, (far, far), [], 0.2, 2, 2)(
-        flat, flags.reshape(3 * nx * ny, nz), near_twin, near_other
-    )
     *prepared, patches = call(
         prepare_kernel,
         (
@@ -747,11 +745,19 @@
         3,
         2,
     )(fields, kernel, heads, near_twin, near_other)
-    far_rims = (
-        lax.ppermute(far_twin, "gy", with_twin),
-        lax.ppermute(far_other, "gy", with_other),
-    )
-    near_rims, patches = lax.optimization_barrier((near_rims, patches))
+    first = call(
+        x_kernel,
+        full,
+        [
+            vm((5, nx + 5, ny, nz), F32),
+            vm((5, nx + 1, ny, nz), F32),
+            vm((5, nx + 5, ny, nz), F32),
+        ],
+        2.8,
+        2,
+        2,
+    )(fields, flags, near_twin, near_other)
+    near_rims, patches, first = lax.optimization_barrier((near_rims, patches, first))
     own, parts = call(
         c_kernel,
         (full, shape(ch, 256)),
@@ -773,25 +779,19 @@
     for bit in bits[:-4]:
         sums = sums + exchanged(sums, bit)
     z_half = lambda half, before, order: call(
-        functools.partial(z_kernel, half), full, [], 1.9, 3, 1
-    )(fields, flags, before, order)
+        functools.partial(z_kernel, half), full, [], 1.9, 4, 1
+    )(fields, flags, before, first, order)
     got = exchanged(sums, bits[-4])
-    total = z_half(0, own, sums)
-    got, total = lax.optimization_barrier((got, total))
+    far_twin, far_other = call(far_kernel, (far, far), [], 0.2, 2, 1)(
+        flat, flags.reshape(3 * nx * ny, nz), parts
+    )
+    far_rims = (
+        lax.ppermute(far_twin, "gy", with_twin),
+        lax.ppermute(far_other, "gy", with_other),
+    )
     sums = sums + got
     got = exchanged(sums, bits[-3])
-    total = call(
-        x_kernel,
-        full,
-        [
-            vm((5, nx + 5, ny, nz), F32),
-            vm((5, nx + 1, ny, nz), F32),
-            vm((5, nx + 5, ny, nz), F32),
-        ],
-        2.8,
-        3,
-        1,
-    )(fields, flags, total, sums)
+    total = z_half(0, own, sums)
     got, total = lax.optimization_barrier((got, total))
     sums = sums + got
     got = exchanged(sums, bits[-2])

time: 34.4 us -> 35.4 us (1.029)
  waiting for transfers between devices: 0.68 us -> 5.5 us
  starting transfers between devices: 13.8 us -> 10 us
    ppermute x4, starting transfers between devices: 6.75 us -> 0.15 us  [exchanged(): return lax.ppermute(value, 'gy', [(i, i ^ bit) for i in range(count)])]
    ppermute x4, waiting for transfers between devices: 0.13 us -> 5.49 us  [exchanged(): return lax.ppermute(value, 'gy', [(i, i ^ bit) for i in range(count)])]
    ppermute x1, starting transfers between devices: 0.78 us -> 3.11 us  [body(): lax.ppermute(far_other, 'gy', with_other)]
    ppermute x1, waiting for transfers between devices: 0.54 us -> 0.01 us  [body(): lax.ppermute(near_other, 'gy', with_other)]
    ppermute x1, starting transfers between devices: 0.07 us -> 0.56 us  [body(): lax.ppermute(far_twin, 'gy', with_twin)]
  transfers between devices with their start and end apart: 8 -> 8, of which waited for: 2 -> 2; matrix products, arithmetic and copies ran while one was open for 0% -> 0% of each run, Pallas kernels for 50% -> 35%
where the time goes in v6:
time: 35.4 us; the launch traced here: 35.3 us
  Pallas kernels  17.9 us (51%)
  starting transfers between devices  10 us (28%)
  waiting for transfers between devices  5.5 us (16%)
  other arithmetic  1.13 us (3%)
  between operations  0.76 us (2%)
    ppermute x1, starting transfers between devices, body(): lax.ppermute(near_other, 'gy', with_other)  5.67 us
    ppermute x4, waiting for transfers between devices, exchanged(): return lax.ppermute(value, 'gy', [(i, i ^ bit) for i in range(count)])  5.49 us
    pallas_call x1, Pallas kernels, body(): call(y_kernel, full, [vm((lines, nz), F32)] * 3, 4.5, 8, 1)  4.82 us
    pallas_call x1, Pallas kernels, body(): call(c_kernel, (full, shape(ch, 256)), [vm(((nx + 2) * 3 * RIM, nz), BF16...  4.71 us
    pallas_call x2, Pallas kernels, body(): call(functools.partial(z_kernel, half), full, [], 1.9, 4, 1)  3.68 us
    ppermute x1, starting transfers between devices, body(): lax.ppermute(far_other, 'gy', with_other)  3.11 us
    pallas_call x1, Pallas kernels, body(): call(x_kernel, full, [vm((5, nx + 5, ny, nz), F32), vm((5, nx + 1, ny, nz...  2.78 us
    concatenate x1, other arithmetic, body(): flat = jnp.concatenate([state.reshape(lines, nz), cot.reshape(lines, nz)])  1.12 us
  transfers between devices with their start and end apart: 8, of which 2 were waited for; matrix products, arithmetic and copies ran while one was open for 0% of the time, Pallas kernels for 35%

profile of v6, /device:TPU:0, one launch (start us, length us, event | category | flops | bytes accessed | tf_op | source)
XLA Modules:
  0.0 35.3 jit_solution(13066537522827805825)
XLA Ops:
  0.6 1.1 %pad_maximum_fusion.flat = f32[1280,128]{1,0:T(8,128)S(1)} fusion(f32[640,128]{1,0:T(8,128)} %bitcast.11, f32[640,128]{1,0:T(8,128)} %bitcast.12), kind=kLoop, calls=%fused_computation | loop fusion | flops 163840 | bytes 1310720 | tf_op jit(solution)/shard_map/concatenate | solution.py:726
  1.7 0.0 copy-start
  1.8 0.5 %collective-permute-start = (f32[15,16,128]{2,1,0:T(8,128)S(1)}, f32[15,16,128]{2,1,0:T(8,128)S(1)}, u32[]{:S(2)}, u32[]{:S(2)}) collective-permute-start(f32[15,16,128]{2,1,0:T(8,128)S(1)} %get-tuple-element.26.order), channel_id=1, source_target_pairs={{0,1},{1,0},{2,3},{3,2},{4,5},{5,4},{6,7},{7,6},{8,9},{9,8},{10,11... | collective-permute-start | bytes 368648 | tf_op jit(solution)/shard_map/ppermute | solution.py:731
  2.3 5.7 %collective-permute-start.1 = (f32[15,16,128]{2,1,0:T(8,128)S(1)}, f32[15,16,128]{2,1,0:T(8,128)S(1)}, u32[]{:S(2)}, u32[]{:S(2)}) collective-permute-start(f32[15,16,128]{2,1,0:T(8,128)S(1)} %get-tuple-element.27.order2), channel_id=1, source_target_pairs={{0,15},{1,2},{2,1},{3,4},{4,3},{5,6},{6,5},{7,8},{8,7},{9,10},{10,... | collective-permute-start | bytes 368648 | tf_op jit(solution)/shard_map/ppermute | solution.py:732
  8.0 0.0 copy-done
  8.0 0.0 copy-start.1
  8.0 0.0 copy-start.2
  8.0 2.8 %shard_map.78.more = f32[5,16,8,128]{3,2,1,0:T(8,128)S(1)} custom-call(f32[10,16,8,128]{3,2,1,0:T(8,128)S(1)} %bitcast.4, s32[3,16,8,128]{3,2,1,0:T(8,128)S(1)} %copy-done, f32[15,16,128]{2,1,0:T(8,128)S(1)} %get-tuple-element.26.order, f32[15,16,128]{2,1,0:T(8,128)S(1)} %get-tuple-element.27.order2), custom_call_target="tpu_custom_call" | custom-call | flops 3220000000 | bytes 10332000 | tf_op jit(solution)/shard_map/pallas_call | solution.py:748
  10.8 0.0 copy-done.1
  10.8 0.0 copy-done.2
  10.8 1.1 %shard_map.77 = (bf16[320,720]{1,0:T(8,128)(2,1)S(1)}, bf16[384,512]{1,0:T(8,128)(2,1)S(1)}, bf16[160,192]{1,0:T(8,128)(2,1)S(1)}, f32[160,128]{1,0:T(8,128)S(1)}, bf16[2592,128]{1,0:T(8,128)(2,1)S(1)}) custom-call(f32[10,16,8,128]{3,2,1,0:T(8,128)S(1)} %bitcast.5, f32[16,135]{1,0:T(8,128)S(1)} %copy-done.1, f32[5,16]{1,0:T(8,128)S(1)} %copy-done.2, ...), custom_call_target="tpu_custom_call" | custom-call | flops 1724999936 | bytes 5535000 | tf_op jit(solution)/shard_map/pallas_call | solution.py:734
  11.9 0.0 collective-permute-done.near_twin
  11.9 0.0 collective-permute-done.1.near_other
  11.9 4.7 %shard_map.79 = (f32[5,16,8,128]{3,2,1,0:T(8,128)S(1)}, f32[16,256]{1,0:T(8,128)S(1)}) custom-call(f32[10,16,8,128]{3,2,1,0:T(8,128)S(1)} %bitcast.6, f32[15,16,128]{2,1,0:T(8,128)S(1)} %collective-permute-done.near_twin, f32[15,16,128]{2,1,0:T(8,128)S(1)} %collective-permute-done.1.near_other, f32[16,135]{1,0:T(8,128)S(1)} %copy-done.1, ...), custom_call_target="tpu_custom_call" | custom-call | flops 4024999936 | bytes 12915000 | tf_op jit(solution)/shard_map/pallas_call | solution.py:761
  16.6 0.1 collective-permute-start.2
  16.7 0.1 shard_map.82
  16.8 0.6 %collective-permute-start.6 = (f32[28,16,128]{2,1,0:T(8,128)S(1)}, f32[28,16,128]{2,1,0:T(8,128)S(1)}, u32[]{:S(2)}, u32[]{:S(2)}) collective-permute-start(f32[28,16,128]{2,1,0:T(8,128)S(1)} %get-tuple-element.42), channel_id=1, source_target_pairs={{0,1},{1,0},{2,3},{3,2},{4,5},{5,4},{6,7},{7,6},{8,9},{9,8},{10,11... | collective-permute-start | bytes 688136 | tf_op jit(solution)/shard_map/ppermute | solution.py:789
  17.3 3.1 %collective-permute-start.7 = (f32[28,16,128]{2,1,0:T(8,128)S(1)}, f32[28,16,128]{2,1,0:T(8,128)S(1)}, u32[]{:S(2)}, u32[]{:S(2)}) collective-permute-start(f32[28,16,128]{2,1,0:T(8,128)S(1)} %get-tuple-element.43), channel_id=1, source_target_pairs={{0,15},{1,2},{2,1},{3,4},{4,3},{5,6},{6,5},{7,8},{8,7},{9,10},{10,... | collective-permute-start | bytes 688136 | tf_op jit(solution)/shard_map/ppermute | solution.py:790
  20.4 0.0 collective-permute-done.2
  20.4 0.1 collective-permute-start.3
  20.5 1.8 %shard_map.80.before = f32[5,16,8,128]{3,2,1,0:T(8,128)S(1)} custom-call(f32[10,16,8,128]{3,2,1,0:T(8,128)S(1)} %bitcast.7, s32[3,16,8,128]{3,2,1,0:T(8,128)S(1)} %copy-done, f32[5,16,8,128]{3,2,1,0:T(8,128)S(1)} %get-tuple-element.37.before, f32[5,16,8,128]{3,2,1,0:T(8,128)S(1)} %shard_map.78.more, f32[16,256]{1,0:T(8,128)S(1)} %add.9.order), custom_call_target="tpu_custom_call" | custom-call | flops 2184999936 | bytes 7011000 | tf_op jit(solution)/shard_map/pallas_call | solution.py:781
  22.4 3.5 %collective-permute-done.3 = f32[16,256]{1,0:T(8,128)S(1)} collective-permute-done((f32[16,256]{1,0:T(8,128)S(1)}, f32[16,256]{1,0:T(8,128)S(1)}, u32[]{:S(2)}, u32[]{:S(2)}) %collective-permute-start.3) | collective-permute-done | bytes 16416 | tf_op jit(solution)/shard_map/ppermute | solution.py:775
  25.8 0.0 collective-permute-start.4
  25.8 1.8 %shard_map.81.before = f32[5,16,8,128]{3,2,1,0:T(8,128)S(1)} custom-call(f32[10,16,8,128]{3,2,1,0:T(8,128)S(1)} %bitcast.8, s32[3,16,8,128]{3,2,1,0:T(8,128)S(1)} %copy-done, f32[5,16,8,128]{3,2,1,0:T(8,128)S(1)} %shard_map.80.before, f32[5,16,8,128]{3,2,1,0:T(8,128)S(1)} %shard_map.78.more, f32[16,256]{1,0:T(8,128)S(1)} %add.10.order), custom_call_target="tpu_custom_call" | custom-call | flops 2184999936 | bytes 7011000 | tf_op jit(solution)/shard_map/pallas_call | solution.py:781
  27.7 2.0 %collective-permute-done.4 = f32[16,256]{1,0:T(8,128)S(1)} collective-permute-done((f32[16,256]{1,0:T(8,128)S(1)}, f32[16,256]{1,0:T(8,128)S(1)}, u32[]{:S(2)}, u32[]{:S(2)}) %collective-permute-start.4) | collective-permute-done | bytes 16416 | tf_op jit(solution)/shard_map/ppermute | solution.py:775
  29.7 0.0 collective-permute-start.5
  29.7 0.0 collective-permute-done.6.far_twin
  29.7 0.0 collective-permute-done.7.far_other
  29.7 4.8 %shard_map.83 = f32[5,16,8,128]{3,2,1,0:T(8,128)} custom-call(f32[10,16,8,128]{3,2,1,0:T(8,128)S(1)} %bitcast.9, f32[1280,128]{1,0:T(8,128)S(1)} %pad_maximum_fusion.flat, s32[3,16,8,128]{3,2,1,0:T(8,128)S(1)} %copy-done, f32[15,16,128]{2,1,0:T(8,128)S(1)} %collective-permute-done.near_twin, f32[15,16,128]{2,1,0:T(8,128)S(1)} %collective-permute-done.1.near_other, ...), custom_call_target="tpu_custom_call" | custom-call | flops 5175000064 | bytes 16605000 | tf_op jit(solution)/shard_map/pallas_call | solution.py:802
  34.5 0.0 collective-permute-done.5.theirs
  34.6 0.7 %shard_map.84 = (f32[16,135]{1,0:T(8,128)}, f32[5,16]{1,0:T(8,128)}) custom-call(f32[16,256]{1,0:T(8,128)S(1)} %add.11.order.mine, f32[16,256]{1,0:T(8,128)S(1)} %collective-permute-done.5.theirs), custom_call_target="tpu_custom_call" | custom-call | flops 575000000 | bytes 1845000 | tf_op jit(solution)/shard_map/pallas_call | solution.py:807
  (4 shorter events, 0.1 us)
Async XLA Ops:
  1.7 6.3 %copy-start = (s32[3,16,8,128]{3,2,1,0:T(8,128)S(1)}, s32[3,16,8,128]{3,2,1,0:T(8,128)}, u32[]{:S(2)}) copy-start(s32[3,16,8,128]{3,2,1,0:T(8,128)} %flags.7) | copy-start | bytes 589828
  1.8 10.1 %collective-permute-start = (f32[15,16,128]{2,1,0:T(8,128)S(1)}, f32[15,16,128]{2,1,0:T(8,128)S(1)}, u32[]{:S(2)}, u32[]{:S(2)}) collective-permute-start(f32[15,16,128]{2,1,0:T(8,128)S(1)} %get-tuple-element.26.order), channel_id=1, source_target_pairs={{0,1},{1,0},{2,3},{3,2},{4,5},{5,4},{6,7},{7,6},{8,9},{9,8},{10,11... | collective-permute-start | bytes 368648 | tf_op jit(solution)/shard_map/ppermute | solution.py:731
  2.3 9.5 %collective-permute-start.1 = (f32[15,16,128]{2,1,0:T(8,128)S(1)}, f32[15,16,128]{2,1,0:T(8,128)S(1)}, u32[]{:S(2)}, u32[]{:S(2)}) collective-permute-start(f32[15,16,128]{2,1,0:T(8,128)S(1)} %get-tuple-element.27.order2), channel_id=1, source_target_pairs={{0,15},{1,2},{2,1},{3,4},{4,3},{5,6},{6,5},{7,8},{8,7},{9,10},{10,... | collective-permute-start | bytes 368648 | tf_op jit(solution)/shard_map/ppermute | solution.py:732
  8.0 2.8 %copy-start.1 = (f32[16,135]{1,0:T(8,128)S(1)}, f32[16,135]{1,0:T(8,128)}, u32[]{:S(2)}) copy-start(f32[16,135]{1,0:T(8,128)} %kernel.3) | copy-start | bytes 25924
  8.0 2.8 %copy-start.2 = (f32[5,16]{1,0:T(8,128)S(1)}, f32[5,16]{1,0:T(8,128)}, u32[]{:S(2)}) copy-start(f32[5,16]{1,0:T(8,128)} %heads.1) | copy-start | bytes 964
  16.6 3.8 %collective-permute-start.2 = (f32[16,256]{1,0:T(8,128)S(1)}, f32[16,256]{1,0:T(8,128)S(1)}, u32[]{:S(2)}, u32[]{:S(2)}) collective-permute-start(f32[16,256]{1,0:T(8,128)S(1)} %get-tuple-element.36.order), channel_id=1, source_target_pairs={{0,1},{1,0},{2,3},{3,2},{4,5},{5,4},{6,7},{7,6},{8,9},{9,8},{10,11... | collective-permute-start | bytes 49160 | tf_op jit(solution)/shard_map/ppermute | solution.py:775
  16.8 13.0 %collective-permute-start.6 = (f32[28,16,128]{2,1,0:T(8,128)S(1)}, f32[28,16,128]{2,1,0:T(8,128)S(1)}, u32[]{:S(2)}, u32[]{:S(2)}) collective-permute-start(f32[28,16,128]{2,1,0:T(8,128)S(1)} %get-tuple-element.42), channel_id=1, source_target_pairs={{0,1},{1,0},{2,3},{3,2},{4,5},{5,4},{6,7},{7,6},{8,9},{9,8},{10,11... | collective-permute-start | bytes 688136 | tf_op jit(solution)/shard_map/ppermute | solution.py:789
  17.3 12.4 %collective-permute-start.7 = (f32[28,16,128]{2,1,0:T(8,128)S(1)}, f32[28,16,128]{2,1,0:T(8,128)S(1)}, u32[]{:S(2)}, u32[]{:S(2)}) collective-permute-start(f32[28,16,128]{2,1,0:T(8,128)S(1)} %get-tuple-element.43), channel_id=1, source_target_pairs={{0,15},{1,2},{2,1},{3,4},{4,3},{5,6},{6,5},{7,8},{8,7},{9,10},{10,... | collective-permute-start | bytes 688136 | tf_op jit(solution)/shard_map/ppermute | solution.py:790
  20.4 5.4 %collective-permute-start.3 = (f32[16,256]{1,0:T(8,128)S(1)}, f32[16,256]{1,0:T(8,128)S(1)}, u32[]{:S(2)}, u32[]{:S(2)}) collective-permute-start(f32[16,256]{1,0:T(8,128)S(1)} %add.9.order), channel_id=1, source_target_pairs={{0,2},{1,3},{2,0},{3,1},{4,6},{5,7},{6,4},{7,5},{8,10},{9,11},{10,... | collective-permute-start | bytes 49160 | tf_op jit(solution)/shard_map/ppermute | solution.py:775
  25.8 3.9 %collective-permute-start.4 = (f32[16,256]{1,0:T(8,128)S(1)}, f32[16,256]{1,0:T(8,128)S(1)}, u32[]{:S(2)}, u32[]{:S(2)}) collective-permute-start(f32[16,256]{1,0:T(8,128)S(1)} %add.10.order), channel_id=1, source_target_pairs={{0,4},{1,5},{2,6},{3,7},{4,0},{5,1},{6,2},{7,3},{8,12},{9,13},{10,... | collective-permute-start | bytes 49160 | tf_op jit(solution)/shard_map/ppermute | solution.py:775
  29.7 4.8 %collective-permute-start.5 = (f32[16,256]{1,0:T(8,128)S(1)}, f32[16,256]{1,0:T(8,128)S(1)}, u32[]{:S(2)}, u32[]{:S(2)}) collective-permute-start(f32[16,256]{1,0:T(8,128)S(1)} %add.11.order.mine), channel_id=1, source_target_pairs={{0,8},{1,9},{2,10},{3,11},{4,12},{5,13},{6,14},{7,15},{8,0},{9,1},... | collective-permute-start | bytes 49160 | tf_op jit(solution)/shard_map/ppermute | solution.py:775

commit v7 on v6

--- a/solution.py
+++ b/solution.py
@@ -313,9 +313,11 @@
     lax.fori_loop(0, nx // SLABS, z_step, 0)
 
 
-def e_faces(state, cot, rims, out):
+def e_kernel(flat, near_twin, near_other, far_twin, far_other, order, out):
+    del order
+    state, cot = views(flat)
     nx = out.shape[0] // 40
-    rim_state, rim_cot, rim_flags = rims
+    rim_state, rim_cot, rim_flags = from_rims(near_twin, near_other, far_twin, far_other)
 
     def own(ref, row, v):
         return ref[pl.ds(v * nx * 8 + row, nx, stride=8), :]
@@ -344,11 +346,10 @@
             out[pl.ds(v * nx * 8 + row, nx, stride=8), :] = value
 
 
-def y_kernel(fields, flat, flags, near_twin, near_other, far_twin, far_other, before, order, out, rim, halo, ghalo):
+def y_kernel(fields, flags, near_twin, near_other, far_twin, far_other, before, rim, order, out, halo, ghalo):
     del order
     state, cot = views(fields)
     rims = from_rims(near_twin, near_other, far_twin, far_other)
-    e_faces(*views(flat), rims, rim)
     rim_state, rim_cot, _ = rims
     nx = out.shape[1]
     for v in range(5):
@@ -731,6 +732,25 @@
         lax.ppermute(near_twin, "gy", with_twin),
         lax.ppermute(near_other, "gy", with_other),
     )
+    first = call(
+        x_kernel,
+        full,
+        [
+            vm((5, nx + 5, ny, nz), F32),
+            vm((5, nx + 1, ny, nz), F32),
+            vm((5, nx + 5, ny, nz), F32),
+        ],
+        2.8,
+        2,
+        2,
+    )(fields, flags, near_twin, near_other)
+    far_twin, far_other = call(far_kernel, (far, far), [], 0.2, 2, 1)(
+        flat, flags.reshape(3 * nx * ny, nz), first
+    )
+    far_rims = (
+        lax.ppermute(far_twin, "gy", with_twin),
+        lax.ppermute(far_other, "gy", with_other),
+    )
     *prepared, patches = call(
         prepare_kernel,
         (
@@ -744,19 +764,7 @@
         1.5,
         3,
         2,
-    )(fields, kernel, heads, near_twin, near_other)
-    first = call(
-        x_kernel,
-        full,
-        [
-            vm((5, nx + 5, ny, nz), F32),
-            vm((5, nx + 1, ny, nz), F32),
-            vm((5, nx + 5, ny, nz), F32),
-        ],
-        2.8,
-        2,
-        2,
-    )(fields, flags, near_twin, near_other)
+    )(fields, kernel, heads, far_twin, far_other)
     near_rims, patches, first = lax.optimization_barrier((near_rims, patches, first))
     own, parts = call(
         c_kernel,
@@ -782,25 +790,20 @@
         functools.partial(z_kernel, half), full, [], 1.9, 4, 1
     )(fields, flags, before, first, order)
     got = exchanged(sums, bits[-4])
-    far_twin, far_other = call(far_kernel, (far, far), [], 0.2, 2, 1)(
-        flat, flags.reshape(3 * nx * ny, nz), parts
-    )
-    far_rims = (
-        lax.ppermute(far_twin, "gy", with_twin),
-        lax.ppermute(far_other, "gy", with_other),
-    )
-    sums = sums + got
-    got = exchanged(sums, bits[-3])
     total = z_half(0, own, sums)
     got, total = lax.optimization_barrier((got, total))
     sums = sums + got
-    got = exchanged(sums, bits[-2])
+    got = exchanged(sums, bits[-3])
     total = z_half(1, total, sums)
     got, total = lax.optimization_barrier((got, total))
     sums = sums + got
+    got = exchanged(sums, bits[-2])
+    rim = call(e_kernel, shape(lines, nz), [], 1.1, 5, 1)(flat, *near_rims, *far_rims, sums)
+    got, rim = lax.optimization_barrier((got, rim))
+    sums = sums + got
     got = exchanged(sums, bits[-1])
-    flow = call(y_kernel, full, [vm((lines, nz), F32)] * 3, 4.5, 8, 1)(
-        fields, flat, flags, *near_rims, *far_rims, total, sums
+    flow = call(y_kernel, full, [vm((lines, nz), F32)] * 2, 3.7, 8, 1)(
+        fields, flags, *near_rims, *far_rims, total, rim, sums
     )
     got, flow = lax.optimization_barrier((got, flow))
     scale = float(cells * count) ** (-0.5)

time: 35.4 us -> 33.1 us (0.935)
  waiting for transfers between devices: 5.5 us -> 3.18 us
    ppermute x4, starting transfers between devices: 0.15 us -> 2.88 us  [exchanged(): return lax.ppermute(value, 'gy', [(i, i ^ bit) for i in range(count)])]
    ppermute x1, starting transfers between devices: 3.11 us -> 0.78 us  [body(): lax.ppermute(far_other, 'gy', with_other)]
    ppermute x4, waiting for transfers between devices: 5.49 us -> 3.17 us  [exchanged(): return lax.ppermute(value, 'gy', [(i, i ^ bit) for i in range(count)])]
    ppermute x1, starting transfers between devices: 0.56 us -> 0.07 us  [body(): lax.ppermute(far_twin, 'gy', with_twin)]
    pallas_call x1 -> x2, Pallas kernels: 4.82 us -> 4.81 us  [the longest x1 3.71 us: body(): call(y_kernel, full, [vm((lines, nz), F32)] * 2, 3.7, 8, 1)]
  transfers between devices with their start and end apart: 8 -> 8, of which waited for: 2 -> 2; matrix products, arithmetic and copies ran while one was open for 0% -> 0% of each run, Pallas kernels for 35% -> 52%
where the time goes in v7:
time: 33.1 us; the launch traced here: 32.9 us
  Pallas kernels  17.9 us (54%)
  starting transfers between devices  9.91 us (30%)
  waiting for transfers between devices  3.18 us (10%)
  other arithmetic  1.13 us (3%)
  between operations  0.78 us (2%)
    ppermute x1, starting transfers between devices, body(): lax.ppermute(near_other, 'gy', with_other)  5.67 us
    pallas_call x1, Pallas kernels, body(): call(c_kernel, (full, shape(ch, 256)), [vm(((nx + 2) * 3 * RIM, nz), BF16...  4.73 us
    pallas_call x1, Pallas kernels, body(): call(y_kernel, full, [vm((lines, nz), F32)] * 2, 3.7, 8, 1)  3.71 us
    pallas_call x2, Pallas kernels, body(): call(functools.partial(z_kernel, half), full, [], 1.9, 4, 1)  3.67 us
    ppermute x4, waiting for transfers between devices, exchanged(): return lax.ppermute(value, 'gy', [(i, i ^ bit) for i in range(count)])  3.17 us
    ppermute x4, starting transfers between devices, exchanged(): return lax.ppermute(value, 'gy', [(i, i ^ bit) for i in range(count)])  2.88 us
    pallas_call x1, Pallas kernels, body(): call(x_kernel, full, [vm((5, nx + 5, ny, nz), F32), vm((5, nx + 1, ny, nz...  2.78 us
    concatenate x1, other arithmetic, body(): flat = jnp.concatenate([state.reshape(lines, nz), cot.reshape(lines, nz)])  1.12 us
  transfers between devices with their start and end apart: 8, of which 2 were waited for; matrix products, arithmetic and copies ran while one was open for 0% of the time, Pallas kernels for 52%

profile of v7, /device:TPU:0, one launch (start us, length us, event | category | flops | bytes accessed | tf_op | source)
XLA Modules:
  0.0 32.9 jit_solution(3765493921511415172)
XLA Ops:
  0.6 1.1 %pad_maximum_fusion.flat = f32[1280,128]{1,0:T(8,128)S(1)} fusion(f32[640,128]{1,0:T(8,128)} %bitcast.11, f32[640,128]{1,0:T(8,128)} %bitcast.12), kind=kLoop, calls=%fused_computation | loop fusion | flops 163840 | bytes 1310720 | tf_op jit(solution)/shard_map/concatenate | solution.py:727
  1.7 0.0 copy-start
  1.8 0.5 %collective-permute-start = (f32[15,16,128]{2,1,0:T(8,128)S(1)}, f32[15,16,128]{2,1,0:T(8,128)S(1)}, u32[]{:S(2)}, u32[]{:S(2)}) collective-permute-start(f32[15,16,128]{2,1,0:T(8,128)S(1)} %get-tuple-element.28.order), channel_id=1, source_target_pairs={{0,1},{1,0},{2,3},{3,2},{4,5},{5,4},{6,7},{7,6},{8,9},{9,8},{10,11... | collective-permute-start | bytes 368648 | tf_op jit(solution)/shard_map/ppermute | solution.py:732
  2.3 5.7 %collective-permute-start.1 = (f32[15,16,128]{2,1,0:T(8,128)S(1)}, f32[15,16,128]{2,1,0:T(8,128)S(1)}, u32[]{:S(2)}, u32[]{:S(2)}) collective-permute-start(f32[15,16,128]{2,1,0:T(8,128)S(1)} %get-tuple-element.29.order2), channel_id=1, source_target_pairs={{0,15},{1,2},{2,1},{3,4},{4,3},{5,6},{6,5},{7,8},{8,7},{9,10},{10,... | collective-permute-start | bytes 368648 | tf_op jit(solution)/shard_map/ppermute | solution.py:733
  8.0 0.0 copy-done
  8.0 2.8 %shard_map.77.order.more = f32[5,16,8,128]{3,2,1,0:T(8,128)S(1)} custom-call(f32[10,16,8,128]{3,2,1,0:T(8,128)S(1)} %bitcast.4, s32[3,16,8,128]{3,2,1,0:T(8,128)S(1)} %copy-done, f32[15,16,128]{2,1,0:T(8,128)S(1)} %get-tuple-element.28.order, f32[15,16,128]{2,1,0:T(8,128)S(1)} %get-tuple-element.29.order2), custom_call_target="tpu_custom_call" | custom-call | flops 3220000000 | bytes 10332000 | tf_op jit(solution)/shard_map/pallas_call | solution.py:735
  10.8 0.0 copy-start.1
  10.8 0.0 copy-start.2
  10.8 0.1 shard_map.78
  10.9 0.1 collective-permute-start.5
  11.0 0.8 %collective-permute-start.6 = (f32[28,16,128]{2,1,0:T(8,128)S(1)}, f32[28,16,128]{2,1,0:T(8,128)S(1)}, u32[]{:S(2)}, u32[]{:S(2)}) collective-permute-start(f32[28,16,128]{2,1,0:T(8,128)S(1)} %get-tuple-element.31.order2), channel_id=1, source_target_pairs={{0,15},{1,2},{2,1},{3,4},{4,3},{5,6},{6,5},{7,8},{8,7},{9,10},{10,... | collective-permute-start | bytes 688136 | tf_op jit(solution)/shard_map/ppermute | solution.py:752
  11.8 0.0 copy-done.1
  11.8 0.0 copy-done.2
  11.8 1.1 %shard_map.79 = (bf16[320,720]{1,0:T(8,128)(2,1)S(1)}, bf16[384,512]{1,0:T(8,128)(2,1)S(1)}, bf16[160,192]{1,0:T(8,128)(2,1)S(1)}, f32[160,128]{1,0:T(8,128)S(1)}, bf16[2592,128]{1,0:T(8,128)(2,1)S(1)}) custom-call(f32[10,16,8,128]{3,2,1,0:T(8,128)S(1)} %bitcast.5, f32[16,135]{1,0:T(8,128)S(1)} %copy-done.1, f32[5,16]{1,0:T(8,128)S(1)} %copy-done.2, ...), custom_call_target="tpu_custom_call" | custom-call | flops 1724999936 | bytes 5535000 | tf_op jit(solution)/shard_map/pallas_call | solution.py:754
  12.8 0.0 collective-permute-done.near_twin
  12.8 0.0 collective-permute-done.1.near_other
  12.8 4.7 %shard_map.80 = (f32[5,16,8,128]{3,2,1,0:T(8,128)S(1)}, f32[16,256]{1,0:T(8,128)S(1)}) custom-call(f32[10,16,8,128]{3,2,1,0:T(8,128)S(1)} %bitcast.6, f32[15,16,128]{2,1,0:T(8,128)S(1)} %collective-permute-done.near_twin, f32[15,16,128]{2,1,0:T(8,128)S(1)} %collective-permute-done.1.near_other, f32[16,135]{1,0:T(8,128)S(1)} %copy-done.1, ...), custom_call_target="tpu_custom_call" | custom-call | flops 4024999936 | bytes 12915000 | tf_op jit(solution)/shard_map/pallas_call | solution.py:769
  17.6 0.1 collective-permute-start.2
  17.6 1.8 %shard_map.81.before = f32[5,16,8,128]{3,2,1,0:T(8,128)S(1)} custom-call(f32[10,16,8,128]{3,2,1,0:T(8,128)S(1)} %bitcast.7, s32[3,16,8,128]{3,2,1,0:T(8,128)S(1)} %copy-done, f32[5,16,8,128]{3,2,1,0:T(8,128)S(1)} %get-tuple-element.41.before, f32[5,16,8,128]{3,2,1,0:T(8,128)S(1)} %shard_map.77.order.more, f32[16,256]{1,0:T(8,128)S(1)} %get-tuple-element.40.order), custom_call_target="tpu_custom_call" | custom-call | flops 2184999936 | bytes 7011000 | tf_op jit(solution)/shard_map/pallas_call | solution.py:789
  19.5 0.0 collective-permute-done.2
  19.5 1.4 %collective-permute-start.3 = (f32[16,256]{1,0:T(8,128)S(1)}, f32[16,256]{1,0:T(8,128)S(1)}, u32[]{:S(2)}, u32[]{:S(2)}) collective-permute-start(f32[16,256]{1,0:T(8,128)S(1)} %add.9.order), channel_id=1, source_target_pairs={{0,2},{1,3},{2,0},{3,1},{4,6},{5,7},{6,4},{7,5},{8,10},{9,11},{10,... | collective-permute-start | bytes 49160 | tf_op jit(solution)/shard_map/ppermute | solution.py:783
  20.9 1.8 %shard_map.82.before = f32[5,16,8,128]{3,2,1,0:T(8,128)S(1)} custom-call(f32[10,16,8,128]{3,2,1,0:T(8,128)S(1)} %bitcast.8, s32[3,16,8,128]{3,2,1,0:T(8,128)S(1)} %copy-done, f32[5,16,8,128]{3,2,1,0:T(8,128)S(1)} %shard_map.81.before, f32[5,16,8,128]{3,2,1,0:T(8,128)S(1)} %shard_map.77.order.more, f32[16,256]{1,0:T(8,128)S(1)} %add.9.order), custom_call_target="tpu_custom_call" | custom-call | flops 2184999936 | bytes 7011000 | tf_op jit(solution)/shard_map/pallas_call | solution.py:789
  22.8 0.6 %collective-permute-done.3 = f32[16,256]{1,0:T(8,128)S(1)} collective-permute-done((f32[16,256]{1,0:T(8,128)S(1)}, f32[16,256]{1,0:T(8,128)S(1)}, u32[]{:S(2)}, u32[]{:S(2)}) %collective-permute-start.3) | collective-permute-done | bytes 16416 | tf_op jit(solution)/shard_map/ppermute | solution.py:783
  23.3 0.0 collective-permute-start.4
  23.3 0.0 collective-permute-done.5.far_twin
  23.3 0.0 collective-permute-done.6.far_other
  23.4 1.1 %shard_map.83.rim = f32[640,128]{1,0:T(8,128)S(1)} custom-call(f32[1280,128]{1,0:T(8,128)S(1)} %pad_maximum_fusion.flat, f32[15,16,128]{2,1,0:T(8,128)S(1)} %collective-permute-done.near_twin, f32[15,16,128]{2,1,0:T(8,128)S(1)} %collective-permute-done.1.near_other, f32[28,16,128]{2,1,0:T(8,128)S(1)} %collective-permute-done.5.far_twin, ...), custom_call_target="tpu_custom_call" | custom-call | flops 1264999936 | bytes 4059000 | tf_op jit(solution)/shard_map/pallas_call | solution.py:801
  24.5 2.6 %collective-permute-done.4 = f32[16,256]{1,0:T(8,128)S(1)} collective-permute-done((f32[16,256]{1,0:T(8,128)S(1)}, f32[16,256]{1,0:T(8,128)S(1)}, u32[]{:S(2)}, u32[]{:S(2)}) %collective-permute-start.4) | collective-permute-done | bytes 16416 | tf_op jit(solution)/shard_map/ppermute | solution.py:783
  27.1 1.4 %collective-permute-start.7 = (f32[16,256]{1,0:T(8,128)S(1)}, f32[16,256]{1,0:T(8,128)S(1)}, u32[]{:S(2)}, u32[]{:S(2)}) collective-permute-start(f32[16,256]{1,0:T(8,128)S(1)} %add.11.order.mine), channel_id=1, source_target_pairs={{0,8},{1,9},{2,10},{3,11},{4,12},{5,13},{6,14},{7,15},{8,0},{9,1},... | collective-permute-start | bytes 49160 | tf_op jit(solution)/shard_map/ppermute | solution.py:783
  28.5 3.7 %shard_map.84 = f32[5,16,8,128]{3,2,1,0:T(8,128)} custom-call(f32[10,16,8,128]{3,2,1,0:T(8,128)S(1)} %bitcast.9, s32[3,16,8,128]{3,2,1,0:T(8,128)S(1)} %copy-done, f32[15,16,128]{2,1,0:T(8,128)S(1)} %collective-permute-done.near_twin, f32[15,16,128]{2,1,0:T(8,128)S(1)} %collective-permute-done.1.near_other, ...), custom_call_target="tpu_custom_call" | custom-call | flops 4255000064 | bytes 13653000 | tf_op jit(solution)/shard_map/pallas_call | solution.py:805
  32.2 0.0 collective-permute-done.7.theirs
  32.2 0.7 %shard_map.85 = (f32[16,135]{1,0:T(8,128)}, f32[5,16]{1,0:T(8,128)}) custom-call(f32[16,256]{1,0:T(8,128)S(1)} %add.11.order.mine, f32[16,256]{1,0:T(8,128)S(1)} %collective-permute-done.7.theirs), custom_call_target="tpu_custom_call" | custom-call | flops 575000000 | bytes 1845000 | tf_op jit(solution)/shard_map/pallas_call | solution.py:810
  (4 shorter events, 0.1 us)
Async XLA Ops:
  1.7 6.3 %copy-start = (s32[3,16,8,128]{3,2,1,0:T(8,128)S(1)}, s32[3,16,8,128]{3,2,1,0:T(8,128)}, u32[]{:S(2)}) copy-start(s32[3,16,8,128]{3,2,1,0:T(8,128)} %flags.7) | copy-start | bytes 589828
  1.8 11.0 %collective-permute-start = (f32[15,16,128]{2,1,0:T(8,128)S(1)}, f32[15,16,128]{2,1,0:T(8,128)S(1)}, u32[]{:S(2)}, u32[]{:S(2)}) collective-permute-start(f32[15,16,128]{2,1,0:T(8,128)S(1)} %get-tuple-element.28.order), channel_id=1, source_target_pairs={{0,1},{1,0},{2,3},{3,2},{4,5},{5,4},{6,7},{7,6},{8,9},{9,8},{10,11... | collective-permute-start | bytes 368648 | tf_op jit(solution)/shard_map/ppermute | solution.py:732
  2.3 10.5 %collective-permute-start.1 = (f32[15,16,128]{2,1,0:T(8,128)S(1)}, f32[15,16,128]{2,1,0:T(8,128)S(1)}, u32[]{:S(2)}, u32[]{:S(2)}) collective-permute-start(f32[15,16,128]{2,1,0:T(8,128)S(1)} %get-tuple-element.29.order2), channel_id=1, source_target_pairs={{0,15},{1,2},{2,1},{3,4},{4,3},{5,6},{6,5},{7,8},{8,7},{9,10},{10,... | collective-permute-start | bytes 368648 | tf_op jit(solution)/shard_map/ppermute | solution.py:733
  10.8 1.0 %copy-start.1 = (f32[16,135]{1,0:T(8,128)S(1)}, f32[16,135]{1,0:T(8,128)}, u32[]{:S(2)}) copy-start(f32[16,135]{1,0:T(8,128)} %kernel.3) | copy-start | bytes 25924
  10.8 1.0 %copy-start.2 = (f32[5,16]{1,0:T(8,128)S(1)}, f32[5,16]{1,0:T(8,128)}, u32[]{:S(2)}) copy-start(f32[5,16]{1,0:T(8,128)} %heads.1) | copy-start | bytes 964
  10.9 12.4 %collective-permute-start.5 = (f32[28,16,128]{2,1,0:T(8,128)S(1)}, f32[28,16,128]{2,1,0:T(8,128)S(1)}, u32[]{:S(2)}, u32[]{:S(2)}) collective-permute-start(f32[28,16,128]{2,1,0:T(8,128)S(1)} %get-tuple-element.30.order), channel_id=1, source_target_pairs={{0,1},{1,0},{2,3},{3,2},{4,5},{5,4},{6,7},{7,6},{8,9},{9,8},{10,11... | collective-permute-start | bytes 688136 | tf_op jit(solution)/shard_map/ppermute | solution.py:751
  11.0 12.4 %collective-permute-start.6 = (f32[28,16,128]{2,1,0:T(8,128)S(1)}, f32[28,16,128]{2,1,0:T(8,128)S(1)}, u32[]{:S(2)}, u32[]{:S(2)}) collective-permute-start(f32[28,16,128]{2,1,0:T(8,128)S(1)} %get-tuple-element.31.order2), channel_id=1, source_target_pairs={{0,15},{1,2},{2,1},{3,4},{4,3},{5,6},{6,5},{7,8},{8,7},{9,10},{10,... | collective-permute-start | bytes 688136 | tf_op jit(solution)/shard_map/ppermute | solution.py:752
  17.6 1.9 %collective-permute-start.2 = (f32[16,256]{1,0:T(8,128)S(1)}, f32[16,256]{1,0:T(8,128)S(1)}, u32[]{:S(2)}, u32[]{:S(2)}) collective-permute-start(f32[16,256]{1,0:T(8,128)S(1)} %get-tuple-element.40.order), channel_id=1, source_target_pairs={{0,1},{1,0},{2,3},{3,2},{4,5},{5,4},{6,7},{7,6},{8,9},{9,8},{10,11... | collective-permute-start | bytes 49160 | tf_op jit(solution)/shard_map/ppermute | solution.py:783
  19.5 3.8 %collective-permute-start.3 = (f32[16,256]{1,0:T(8,128)S(1)}, f32[16,256]{1,0:T(8,128)S(1)}, u32[]{:S(2)}, u32[]{:S(2)}) collective-permute-start(f32[16,256]{1,0:T(8,128)S(1)} %add.9.order), channel_id=1, source_target_pairs={{0,2},{1,3},{2,0},{3,1},{4,6},{5,7},{6,4},{7,5},{8,10},{9,11},{10,... | collective-permute-start | bytes 49160 | tf_op jit(solution)/shard_map/ppermute | solution.py:783
  23.3 3.7 %collective-permute-start.4 = (f32[16,256]{1,0:T(8,128)S(1)}, f32[16,256]{1,0:T(8,128)S(1)}, u32[]{:S(2)}, u32[]{:S(2)}) collective-permute-start(f32[16,256]{1,0:T(8,128)S(1)} %add.10.order), channel_id=1, source_target_pairs={{0,4},{1,5},{2,6},{3,7},{4,0},{5,1},{6,2},{7,3},{8,12},{9,13},{10,... | collective-permute-start | bytes 49160 | tf_op jit(solution)/shard_map/ppermute | solution.py:783
  27.1 5.1 %collective-permute-start.7 = (f32[16,256]{1,0:T(8,128)S(1)}, f32[16,256]{1,0:T(8,128)S(1)}, u32[]{:S(2)}, u32[]{:S(2)}) collective-permute-start(f32[16,256]{1,0:T(8,128)S(1)} %add.11.order.mine), channel_id=1, source_target_pairs={{0,8},{1,9},{2,10},{3,11},{4,12},{5,13},{6,14},{7,15},{8,0},{9,1},... | collective-permute-start | bytes 49160 | tf_op jit(solution)/shard_map/ppermute | solution.py:783

commit v8 on v7

--- a/solution.py
+++ b/solution.py
@@ -42,16 +42,17 @@
     o0 = jnp.where(smooth, w0 * r, c0)
     o2 = jnp.where(smooth, w2 * r, c2)
     u = o0 * td + o2 * t1
-    return (pa + pm2) - u, (i0, i1, i2, w0, w1, w2, r, o0, o2, u)
-
-
-def side_pull(mu, pa, pm, m0, m2, td, t1, smooth, saved):
-    i0, i1, i2, w0, w1, w2, r, o0, o2, u = saved
+    b0 = w0 * i0 * (td - u)
+    b1 = w1 * i1 * u
+    b2 = w2 * i2 * (t1 - u)
+    return (pa + pm2) - u, (b0, b1, b2, r, o0, o2)
+
+
+def side_pull(mu, pa, pm, m0, m2, smooth, saved):
+    b0, b1, b2, r, o0, o2 = saved
     mu2 = mu + mu
     rm = jnp.where(smooth, mu2, 0.0) * r
-    s0 = (w0 * i0) * rm * (td - u)
-    s1 = (w1 * i1) * rm * u
-    s2 = (w2 * i2) * rm * (t1 - u)
+    s0, s1, s2 = b0 * rm, b1 * rm, b2 * rm
     pa_bar = s0 * (m0 + pa) - s1 * pm + mu
     pm_bar = s2 * (m2 + pm) - s1 * pa + mu2
     return s0, s1, s2, pa_bar, pm_bar, o0 * mu2, o2 * mu
@@ -145,7 +146,7 @@
         )
         left.append(v[2] + hl * (1.0 / 6.0))
         right.append(v[3] - hr * (1.0 / 6.0))
-        kept.append((p, g, args_l, args_r, saved_l, saved_r))
+        kept.append((p, g, args_l[:4], args_r[:4], saved_l, saved_r))
     l_bar, r_bar = hllc_pull(left, right, normal, flags, cot)
     out = []
     for i in range(5):
@@ -413,8 +414,9 @@
     h_out[...] = heads[: h_out.shape[0], :ch]
 
 
-MAIN, RIM = 48, 32
-COLUMNS = 9 * (MAIN + RIM)
+MAIN, RIM = 48, 16
+OWN_COLUMNS = 9 * (MAIN + RIM)
+COLUMNS = OWN_COLUMNS + 9 * RIM
 
 
 def split(x):
@@ -430,19 +432,32 @@
     return lax.rem(lax.axis_index("gy"), 2) == 0
 
 
-def prepare_kernel(fields, kernel, heads, order, order2, w_rows, w_cols, w_head, bias, t, wide):
+def put_patches(high, low, x, rows):
+    n = rows.shape[0]
+    hi, lo = split(rows)
+    hi32, lo32 = hi.astype(F32), lo.astype(F32)
+    for q, turn in enumerate((1, 0, 127)):
+        at = pl.ds((x + 1) * 3 * n + q * n, n)
+        high[at, :] = pltpu.roll(hi32, turn, 1).astype(BF16) if turn else hi
+        low[at, :] = pltpu.roll(lo32, turn, 1).astype(BF16) if turn else lo
+
+
+def wrap_patches(high, low, nx, rows):
+    n = 3 * rows
+    for ref in (high, low):
+        ref[pl.ds(0, n), :] = ref[pl.ds(nx * n, n), :]
+        ref[pl.ds((nx + 1) * n, n), :] = ref[pl.ds(n, n), :]
+
+
+def prepare_kernel(fields, kernel, heads, order, order2, w_rows, w_cols, w_head, bias, t, t_low, wide):
     del order, order2
     state, _ = views(fields)
     nx = state.shape[1]
     for x in range(nx):
         rows = [state[v, x] - (1.0 if v in (0, 4) else 0.0) for v in range(5)]
         mid = jnp.concatenate([*rows, jnp.zeros((8, 128), F32)], axis=0)
-        at = (x + 1) * 3 * MAIN
-        t[pl.ds(at, MAIN), :] = pltpu.roll(mid, 1, 1).astype(BF16)
-        t[pl.ds(at + MAIN, MAIN), :] = mid.astype(BF16)
-        t[pl.ds(at + 2 * MAIN, MAIN), :] = pltpu.roll(mid, 127, 1).astype(BF16)
-    t[pl.ds(0, 3 * MAIN), :] = t[pl.ds(nx * 3 * MAIN, 3 * MAIN), :]
-    t[pl.ds((nx + 1) * 3 * MAIN, 3 * MAIN), :] = t[pl.ds(3 * MAIN, 3 * MAIN), :]
+        put_patches(t, t_low, x, mid)
+    wrap_patches(t, t_low, nx, MAIN)
 
     ch, taps = kernel.shape
     w = kernel[...]
@@ -451,7 +466,7 @@
     wide[pl.ds(0, ch), pl.ds(0, taps)] = hi.astype(F32)
     wide[pl.ds(ch, ch), pl.ds(0, taps)] = lo.astype(F32)
     both = wide[...].astype(BF16)
-    kind, tap = columns()
+    kind, tap = columns(COLUMNS)
     base = jnp.dot(both, own_taps(kind, tap), preferred_element_type=F32)
     rim = jnp.dot(both, rim_taps(kind, tap), preferred_element_type=F32)
     n = base.shape[1]
@@ -513,9 +528,9 @@
 
 
 def c_kernel(
-    fields, near_twin, near_other, kernel, w_rows, w_cols, w_head, bias, t,
+    fields, near_twin, near_other, kernel, w_rows, w_cols, w_head, bias, t, t_low,
     own, parts,
-    t_rim, acc, edge, gedge,
+    rim, rim_low, outer, outer_low, acc, edge, gedge,
 ):
     _, cot = views(fields)
     nx = cot.shape[1]
@@ -524,46 +539,49 @@
 
     for v in range(5):
         level = 1.0 if v in (0, 4) else 0.0
-        for q, row in enumerate((-1, -2, 8, 9)):
-            edge[pl.ds(5 * q + v, nx, stride=RIM), :] = rim_state(row, v) - level
+        for q, row in enumerate((-1, 8, -2, 9)):
+            at = q // 2 * RIM + 5 * (q % 2) + v
+            edge[pl.ds(at, nx, stride=2 * RIM), :] = rim_state(row, v) - level
         gedge[pl.ds(v, nx, stride=16), :] = rim_cot(-1, v)
         gedge[pl.ds(8 + v, nx, stride=16), :] = rim_cot(8, v)
     none = jnp.zeros((nx, 128), F32)
-    for q in range(20, RIM):
-        edge[pl.ds(q, nx, stride=RIM), :] = none
+    for q in range(10, RIM):
+        edge[pl.ds(q, nx, stride=2 * RIM), :] = none
+        edge[pl.ds(RIM + q, nx, stride=2 * RIM), :] = none
     for q in (5, 6, 7):
         gedge[pl.ds(q, nx, stride=16), :] = none
         gedge[pl.ds(8 + q, nx, stride=16), :] = none
     for x in range(nx):
-        mid = edge[pl.ds(x * RIM, RIM), :]
-        at = (x + 1) * 3 * RIM
-        t_rim[pl.ds(at, RIM), :] = pltpu.roll(mid, 1, 1).astype(BF16)
-        t_rim[pl.ds(at + RIM, RIM), :] = mid.astype(BF16)
-        t_rim[pl.ds(at + 2 * RIM, RIM), :] = pltpu.roll(mid, 127, 1).astype(BF16)
-    t_rim[pl.ds(0, 3 * RIM), :] = t_rim[pl.ds(nx * 3 * RIM, 3 * RIM), :]
-    t_rim[pl.ds((nx + 1) * 3 * RIM, 3 * RIM), :] = t_rim[pl.ds(3 * RIM, 3 * RIM), :]
+        put_patches(rim, rim_low, x, edge[pl.ds(2 * x * RIM, RIM), :])
+        put_patches(outer, outer_low, x, edge[pl.ds((2 * x + 1) * RIM, RIM), :])
+    wrap_patches(rim, rim_low, nx, RIM)
+    wrap_patches(outer, outer_low, nx, RIM)
+
+    def gathered(x, *blocks):
+        columns = []
+        for j in range(WIDE):
+            rows = [ref[pl.ds((x + j) * 3 * n, 9 * n), :] for ref, n in blocks]
+            columns.append(jnp.concatenate(rows, axis=0) if len(rows) > 1 else rows[0])
+        return jnp.concatenate(columns, axis=1)
 
     kept = 8 * ch
     kg = hg = dsum = None
     zeros8 = jnp.zeros((8, 128 * WIDE), F32)
     written = set()
     for x in range(0, nx, WIDE):
-        s = jnp.concatenate(
-            [
-                jnp.concatenate(
-                    [
-                        t[pl.ds((x + j) * 3 * MAIN, 9 * MAIN), :],
-                        t_rim[pl.ds((x + j) * 3 * RIM, 9 * RIM), :],
-                    ],
-                    axis=0,
-                )
-                for j in range(WIDE)
-            ],
-            axis=1,
-        )
-        z2 = jnp.dot(w_rows[...], s, preferred_element_type=F32)
+        s_hi = gathered(x, (t, MAIN), (rim, RIM))
+        s_lo = gathered(x, (t_low, MAIN), (rim_low, RIM))
+        far_hi, far_lo = gathered(x, (outer, RIM)), gathered(x, (outer_low, RIM))
+        z2 = jnp.dot(
+            w_rows[...], jnp.concatenate([s_hi, far_hi], axis=0), preferred_element_type=F32
+        )
         rows = z2.shape[0] // 2
-        z = z2[:rows] + z2[rows:] + jnp.concatenate([bias[...]] * WIDE, axis=1)
+        z3 = jnp.dot(
+            w_rows[pl.ds(0, rows), :],
+            jnp.concatenate([s_lo, far_lo], axis=0),
+            preferred_element_type=F32,
+        )
+        z = z2[:rows] + (z2[rows:] + z3) + jnp.concatenate([bias[...]] * WIDE, axis=1)
         hidden = jnp.tanh(z)
         g = jnp.concatenate(
             [
@@ -587,8 +605,11 @@
             jnp.concatenate([d_hi, d_lo, d_hi, zeros], axis=0),
             preferred_element_type=F32,
         )
-        k2 = over_lanes(s, jnp.concatenate([d_hi[:kept], d_lo[:kept]], axis=0))
-        k2 = k2[:, :kept] + k2[:, kept:]
+        k2 = over_lanes(
+            jnp.concatenate([s_hi, s_lo], axis=0),
+            jnp.concatenate([d_hi[:kept], d_lo[:kept]], axis=0),
+        )
+        k2 = k2[:OWN_COLUMNS, :kept] + (k2[:OWN_COLUMNS, kept:] + k2[OWN_COLUMNS:, :kept])
         kg = k2 if kg is None else kg + k2
         hid2 = jnp.concatenate(split(hidden[:kept]), axis=0)
         g2 = jnp.concatenate([g_hi32[:40], g_lo32[:40]], axis=0).astype(BF16)
@@ -634,7 +655,7 @@
     level_sum = jnp.zeros((ch, 1), F32)
     head_sum = jnp.zeros((ch, 128), F32)
     n = kg.shape[1]
-    columns_at, tap = columns()
+    columns_at, tap = columns(n)
     kind = jnp.broadcast_to(columns_at[0:1], (ch, n))
     total = jnp.zeros((ch, n), F32)
     for y in range(8):
@@ -658,16 +679,18 @@
     parts[:, pl.ds(128, 128)] = parts[:, pl.ds(128, 128)] + pltpu.roll(head_sum * STEP, 16, 1)
 
 
-def columns():
-    lane = lax.broadcasted_iota(jnp.int32, (8, COLUMNS), 1)
+def columns(n):
+    lane = lax.broadcasted_iota(jnp.int32, (8, n), 1)
     main = lane < 9 * MAIN
-    past = lane - 9 * MAIN
+    far = lane >= OWN_COLUMNS
+    past = lane - jnp.where(far, OWN_COLUMNS, 9 * MAIN)
     block = sum((lane >= MAIN * i).astype(jnp.int32) for i in range(1, 9))
-    o = jnp.where(main, block, past >> 5)
+    o = jnp.where(main, block, past >> 4)
     r = jnp.where(main, lane - MAIN * block, past & (RIM - 1))
-    which = sum((r >= 5 * i).astype(jnp.int32) for i in (1, 2, 3, 4))
-    kind = jnp.where(main, jnp.where(r < 40, r & 7, 12), 8 + which)
-    v = jnp.where(main, r >> 3, r - 5 * which)
+    second = (r >= 5).astype(jnp.int32)
+    rim = jnp.where(r < 10, 8 + 2 * second + far.astype(jnp.int32), 12)
+    kind = jnp.where(main, jnp.where(r < 40, r & 7, 12), rim)
+    v = jnp.where(main, r >> 3, r - 5 * second)
     return kind, o * 5 + v
 
 
@@ -751,13 +774,14 @@
         lax.ppermute(far_twin, "gy", with_twin),
         lax.ppermute(far_other, "gy", with_other),
     )
-    *prepared, patches = call(
+    *prepared, patches, patches_low = call(
         prepare_kernel,
         (
             half_shape(20 * ch, COLUMNS),
             half_shape(384, 512),
             half_shape(10 * ch, 192),
             shape(10 * ch, 128),
+            half_shape((nx + 2) * 3 * MAIN, nz),
             half_shape((nx + 2) * 3 * MAIN, nz),
         ),
         [vm((2 * ch, 144), F32)],
@@ -770,14 +794,14 @@
         c_kernel,
         (full, shape(ch, 256)),
         [
-            vm(((nx + 2) * 3 * RIM, nz), BF16),
+            *[vm(((nx + 2) * 3 * RIM, nz), BF16)] * 4,
             vm((nx * 120, nz), F32),
-            vm((RIM * nx, nz), F32),
+            vm((2 * RIM * nx, nz), F32),
             vm((16 * nx, nz), F32),
         ],
-        3.5,
-        9,
-    )(fields, *near_rims, kernel, *prepared, patches)
+        5.5,
+        10,
+    )(fields, *near_rims, kernel, *prepared, patches, patches_low)
 
     def exchanged(value, bit):
         return lax.ppermute(value, "gy", [(i, i ^ bit) for i in range(count)])

time: 33.1 us -> 34.4 us (1.039)
  Pallas kernels: 17.9 us -> 19.3 us
    pallas_call x1, Pallas kernels: 4.73 us -> 6.06 us  [body(): call(c_kernel, (full, shape(ch, 256)), [*[vm(((nx + 2) * 3 * RIM, nz), BF...]
  transfers between devices with their start and end apart: 8 -> 8, of which waited for: 2 -> 2; matrix products, arithmetic and copies ran while one was open for 0% -> 0% of each run, Pallas kernels for 52% -> 54%
where the time goes in v8:
time: 34.4 us; the launch traced here: 34.3 us
  Pallas kernels  19.3 us (56%)
  starting transfers between devices  9.91 us (29%)
  waiting for transfers between devices  3.19 us (9%)
  other arithmetic  1.13 us (3%)
  between operations  0.78 us (2%)
    pallas_call x1, Pallas kernels, body(): call(c_kernel, (full, shape(ch, 256)), [*[vm(((nx + 2) * 3 * RIM, nz), BF...  6.06 us
    ppermute x1, starting transfers between devices, body(): lax.ppermute(near_other, 'gy', with_other)  5.67 us
    pallas_call x2, Pallas kernels, body(): call(functools.partial(z_kernel, half), full, [], 1.9, 4, 1)  3.65 us
    pallas_call x1, Pallas kernels, body(): call(y_kernel, full, [vm((lines, nz), F32)] * 2, 3.7, 8, 1)  3.63 us
    ppermute x4, waiting for transfers between devices, exchanged(): return lax.ppermute(value, 'gy', [(i, i ^ bit) for i in range(count)])  3.18 us
    ppermute x4, starting transfers between devices, exchanged(): return lax.ppermute(value, 'gy', [(i, i ^ bit) for i in range(count)])  2.87 us
    pallas_call x1, Pallas kernels, body(): call(x_kernel, full, [vm((5, nx + 5, ny, nz), F32), vm((5, nx + 1, ny, nz...  2.78 us
    pallas_call x1, Pallas kernels, body(): call(prepare_kernel, (half_shape(20 * ch, COLUMNS), half_shape(384, 512),...  1.19 us
  transfers between devices with their start and end apart: 8, of which 2 were waited for; matrix products, arithmetic and copies ran while one was open for 0% of the time, Pallas kernels for 54%

profile of v8, /device:TPU:0, one launch (start us, length us, event | category | flops | bytes accessed | tf_op | source)
XLA Modules:
  0.0 34.3 jit_solution(4885747367387512756)
XLA Ops:
  0.6 1.1 %pad_maximum_fusion.flat = f32[1280,128]{1,0:T(8,128)S(1)} fusion(f32[640,128]{1,0:T(8,128)} %bitcast.11, f32[640,128]{1,0:T(8,128)} %bitcast.12), kind=kLoop, calls=%fused_computation | loop fusion | flops 163840 | bytes 1310720 | tf_op jit(solution)/shard_map/concatenate | solution.py:750
  1.7 0.0 copy-start
  1.8 0.5 %collective-permute-start = (f32[15,16,128]{2,1,0:T(8,128)S(1)}, f32[15,16,128]{2,1,0:T(8,128)S(1)}, u32[]{:S(2)}, u32[]{:S(2)}) collective-permute-start(f32[15,16,128]{2,1,0:T(8,128)S(1)} %get-tuple-element.29.order), channel_id=1, source_target_pairs={{0,1},{1,0},{2,3},{3,2},{4,5},{5,4},{6,7},{7,6},{8,9},{9,8},{10,11... | collective-permute-start | bytes 368648 | tf_op jit(solution)/shard_map/ppermute | solution.py:755
  2.3 5.7 %collective-permute-start.1 = (f32[15,16,128]{2,1,0:T(8,128)S(1)}, f32[15,16,128]{2,1,0:T(8,128)S(1)}, u32[]{:S(2)}, u32[]{:S(2)}) collective-permute-start(f32[15,16,128]{2,1,0:T(8,128)S(1)} %get-tuple-element.30.order2), channel_id=1, source_target_pairs={{0,15},{1,2},{2,1},{3,4},{4,3},{5,6},{6,5},{7,8},{8,7},{9,10},{10,... | collective-permute-start | bytes 368648 | tf_op jit(solution)/shard_map/ppermute | solution.py:756
  8.0 0.0 copy-done
  8.0 2.8 %shard_map.77.order.more = f32[5,16,8,128]{3,2,1,0:T(8,128)S(1)} custom-call(f32[10,16,8,128]{3,2,1,0:T(8,128)S(1)} %bitcast.4, s32[3,16,8,128]{3,2,1,0:T(8,128)S(1)} %copy-done, f32[15,16,128]{2,1,0:T(8,128)S(1)} %get-tuple-element.29.order, f32[15,16,128]{2,1,0:T(8,128)S(1)} %get-tuple-element.30.order2), custom_call_target="tpu_custom_call" | custom-call | flops 3220000000 | bytes 10332000 | tf_op jit(solution)/shard_map/pallas_call | solution.py:758
  10.8 0.0 copy-start.1
  10.8 0.0 copy-start.2
  10.8 0.1 shard_map.78
  10.9 0.1 collective-permute-start.5
  11.0 0.8 %collective-permute-start.6 = (f32[28,16,128]{2,1,0:T(8,128)S(1)}, f32[28,16,128]{2,1,0:T(8,128)S(1)}, u32[]{:S(2)}, u32[]{:S(2)}) collective-permute-start(f32[28,16,128]{2,1,0:T(8,128)S(1)} %get-tuple-element.32.order2), channel_id=1, source_target_pairs={{0,15},{1,2},{2,1},{3,4},{4,3},{5,6},{6,5},{7,8},{8,7},{9,10},{10,... | collective-permute-start | bytes 688136 | tf_op jit(solution)/shard_map/ppermute | solution.py:775
  11.8 0.0 copy-done.1
  11.8 0.0 copy-done.2
  11.8 1.2 %shard_map.79 = (bf16[320,720]{1,0:T(8,128)(2,1)S(1)}, bf16[384,512]{1,0:T(8,128)(2,1)S(1)}, bf16[160,192]{1,0:T(8,128)(2,1)S(1)}, f32[160,128]{1,0:T(8,128)S(1)...) custom-call(f32[10,16,8,128]{3,2,1,0:T(8,128)S(1)} %bitcast.5, f32[16,135]{1,0:T(8,128)S(1)} %copy-done.1, ...), custom_call_target="tpu_custom_call" | custom-call | flops 1724999936 | bytes 5535000 | tf_op jit(solution)/shard_map/pallas_call | solution.py:777
  13.0 0.0 collective-permute-done.near_twin
  13.0 0.0 collective-permute-done.1.near_other
  13.0 6.1 %shard_map.80 = (f32[5,16,8,128]{3,2,1,0:T(8,128)S(1)}, f32[16,256]{1,0:T(8,128)S(1)}) custom-call(f32[10,16,8,128]{3,2,1,0:T(8,128)S(1)} %bitcast.6, f32[15,16,128]{2,1,0:T(8,128)S(1)} %collective-permute-done.near_twin, f32[15,16,128]{2,1,0:T(8,128)S(1)} %collective-permute-done.1.near_other, f32[16,135]{1,0:T(8,128)S(1)} %copy-done.1, ...), custom_call_target="tpu_custom_call" | custom-call | flops 6325000192 | bytes 20295000 | tf_op jit(solution)/shard_map/pallas_call | solution.py:793
  19.0 0.1 collective-permute-start.2
  19.1 1.8 %shard_map.81.before = f32[5,16,8,128]{3,2,1,0:T(8,128)S(1)} custom-call(f32[10,16,8,128]{3,2,1,0:T(8,128)S(1)} %bitcast.7, s32[3,16,8,128]{3,2,1,0:T(8,128)S(1)} %copy-done, f32[5,16,8,128]{3,2,1,0:T(8,128)S(1)} %get-tuple-element.43.before, f32[5,16,8,128]{3,2,1,0:T(8,128)S(1)} %shard_map.77.order.more, f32[16,256]{1,0:T(8,128)S(1)} %get-tuple-element.42.order), custom_call_target="tpu_custom_call" | custom-call | flops 2184999936 | bytes 7011000 | tf_op jit(solution)/shard_map/pallas_call | solution.py:813
  20.9 0.0 collective-permute-done.2
  21.0 1.4 %collective-permute-start.3 = (f32[16,256]{1,0:T(8,128)S(1)}, f32[16,256]{1,0:T(8,128)S(1)}, u32[]{:S(2)}, u32[]{:S(2)}) collective-permute-start(f32[16,256]{1,0:T(8,128)S(1)} %add.9.order), channel_id=1, source_target_pairs={{0,2},{1,3},{2,0},{3,1},{4,6},{5,7},{6,4},{7,5},{8,10},{9,11},{10,... | collective-permute-start | bytes 49160 | tf_op jit(solution)/shard_map/ppermute | solution.py:807
  22.4 1.8 %shard_map.82.before = f32[5,16,8,128]{3,2,1,0:T(8,128)S(1)} custom-call(f32[10,16,8,128]{3,2,1,0:T(8,128)S(1)} %bitcast.8, s32[3,16,8,128]{3,2,1,0:T(8,128)S(1)} %copy-done, f32[5,16,8,128]{3,2,1,0:T(8,128)S(1)} %shard_map.81.before, f32[5,16,8,128]{3,2,1,0:T(8,128)S(1)} %shard_map.77.order.more, f32[16,256]{1,0:T(8,128)S(1)} %add.9.order), custom_call_target="tpu_custom_call" | custom-call | flops 2184999936 | bytes 7011000 | tf_op jit(solution)/shard_map/pallas_call | solution.py:813
  24.2 0.6 %collective-permute-done.3 = f32[16,256]{1,0:T(8,128)S(1)} collective-permute-done((f32[16,256]{1,0:T(8,128)S(1)}, f32[16,256]{1,0:T(8,128)S(1)}, u32[]{:S(2)}, u32[]{:S(2)}) %collective-permute-start.3) | collective-permute-done | bytes 16416 | tf_op jit(solution)/shard_map/ppermute | solution.py:807
  24.8 0.0 collective-permute-start.4
  24.8 0.0 collective-permute-done.5.far_twin
  24.8 0.0 collective-permute-done.6.far_other
  24.8 1.1 %shard_map.83.rim = f32[640,128]{1,0:T(8,128)S(1)} custom-call(f32[1280,128]{1,0:T(8,128)S(1)} %pad_maximum_fusion.flat, f32[15,16,128]{2,1,0:T(8,128)S(1)} %collective-permute-done.near_twin, f32[15,16,128]{2,1,0:T(8,128)S(1)} %collective-permute-done.1.near_other, f32[28,16,128]{2,1,0:T(8,128)S(1)} %collective-permute-done.5.far_twin, ...), custom_call_target="tpu_custom_call" | custom-call | flops 1264999936 | bytes 4059000 | tf_op jit(solution)/shard_map/pallas_call | solution.py:825
  25.9 2.6 %collective-permute-done.4 = f32[16,256]{1,0:T(8,128)S(1)} collective-permute-done((f32[16,256]{1,0:T(8,128)S(1)}, f32[16,256]{1,0:T(8,128)S(1)}, u32[]{:S(2)}, u32[]{:S(2)}) %collective-permute-start.4) | collective-permute-done | bytes 16416 | tf_op jit(solution)/shard_map/ppermute | solution.py:807
  28.5 1.4 %collective-permute-start.7 = (f32[16,256]{1,0:T(8,128)S(1)}, f32[16,256]{1,0:T(8,128)S(1)}, u32[]{:S(2)}, u32[]{:S(2)}) collective-permute-start(f32[16,256]{1,0:T(8,128)S(1)} %add.11.order.mine), channel_id=1, source_target_pairs={{0,8},{1,9},{2,10},{3,11},{4,12},{5,13},{6,14},{7,15},{8,0},{9,1},... | collective-permute-start | bytes 49160 | tf_op jit(solution)/shard_map/ppermute | solution.py:807
  29.9 3.6 %shard_map.84 = f32[5,16,8,128]{3,2,1,0:T(8,128)} custom-call(f32[10,16,8,128]{3,2,1,0:T(8,128)S(1)} %bitcast.9, s32[3,16,8,128]{3,2,1,0:T(8,128)S(1)} %copy-done, f32[15,16,128]{2,1,0:T(8,128)S(1)} %collective-permute-done.near_twin, f32[15,16,128]{2,1,0:T(8,128)S(1)} %collective-permute-done.1.near_other, ...), custom_call_target="tpu_custom_call" | custom-call | flops 4255000064 | bytes 13653000 | tf_op jit(solution)/shard_map/pallas_call | solution.py:829
  33.5 0.0 collective-permute-done.7.theirs
  33.6 0.7 %shard_map.85 = (f32[16,135]{1,0:T(8,128)}, f32[5,16]{1,0:T(8,128)}) custom-call(f32[16,256]{1,0:T(8,128)S(1)} %add.11.order.mine, f32[16,256]{1,0:T(8,128)S(1)} %collective-permute-done.7.theirs), custom_call_target="tpu_custom_call" | custom-call | flops 575000000 | bytes 1845000 | tf_op jit(solution)/shard_map/pallas_call | solution.py:834
  (4 shorter events, 0.1 us)
Async XLA Ops:
  1.7 6.3 %copy-start = (s32[3,16,8,128]{3,2,1,0:T(8,128)S(1)}, s32[3,16,8,128]{3,2,1,0:T(8,128)}, u32[]{:S(2)}) copy-start(s32[3,16,8,128]{3,2,1,0:T(8,128)} %flags.7) | copy-start | bytes 589828
  1.8 11.1 %collective-permute-start = (f32[15,16,128]{2,1,0:T(8,128)S(1)}, f32[15,16,128]{2,1,0:T(8,128)S(1)}, u32[]{:S(2)}, u32[]{:S(2)}) collective-permute-start(f32[15,16,128]{2,1,0:T(8,128)S(1)} %get-tuple-element.29.order), channel_id=1, source_target_pairs={{0,1},{1,0},{2,3},{3,2},{4,5},{5,4},{6,7},{7,6},{8,9},{9,8},{10,11... | collective-permute-start | bytes 368648 | tf_op jit(solution)/shard_map/ppermute | solution.py:755
  2.3 10.6 %collective-permute-start.1 = (f32[15,16,128]{2,1,0:T(8,128)S(1)}, f32[15,16,128]{2,1,0:T(8,128)S(1)}, u32[]{:S(2)}, u32[]{:S(2)}) collective-permute-start(f32[15,16,128]{2,1,0:T(8,128)S(1)} %get-tuple-element.30.order2), channel_id=1, source_target_pairs={{0,15},{1,2},{2,1},{3,4},{4,3},{5,6},{6,5},{7,8},{8,7},{9,10},{10,... | collective-permute-start | bytes 368648 | tf_op jit(solution)/shard_map/ppermute | solution.py:756
  10.8 1.0 %copy-start.1 = (f32[16,135]{1,0:T(8,128)S(1)}, f32[16,135]{1,0:T(8,128)}, u32[]{:S(2)}) copy-start(f32[16,135]{1,0:T(8,128)} %kernel.3) | copy-start | bytes 25924
  10.8 1.0 %copy-start.2 = (f32[5,16]{1,0:T(8,128)S(1)}, f32[5,16]{1,0:T(8,128)}, u32[]{:S(2)}) copy-start(f32[5,16]{1,0:T(8,128)} %heads.1) | copy-start | bytes 964
  10.9 13.9 %collective-permute-start.5 = (f32[28,16,128]{2,1,0:T(8,128)S(1)}, f32[28,16,128]{2,1,0:T(8,128)S(1)}, u32[]{:S(2)}, u32[]{:S(2)}) collective-permute-start(f32[28,16,128]{2,1,0:T(8,128)S(1)} %get-tuple-element.31.order), channel_id=1, source_target_pairs={{0,1},{1,0},{2,3},{3,2},{4,5},{5,4},{6,7},{7,6},{8,9},{9,8},{10,11... | collective-permute-start | bytes 688136 | tf_op jit(solution)/shard_map/ppermute | solution.py:774
  11.0 13.8 %collective-permute-start.6 = (f32[28,16,128]{2,1,0:T(8,128)S(1)}, f32[28,16,128]{2,1,0:T(8,128)S(1)}, u32[]{:S(2)}, u32[]{:S(2)}) collective-permute-start(f32[28,16,128]{2,1,0:T(8,128)S(1)} %get-tuple-element.32.order2), channel_id=1, source_target_pairs={{0,15},{1,2},{2,1},{3,4},{4,3},{5,6},{6,5},{7,8},{8,7},{9,10},{10,... | collective-permute-start | bytes 688136 | tf_op jit(solution)/shard_map/ppermute | solution.py:775
  19.0 1.9 %collective-permute-start.2 = (f32[16,256]{1,0:T(8,128)S(1)}, f32[16,256]{1,0:T(8,128)S(1)}, u32[]{:S(2)}, u32[]{:S(2)}) collective-permute-start(f32[16,256]{1,0:T(8,128)S(1)} %get-tuple-element.42.order), channel_id=1, source_target_pairs={{0,1},{1,0},{2,3},{3,2},{4,5},{5,4},{6,7},{7,6},{8,9},{9,8},{10,11... | collective-permute-start | bytes 49160 | tf_op jit(solution)/shard_map/ppermute | solution.py:807
  21.0 3.8 %collective-permute-start.3 = (f32[16,256]{1,0:T(8,128)S(1)}, f32[16,256]{1,0:T(8,128)S(1)}, u32[]{:S(2)}, u32[]{:S(2)}) collective-permute-start(f32[16,256]{1,0:T(8,128)S(1)} %add.9.order), channel_id=1, source_target_pairs={{0,2},{1,3},{2,0},{3,1},{4,6},{5,7},{6,4},{7,5},{8,10},{9,11},{10,... | collective-permute-start | bytes 49160 | tf_op jit(solution)/shard_map/ppermute | solution.py:807
  24.8 3.7 %collective-permute-start.4 = (f32[16,256]{1,0:T(8,128)S(1)}, f32[16,256]{1,0:T(8,128)S(1)}, u32[]{:S(2)}, u32[]{:S(2)}) collective-permute-start(f32[16,256]{1,0:T(8,128)S(1)} %add.10.order), channel_id=1, source_target_pairs={{0,4},{1,5},{2,6},{3,7},{4,0},{5,1},{6,2},{7,3},{8,12},{9,13},{10,... | collective-permute-start | bytes 49160 | tf_op jit(solution)/shard_map/ppermute | solution.py:807
  28.5 5.0 %collective-permute-start.7 = (f32[16,256]{1,0:T(8,128)S(1)}, f32[16,256]{1,0:T(8,128)S(1)}, u32[]{:S(2)}, u32[]{:S(2)}) collective-permute-start(f32[16,256]{1,0:T(8,128)S(1)} %add.11.order.mine), channel_id=1, source_target_pairs={{0,8},{1,9},{2,10},{3,11},{4,12},{5,13},{6,14},{7,15},{8,0},{9,1},... | collective-permute-start | bytes 49160 | tf_op jit(solution)/shard_map/ppermute | solution.py:807

commit v9 on v8

--- a/solution.py
+++ b/solution.py
@@ -287,31 +287,21 @@
         out[v] = acc[v, pl.ds(2, nx)]
 
 
-def z_kernel(half, fields, flags, before, more, order, out):
-    del order
-    state, cot = views(fields)
-    nx = state.shape[1] // 2
-    for v in range(5):
-        kept = pl.ds((1 - half) * nx, nx)
-        out[v, kept] = before[v, kept]
-
-    def z_step(i, carry):
-        x = half * nx + i * SLABS
-        cells, face = [], []
-        for v in range(5):
-            mid = state[v, pl.ds(x, SLABS)]
-            cells.append([mid if k == 0 else pltpu.roll(mid, (-k) % 128, 2) for k in range(-2, 4)])
-            g = cot[v, pl.ds(x, SLABS)]
-            face.append(STEP * (pltpu.roll(g, 127, 2) - g))
-        terms = face_pull(cells, face, flags[2, pl.ds(x, SLABS)], 2)
-        for v in range(5):
-            t = before[v, pl.ds(x, SLABS)] + more[v, pl.ds(x, SLABS)] + terms[v][2]
-            for k in (-2, -1, 1, 2, 3):
-                t = t + pltpu.roll(terms[v][k + 2], k % 128, 2)
-            out[v, pl.ds(x, SLABS)] = t
-        return carry
-
-    lax.fori_loop(0, nx // SLABS, z_step, 0)
+def z_faces(state, cot, flags, x):
+    cells, face = [], []
+    for v in range(5):
+        mid = state[v, pl.ds(x, SLABS)]
+        cells.append([mid if k == 0 else pltpu.roll(mid, (-k) % 128, 2) for k in range(-2, 4)])
+        g = cot[v, pl.ds(x, SLABS)]
+        face.append(STEP * (pltpu.roll(g, 127, 2) - g))
+    terms = face_pull(cells, face, flags[2, pl.ds(x, SLABS)], 2)
+    total = []
+    for v in range(5):
+        t = terms[v][2]
+        for k in (-2, -1, 1, 2, 3):
+            t = t + pltpu.roll(terms[v][k + 2], k % 128, 2)
+        total.append(t)
+    return total
 
 
 def e_kernel(flat, near_twin, near_other, far_twin, far_other, order, out):
@@ -347,12 +337,16 @@
             out[pl.ds(v * nx * 8 + row, nx, stride=8), :] = value
 
 
-def y_kernel(fields, flags, near_twin, near_other, far_twin, far_other, before, rim, order, out, halo, ghalo):
+def y_kernel(half, fields, flags, near_twin, near_other, far_twin, far_other, before, rim, order, out, halo, ghalo):
     del order
     state, cot = views(fields)
     rims = from_rims(near_twin, near_other, far_twin, far_other)
     rim_state, rim_cot, _ = rims
     nx = out.shape[1]
+    part = nx // 2
+    for v in range(5):
+        kept = pl.ds((1 - half) * part, part)
+        out[v, kept] = before[v, kept]
     for v in range(5):
         base = v * nx * 8
         for r in range(ABOVE):
@@ -366,7 +360,7 @@
         inside[k] = (row < 8 + k) if k < 0 else (row >= k)
 
     def step(i, carry):
-        x = i * SLABS
+        x = half * part + i * SLABS
         cells, face = [], []
         for v in range(5):
             at = pl.multiple_of((v * nx + x) * 8, 8)
@@ -393,7 +387,7 @@
             out[v, pl.ds(x, SLABS)] = total
         return carry
 
-    lax.fori_loop(0, nx // SLABS, step, 0)
+    lax.fori_loop(0, part // SLABS, step, 0)
 
 
 def sum_kernel(scale, mine, theirs, k_out, h_out):
@@ -528,11 +522,11 @@
 
 
 def c_kernel(
-    fields, near_twin, near_other, kernel, w_rows, w_cols, w_head, bias, t, t_low,
+    fields, flags, near_twin, near_other, kernel, w_rows, w_cols, w_head, bias, t, t_low, before,
     own, parts,
     rim, rim_low, outer, outer_low, acc, edge, gedge,
 ):
-    _, cot = views(fields)
+    state, cot = views(fields)
     nx = cot.shape[1]
     ch, taps = kernel.shape
     rim_state, rim_cot, _ = from_rims(near_twin, near_other)
@@ -581,6 +575,10 @@
             jnp.concatenate([s_lo, far_lo], axis=0),
             preferred_element_type=F32,
         )
+        for here in range(x, x + WIDE, SLABS):
+            faces = z_faces(state, cot, flags, here)
+            for v in range(5):
+                own[v, pl.ds(here, SLABS)] = before[v, pl.ds(here, SLABS)] + faces[v]
         z = z2[:rows] + (z2[rows:] + z3) + jnp.concatenate([bias[...]] * WIDE, axis=1)
         hidden = jnp.tanh(z)
         g = jnp.concatenate(
@@ -638,7 +636,7 @@
             + pltpu.roll(acc[pl.ds(at + 80, 40), :], 1, 1)
         )
         for v in range(5):
-            own[v, x] = total[8 * v : 8 * v + 8]
+            own[v, x] = own[v, x] + total[8 * v : 8 * v + 8]
 
     sums = jnp.sum(dsum, axis=1, keepdims=True)
     kg = kg.T
@@ -799,9 +797,9 @@
             vm((2 * RIM * nx, nz), F32),
             vm((16 * nx, nz), F32),
         ],
-        5.5,
-        10,
-    )(fields, *near_rims, kernel, *prepared, patches, patches_low)
+        8.0,
+        12,
+    )(fields, flags, *near_rims, kernel, *prepared, patches, patches_low, first)
 
     def exchanged(value, bit):
         return lax.ppermute(value, "gy", [(i, i ^ bit) for i in range(count)])
@@ -810,25 +808,20 @@
     sums = parts
     for bit in bits[:-4]:
         sums = sums + exchanged(sums, bit)
-    z_half = lambda half, before, order: call(
-        functools.partial(z_kernel, half), full, [], 1.9, 4, 1
-    )(fields, flags, before, first, order)
-    got = exchanged(sums, bits[-4])
-    total = z_half(0, own, sums)
-    got, total = lax.optimization_barrier((got, total))
-    sums = sums + got
+    y_half = lambda half, before, order: call(
+        functools.partial(y_kernel, half), full, [vm((lines, nz), F32)] * 2, 1.9, 8, 1
+    )(fields, flags, *near_rims, *far_rims, before, rim, order)
+    sums = sums + exchanged(sums, bits[-4])
     got = exchanged(sums, bits[-3])
-    total = z_half(1, total, sums)
-    got, total = lax.optimization_barrier((got, total))
-    sums = sums + got
-    got = exchanged(sums, bits[-2])
     rim = call(e_kernel, shape(lines, nz), [], 1.1, 5, 1)(flat, *near_rims, *far_rims, sums)
     got, rim = lax.optimization_barrier((got, rim))
     sums = sums + got
+    got = exchanged(sums, bits[-2])
+    total = y_half(0, own, sums)
+    got, total = lax.optimization_barrier((got, total))
+    sums = sums + got
     got = exchanged(sums, bits[-1])
-    flow = call(y_kernel, full, [vm((lines, nz), F32)] * 2, 3.7, 8, 1)(
-        fields, flags, *near_rims, *far_rims, total, rim, sums
-    )
+    flow = y_half(1, total, sums)
     got, flow = lax.optimization_barrier((got, flow))
     scale = float(cells * count) ** (-0.5)
     k_out, h_out = call(

time: 34.4 us -> 34.8 us (1.012)
  waiting for transfers between devices: 3.19 us -> 6.3 us
  Pallas kernels: 19.3 us -> 17.2 us
  starting transfers between devices: 9.91 us -> 9.31 us
    pallas_call x3 -> x2, Pallas kernels: 7.28 us -> 3.68 us  [body(): call(functools.partial(y_kernel, half), full, [vm((lines, nz), F32)] * 2,...]
    ppermute x4, waiting for transfers between devices: 3.18 us -> 6.29 us  [exchanged(): return lax.ppermute(value, 'gy', [(i, i ^ bit) for i in range(count)])]
    pallas_call x1, Pallas kernels: 6.06 us -> 7.59 us  [body(): call(c_kernel, (full, shape(ch, 256)), [*[vm(((nx + 2) * 3 * RIM, nz), BF...]
    ppermute x4, starting transfers between devices: 2.87 us -> 2.27 us  [exchanged(): return lax.ppermute(value, 'gy', [(i, i ^ bit) for i in range(count)])]
  transfers between devices with their start and end apart: 8 -> 8, of which waited for: 2 -> 4; matrix products, arithmetic and copies ran while one was open for 0% -> 0% of each run, Pallas kernels for 54% -> 47%
where the time goes in v9:
time: 34.8 us; the launch traced here: 34.7 us
  Pallas kernels  17.2 us (49%)
  starting transfers between devices  9.31 us (27%)
  waiting for transfers between devices  6.3 us (18%)
  other arithmetic  1.13 us (3%)
  between operations  0.74 us (2%)
    pallas_call x1, Pallas kernels, body(): call(c_kernel, (full, shape(ch, 256)), [*[vm(((nx + 2) * 3 * RIM, nz), BF...  7.59 us
    ppermute x4, waiting for transfers between devices, exchanged(): return lax.ppermute(value, 'gy', [(i, i ^ bit) for i in range(count)])  6.29 us
    ppermute x1, starting transfers between devices, body(): lax.ppermute(near_other, 'gy', with_other)  5.67 us
    pallas_call x2, Pallas kernels, body(): call(functools.partial(y_kernel, half), full, [vm((lines, nz), F32)] * 2,...  3.68 us
    pallas_call x1, Pallas kernels, body(): call(x_kernel, full, [vm((5, nx + 5, ny, nz), F32), vm((5, nx + 1, ny, nz...  2.78 us
    ppermute x4, starting transfers between devices, exchanged(): return lax.ppermute(value, 'gy', [(i, i ^ bit) for i in range(count)])  2.27 us
    pallas_call x1, Pallas kernels, body(): call(prepare_kernel, (half_shape(20 * ch, COLUMNS), half_shape(384, 512),...  1.19 us
    concatenate x1, other arithmetic, body(): flat = jnp.concatenate([state.reshape(lines, nz), cot.reshape(lines, nz)])  1.12 us
  transfers between devices with their start and end apart: 8, of which 4 were waited for; matrix products, arithmetic and copies ran while one was open for 0% of the time, Pallas kernels for 47%

profile of v9, /device:TPU:0, one launch (start us, length us, event | category | flops | bytes accessed | tf_op | source)
XLA Modules:
  0.0 34.7 jit_solution(13436145412909288540)
XLA Ops:
  0.6 1.1 %pad_maximum_fusion.flat = f32[1280,128]{1,0:T(8,128)S(1)} fusion(f32[640,128]{1,0:T(8,128)} %bitcast.10, f32[640,128]{1,0:T(8,128)} %bitcast.11), kind=kLoop, calls=%fused_computation | loop fusion | flops 163840 | bytes 1310720 | tf_op jit(solution)/shard_map/concatenate | solution.py:748
  1.7 0.0 copy-start
  1.8 0.5 %collective-permute-start = (f32[15,16,128]{2,1,0:T(8,128)S(1)}, f32[15,16,128]{2,1,0:T(8,128)S(1)}, u32[]{:S(2)}, u32[]{:S(2)}) collective-permute-start(f32[15,16,128]{2,1,0:T(8,128)S(1)} %get-tuple-element.27.order), channel_id=1, source_target_pairs={{0,1},{1,0},{2,3},{3,2},{4,5},{5,4},{6,7},{7,6},{8,9},{9,8},{10,11... | collective-permute-start | bytes 368648 | tf_op jit(solution)/shard_map/ppermute | solution.py:753
  2.3 5.7 %collective-permute-start.1 = (f32[15,16,128]{2,1,0:T(8,128)S(1)}, f32[15,16,128]{2,1,0:T(8,128)S(1)}, u32[]{:S(2)}, u32[]{:S(2)}) collective-permute-start(f32[15,16,128]{2,1,0:T(8,128)S(1)} %get-tuple-element.28.order2), channel_id=1, source_target_pairs={{0,15},{1,2},{2,1},{3,4},{4,3},{5,6},{6,5},{7,8},{8,7},{9,10},{10,... | collective-permute-start | bytes 368648 | tf_op jit(solution)/shard_map/ppermute | solution.py:754
  8.0 0.0 copy-done
  8.0 2.8 %shard_map.77.order.before = f32[5,16,8,128]{3,2,1,0:T(8,128)S(1)} custom-call(f32[10,16,8,128]{3,2,1,0:T(8,128)S(1)} %bitcast.4, s32[3,16,8,128]{3,2,1,0:T(8,128)S(1)} %copy-done, f32[15,16,128]{2,1,0:T(8,128)S(1)} %get-tuple-element.27.order, f32[15,16,128]{2,1,0:T(8,128)S(1)} %get-tuple-element.28.order2), custom_call_target="tpu_custom_call" | custom-call | flops 3220000000 | bytes 10332000 | tf_op jit(solution)/shard_map/pallas_call | solution.py:756
  10.8 0.0 copy-start.1
  10.8 0.0 copy-start.2
  10.8 0.1 shard_map.78
  10.9 0.1 collective-permute-start.4
  11.0 0.8 %collective-permute-start.5 = (f32[28,16,128]{2,1,0:T(8,128)S(1)}, f32[28,16,128]{2,1,0:T(8,128)S(1)}, u32[]{:S(2)}, u32[]{:S(2)}) collective-permute-start(f32[28,16,128]{2,1,0:T(8,128)S(1)} %get-tuple-element.30.order2), channel_id=1, source_target_pairs={{0,15},{1,2},{2,1},{3,4},{4,3},{5,6},{6,5},{7,8},{8,7},{9,10},{10,... | collective-permute-start | bytes 688136 | tf_op jit(solution)/shard_map/ppermute | solution.py:773
  11.8 0.0 copy-done.1
  11.8 0.0 copy-done.2
  11.8 1.2 %shard_map.79 = (bf16[320,720]{1,0:T(8,128)(2,1)S(1)}, bf16[384,512]{1,0:T(8,128)(2,1)S(1)}, bf16[160,192]{1,0:T(8,128)(2,1)S(1)}, f32[160,128]{1,0:T(8,128)S(1)...) custom-call(f32[10,16,8,128]{3,2,1,0:T(8,128)S(1)} %bitcast.5, f32[16,135]{1,0:T(8,128)S(1)} %copy-done.1, ...), custom_call_target="tpu_custom_call" | custom-call | flops 1724999936 | bytes 5535000 | tf_op jit(solution)/shard_map/pallas_call | solution.py:775
  13.0 0.0 collective-permute-done.near_twin
  13.0 0.0 collective-permute-done.1.near_other
  13.0 7.6 %shard_map.80 = (f32[5,16,8,128]{3,2,1,0:T(8,128)S(1)}, f32[16,256]{1,0:T(8,128)S(1)}) custom-call(f32[10,16,8,128]{3,2,1,0:T(8,128)S(1)} %bitcast.6, s32[3,16,8,128]{3,2,1,0:T(8,128)S(1)} %copy-done, f32[15,16,128]{2,1,0:T(8,128)S(1)} %collective-permute-done.near_twin, f32[15,16,128]{2,1,0:T(8,128)S(1)} %collective-permute-done.1.near_other, ...), custom_call_target="tpu_custom_call" | custom-call | flops 9200000000 | bytes 29520000 | tf_op jit(solution)/shard_map/pallas_call | solution.py:791
  20.6 0.1 collective-permute-start.2
  20.6 1.2 %collective-permute-done.2 = f32[16,256]{1,0:T(8,128)S(1)} collective-permute-done((f32[16,256]{1,0:T(8,128)S(1)}, f32[16,256]{1,0:T(8,128)S(1)}, u32[]{:S(2)}, u32[]{:S(2)}) %collective-permute-start.2) | collective-permute-done | bytes 16416 | tf_op jit(solution)/shard_map/ppermute | solution.py:805
  21.8 1.4 %collective-permute-start.3 = (f32[16,256]{1,0:T(8,128)S(1)}, f32[16,256]{1,0:T(8,128)S(1)}, u32[]{:S(2)}, u32[]{:S(2)}) collective-permute-start(f32[16,256]{1,0:T(8,128)S(1)} %add.9.order), channel_id=1, source_target_pairs={{0,2},{1,3},{2,0},{3,1},{4,6},{5,7},{6,4},{7,5},{8,10},{9,11},{10,... | collective-permute-start | bytes 49160 | tf_op jit(solution)/shard_map/ppermute | solution.py:805
  23.2 0.0 collective-permute-done.4.far_twin
  23.2 0.0 collective-permute-done.5.far_other
  23.2 1.1 %shard_map.81.rim = f32[640,128]{1,0:T(8,128)S(1)} custom-call(f32[1280,128]{1,0:T(8,128)S(1)} %pad_maximum_fusion.flat, f32[15,16,128]{2,1,0:T(8,128)S(1)} %collective-permute-done.near_twin, f32[15,16,128]{2,1,0:T(8,128)S(1)} %collective-permute-done.1.near_other, f32[28,16,128]{2,1,0:T(8,128)S(1)} %collective-permute-done.4.far_twin, ...), custom_call_target="tpu_custom_call" | custom-call | flops 1264999936 | bytes 4059000 | tf_op jit(solution)/shard_map/pallas_call | solution.py:816
  24.3 1.3 %collective-permute-done.3 = f32[16,256]{1,0:T(8,128)S(1)} collective-permute-done((f32[16,256]{1,0:T(8,128)S(1)}, f32[16,256]{1,0:T(8,128)S(1)}, u32[]{:S(2)}, u32[]{:S(2)}) %collective-permute-start.3) | collective-permute-done | bytes 16416 | tf_op jit(solution)/shard_map/ppermute | solution.py:805
  25.6 0.0 collective-permute-start.6
  25.6 1.5 %shard_map.82.before = f32[5,16,8,128]{3,2,1,0:T(8,128)S(1)} custom-call(f32[10,16,8,128]{3,2,1,0:T(8,128)S(1)} %bitcast.7, s32[3,16,8,128]{3,2,1,0:T(8,128)S(1)} %copy-done, f32[15,16,128]{2,1,0:T(8,128)S(1)} %collective-permute-done.near_twin, f32[15,16,128]{2,1,0:T(8,128)S(1)} %collective-permute-done.1.near_other, ...), custom_call_target="tpu_custom_call" | custom-call | flops 2184999936 | bytes 7011000 | tf_op jit(solution)/shard_map/pallas_call | solution.py:811
  27.1 2.2 %collective-permute-done.6 = f32[16,256]{1,0:T(8,128)S(1)} collective-permute-done((f32[16,256]{1,0:T(8,128)S(1)}, f32[16,256]{1,0:T(8,128)S(1)}, u32[]{:S(2)}, u32[]{:S(2)}) %collective-permute-start.6) | collective-permute-done | bytes 16416 | tf_op jit(solution)/shard_map/ppermute | solution.py:805
  29.3 0.9 %collective-permute-start.7 = (f32[16,256]{1,0:T(8,128)S(1)}, f32[16,256]{1,0:T(8,128)S(1)}, u32[]{:S(2)}, u32[]{:S(2)}) collective-permute-start(f32[16,256]{1,0:T(8,128)S(1)} %add.11.order.mine), channel_id=1, source_target_pairs={{0,8},{1,9},{2,10},{3,11},{4,12},{5,13},{6,14},{7,15},{8,0},{9,1},... | collective-permute-start | bytes 49160 | tf_op jit(solution)/shard_map/ppermute | solution.py:805
  30.2 2.2 %shard_map.83 = f32[5,16,8,128]{3,2,1,0:T(8,128)} custom-call(f32[10,16,8,128]{3,2,1,0:T(8,128)S(1)} %bitcast.8, s32[3,16,8,128]{3,2,1,0:T(8,128)S(1)} %copy-done, f32[15,16,128]{2,1,0:T(8,128)S(1)} %collective-permute-done.near_twin, f32[15,16,128]{2,1,0:T(8,128)S(1)} %collective-permute-done.1.near_other, ...), custom_call_target="tpu_custom_call" | custom-call | flops 2184999936 | bytes 7011000 | tf_op jit(solution)/shard_map/pallas_call | solution.py:811
  32.4 1.6 %collective-permute-done.7.theirs = f32[16,256]{1,0:T(8,128)S(1)} collective-permute-done((f32[16,256]{1,0:T(8,128)S(1)}, f32[16,256]{1,0:T(8,128)S(1)}, u32[]{:S(2)}, u32[]{:S(2)}) %collective-permute-start.7) | collective-permute-done | bytes 16416 | tf_op jit(solution)/shard_map/ppermute | solution.py:805
  33.9 0.7 %shard_map.84 = (f32[16,135]{1,0:T(8,128)}, f32[5,16]{1,0:T(8,128)}) custom-call(f32[16,256]{1,0:T(8,128)S(1)} %add.11.order.mine, f32[16,256]{1,0:T(8,128)S(1)} %collective-permute-done.7.theirs), custom_call_target="tpu_custom_call" | custom-call | flops 575000000 | bytes 1845000 | tf_op jit(solution)/shard_map/pallas_call | solution.py:827
  (4 shorter events, 0.1 us)
Async XLA Ops:
  1.7 6.3 %copy-start = (s32[3,16,8,128]{3,2,1,0:T(8,128)S(1)}, s32[3,16,8,128]{3,2,1,0:T(8,128)}, u32[]{:S(2)}) copy-start(s32[3,16,8,128]{3,2,1,0:T(8,128)} %flags.7) | copy-start | bytes 589828
  1.8 11.1 %collective-permute-start = (f32[15,16,128]{2,1,0:T(8,128)S(1)}, f32[15,16,128]{2,1,0:T(8,128)S(1)}, u32[]{:S(2)}, u32[]{:S(2)}) collective-permute-start(f32[15,16,128]{2,1,0:T(8,128)S(1)} %get-tuple-element.27.order), channel_id=1, source_target_pairs={{0,1},{1,0},{2,3},{3,2},{4,5},{5,4},{6,7},{7,6},{8,9},{9,8},{10,11... | collective-permute-start | bytes 368648 | tf_op jit(solution)/shard_map/ppermute | solution.py:753
  2.3 10.6 %collective-permute-start.1 = (f32[15,16,128]{2,1,0:T(8,128)S(1)}, f32[15,16,128]{2,1,0:T(8,128)S(1)}, u32[]{:S(2)}, u32[]{:S(2)}) collective-permute-start(f32[15,16,128]{2,1,0:T(8,128)S(1)} %get-tuple-element.28.order2), channel_id=1, source_target_pairs={{0,15},{1,2},{2,1},{3,4},{4,3},{5,6},{6,5},{7,8},{8,7},{9,10},{10,... | collective-permute-start | bytes 368648 | tf_op jit(solution)/shard_map/ppermute | solution.py:754
  10.8 1.0 %copy-start.1 = (f32[16,135]{1,0:T(8,128)S(1)}, f32[16,135]{1,0:T(8,128)}, u32[]{:S(2)}) copy-start(f32[16,135]{1,0:T(8,128)} %kernel.3) | copy-start | bytes 25924
  10.8 1.0 %copy-start.2 = (f32[5,16]{1,0:T(8,128)S(1)}, f32[5,16]{1,0:T(8,128)}, u32[]{:S(2)}) copy-start(f32[5,16]{1,0:T(8,128)} %heads.1) | copy-start | bytes 964
  10.9 12.3 %collective-permute-start.4 = (f32[28,16,128]{2,1,0:T(8,128)S(1)}, f32[28,16,128]{2,1,0:T(8,128)S(1)}, u32[]{:S(2)}, u32[]{:S(2)}) collective-permute-start(f32[28,16,128]{2,1,0:T(8,128)S(1)} %get-tuple-element.29.order), channel_id=1, source_target_pairs={{0,1},{1,0},{2,3},{3,2},{4,5},{5,4},{6,7},{7,6},{8,9},{9,8},{10,11... | collective-permute-start | bytes 688136 | tf_op jit(solution)/shard_map/ppermute | solution.py:772
  11.0 12.2 %collective-permute-start.5 = (f32[28,16,128]{2,1,0:T(8,128)S(1)}, f32[28,16,128]{2,1,0:T(8,128)S(1)}, u32[]{:S(2)}, u32[]{:S(2)}) collective-permute-start(f32[28,16,128]{2,1,0:T(8,128)S(1)} %get-tuple-element.30.order2), channel_id=1, source_target_pairs={{0,15},{1,2},{2,1},{3,4},{4,3},{5,6},{6,5},{7,8},{8,7},{9,10},{10,... | collective-permute-start | bytes 688136 | tf_op jit(solution)/shard_map/ppermute | solution.py:773
  20.6 1.2 %collective-permute-start.2 = (f32[16,256]{1,0:T(8,128)S(1)}, f32[16,256]{1,0:T(8,128)S(1)}, u32[]{:S(2)}, u32[]{:S(2)}) collective-permute-start(f32[16,256]{1,0:T(8,128)S(1)} %get-tuple-element.41), channel_id=1, source_target_pairs={{0,1},{1,0},{2,3},{3,2},{4,5},{5,4},{6,7},{7,6},{8,9},{9,8},{10,11... | collective-permute-start | bytes 49160 | tf_op jit(solution)/shard_map/ppermute | solution.py:805
  21.8 3.7 %collective-permute-start.3 = (f32[16,256]{1,0:T(8,128)S(1)}, f32[16,256]{1,0:T(8,128)S(1)}, u32[]{:S(2)}, u32[]{:S(2)}) collective-permute-start(f32[16,256]{1,0:T(8,128)S(1)} %add.9.order), channel_id=1, source_target_pairs={{0,2},{1,3},{2,0},{3,1},{4,6},{5,7},{6,4},{7,5},{8,10},{9,11},{10,... | collective-permute-start | bytes 49160 | tf_op jit(solution)/shard_map/ppermute | solution.py:805
  25.6 3.7 %collective-permute-start.6 = (f32[16,256]{1,0:T(8,128)S(1)}, f32[16,256]{1,0:T(8,128)S(1)}, u32[]{:S(2)}, u32[]{:S(2)}) collective-permute-start(f32[16,256]{1,0:T(8,128)S(1)} %add.10.order), channel_id=1, source_target_pairs={{0,4},{1,5},{2,6},{3,7},{4,0},{5,1},{6,2},{7,3},{8,12},{9,13},{10,... | collective-permute-start | bytes 49160 | tf_op jit(solution)/shard_map/ppermute | solution.py:805
  29.3 4.6 %collective-permute-start.7 = (f32[16,256]{1,0:T(8,128)S(1)}, f32[16,256]{1,0:T(8,128)S(1)}, u32[]{:S(2)}, u32[]{:S(2)}) collective-permute-start(f32[16,256]{1,0:T(8,128)S(1)} %add.11.order.mine), channel_id=1, source_target_pairs={{0,8},{1,9},{2,10},{3,11},{4,12},{5,13},{6,14},{7,15},{8,0},{9,1},... | collective-permute-start | bytes 49160 | tf_op jit(solution)/shard_map/ppermute | solution.py:805

commit v10 on v9

--- a/solution.py
+++ b/solution.py
@@ -248,8 +248,8 @@
     return state, cot, flags
 
 
-def x_kernel(fields, flags, order, order2, out, pad, gpad, acc):
-    del order, order2
+def x_kernel(fields, flags, before, order, out, pad, gpad, acc):
+    del order
     state, cot = views(fields)
     nx = state.shape[1]
     for v in range(5):
@@ -284,7 +284,7 @@
         acc[v, pl.ds(2, 3)] = acc[v, pl.ds(2, 3)] + acc[v, pl.ds(nx + 2, 3)]
 
     for v in range(5):
-        out[v] = acc[v, pl.ds(2, nx)]
+        out[v] = acc[v, pl.ds(2, nx)] + before[v]
 
 
 def z_faces(state, cot, flags, x):
@@ -337,7 +337,7 @@
             out[pl.ds(v * nx * 8 + row, nx, stride=8), :] = value
 
 
-def y_kernel(half, fields, flags, near_twin, near_other, far_twin, far_other, before, rim, order, out, halo, ghalo):
+def yz_kernel(half, fields, flags, near_twin, near_other, far_twin, far_other, before, rim, order, out, halo, ghalo):
     del order
     state, cot = views(fields)
     rims = from_rims(near_twin, near_other, far_twin, far_other)
@@ -377,9 +377,10 @@
             g_rim = ghalo[pl.ds(at, 8 * SLABS), :].reshape(SLABS, 8, 128)
             face.append(STEP * (pltpu.roll(jnp.where(inside[1], g, g_rim), 7, 1) - g))
         terms = face_pull(cells, face, flags[1, pl.ds(x, SLABS)], 1)
+        along_z = z_faces(state, cot, flags, x)
         for v in range(5):
             at = pl.multiple_of((v * nx + x) * 8, 8)
-            total = before[v, pl.ds(x, SLABS)] + terms[v][2]
+            total = before[v, pl.ds(x, SLABS)] + along_z[v] + terms[v][2]
             total = total + rim[pl.ds(at, 8 * SLABS), :].reshape(SLABS, 8, 128)
             for k in (-2, -1, 1, 2, 3):
                 moved = pltpu.roll(terms[v][k + 2], k % 8, 1)
@@ -522,11 +523,11 @@
 
 
 def c_kernel(
-    fields, flags, near_twin, near_other, kernel, w_rows, w_cols, w_head, bias, t, t_low, before,
+    fields, near_twin, near_other, kernel, w_rows, w_cols, w_head, bias, t, t_low,
     own, parts,
     rim, rim_low, outer, outer_low, acc, edge, gedge,
 ):
-    state, cot = views(fields)
+    _, cot = views(fields)
     nx = cot.shape[1]
     ch, taps = kernel.shape
     rim_state, rim_cot, _ = from_rims(near_twin, near_other)
@@ -575,10 +576,6 @@
             jnp.concatenate([s_lo, far_lo], axis=0),
             preferred_element_type=F32,
         )
-        for here in range(x, x + WIDE, SLABS):
-            faces = z_faces(state, cot, flags, here)
-            for v in range(5):
-                own[v, pl.ds(here, SLABS)] = before[v, pl.ds(here, SLABS)] + faces[v]
         z = z2[:rows] + (z2[rows:] + z3) + jnp.concatenate([bias[...]] * WIDE, axis=1)
         hidden = jnp.tanh(z)
         g = jnp.concatenate(
@@ -636,7 +633,7 @@
             + pltpu.roll(acc[pl.ds(at + 80, 40), :], 1, 1)
         )
         for v in range(5):
-            own[v, x] = own[v, x] + total[8 * v : 8 * v + 8]
+            own[v, x] = total[8 * v : 8 * v + 8]
 
     sums = jnp.sum(dsum, axis=1, keepdims=True)
     kg = kg.T
@@ -753,25 +750,6 @@
         lax.ppermute(near_twin, "gy", with_twin),
         lax.ppermute(near_other, "gy", with_other),
     )
-    first = call(
-        x_kernel,
-        full,
-        [
-            vm((5, nx + 5, ny, nz), F32),
-            vm((5, nx + 1, ny, nz), F32),
-            vm((5, nx + 5, ny, nz), F32),
-        ],
-        2.8,
-        2,
-        2,
-    )(fields, flags, near_twin, near_other)
-    far_twin, far_other = call(far_kernel, (far, far), [], 0.2, 2, 1)(
-        flat, flags.reshape(3 * nx * ny, nz), first
-    )
-    far_rims = (
-        lax.ppermute(far_twin, "gy", with_twin),
-        lax.ppermute(far_other, "gy", with_other),
-    )
     *prepared, patches, patches_low = call(
         prepare_kernel,
         (
@@ -786,8 +764,15 @@
         1.5,
         3,
         2,
-    )(fields, kernel, heads, far_twin, far_other)
-    near_rims, patches, first = lax.optimization_barrier((near_rims, patches, first))
+    )(fields, kernel, heads, near_twin, near_other)
+    far_twin, far_other = call(far_kernel, (far, far), [], 0.2, 2, 1)(
+        flat, flags.reshape(3 * nx * ny, nz), patches
+    )
+    far_rims = (
+        lax.ppermute(far_twin, "gy", with_twin),
+        lax.ppermute(far_other, "gy", with_other),
+    )
+    near_rims, patches = lax.optimization_barrier((near_rims, patches))
     own, parts = call(
         c_kernel,
         (full, shape(ch, 256)),
@@ -797,9 +782,9 @@
             vm((2 * RIM * nx, nz), F32),
             vm((16 * nx, nz), F32),
         ],
-        8.0,
-        12,
-    )(fields, flags, *near_rims, kernel, *prepared, patches, patches_low, first)
+        6.0,
+        10,
+    )(fields, *near_rims, kernel, *prepared, patches, patches_low)
 
     def exchanged(value, bit):
         return lax.ppermute(value, "gy", [(i, i ^ bit) for i in range(count)])
@@ -808,20 +793,34 @@
     sums = parts
     for bit in bits[:-4]:
         sums = sums + exchanged(sums, bit)
-    y_half = lambda half, before, order: call(
-        functools.partial(y_kernel, half), full, [vm((lines, nz), F32)] * 2, 1.9, 8, 1
+    yz_half = lambda half, before, order: call(
+        functools.partial(yz_kernel, half), full, [vm((lines, nz), F32)] * 2, 3.3, 8, 1
     )(fields, flags, *near_rims, *far_rims, before, rim, order)
-    sums = sums + exchanged(sums, bits[-4])
-    got = exchanged(sums, bits[-3])
+    got = exchanged(sums, bits[-4])
     rim = call(e_kernel, shape(lines, nz), [], 1.1, 5, 1)(flat, *near_rims, *far_rims, sums)
     got, rim = lax.optimization_barrier((got, rim))
     sums = sums + got
+    got = exchanged(sums, bits[-3])
+    total = call(
+        x_kernel,
+        full,
+        [
+            vm((5, nx + 5, ny, nz), F32),
+            vm((5, nx + 1, ny, nz), F32),
+            vm((5, nx + 5, ny, nz), F32),
+        ],
+        2.8,
+        3,
+        1,
+    )(fields, flags, own, sums)
+    got, total = lax.optimization_barrier((got, total))
+    sums = sums + got
     got = exchanged(sums, bits[-2])
-    total = y_half(0, own, sums)
+    total = yz_half(0, total, sums)
     got, total = lax.optimization_barrier((got, total))
     sums = sums + got
     got = exchanged(sums, bits[-1])
-    flow = y_half(1, total, sums)
+    flow = yz_half(1, total, sums)
     got, flow = lax.optimization_barrier((got, flow))
     scale = float(cells * count) ** (-0.5)
     k_out, h_out = call(

time: 34.8 us -> 34.1 us (0.980)
  waiting for transfers between devices: 6.3 us -> 3.52 us
  Pallas kernels: 17.2 us -> 18.2 us
  starting transfers between devices: 9.31 us -> 10.3 us
    ppermute x4, waiting for transfers between devices: 6.29 us -> 1.88 us  [exchanged(): return lax.ppermute(value, 'gy', [(i, i ^ bit) for i in range(count)])]
    pallas_call x2, Pallas kernels: 3.68 us -> 6.27 us  [body(): call(functools.partial(yz_kernel, half), full, [vm((lines, nz), F32)] * 2...]
    pallas_call x1, Pallas kernels: 7.59 us -> 6 us  [body(): call(c_kernel, (full, shape(ch, 256)), [*[vm(((nx + 2) * 3 * RIM, nz), BF...]
    ppermute x4, starting transfers between devices: 2.27 us -> 3.4 us  [exchanged(): return lax.ppermute(value, 'gy', [(i, i ^ bit) for i in range(count)])]
    ppermute x1, waiting for transfers between devices: 0.01 us -> 1.05 us  [body(): lax.ppermute(far_other, 'gy', with_other)]
    ppermute x1, waiting for transfers between devices: 0.01 us -> 0.58 us  [body(): lax.ppermute(near_other, 'gy', with_other)]
  transfers between devices with their start and end apart: 8 -> 8, of which waited for: 4 -> 4; matrix products, arithmetic and copies ran while one was open for 0% -> 0% of each run, Pallas kernels for 47% -> 51%
where the time goes in v10:
time: 34.1 us; the launch traced here: 33.9 us
  Pallas kernels  18.2 us (53%)
  starting transfers between devices  10.3 us (30%)
  waiting for transfers between devices  3.52 us (10%)
  other arithmetic  1.13 us (3%)
  between operations  0.75 us (2%)
    pallas_call x2, Pallas kernels, body(): call(functools.partial(yz_kernel, half), full, [vm((lines, nz), F32)] * 2...  6.27 us
    pallas_call x1, Pallas kernels, body(): call(c_kernel, (full, shape(ch, 256)), [*[vm(((nx + 2) * 3 * RIM, nz), BF...  6 us
    ppermute x1, starting transfers between devices, body(): lax.ppermute(near_other, 'gy', with_other)  5.67 us
    ppermute x4, starting transfers between devices, exchanged(): return lax.ppermute(value, 'gy', [(i, i ^ bit) for i in range(count)])  3.4 us
    pallas_call x1, Pallas kernels, body(): call(x_kernel, full, [vm((5, nx + 5, ny, nz), F32), vm((5, nx + 1, ny, nz...  2.8 us
    ppermute x4, waiting for transfers between devices, exchanged(): return lax.ppermute(value, 'gy', [(i, i ^ bit) for i in range(count)])  1.88 us
    pallas_call x1, Pallas kernels, body(): call(prepare_kernel, (half_shape(20 * ch, COLUMNS), half_shape(384, 512),...  1.19 us
    concatenate x1, other arithmetic, body(): flat = jnp.concatenate([state.reshape(lines, nz), cot.reshape(lines, nz)])  1.12 us
  transfers between devices with their start and end apart: 8, of which 4 were waited for; matrix products, arithmetic and copies ran while one was open for 0% of the time, Pallas kernels for 51%

profile of v10, /device:TPU:0, one launch (start us, length us, event | category | flops | bytes accessed | tf_op | source)
XLA Modules:
  0.0 33.9 jit_solution(6766558551251833900)
XLA Ops:
  0.6 1.1 %pad_maximum_fusion.flat = f32[1280,128]{1,0:T(8,128)S(1)} fusion(f32[640,128]{1,0:T(8,128)} %bitcast.10, f32[640,128]{1,0:T(8,128)} %bitcast.11), kind=kLoop, calls=%fused_computation | loop fusion | flops 163840 | bytes 1310720 | tf_op jit(solution)/shard_map/concatenate | solution.py:745
  1.7 0.0 copy-start.1
  1.8 0.0 copy-start.2
  1.8 0.5 %collective-permute-start = (f32[15,16,128]{2,1,0:T(8,128)S(1)}, f32[15,16,128]{2,1,0:T(8,128)S(1)}, u32[]{:S(2)}, u32[]{:S(2)}) collective-permute-start(f32[15,16,128]{2,1,0:T(8,128)S(1)} %get-tuple-element.28.order), channel_id=1, source_target_pairs={{0,1},{1,0},{2,3},{3,2},{4,5},{5,4},{6,7},{7,6},{8,9},{9,8},{10,11... | collective-permute-start | bytes 368648 | tf_op jit(solution)/shard_map/ppermute | solution.py:750
  2.3 5.7 %collective-permute-start.1 = (f32[15,16,128]{2,1,0:T(8,128)S(1)}, f32[15,16,128]{2,1,0:T(8,128)S(1)}, u32[]{:S(2)}, u32[]{:S(2)}) collective-permute-start(f32[15,16,128]{2,1,0:T(8,128)S(1)} %get-tuple-element.29.order2), channel_id=1, source_target_pairs={{0,15},{1,2},{2,1},{3,4},{4,3},{5,6},{6,5},{7,8},{8,7},{9,10},{10,... | collective-permute-start | bytes 368648 | tf_op jit(solution)/shard_map/ppermute | solution.py:751
  8.0 0.0 copy-done.1
  8.0 0.0 copy-done.2
  8.0 0.0 copy-start
  8.0 1.2 %shard_map.77 = (bf16[320,720]{1,0:T(8,128)(2,1)S(1)}, bf16[384,512]{1,0:T(8,128)(2,1)S(1)}, bf16[160,192]{1,0:T(8,128)(2,1)S(1)}, f32[160,128]{1,0:T(8,128)S(1)...) custom-call(f32[10,16,8,128]{3,2,1,0:T(8,128)S(1)} %bitcast.4, f32[16,135]{1,0:T(8,128)S(1)} %copy-done.1, ...), custom_call_target="tpu_custom_call" | custom-call | flops 1724999936 | bytes 5535000 | tf_op jit(solution)/shard_map/pallas_call | solution.py:753
  9.2 0.0 copy-done
  9.2 0.1 shard_map.79
  9.3 0.1 collective-permute-start.3
  9.4 0.6 %collective-permute-start.4 = (f32[28,16,128]{2,1,0:T(8,128)S(1)}, f32[28,16,128]{2,1,0:T(8,128)S(1)}, u32[]{:S(2)}, u32[]{:S(2)}) collective-permute-start(f32[28,16,128]{2,1,0:T(8,128)S(1)} %get-tuple-element.41), channel_id=1, source_target_pairs={{0,15},{1,2},{2,1},{3,4},{4,3},{5,6},{6,5},{7,8},{8,7},{9,10},{10,... | collective-permute-start | bytes 688136 | tf_op jit(solution)/shard_map/ppermute | solution.py:773
  10.0 0.0 collective-permute-done.near_twin
  10.0 0.6 %collective-permute-done.1.near_other = f32[15,16,128]{2,1,0:T(8,128)S(1)} collective-permute-done((f32[15,16,128]{2,1,0:T(8,128)S(1)}, f32[15,16,128]{2,1,0:T(8,128)S(1)}, u32[]{:S(2)}, u32[]{:S(2)}) %collective-permute-start.1) | collective-permute-done | bytes 122912 | tf_op jit(solution)/shard_map/ppermute | solution.py:751
  10.6 6.0 %shard_map.78 = (f32[5,16,8,128]{3,2,1,0:T(8,128)S(1)}, f32[16,256]{1,0:T(8,128)S(1)}) custom-call(f32[10,16,8,128]{3,2,1,0:T(8,128)S(1)} %bitcast.5, f32[15,16,128]{2,1,0:T(8,128)S(1)} %collective-permute-done.near_twin, f32[15,16,128]{2,1,0:T(8,128)S(1)} %collective-permute-done.1.near_other, f32[16,135]{1,0:T(8,128)S(1)} %copy-done.1, ...), custom_call_target="tpu_custom_call" | custom-call | flops 6899999744 | bytes 22140000 | tf_op jit(solution)/shard_map/pallas_call | solution.py:776
  16.6 0.1 collective-permute-start.2
  16.6 0.0 collective-permute-done.3.far_twin
  16.7 1.1 %collective-permute-done.4.far_other = f32[28,16,128]{2,1,0:T(8,128)S(1)} collective-permute-done((f32[28,16,128]{2,1,0:T(8,128)S(1)}, f32[28,16,128]{2,1,0:T(8,128)S(1)}, u32[]{:S(2)}, u32[]{:S(2)}) %collective-permute-start.4) | collective-permute-done | bytes 229408 | tf_op jit(solution)/shard_map/ppermute | solution.py:773
  17.7 1.1 %shard_map.80.rim = f32[640,128]{1,0:T(8,128)S(1)} custom-call(f32[1280,128]{1,0:T(8,128)S(1)} %pad_maximum_fusion.flat, f32[15,16,128]{2,1,0:T(8,128)S(1)} %collective-permute-done.near_twin, f32[15,16,128]{2,1,0:T(8,128)S(1)} %collective-permute-done.1.near_other, f32[28,16,128]{2,1,0:T(8,128)S(1)} %collective-permute-done.3.far_twin, ...), custom_call_target="tpu_custom_call" | custom-call | flops 1264999936 | bytes 4059000 | tf_op jit(solution)/shard_map/pallas_call | solution.py:800
  18.8 0.0 collective-permute-done.2
  18.8 0.1 collective-permute-start.5
  18.9 2.8 %shard_map.81.before = f32[5,16,8,128]{3,2,1,0:T(8,128)S(1)} custom-call(f32[10,16,8,128]{3,2,1,0:T(8,128)S(1)} %bitcast.6, s32[3,16,8,128]{3,2,1,0:T(8,128)S(1)} %copy-done, f32[5,16,8,128]{3,2,1,0:T(8,128)S(1)} %get-tuple-element.43.before, f32[16,256]{1,0:T(8,128)S(1)} %add.9.order), custom_call_target="tpu_custom_call" | custom-call | flops 3220000000 | bytes 10332000 | tf_op jit(solution)/shard_map/pallas_call | solution.py:804
  21.7 0.9 %collective-permute-done.5 = f32[16,256]{1,0:T(8,128)S(1)} collective-permute-done((f32[16,256]{1,0:T(8,128)S(1)}, f32[16,256]{1,0:T(8,128)S(1)}, u32[]{:S(2)}, u32[]{:S(2)}) %collective-permute-start.5) | collective-permute-done | bytes 16416 | tf_op jit(solution)/shard_map/ppermute | solution.py:790
  22.6 0.0 collective-permute-start.6
  22.6 2.8 %shard_map.82.before = f32[5,16,8,128]{3,2,1,0:T(8,128)S(1)} custom-call(f32[10,16,8,128]{3,2,1,0:T(8,128)S(1)} %bitcast.7, s32[3,16,8,128]{3,2,1,0:T(8,128)S(1)} %copy-done, f32[15,16,128]{2,1,0:T(8,128)S(1)} %collective-permute-done.near_twin, f32[15,16,128]{2,1,0:T(8,128)S(1)} %collective-permute-done.1.near_other, ...), custom_call_target="tpu_custom_call" | custom-call | flops 3795000064 | bytes 12177000 | tf_op jit(solution)/shard_map/pallas_call | solution.py:796
  25.4 1.0 %collective-permute-done.6 = f32[16,256]{1,0:T(8,128)S(1)} collective-permute-done((f32[16,256]{1,0:T(8,128)S(1)}, f32[16,256]{1,0:T(8,128)S(1)}, u32[]{:S(2)}, u32[]{:S(2)}) %collective-permute-start.6) | collective-permute-done | bytes 16416 | tf_op jit(solution)/shard_map/ppermute | solution.py:790
  26.4 3.3 %collective-permute-start.7 = (f32[16,256]{1,0:T(8,128)S(1)}, f32[16,256]{1,0:T(8,128)S(1)}, u32[]{:S(2)}, u32[]{:S(2)}) collective-permute-start(f32[16,256]{1,0:T(8,128)S(1)} %add.11.order.mine), channel_id=1, source_target_pairs={{0,8},{1,9},{2,10},{3,11},{4,12},{5,13},{6,14},{7,15},{8,0},{9,1},... | collective-permute-start | bytes 49160 | tf_op jit(solution)/shard_map/ppermute | solution.py:790
  29.6 3.5 %shard_map.83 = f32[5,16,8,128]{3,2,1,0:T(8,128)} custom-call(f32[10,16,8,128]{3,2,1,0:T(8,128)S(1)} %bitcast.8, s32[3,16,8,128]{3,2,1,0:T(8,128)S(1)} %copy-done, f32[15,16,128]{2,1,0:T(8,128)S(1)} %collective-permute-done.near_twin, f32[15,16,128]{2,1,0:T(8,128)S(1)} %collective-permute-done.1.near_other, ...), custom_call_target="tpu_custom_call" | custom-call | flops 3795000064 | bytes 12177000 | tf_op jit(solution)/shard_map/pallas_call | solution.py:796
  33.1 0.0 collective-permute-done.7.theirs
  33.2 0.7 %shard_map.84 = (f32[16,135]{1,0:T(8,128)}, f32[5,16]{1,0:T(8,128)}) custom-call(f32[16,256]{1,0:T(8,128)S(1)} %add.11.order.mine, f32[16,256]{1,0:T(8,128)S(1)} %collective-permute-done.7.theirs), custom_call_target="tpu_custom_call" | custom-call | flops 575000000 | bytes 1845000 | tf_op jit(solution)/shard_map/pallas_call | solution.py:826
  (4 shorter events, 0.1 us)
Async XLA Ops:
  1.7 6.3 %copy-start.1 = (f32[16,135]{1,0:T(8,128)S(1)}, f32[16,135]{1,0:T(8,128)}, u32[]{:S(2)}) copy-start(f32[16,135]{1,0:T(8,128)} %kernel.3) | copy-start | bytes 25924
  1.8 6.2 %copy-start.2 = (f32[5,16]{1,0:T(8,128)S(1)}, f32[5,16]{1,0:T(8,128)}, u32[]{:S(2)}) copy-start(f32[5,16]{1,0:T(8,128)} %heads.1) | copy-start | bytes 964
  1.8 8.2 %collective-permute-start = (f32[15,16,128]{2,1,0:T(8,128)S(1)}, f32[15,16,128]{2,1,0:T(8,128)S(1)}, u32[]{:S(2)}, u32[]{:S(2)}) collective-permute-start(f32[15,16,128]{2,1,0:T(8,128)S(1)} %get-tuple-element.28.order), channel_id=1, source_target_pairs={{0,1},{1,0},{2,3},{3,2},{4,5},{5,4},{6,7},{7,6},{8,9},{9,8},{10,11... | collective-permute-start | bytes 368648 | tf_op jit(solution)/shard_map/ppermute | solution.py:750
  2.3 8.2 %collective-permute-start.1 = (f32[15,16,128]{2,1,0:T(8,128)S(1)}, f32[15,16,128]{2,1,0:T(8,128)S(1)}, u32[]{:S(2)}, u32[]{:S(2)}) collective-permute-start(f32[15,16,128]{2,1,0:T(8,128)S(1)} %get-tuple-element.29.order2), channel_id=1, source_target_pairs={{0,15},{1,2},{2,1},{3,4},{4,3},{5,6},{6,5},{7,8},{8,7},{9,10},{10,... | collective-permute-start | bytes 368648 | tf_op jit(solution)/shard_map/ppermute | solution.py:751
  8.0 1.2 %copy-start = (s32[3,16,8,128]{3,2,1,0:T(8,128)S(1)}, s32[3,16,8,128]{3,2,1,0:T(8,128)}, u32[]{:S(2)}) copy-start(s32[3,16,8,128]{3,2,1,0:T(8,128)} %flags.5) | copy-start | bytes 589828
  9.3 7.3 %collective-permute-start.3 = (f32[28,16,128]{2,1,0:T(8,128)S(1)}, f32[28,16,128]{2,1,0:T(8,128)S(1)}, u32[]{:S(2)}, u32[]{:S(2)}) collective-permute-start(f32[28,16,128]{2,1,0:T(8,128)S(1)} %get-tuple-element.40), channel_id=1, source_target_pairs={{0,1},{1,0},{2,3},{3,2},{4,5},{5,4},{6,7},{7,6},{8,9},{9,8},{10,11... | collective-permute-start | bytes 688136 | tf_op jit(solution)/shard_map/ppermute | solution.py:772
  9.4 8.3 %collective-permute-start.4 = (f32[28,16,128]{2,1,0:T(8,128)S(1)}, f32[28,16,128]{2,1,0:T(8,128)S(1)}, u32[]{:S(2)}, u32[]{:S(2)}) collective-permute-start(f32[28,16,128]{2,1,0:T(8,128)S(1)} %get-tuple-element.41), channel_id=1, source_target_pairs={{0,15},{1,2},{2,1},{3,4},{4,3},{5,6},{6,5},{7,8},{8,7},{9,10},{10,... | collective-permute-start | bytes 688136 | tf_op jit(solution)/shard_map/ppermute | solution.py:773
  16.6 2.2 %collective-permute-start.2 = (f32[16,256]{1,0:T(8,128)S(1)}, f32[16,256]{1,0:T(8,128)S(1)}, u32[]{:S(2)}, u32[]{:S(2)}) collective-permute-start(f32[16,256]{1,0:T(8,128)S(1)} %get-tuple-element.39.order), channel_id=1, source_target_pairs={{0,1},{1,0},{2,3},{3,2},{4,5},{5,4},{6,7},{7,6},{8,9},{9,8},{10,11... | collective-permute-start | bytes 49160 | tf_op jit(solution)/shard_map/ppermute | solution.py:790
  18.8 3.8 %collective-permute-start.5 = (f32[16,256]{1,0:T(8,128)S(1)}, f32[16,256]{1,0:T(8,128)S(1)}, u32[]{:S(2)}, u32[]{:S(2)}) collective-permute-start(f32[16,256]{1,0:T(8,128)S(1)} %add.9.order), channel_id=1, source_target_pairs={{0,2},{1,3},{2,0},{3,1},{4,6},{5,7},{6,4},{7,5},{8,10},{9,11},{10,... | collective-permute-start | bytes 49160 | tf_op jit(solution)/shard_map/ppermute | solution.py:790
  22.6 3.7 %collective-permute-start.6 = (f32[16,256]{1,0:T(8,128)S(1)}, f32[16,256]{1,0:T(8,128)S(1)}, u32[]{:S(2)}, u32[]{:S(2)}) collective-permute-start(f32[16,256]{1,0:T(8,128)S(1)} %add.10.order), channel_id=1, source_target_pairs={{0,4},{1,5},{2,6},{3,7},{4,0},{5,1},{6,2},{7,3},{8,12},{9,13},{10,... | collective-permute-start | bytes 49160 | tf_op jit(solution)/shard_map/ppermute | solution.py:790
  26.4 6.8 %collective-permute-start.7 = (f32[16,256]{1,0:T(8,128)S(1)}, f32[16,256]{1,0:T(8,128)S(1)}, u32[]{:S(2)}, u32[]{:S(2)}) collective-permute-start(f32[16,256]{1,0:T(8,128)S(1)} %add.11.order.mine), channel_id=1, source_target_pairs={{0,8},{1,9},{2,10},{3,11},{4,12},{5,13},{6,14},{7,15},{8,0},{9,1},... | collective-permute-start | bytes 49160 | tf_op jit(solution)/shard_map/ppermute | solution.py:790

commit v11 on v10

--- a/solution.py
+++ b/solution.py
@@ -10,7 +10,7 @@
 STEP = 0.3
 FLOOR = 0.01
 BELOW, ABOVE = 2, 3
-SLABS = 2
+SLABS = 4
 WIDE = 4
 VMEM = 48 * 1024 * 1024
 F32 = jnp.float32

time: 34.1 us -> 34 us (level)
  no operation moved by 1% of the time
where the time goes in v11:
time: 34 us; the launch traced here: 33.8 us
  Pallas kernels  18.1 us (53%)
  starting transfers between devices  10.2 us (30%)
  waiting for transfers between devices  3.59 us (11%)
  other arithmetic  1.13 us (3%)
  between operations  0.75 us (2%)
    pallas_call x2, Pallas kernels, body(): call(functools.partial(yz_kernel, half), full, [vm((lines, nz), F32)] * 2...  6.2 us
    pallas_call x1, Pallas kernels, body(): call(c_kernel, (full, shape(ch, 256)), [*[vm(((nx + 2) * 3 * RIM, nz), BF...  6 us
    ppermute x1, starting transfers between devices, body(): lax.ppermute(near_other, 'gy', with_other)  5.67 us
    ppermute x4, starting transfers between devices, exchanged(): return lax.ppermute(value, 'gy', [(i, i ^ bit) for i in range(count)])  3.33 us
    pallas_call x1, Pallas kernels, body(): call(x_kernel, full, [vm((5, nx + 5, ny, nz), F32), vm((5, nx + 1, ny, nz...  2.77 us
    ppermute x4, waiting for transfers between devices, exchanged(): return lax.ppermute(value, 'gy', [(i, i ^ bit) for i in range(count)])  1.95 us
    pallas_call x1, Pallas kernels, body(): call(prepare_kernel, (half_shape(20 * ch, COLUMNS), half_shape(384, 512),...  1.19 us
    concatenate x1, other arithmetic, body(): flat = jnp.concatenate([state.reshape(lines, nz), cot.reshape(lines, nz)])  1.12 us
  transfers between devices with their start and end apart: 8, of which 4 were waited for; matrix products, arithmetic and copies ran while one was open for 0% of the time, Pallas kernels for 51%

profile of v11, /device:TPU:0, one launch (start us, length us, event | category | flops | bytes accessed | tf_op | source)
XLA Modules:
  0.0 33.8 jit_solution(9092704614881326504)
XLA Ops:
  0.6 1.1 %pad_maximum_fusion.flat = f32[1280,128]{1,0:T(8,128)S(1)} fusion(f32[640,128]{1,0:T(8,128)} %bitcast.10, f32[640,128]{1,0:T(8,128)} %bitcast.11), kind=kLoop, calls=%fused_computation | loop fusion | flops 163840 | bytes 1310720 | tf_op jit(solution)/shard_map/concatenate | solution.py:745
  1.7 0.0 copy-start.1
  1.8 0.0 copy-start.2
  1.8 0.5 %collective-permute-start = (f32[15,16,128]{2,1,0:T(8,128)S(1)}, f32[15,16,128]{2,1,0:T(8,128)S(1)}, u32[]{:S(2)}, u32[]{:S(2)}) collective-permute-start(f32[15,16,128]{2,1,0:T(8,128)S(1)} %get-tuple-element.28.order), channel_id=1, source_target_pairs={{0,1},{1,0},{2,3},{3,2},{4,5},{5,4},{6,7},{7,6},{8,9},{9,8},{10,11... | collective-permute-start | bytes 368648 | tf_op jit(solution)/shard_map/ppermute | solution.py:750
  2.3 5.7 %collective-permute-start.1 = (f32[15,16,128]{2,1,0:T(8,128)S(1)}, f32[15,16,128]{2,1,0:T(8,128)S(1)}, u32[]{:S(2)}, u32[]{:S(2)}) collective-permute-start(f32[15,16,128]{2,1,0:T(8,128)S(1)} %get-tuple-element.29.order2), channel_id=1, source_target_pairs={{0,15},{1,2},{2,1},{3,4},{4,3},{5,6},{6,5},{7,8},{8,7},{9,10},{10,... | collective-permute-start | bytes 368648 | tf_op jit(solution)/shard_map/ppermute | solution.py:751
  8.0 0.0 copy-done.1
  8.0 0.0 copy-done.2
  8.0 0.0 copy-start
  8.0 1.2 %shard_map.77 = (bf16[320,720]{1,0:T(8,128)(2,1)S(1)}, bf16[384,512]{1,0:T(8,128)(2,1)S(1)}, bf16[160,192]{1,0:T(8,128)(2,1)S(1)}, f32[160,128]{1,0:T(8,128)S(1)...) custom-call(f32[10,16,8,128]{3,2,1,0:T(8,128)S(1)} %bitcast.4, f32[16,135]{1,0:T(8,128)S(1)} %copy-done.1, ...), custom_call_target="tpu_custom_call" | custom-call | flops 1724999936 | bytes 5535000 | tf_op jit(solution)/shard_map/pallas_call | solution.py:753
  9.2 0.0 copy-done
  9.2 0.1 shard_map.79
  9.3 0.1 collective-permute-start.3
  9.4 0.6 %collective-permute-start.4 = (f32[28,16,128]{2,1,0:T(8,128)S(1)}, f32[28,16,128]{2,1,0:T(8,128)S(1)}, u32[]{:S(2)}, u32[]{:S(2)}) collective-permute-start(f32[28,16,128]{2,1,0:T(8,128)S(1)} %get-tuple-element.41), channel_id=1, source_target_pairs={{0,15},{1,2},{2,1},{3,4},{4,3},{5,6},{6,5},{7,8},{8,7},{9,10},{10,... | collective-permute-start | bytes 688136 | tf_op jit(solution)/shard_map/ppermute | solution.py:773
  10.0 0.0 collective-permute-done.near_twin
  10.0 0.6 %collective-permute-done.1.near_other = f32[15,16,128]{2,1,0:T(8,128)S(1)} collective-permute-done((f32[15,16,128]{2,1,0:T(8,128)S(1)}, f32[15,16,128]{2,1,0:T(8,128)S(1)}, u32[]{:S(2)}, u32[]{:S(2)}) %collective-permute-start.1) | collective-permute-done | bytes 122912 | tf_op jit(solution)/shard_map/ppermute | solution.py:751
  10.6 6.0 %shard_map.78 = (f32[5,16,8,128]{3,2,1,0:T(8,128)S(1)}, f32[16,256]{1,0:T(8,128)S(1)}) custom-call(f32[10,16,8,128]{3,2,1,0:T(8,128)S(1)} %bitcast.5, f32[15,16,128]{2,1,0:T(8,128)S(1)} %collective-permute-done.near_twin, f32[15,16,128]{2,1,0:T(8,128)S(1)} %collective-permute-done.1.near_other, f32[16,135]{1,0:T(8,128)S(1)} %copy-done.1, ...), custom_call_target="tpu_custom_call" | custom-call | flops 6899999744 | bytes 22140000 | tf_op jit(solution)/shard_map/pallas_call | solution.py:776
  16.6 0.1 collective-permute-start.2
  16.6 0.0 collective-permute-done.3.far_twin
  16.7 1.1 %collective-permute-done.4.far_other = f32[28,16,128]{2,1,0:T(8,128)S(1)} collective-permute-done((f32[28,16,128]{2,1,0:T(8,128)S(1)}, f32[28,16,128]{2,1,0:T(8,128)S(1)}, u32[]{:S(2)}, u32[]{:S(2)}) %collective-permute-start.4) | collective-permute-done | bytes 229408 | tf_op jit(solution)/shard_map/ppermute | solution.py:773
  17.7 1.1 %shard_map.80.rim = f32[640,128]{1,0:T(8,128)S(1)} custom-call(f32[1280,128]{1,0:T(8,128)S(1)} %pad_maximum_fusion.flat, f32[15,16,128]{2,1,0:T(8,128)S(1)} %collective-permute-done.near_twin, f32[15,16,128]{2,1,0:T(8,128)S(1)} %collective-permute-done.1.near_other, f32[28,16,128]{2,1,0:T(8,128)S(1)} %collective-permute-done.3.far_twin, ...), custom_call_target="tpu_custom_call" | custom-call | flops 1264999936 | bytes 4059000 | tf_op jit(solution)/shard_map/pallas_call | solution.py:800
  18.8 0.0 collective-permute-done.2
  18.8 0.1 collective-permute-start.5
  18.9 2.8 %shard_map.81.before = f32[5,16,8,128]{3,2,1,0:T(8,128)S(1)} custom-call(f32[10,16,8,128]{3,2,1,0:T(8,128)S(1)} %bitcast.6, s32[3,16,8,128]{3,2,1,0:T(8,128)S(1)} %copy-done, f32[5,16,8,128]{3,2,1,0:T(8,128)S(1)} %get-tuple-element.43.before, f32[16,256]{1,0:T(8,128)S(1)} %add.9.order), custom_call_target="tpu_custom_call" | custom-call | flops 3220000000 | bytes 10332000 | tf_op jit(solution)/shard_map/pallas_call | solution.py:804
  21.7 1.0 %collective-permute-done.5 = f32[16,256]{1,0:T(8,128)S(1)} collective-permute-done((f32[16,256]{1,0:T(8,128)S(1)}, f32[16,256]{1,0:T(8,128)S(1)}, u32[]{:S(2)}, u32[]{:S(2)}) %collective-permute-start.5) | collective-permute-done | bytes 16416 | tf_op jit(solution)/shard_map/ppermute | solution.py:790
  22.6 0.0 collective-permute-start.6
  22.6 2.7 %shard_map.82.before = f32[5,16,8,128]{3,2,1,0:T(8,128)S(1)} custom-call(f32[10,16,8,128]{3,2,1,0:T(8,128)S(1)} %bitcast.7, s32[3,16,8,128]{3,2,1,0:T(8,128)S(1)} %copy-done, f32[15,16,128]{2,1,0:T(8,128)S(1)} %collective-permute-done.near_twin, f32[15,16,128]{2,1,0:T(8,128)S(1)} %collective-permute-done.1.near_other, ...), custom_call_target="tpu_custom_call" | custom-call | flops 3795000064 | bytes 12177000 | tf_op jit(solution)/shard_map/pallas_call | solution.py:796
  25.4 1.0 %collective-permute-done.6 = f32[16,256]{1,0:T(8,128)S(1)} collective-permute-done((f32[16,256]{1,0:T(8,128)S(1)}, f32[16,256]{1,0:T(8,128)S(1)}, u32[]{:S(2)}, u32[]{:S(2)}) %collective-permute-start.6) | collective-permute-done | bytes 16416 | tf_op jit(solution)/shard_map/ppermute | solution.py:790
  26.4 3.2 %collective-permute-start.7 = (f32[16,256]{1,0:T(8,128)S(1)}, f32[16,256]{1,0:T(8,128)S(1)}, u32[]{:S(2)}, u32[]{:S(2)}) collective-permute-start(f32[16,256]{1,0:T(8,128)S(1)} %add.11.order.mine), channel_id=1, source_target_pairs={{0,8},{1,9},{2,10},{3,11},{4,12},{5,13},{6,14},{7,15},{8,0},{9,1},... | collective-permute-start | bytes 49160 | tf_op jit(solution)/shard_map/ppermute | solution.py:790
  29.6 3.5 %shard_map.83 = f32[5,16,8,128]{3,2,1,0:T(8,128)} custom-call(f32[10,16,8,128]{3,2,1,0:T(8,128)S(1)} %bitcast.8, s32[3,16,8,128]{3,2,1,0:T(8,128)S(1)} %copy-done, f32[15,16,128]{2,1,0:T(8,128)S(1)} %collective-permute-done.near_twin, f32[15,16,128]{2,1,0:T(8,128)S(1)} %collective-permute-done.1.near_other, ...), custom_call_target="tpu_custom_call" | custom-call | flops 3795000064 | bytes 12177000 | tf_op jit(solution)/shard_map/pallas_call | solution.py:796
  33.0 0.0 collective-permute-done.7.theirs
  33.0 0.7 %shard_map.84 = (f32[16,135]{1,0:T(8,128)}, f32[5,16]{1,0:T(8,128)}) custom-call(f32[16,256]{1,0:T(8,128)S(1)} %add.11.order.mine, f32[16,256]{1,0:T(8,128)S(1)} %collective-permute-done.7.theirs), custom_call_target="tpu_custom_call" | custom-call | flops 575000000 | bytes 1845000 | tf_op jit(solution)/shard_map/pallas_call | solution.py:826
  (4 shorter events, 0.1 us)
Async XLA Ops:
  1.7 6.3 %copy-start.1 = (f32[16,135]{1,0:T(8,128)S(1)}, f32[16,135]{1,0:T(8,128)}, u32[]{:S(2)}) copy-start(f32[16,135]{1,0:T(8,128)} %kernel.3) | copy-start | bytes 25924
  1.8 6.2 %copy-start.2 = (f32[5,16]{1,0:T(8,128)S(1)}, f32[5,16]{1,0:T(8,128)}, u32[]{:S(2)}) copy-start(f32[5,16]{1,0:T(8,128)} %heads.1) | copy-start | bytes 964
  1.8 8.2 %collective-permute-start = (f32[15,16,128]{2,1,0:T(8,128)S(1)}, f32[15,16,128]{2,1,0:T(8,128)S(1)}, u32[]{:S(2)}, u32[]{:S(2)}) collective-permute-start(f32[15,16,128]{2,1,0:T(8,128)S(1)} %get-tuple-element.28.order), channel_id=1, source_target_pairs={{0,1},{1,0},{2,3},{3,2},{4,5},{5,4},{6,7},{7,6},{8,9},{9,8},{10,11... | collective-permute-start | bytes 368648 | tf_op jit(solution)/shard_map/ppermute | solution.py:750
  2.3 8.2 %collective-permute-start.1 = (f32[15,16,128]{2,1,0:T(8,128)S(1)}, f32[15,16,128]{2,1,0:T(8,128)S(1)}, u32[]{:S(2)}, u32[]{:S(2)}) collective-permute-start(f32[15,16,128]{2,1,0:T(8,128)S(1)} %get-tuple-element.29.order2), channel_id=1, source_target_pairs={{0,15},{1,2},{2,1},{3,4},{4,3},{5,6},{6,5},{7,8},{8,7},{9,10},{10,... | collective-permute-start | bytes 368648 | tf_op jit(solution)/shard_map/ppermute | solution.py:751
  8.0 1.2 %copy-start = (s32[3,16,8,128]{3,2,1,0:T(8,128)S(1)}, s32[3,16,8,128]{3,2,1,0:T(8,128)}, u32[]{:S(2)}) copy-start(s32[3,16,8,128]{3,2,1,0:T(8,128)} %flags.5) | copy-start | bytes 589828
  9.3 7.3 %collective-permute-start.3 = (f32[28,16,128]{2,1,0:T(8,128)S(1)}, f32[28,16,128]{2,1,0:T(8,128)S(1)}, u32[]{:S(2)}, u32[]{:S(2)}) collective-permute-start(f32[28,16,128]{2,1,0:T(8,128)S(1)} %get-tuple-element.40), channel_id=1, source_target_pairs={{0,1},{1,0},{2,3},{3,2},{4,5},{5,4},{6,7},{7,6},{8,9},{9,8},{10,11... | collective-permute-start | bytes 688136 | tf_op jit(solution)/shard_map/ppermute | solution.py:772
  9.4 8.3 %collective-permute-start.4 = (f32[28,16,128]{2,1,0:T(8,128)S(1)}, f32[28,16,128]{2,1,0:T(8,128)S(1)}, u32[]{:S(2)}, u32[]{:S(2)}) collective-permute-start(f32[28,16,128]{2,1,0:T(8,128)S(1)} %get-tuple-element.41), channel_id=1, source_target_pairs={{0,15},{1,2},{2,1},{3,4},{4,3},{5,6},{6,5},{7,8},{8,7},{9,10},{10,... | collective-permute-start | bytes 688136 | tf_op jit(solution)/shard_map/ppermute | solution.py:773
  16.6 2.2 %collective-permute-start.2 = (f32[16,256]{1,0:T(8,128)S(1)}, f32[16,256]{1,0:T(8,128)S(1)}, u32[]{:S(2)}, u32[]{:S(2)}) collective-permute-start(f32[16,256]{1,0:T(8,128)S(1)} %get-tuple-element.39.order), channel_id=1, source_target_pairs={{0,1},{1,0},{2,3},{3,2},{4,5},{5,4},{6,7},{7,6},{8,9},{9,8},{10,11... | collective-permute-start | bytes 49160 | tf_op jit(solution)/shard_map/ppermute | solution.py:790
  18.8 3.8 %collective-permute-start.5 = (f32[16,256]{1,0:T(8,128)S(1)}, f32[16,256]{1,0:T(8,128)S(1)}, u32[]{:S(2)}, u32[]{:S(2)}) collective-permute-start(f32[16,256]{1,0:T(8,128)S(1)} %add.9.order), channel_id=1, source_target_pairs={{0,2},{1,3},{2,0},{3,1},{4,6},{5,7},{6,4},{7,5},{8,10},{9,11},{10,... | collective-permute-start | bytes 49160 | tf_op jit(solution)/shard_map/ppermute | solution.py:790
  22.6 3.7 %collective-permute-start.6 = (f32[16,256]{1,0:T(8,128)S(1)}, f32[16,256]{1,0:T(8,128)S(1)}, u32[]{:S(2)}, u32[]{:S(2)}) collective-permute-start(f32[16,256]{1,0:T(8,128)S(1)} %add.10.order), channel_id=1, source_target_pairs={{0,4},{1,5},{2,6},{3,7},{4,0},{5,1},{6,2},{7,3},{8,12},{9,13},{10,... | collective-permute-start | bytes 49160 | tf_op jit(solution)/shard_map/ppermute | solution.py:790
  26.4 6.7 %collective-permute-start.7 = (f32[16,256]{1,0:T(8,128)S(1)}, f32[16,256]{1,0:T(8,128)S(1)}, u32[]{:S(2)}, u32[]{:S(2)}) collective-permute-start(f32[16,256]{1,0:T(8,128)S(1)} %add.11.order.mine), channel_id=1, source_target_pairs={{0,8},{1,9},{2,10},{3,11},{4,12},{5,13},{6,14},{7,15},{8,0},{9,1},... | collective-permute-start | bytes 49160 | tf_op jit(solution)/shard_map/ppermute | solution.py:790

commit v12 on v10

--- a/solution.py
+++ b/solution.py
@@ -204,7 +204,8 @@
             other[i] = jnp.where(even, low, top)
 
 
-def near_kernel(flat, twin, other):
+def near_kernel(flat, order, twin, other):
+    del order
     s, g = views(flat)
     pack(s, range(NEAR_STATE), 0, twin, other, 0)
     pack(g, range(NEAR_COT), 0, twin, other, 5 * NEAR_STATE)
@@ -248,8 +249,7 @@
     return state, cot, flags
 
 
-def x_kernel(fields, flags, before, order, out, pad, gpad, acc):
-    del order
+def x_faces(fields, flags, out, pad, gpad, acc):
     state, cot = views(fields)
     nx = state.shape[1]
     for v in range(5):
@@ -284,7 +284,26 @@
         acc[v, pl.ds(2, 3)] = acc[v, pl.ds(2, 3)] + acc[v, pl.ds(nx + 2, 3)]
 
     for v in range(5):
-        out[v] = acc[v, pl.ds(2, nx)] + before[v]
+        out[v] = acc[v, pl.ds(2, nx)]
+
+
+def x_early_kernel(fields, flags, out, *scratch):
+    @pl.when(lax.axis_index("gy") == 0)
+    def _():
+        x_faces(fields, flags, out, *scratch)
+
+
+def x_late_kernel(fields, flags, early, order, out, *scratch):
+    del order
+    first = lax.axis_index("gy") == 0
+
+    @pl.when(first)
+    def _():
+        out[...] = early[...]
+
+    @pl.when(jnp.logical_not(first))
+    def _():
+        x_faces(fields, flags, out, *scratch)
 
 
 def z_faces(state, cot, flags, x):
@@ -337,16 +356,16 @@
             out[pl.ds(v * nx * 8 + row, nx, stride=8), :] = value
 
 
-def yz_kernel(half, fields, flags, near_twin, near_other, far_twin, far_other, before, rim, order, out, halo, ghalo):
+def yz_kernel(lo, hi, fields, flags, near_twin, near_other, far_twin, far_other, first, before, rim, order, out, halo, ghalo):
     del order
     state, cot = views(fields)
     rims = from_rims(near_twin, near_other, far_twin, far_other)
     rim_state, rim_cot, _ = rims
     nx = out.shape[1]
-    part = nx // 2
-    for v in range(5):
-        kept = pl.ds((1 - half) * part, part)
-        out[v, kept] = before[v, kept]
+    for v in range(5):
+        for kept in (pl.ds(0, lo), pl.ds(hi, nx - hi)):
+            if kept.size:
+                out[v, kept] = before[v, kept]
     for v in range(5):
         base = v * nx * 8
         for r in range(ABOVE):
@@ -360,7 +379,7 @@
         inside[k] = (row < 8 + k) if k < 0 else (row >= k)
 
     def step(i, carry):
-        x = half * part + i * SLABS
+        x = lo + i * SLABS
         cells, face = [], []
         for v in range(5):
             at = pl.multiple_of((v * nx + x) * 8, 8)
@@ -380,7 +399,8 @@
         along_z = z_faces(state, cot, flags, x)
         for v in range(5):
             at = pl.multiple_of((v * nx + x) * 8, 8)
-            total = before[v, pl.ds(x, SLABS)] + along_z[v] + terms[v][2]
+            total = before[v, pl.ds(x, SLABS)] + first[v, pl.ds(x, SLABS)]
+            total = total + along_z[v] + terms[v][2]
             total = total + rim[pl.ds(at, 8 * SLABS), :].reshape(SLABS, 8, 128)
             for k in (-2, -1, 1, 2, 3):
                 moved = pltpu.roll(terms[v][k + 2], k % 8, 1)
@@ -388,7 +408,7 @@
             out[v, pl.ds(x, SLABS)] = total
         return carry
 
-    lax.fori_loop(0, part // SLABS, step, 0)
+    lax.fori_loop(0, (hi - lo) // SLABS, step, 0)
 
 
 def sum_kernel(scale, mine, theirs, k_out, h_out):
@@ -745,7 +765,13 @@
     flat = jnp.concatenate([state.reshape(lines, nz), cot.reshape(lines, nz)])
     fields = flat.reshape(10, nx, ny, nz)
     near, far = shape(NEAR, nx, nz), shape(FAR, nx, nz)
-    near_twin, near_other = call(near_kernel, (near, near), [], 0.2, 1)(flat)
+    x_scratch = [
+        vm((5, nx + 5, ny, nz), F32),
+        vm((5, nx + 1, ny, nz), F32),
+        vm((5, nx + 5, ny, nz), F32),
+    ]
+    early = call(x_early_kernel, full, x_scratch, 0.2, 2)(fields, flags)
+    near_twin, near_other = call(near_kernel, (near, near), [], 0.2, 1, 1)(flat, early)
     near_rims = (
         lax.ppermute(near_twin, "gy", with_twin),
         lax.ppermute(near_other, "gy", with_other),
@@ -765,14 +791,15 @@
         3,
         2,
     )(fields, kernel, heads, near_twin, near_other)
+    first = call(x_late_kernel, full, x_scratch, 2.8, 3, 1)(fields, flags, early, patches)
     far_twin, far_other = call(far_kernel, (far, far), [], 0.2, 2, 1)(
-        flat, flags.reshape(3 * nx * ny, nz), patches
+        flat, flags.reshape(3 * nx * ny, nz), first
     )
     far_rims = (
         lax.ppermute(far_twin, "gy", with_twin),
         lax.ppermute(far_other, "gy", with_other),
     )
-    near_rims, patches = lax.optimization_barrier((near_rims, patches))
+    near_rims, patches, first = lax.optimization_barrier((near_rims, patches, first))
     own, parts = call(
         c_kernel,
         (full, shape(ch, 256)),
@@ -793,34 +820,24 @@
     sums = parts
     for bit in bits[:-4]:
         sums = sums + exchanged(sums, bit)
-    yz_half = lambda half, before, order: call(
-        functools.partial(yz_kernel, half), full, [vm((lines, nz), F32)] * 2, 3.3, 8, 1
-    )(fields, flags, *near_rims, *far_rims, before, rim, order)
+    third = nx // 6 * 2
+    yz = lambda lo, hi, before, order: call(
+        functools.partial(yz_kernel, lo, hi), full, [vm((lines, nz), F32)] * 2, 2.2, 9, 1
+    )(fields, flags, *near_rims, *far_rims, first, before, rim, order)
     got = exchanged(sums, bits[-4])
     rim = call(e_kernel, shape(lines, nz), [], 1.1, 5, 1)(flat, *near_rims, *far_rims, sums)
     got, rim = lax.optimization_barrier((got, rim))
     sums = sums + got
     got = exchanged(sums, bits[-3])
-    total = call(
-        x_kernel,
-        full,
-        [
-            vm((5, nx + 5, ny, nz), F32),
-            vm((5, nx + 1, ny, nz), F32),
-            vm((5, nx + 5, ny, nz), F32),
-        ],
-        2.8,
-        3,
-        1,
-    )(fields, flags, own, sums)
+    total = yz(0, third, own, sums)
     got, total = lax.optimization_barrier((got, total))
     sums = sums + got
     got = exchanged(sums, bits[-2])
-    total = yz_half(0, total, sums)
+    total = yz(third, nx - nx // 8 * 3, total, sums)
     got, total = lax.optimization_barrier((got, total))
     sums = sums + got
     got = exchanged(sums, bits[-1])
-    flow = yz_half(1, total, sums)
+    flow = yz(nx - nx // 8 * 3, nx, total, sums)
     got, flow = lax.optimization_barrier((got, flow))
     scale = float(cells * count) ** (-0.5)
     k_out, h_out = call(

time: 34.1 us -> 33.9 us (level)
  starting transfers between devices: 10.3 us -> 7.57 us
  waiting for transfers between devices: 3.52 us -> 5.87 us
    ppermute x4, waiting for transfers between devices: 1.88 us -> 5.86 us  [exchanged(): return lax.ppermute(value, 'gy', [(i, i ^ bit) for i in range(count)])]
    ppermute x1, starting transfers between devices: 0.61 us -> 4 us  [body(): lax.ppermute(far_other, 'gy', with_other)]
    ppermute x4, starting transfers between devices: 3.4 us -> 0.1 us  [exchanged(): return lax.ppermute(value, 'gy', [(i, i ^ bit) for i in range(count)])]
    ppermute x1, starting transfers between devices: 5.67 us -> 3.33 us  [body(): lax.ppermute(near_other, 'gy', with_other)]
    ppermute x1, waiting for transfers between devices: 1.05 us -> 0.01 us  [body(): lax.ppermute(far_other, 'gy', with_other)]
    ppermute x1, waiting for transfers between devices: 0.58 us -> 0.01 us  [body(): lax.ppermute(near_other, 'gy', with_other)]
    ppermute x1, starting transfers between devices: 0.52 us -> 0.07 us  [body(): lax.ppermute(near_twin, 'gy', with_twin)]
    pallas_call x4 -> x6, Pallas kernels: 9.12 us -> 9.24 us  [the longest x3 6.36 us: body(): call(functools.partial(yz_kernel, lo, hi), full, [vm((lines, nz), F32)] *...]
  transfers between devices with their start and end apart: 8 -> 8, of which waited for: 4 -> 4; matrix products, arithmetic and copies ran while one was open for 0% -> 0% of each run, Pallas kernels for 51% -> 44%
where the time goes in v12:
time: 33.9 us; the launch traced here: 33.8 us
  Pallas kernels  18.4 us (54%)
  starting transfers between devices  7.57 us (22%)
  waiting for transfers between devices  5.87 us (17%)
  other arithmetic  1.17 us (3%)
  between operations  0.77 us (2%)
    pallas_call x3, Pallas kernels, body(): call(functools.partial(yz_kernel, lo, hi), full, [vm((lines, nz), F32)] *...  6.36 us
    pallas_call x1, Pallas kernels, body(): call(c_kernel, (full, shape(ch, 256)), [*[vm(((nx + 2) * 3 * RIM, nz), BF...  6.04 us
    ppermute x4, waiting for transfers between devices, exchanged(): return lax.ppermute(value, 'gy', [(i, i ^ bit) for i in range(count)])  5.86 us
    ppermute x1, starting transfers between devices, body(): lax.ppermute(far_other, 'gy', with_other)  4 us
    ppermute x1, starting transfers between devices, body(): lax.ppermute(near_other, 'gy', with_other)  3.33 us
    pallas_call x1, Pallas kernels, body(): early = call(x_early_kernel, full, x_scratch, 0.2, 2)(fields, flags)  2.79 us
    pallas_call x1, Pallas kernels, body(): call(prepare_kernel, (half_shape(20 * ch, COLUMNS), half_shape(384, 512),...  1.19 us
    concatenate x1, other arithmetic, body(): flat = jnp.concatenate([state.reshape(lines, nz), cot.reshape(lines, nz)])  1.15 us
  transfers between devices with their start and end apart: 8, of which 4 were waited for; matrix products, arithmetic and copies ran while one was open for 0% of the time, Pallas kernels for 44%

profile of v12, /device:TPU:0, one launch (start us, length us, event | category | flops | bytes accessed | tf_op | source)
XLA Modules:
  0.0 33.8 jit_solution(15594626766417259197)
XLA Ops:
  0.6 0.0 copy-start
  0.6 1.2 %pad_maximum_fusion.flat = f32[1280,128]{1,0:T(8,128)S(1)} fusion(f32[640,128]{1,0:T(8,128)} %bitcast.12, f32[640,128]{1,0:T(8,128)} %bitcast.13), kind=kLoop, calls=%fused_computation | loop fusion | flops 163840 | bytes 1310720 | tf_op jit(solution)/shard_map/concatenate | solution.py:765
  1.8 0.0 copy-done
  1.8 2.8 %shard_map.76.order.early = f32[5,16,8,128]{3,2,1,0:T(8,128)S(1)} custom-call(f32[10,16,8,128]{3,2,1,0:T(8,128)S(1)} %bitcast.4, s32[3,16,8,128]{3,2,1,0:T(8,128)S(1)} %copy-done), custom_call_target="tpu_custom_call" | custom-call | flops 230000000 | bytes 738000 | tf_op jit(solution)/shard_map/pallas_call | solution.py:773
  4.6 0.0 copy-start.1
  4.6 0.0 copy-start.2
  4.7 0.1 collective-permute-start
  4.8 3.3 %collective-permute-start.1 = (f32[15,16,128]{2,1,0:T(8,128)S(1)}, f32[15,16,128]{2,1,0:T(8,128)S(1)}, u32[]{:S(2)}, u32[]{:S(2)}) collective-permute-start(f32[15,16,128]{2,1,0:T(8,128)S(1)} %get-tuple-element.30.order2), channel_id=1, source_target_pairs={{0,15},{1,2},{2,1},{3,4},{4,3},{5,6},{6,5},{7,8},{8,7},{9,10},{10,... | collective-permute-start | bytes 368648 | tf_op jit(solution)/shard_map/ppermute | solution.py:777
  8.1 0.0 copy-done.1
  8.1 0.0 copy-done.2
  8.1 1.2 %shard_map.78 = (bf16[320,720]{1,0:T(8,128)(2,1)S(1)}, bf16[384,512]{1,0:T(8,128)(2,1)S(1)}, bf16[160,192]{1,0:T(8,128)(2,1)S(1)}, f32[160,128]{1,0:T(8,128)S(1)...) custom-call(f32[10,16,8,128]{3,2,1,0:T(8,128)S(1)} %bitcast.5, f32[16,135]{1,0:T(8,128)S(1)} %copy-done.1, ...), custom_call_target="tpu_custom_call" | custom-call | flops 1724999936 | bytes 5535000 | tf_op jit(solution)/shard_map/pallas_call | solution.py:779
  9.3 0.1 shard_map.81
  9.4 0.1 collective-permute-start.3
  9.5 4.0 %collective-permute-start.4 = (f32[28,16,128]{2,1,0:T(8,128)S(1)}, f32[28,16,128]{2,1,0:T(8,128)S(1)}, u32[]{:S(2)}, u32[]{:S(2)}) collective-permute-start(f32[28,16,128]{2,1,0:T(8,128)S(1)} %get-tuple-element.42), channel_id=1, source_target_pairs={{0,15},{1,2},{2,1},{3,4},{4,3},{5,6},{6,5},{7,8},{8,7},{9,10},{10,... | collective-permute-start | bytes 688136 | tf_op jit(solution)/shard_map/ppermute | solution.py:800
  13.5 0.0 collective-permute-done.near_twin
  13.5 0.0 collective-permute-done.1.near_other
  13.5 6.0 %shard_map.80 = (f32[5,16,8,128]{3,2,1,0:T(8,128)S(1)}, f32[16,256]{1,0:T(8,128)S(1)}) custom-call(f32[10,16,8,128]{3,2,1,0:T(8,128)S(1)} %bitcast.7, f32[15,16,128]{2,1,0:T(8,128)S(1)} %collective-permute-done.near_twin, f32[15,16,128]{2,1,0:T(8,128)S(1)} %collective-permute-done.1.near_other, f32[16,135]{1,0:T(8,128)S(1)} %copy-done.1, ...), custom_call_target="tpu_custom_call" | custom-call | flops 6899999744 | bytes 22140000 | tf_op jit(solution)/shard_map/pallas_call | solution.py:803
  19.5 0.1 collective-permute-start.2
  19.6 0.0 collective-permute-done.3.far_twin
  19.6 0.0 collective-permute-done.4.far_other
  19.6 1.1 %shard_map.82.rim = f32[640,128]{1,0:T(8,128)S(1)} custom-call(f32[1280,128]{1,0:T(8,128)S(1)} %pad_maximum_fusion.flat, f32[15,16,128]{2,1,0:T(8,128)S(1)} %collective-permute-done.near_twin, f32[15,16,128]{2,1,0:T(8,128)S(1)} %collective-permute-done.1.near_other, f32[28,16,128]{2,1,0:T(8,128)S(1)} %collective-permute-done.3.far_twin, ...), custom_call_target="tpu_custom_call" | custom-call | flops 1264999936 | bytes 4059000 | tf_op jit(solution)/shard_map/pallas_call | solution.py:828
  20.7 0.1 collective-permute-done.2
  20.8 0.0 collective-permute-start.5
  20.8 1.4 %shard_map.83.before = f32[5,16,8,128]{3,2,1,0:T(8,128)S(1)} custom-call(f32[10,16,8,128]{3,2,1,0:T(8,128)S(1)} %bitcast.8, s32[3,16,8,128]{3,2,1,0:T(8,128)S(1)} %copy-done, f32[15,16,128]{2,1,0:T(8,128)S(1)} %collective-permute-done.near_twin, f32[15,16,128]{2,1,0:T(8,128)S(1)} %collective-permute-done.1.near_other, ...), custom_call_target="tpu_custom_call" | custom-call | flops 2529999872 | bytes 8118000 | tf_op jit(solution)/shard_map/pallas_call | solution.py:824
  22.3 2.3 %collective-permute-done.5 = f32[16,256]{1,0:T(8,128)S(1)} collective-permute-done((f32[16,256]{1,0:T(8,128)S(1)}, f32[16,256]{1,0:T(8,128)S(1)}, u32[]{:S(2)}, u32[]{:S(2)}) %collective-permute-start.5) | collective-permute-done | bytes 16416 | tf_op jit(solution)/shard_map/ppermute | solution.py:817
  24.6 0.0 collective-permute-start.6
  24.6 2.1 %shard_map.84.before = f32[5,16,8,128]{3,2,1,0:T(8,128)S(1)} custom-call(f32[10,16,8,128]{3,2,1,0:T(8,128)S(1)} %bitcast.9, s32[3,16,8,128]{3,2,1,0:T(8,128)S(1)} %copy-done, f32[15,16,128]{2,1,0:T(8,128)S(1)} %collective-permute-done.near_twin, f32[15,16,128]{2,1,0:T(8,128)S(1)} %collective-permute-done.1.near_other, ...), custom_call_target="tpu_custom_call" | custom-call | flops 2529999872 | bytes 8118000 | tf_op jit(solution)/shard_map/pallas_call | solution.py:824
  26.7 1.6 %collective-permute-done.6 = f32[16,256]{1,0:T(8,128)S(1)} collective-permute-done((f32[16,256]{1,0:T(8,128)S(1)}, f32[16,256]{1,0:T(8,128)S(1)}, u32[]{:S(2)}, u32[]{:S(2)}) %collective-permute-start.6) | collective-permute-done | bytes 16416 | tf_op jit(solution)/shard_map/ppermute | solution.py:817
  28.3 0.0 collective-permute-start.7
  28.3 2.8 %shard_map.85 = f32[5,16,8,128]{3,2,1,0:T(8,128)} custom-call(f32[10,16,8,128]{3,2,1,0:T(8,128)S(1)} %bitcast.10, s32[3,16,8,128]{3,2,1,0:T(8,128)S(1)} %copy-done, f32[15,16,128]{2,1,0:T(8,128)S(1)} %collective-permute-done.near_twin, f32[15,16,128]{2,1,0:T(8,128)S(1)} %collective-permute-done.1.near_other, ...), custom_call_target="tpu_custom_call" | custom-call | flops 2529999872 | bytes 8118000 | tf_op jit(solution)/shard_map/pallas_call | solution.py:824
  31.1 1.9 %collective-permute-done.7.theirs = f32[16,256]{1,0:T(8,128)S(1)} collective-permute-done((f32[16,256]{1,0:T(8,128)S(1)}, f32[16,256]{1,0:T(8,128)S(1)}, u32[]{:S(2)}, u32[]{:S(2)}) %collective-permute-start.7) | collective-permute-done | bytes 16416 | tf_op jit(solution)/shard_map/ppermute | solution.py:817
  33.0 0.7 %shard_map.86 = (f32[16,135]{1,0:T(8,128)}, f32[5,16]{1,0:T(8,128)}) custom-call(f32[16,256]{1,0:T(8,128)S(1)} %add.11.order.mine, f32[16,256]{1,0:T(8,128)S(1)} %collective-permute-done.7.theirs), custom_call_target="tpu_custom_call" | custom-call | flops 575000000 | bytes 1845000 | tf_op jit(solution)/shard_map/pallas_call | solution.py:843
  (5 shorter events, 0.1 us)
Async XLA Ops:
  0.6 1.2 %copy-start = (s32[3,16,8,128]{3,2,1,0:T(8,128)S(1)}, s32[3,16,8,128]{3,2,1,0:T(8,128)}, u32[]{:S(2)}) copy-start(s32[3,16,8,128]{3,2,1,0:T(8,128)} %flags.9) | copy-start | bytes 589828
  4.6 3.5 %copy-start.1 = (f32[16,135]{1,0:T(8,128)S(1)}, f32[16,135]{1,0:T(8,128)}, u32[]{:S(2)}) copy-start(f32[16,135]{1,0:T(8,128)} %kernel.3) | copy-start | bytes 25924
  4.6 3.5 %copy-start.2 = (f32[5,16]{1,0:T(8,128)S(1)}, f32[5,16]{1,0:T(8,128)}, u32[]{:S(2)}) copy-start(f32[5,16]{1,0:T(8,128)} %heads.1) | copy-start | bytes 964
  4.7 8.8 %collective-permute-start = (f32[15,16,128]{2,1,0:T(8,128)S(1)}, f32[15,16,128]{2,1,0:T(8,128)S(1)}, u32[]{:S(2)}, u32[]{:S(2)}) collective-permute-start(f32[15,16,128]{2,1,0:T(8,128)S(1)} %get-tuple-element.29.order), channel_id=1, source_target_pairs={{0,1},{1,0},{2,3},{3,2},{4,5},{5,4},{6,7},{7,6},{8,9},{9,8},{10,11... | collective-permute-start | bytes 368648 | tf_op jit(solution)/shard_map/ppermute | solution.py:776
  4.8 8.7 %collective-permute-start.1 = (f32[15,16,128]{2,1,0:T(8,128)S(1)}, f32[15,16,128]{2,1,0:T(8,128)S(1)}, u32[]{:S(2)}, u32[]{:S(2)}) collective-permute-start(f32[15,16,128]{2,1,0:T(8,128)S(1)} %get-tuple-element.30.order2), channel_id=1, source_target_pairs={{0,15},{1,2},{2,1},{3,4},{4,3},{5,6},{6,5},{7,8},{8,7},{9,10},{10,... | collective-permute-start | bytes 368648 | tf_op jit(solution)/shard_map/ppermute | solution.py:777
  9.4 10.2 %collective-permute-start.3 = (f32[28,16,128]{2,1,0:T(8,128)S(1)}, f32[28,16,128]{2,1,0:T(8,128)S(1)}, u32[]{:S(2)}, u32[]{:S(2)}) collective-permute-start(f32[28,16,128]{2,1,0:T(8,128)S(1)} %get-tuple-element.41), channel_id=1, source_target_pairs={{0,1},{1,0},{2,3},{3,2},{4,5},{5,4},{6,7},{7,6},{8,9},{9,8},{10,11... | collective-permute-start | bytes 688136 | tf_op jit(solution)/shard_map/ppermute | solution.py:799
  9.5 10.1 %collective-permute-start.4 = (f32[28,16,128]{2,1,0:T(8,128)S(1)}, f32[28,16,128]{2,1,0:T(8,128)S(1)}, u32[]{:S(2)}, u32[]{:S(2)}) collective-permute-start(f32[28,16,128]{2,1,0:T(8,128)S(1)} %get-tuple-element.42), channel_id=1, source_target_pairs={{0,15},{1,2},{2,1},{3,4},{4,3},{5,6},{6,5},{7,8},{8,7},{9,10},{10,... | collective-permute-start | bytes 688136 | tf_op jit(solution)/shard_map/ppermute | solution.py:800
  19.5 1.2 %collective-permute-start.2 = (f32[16,256]{1,0:T(8,128)S(1)}, f32[16,256]{1,0:T(8,128)S(1)}, u32[]{:S(2)}, u32[]{:S(2)}) collective-permute-start(f32[16,256]{1,0:T(8,128)S(1)} %get-tuple-element.40.order), channel_id=1, source_target_pairs={{0,1},{1,0},{2,3},{3,2},{4,5},{5,4},{6,7},{7,6},{8,9},{9,8},{10,11... | collective-permute-start | bytes 49160 | tf_op jit(solution)/shard_map/ppermute | solution.py:817
  20.8 3.8 %collective-permute-start.5 = (f32[16,256]{1,0:T(8,128)S(1)}, f32[16,256]{1,0:T(8,128)S(1)}, u32[]{:S(2)}, u32[]{:S(2)}) collective-permute-start(f32[16,256]{1,0:T(8,128)S(1)} %add.9.order), channel_id=1, source_target_pairs={{0,2},{1,3},{2,0},{3,1},{4,6},{5,7},{6,4},{7,5},{8,10},{9,11},{10,... | collective-permute-start | bytes 49160 | tf_op jit(solution)/shard_map/ppermute | solution.py:817
  24.6 3.7 %collective-permute-start.6 = (f32[16,256]{1,0:T(8,128)S(1)}, f32[16,256]{1,0:T(8,128)S(1)}, u32[]{:S(2)}, u32[]{:S(2)}) collective-permute-start(f32[16,256]{1,0:T(8,128)S(1)} %add.10.order), channel_id=1, source_target_pairs={{0,4},{1,5},{2,6},{3,7},{4,0},{5,1},{6,2},{7,3},{8,12},{9,13},{10,... | collective-permute-start | bytes 49160 | tf_op jit(solution)/shard_map/ppermute | solution.py:817
  28.3 4.7 %collective-permute-start.7 = (f32[16,256]{1,0:T(8,128)S(1)}, f32[16,256]{1,0:T(8,128)S(1)}, u32[]{:S(2)}, u32[]{:S(2)}) collective-permute-start(f32[16,256]{1,0:T(8,128)S(1)} %add.11.order.mine), channel_id=1, source_target_pairs={{0,8},{1,9},{2,10},{3,11},{4,12},{5,13},{6,14},{7,15},{8,0},{9,1},... | collective-permute-start | bytes 49160 | tf_op jit(solution)/shard_map/ppermute | solution.py:817

commit v13 on v12

--- a/solution.py
+++ b/solution.py
@@ -543,9 +543,9 @@
 
 
 def c_kernel(
-    fields, near_twin, near_other, kernel, w_rows, w_cols, w_head, bias, t, t_low,
-    own, parts,
-    rim, rim_low, outer, outer_low, acc, edge, gedge,
+    fields, near_twin, near_other, kernel, w_rows, w_head, bias, t, t_low,
+    parts, d_high, d_low,
+    rim, rim_low, outer, outer_low, edge, gedge,
 ):
     _, cot = views(fields)
     nx = cot.shape[1]
@@ -582,7 +582,6 @@
     kept = 8 * ch
     kg = hg = dsum = None
     zeros8 = jnp.zeros((8, 128 * WIDE), F32)
-    written = set()
     for x in range(0, nx, WIDE):
         s_hi = gathered(x, (t, MAIN), (rim, RIM))
         s_lo = gathered(x, (t_low, MAIN), (rim_low, RIM))
@@ -614,12 +613,8 @@
         ).astype(BF16)
         d = (1.0 - hidden * hidden) * jnp.dot(w_head[...], g3, preferred_element_type=F32)
         d_hi, d_lo = split(d)
-        zeros = jnp.zeros((512 - 3 * rows, 128 * WIDE), BF16)
-        back = jnp.dot(
-            w_cols[...],
-            jnp.concatenate([d_hi, d_lo, d_hi, zeros], axis=0),
-            preferred_element_type=F32,
-        )
+        d_high[:, pl.ds(128 * x, 128 * WIDE)] = d_hi
+        d_low[:, pl.ds(128 * x, 128 * WIDE)] = d_lo
         k2 = over_lanes(
             jnp.concatenate([s_hi, s_lo], axis=0),
             jnp.concatenate([d_hi[:kept], d_lo[:kept]], axis=0),
@@ -633,27 +628,6 @@
         for j in range(WIDE):
             level = d[:kept, 128 * j : 128 * (j + 1)]
             dsum = level if dsum is None else dsum + level
-        for m in range(WIDE + 2):
-            total = None
-            for j in range(WIDE):
-                if 0 <= m - j < 3:
-                    q = m - j
-                    piece = back[q * 128 : q * 128 + 120, 128 * j : 128 * (j + 1)]
-                    total = piece if total is None else total + piece
-            here = (x + m - 1) % nx
-            if here in written:
-                total = total + acc[pl.ds(here * 120, 120), :]
-            written.add(here)
-            acc[pl.ds(here * 120, 120), :] = total
-    for x in range(nx):
-        at = x * 120
-        total = (
-            acc[pl.ds(at + 40, 40), :]
-            + pltpu.roll(acc[pl.ds(at, 40), :], 127, 1)
-            + pltpu.roll(acc[pl.ds(at + 80, 40), :], 1, 1)
-        )
-        for v in range(5):
-            own[v, x] = total[8 * v : 8 * v + 8]
 
     sums = jnp.sum(dsum, axis=1, keepdims=True)
     kg = kg.T
@@ -692,6 +666,43 @@
     parts[:, pl.ds(0, n_pick)] = grads[:ch] + grads[ch:]
     parts[:, pl.ds(0, taps)] = parts[:, pl.ds(0, taps)] + level_sum * level_taps((ch, taps))
     parts[:, pl.ds(128, 128)] = parts[:, pl.ds(128, 128)] + pltpu.roll(head_sum * STEP, 16, 1)
+
+
+def c_back_kernel(w_cols, d_high, d_low, order, own, acc):
+    del order
+    nx = own.shape[1]
+    rows = d_high.shape[0]
+    written = set()
+    zeros = jnp.zeros((512 - 3 * rows, 128 * WIDE), BF16)
+    for x in range(0, nx, WIDE):
+        d_hi = d_high[:, pl.ds(128 * x, 128 * WIDE)]
+        d_lo = d_low[:, pl.ds(128 * x, 128 * WIDE)]
+        back = jnp.dot(
+            w_cols[...],
+            jnp.concatenate([d_hi, d_lo, d_hi, zeros], axis=0),
+            preferred_element_type=F32,
+        )
+        for m in range(WIDE + 2):
+            total = None
+            for j in range(WIDE):
+                if 0 <= m - j < 3:
+                    q = m - j
+                    piece = back[q * 128 : q * 128 + 120, 128 * j : 128 * (j + 1)]
+                    total = piece if total is None else total + piece
+            here = (x + m - 1) % nx
+            if here in written:
+                total = total + acc[pl.ds(here * 120, 120), :]
+            written.add(here)
+            acc[pl.ds(here * 120, 120), :] = total
+    for x in range(nx):
+        at = x * 120
+        total = (
+            acc[pl.ds(at + 40, 40), :]
+            + pltpu.roll(acc[pl.ds(at, 40), :], 127, 1)
+            + pltpu.roll(acc[pl.ds(at + 80, 40), :], 1, 1)
+        )
+        for v in range(5):
+            own[v, x] = total[8 * v : 8 * v + 8]
 
 
 def columns(n):
@@ -800,18 +811,22 @@
         lax.ppermute(far_other, "gy", with_other),
     )
     near_rims, patches, first = lax.optimization_barrier((near_rims, patches, first))
-    own, parts = call(
+    w_rows, w_cols, w_head, bias = prepared
+    parts, d_high, d_low = call(
         c_kernel,
-        (full, shape(ch, 256)),
+        (
+            shape(ch, 256),
+            half_shape(10 * ch, nx * nz),
+            half_shape(10 * ch, nx * nz),
+        ),
         [
             *[vm(((nx + 2) * 3 * RIM, nz), BF16)] * 4,
-            vm((nx * 120, nz), F32),
             vm((2 * RIM * nx, nz), F32),
             vm((16 * nx, nz), F32),
         ],
-        6.0,
-        10,
-    )(fields, *near_rims, kernel, *prepared, patches, patches_low)
+        4.2,
+        9,
+    )(fields, *near_rims, kernel, w_rows, w_head, bias, patches, patches_low)
 
     def exchanged(value, bit):
         return lax.ppermute(value, "gy", [(i, i ^ bit) for i in range(count)])
@@ -829,6 +844,9 @@
     got, rim = lax.optimization_barrier((got, rim))
     sums = sums + got
     got = exchanged(sums, bits[-3])
+    own = call(c_back_kernel, full, [vm((nx * 120, nz), F32)], 2.0, 3, 1)(
+        w_cols, d_high, d_low, sums
+    )
     total = yz(0, third, own, sums)
     got, total = lax.optimization_barrier((got, total))
     sums = sums + got

time: 33.9 us -> 32.6 us (0.962)
  waiting for transfers between devices: 5.87 us -> 1.39 us
  starting transfers between devices: 7.57 us -> 10.9 us
    ppermute x4, waiting for transfers between devices: 5.86 us -> 1.38 us  [exchanged(): return lax.ppermute(value, 'gy', [(i, i ^ bit) for i in range(count)])]
    ppermute x4, starting transfers between devices: 0.1 us -> 3.48 us  [exchanged(): return lax.ppermute(value, 'gy', [(i, i ^ bit) for i in range(count)])]
    pallas_call x1 -> x2, Pallas kernels: 6.04 us -> 5.76 us  [the longest x1 4.7 us: body(): call(c_kernel, (shape(ch, 256), half_shape(10 * ch, nx * nz), half_shape(...]
  transfers between devices with their start and end apart: 8 -> 8, of which waited for: 4 -> 3; matrix products, arithmetic and copies ran while one was open for 0% -> 0% of each run, Pallas kernels for 44% -> 45%
where the time goes in v13:
time: 32.6 us; the launch traced here: 32.4 us
  Pallas kernels  18.1 us (56%)
  starting transfers between devices  10.9 us (33%)
  waiting for transfers between devices  1.39 us (4%)
  other arithmetic  1.17 us (4%)
  between operations  0.77 us (2%)
    pallas_call x3, Pallas kernels, body(): call(functools.partial(yz_kernel, lo, hi), full, [vm((lines, nz), F32)] *...  6.36 us
    pallas_call x1, Pallas kernels, body(): call(c_kernel, (shape(ch, 256), half_shape(10 * ch, nx * nz), half_shape(...  4.7 us
    ppermute x1, starting transfers between devices, body(): lax.ppermute(far_other, 'gy', with_other)  4 us
    ppermute x4, starting transfers between devices, exchanged(): return lax.ppermute(value, 'gy', [(i, i ^ bit) for i in range(count)])  3.48 us
    ppermute x1, starting transfers between devices, body(): lax.ppermute(near_other, 'gy', with_other)  3.33 us
    pallas_call x1, Pallas kernels, body(): early = call(x_early_kernel, full, x_scratch, 0.2, 2)(fields, flags)  2.79 us
    ppermute x4, waiting for transfers between devices, exchanged(): return lax.ppermute(value, 'gy', [(i, i ^ bit) for i in range(count)])  1.38 us
    pallas_call x1, Pallas kernels, body(): call(prepare_kernel, (half_shape(20 * ch, COLUMNS), half_shape(384, 512),...  1.19 us
  transfers between devices with their start and end apart: 8, of which 3 were waited for; matrix products, arithmetic and copies ran while one was open for 0% of the time, Pallas kernels for 45%

profile of v13, /device:TPU:0, one launch (start us, length us, event | category | flops | bytes accessed | tf_op | source)
XLA Modules:
  0.0 32.4 jit_solution(4149840394655142928)
XLA Ops:
  0.6 0.0 copy-start
  0.6 1.2 %pad_maximum_fusion.flat = f32[1280,128]{1,0:T(8,128)S(1)} fusion(f32[640,128]{1,0:T(8,128)} %bitcast.12, f32[640,128]{1,0:T(8,128)} %bitcast.13), kind=kLoop, calls=%fused_computation | loop fusion | flops 163840 | bytes 1310720 | tf_op jit(solution)/shard_map/concatenate | solution.py:776
  1.8 0.0 copy-done
  1.8 2.8 %shard_map.76.order.early = f32[5,16,8,128]{3,2,1,0:T(8,128)S(1)} custom-call(f32[10,16,8,128]{3,2,1,0:T(8,128)S(1)} %bitcast.4, s32[3,16,8,128]{3,2,1,0:T(8,128)S(1)} %copy-done), custom_call_target="tpu_custom_call" | custom-call | flops 230000000 | bytes 738000 | tf_op jit(solution)/shard_map/pallas_call | solution.py:784
  4.6 0.0 copy-start.1
  4.6 0.0 copy-start.2
  4.7 0.1 collective-permute-start
  4.8 3.3 %collective-permute-start.1 = (f32[15,16,128]{2,1,0:T(8,128)S(1)}, f32[15,16,128]{2,1,0:T(8,128)S(1)}, u32[]{:S(2)}, u32[]{:S(2)}) collective-permute-start(f32[15,16,128]{2,1,0:T(8,128)S(1)} %get-tuple-element.31.order2), channel_id=1, source_target_pairs={{0,15},{1,2},{2,1},{3,4},{4,3},{5,6},{6,5},{7,8},{8,7},{9,10},{10,... | collective-permute-start | bytes 368648 | tf_op jit(solution)/shard_map/ppermute | solution.py:788
  8.1 0.0 copy-done.1
  8.1 1.2 %shard_map.78 = (bf16[320,720]{1,0:T(8,128)(2,1)S(1)}, bf16[384,512]{1,0:T(8,128)(2,1)S(1)}, bf16[160,192]{1,0:T(8,128)(2,1)S(1)}, f32[160,128]{1,0:T(8,128)S(1)...) custom-call(f32[10,16,8,128]{3,2,1,0:T(8,128)S(1)} %bitcast.5, f32[16,135]{1,0:T(8,128)S(1)} %copy-done.1, ...), custom_call_target="tpu_custom_call" | custom-call | flops 1724999936 | bytes 5535000 | tf_op jit(solution)/shard_map/pallas_call | solution.py:790
  9.3 0.1 shard_map.81
  9.4 0.1 collective-permute-start.3
  9.5 4.0 %collective-permute-start.4 = (f32[28,16,128]{2,1,0:T(8,128)S(1)}, f32[28,16,128]{2,1,0:T(8,128)S(1)}, u32[]{:S(2)}, u32[]{:S(2)}) collective-permute-start(f32[28,16,128]{2,1,0:T(8,128)S(1)} %get-tuple-element.42), channel_id=1, source_target_pairs={{0,15},{1,2},{2,1},{3,4},{4,3},{5,6},{6,5},{7,8},{8,7},{9,10},{10,... | collective-permute-start | bytes 688136 | tf_op jit(solution)/shard_map/ppermute | solution.py:811
  13.5 0.0 collective-permute-done.near_twin
  13.5 0.0 collective-permute-done.1.near_other
  13.5 4.7 %shard_map.80 = (f32[16,256]{1,0:T(8,128)S(1)}, bf16[160,2048]{1,0:T(8,128)(2,1)S(1)}, bf16[160,2048]{1,0:T(8,128)(2,1)S(1)}) custom-call(f32[10,16,8,128]{3,2,1,0:T(8,128)S(1)} %bitcast.7, f32[15,16,128]{2,1,0:T(8,128)S(1)} %collective-permute-done.near_twin, f32[15,16,128]{2,1,0:T(8,128)S(1)} %collective-permute-done.1.near_other, ...), custom_call_target="tpu_custom_call" | custom-call | flops 4830000128 | bytes 15498000 | tf_op jit(solution)/shard_map/pallas_call | solution.py:815
  18.2 0.1 collective-permute-start.2
  18.3 0.0 collective-permute-done.3.far_twin
  18.3 0.0 collective-permute-done.4.far_other
  18.3 1.1 %shard_map.82.rim = f32[640,128]{1,0:T(8,128)S(1)} custom-call(f32[1280,128]{1,0:T(8,128)S(1)} %pad_maximum_fusion.flat, f32[15,16,128]{2,1,0:T(8,128)S(1)} %collective-permute-done.near_twin, f32[15,16,128]{2,1,0:T(8,128)S(1)} %collective-permute-done.1.near_other, f32[28,16,128]{2,1,0:T(8,128)S(1)} %collective-permute-done.3.far_twin, ...), custom_call_target="tpu_custom_call" | custom-call | flops 1264999936 | bytes 4059000 | tf_op jit(solution)/shard_map/pallas_call | solution.py:843
  19.4 0.1 collective-permute-done.2
  19.5 0.8 %collective-permute-start.5 = (f32[16,256]{1,0:T(8,128)S(1)}, f32[16,256]{1,0:T(8,128)S(1)}, u32[]{:S(2)}, u32[]{:S(2)}) collective-permute-start(f32[16,256]{1,0:T(8,128)S(1)} %add.9.order), channel_id=1, source_target_pairs={{0,2},{1,3},{2,0},{3,1},{4,6},{5,7},{6,4},{7,5},{8,10},{9,11},{10,... | collective-permute-start | bytes 49160 | tf_op jit(solution)/shard_map/ppermute | solution.py:832
  20.2 1.1 %shard_map.83.before = f32[5,16,8,128]{3,2,1,0:T(8,128)S(1)} custom-call(bf16[384,512]{1,0:T(8,128)(2,1)S(1)} %get-tuple-element.45.w_cols, bf16[160,2048]{1,0:T(8,128)(2,1)S(1)} %get-tuple-element.46.d_high, bf16[160,2048]{1,0:T(8,128)(2,1)S(1)} %get-tuple-element.47.d_low, f32[16,256]{1,0:T(8,128)S(1)} %add.9.order), custom_call_target="tpu_custom_call" | custom-call | flops 2300000000 | bytes 7380000 | tf_op jit(solution)/shard_map/pallas_call | solution.py:847
  21.3 1.4 %shard_map.84.before = f32[5,16,8,128]{3,2,1,0:T(8,128)S(1)} custom-call(f32[10,16,8,128]{3,2,1,0:T(8,128)S(1)} %bitcast.8, s32[3,16,8,128]{3,2,1,0:T(8,128)S(1)} %copy-done, f32[15,16,128]{2,1,0:T(8,128)S(1)} %collective-permute-done.near_twin, f32[15,16,128]{2,1,0:T(8,128)S(1)} %collective-permute-done.1.near_other, ...), custom_call_target="tpu_custom_call" | custom-call | flops 2529999872 | bytes 8118000 | tf_op jit(solution)/shard_map/pallas_call | solution.py:839
  22.7 0.5 %collective-permute-done.5 = f32[16,256]{1,0:T(8,128)S(1)} collective-permute-done((f32[16,256]{1,0:T(8,128)S(1)}, f32[16,256]{1,0:T(8,128)S(1)}, u32[]{:S(2)}, u32[]{:S(2)}) %collective-permute-start.5) | collective-permute-done | bytes 16416 | tf_op jit(solution)/shard_map/ppermute | solution.py:832
  23.2 0.8 %collective-permute-start.6 = (f32[16,256]{1,0:T(8,128)S(1)}, f32[16,256]{1,0:T(8,128)S(1)}, u32[]{:S(2)}, u32[]{:S(2)}) collective-permute-start(f32[16,256]{1,0:T(8,128)S(1)} %add.10.order), channel_id=1, source_target_pairs={{0,4},{1,5},{2,6},{3,7},{4,0},{5,1},{6,2},{7,3},{8,12},{9,13},{10,... | collective-permute-start | bytes 49160 | tf_op jit(solution)/shard_map/ppermute | solution.py:832
  24.1 2.1 %shard_map.85.before = f32[5,16,8,128]{3,2,1,0:T(8,128)S(1)} custom-call(f32[10,16,8,128]{3,2,1,0:T(8,128)S(1)} %bitcast.9, s32[3,16,8,128]{3,2,1,0:T(8,128)S(1)} %copy-done, f32[15,16,128]{2,1,0:T(8,128)S(1)} %collective-permute-done.near_twin, f32[15,16,128]{2,1,0:T(8,128)S(1)} %collective-permute-done.1.near_other, ...), custom_call_target="tpu_custom_call" | custom-call | flops 2529999872 | bytes 8118000 | tf_op jit(solution)/shard_map/pallas_call | solution.py:839
  26.2 0.8 %collective-permute-done.6 = f32[16,256]{1,0:T(8,128)S(1)} collective-permute-done((f32[16,256]{1,0:T(8,128)S(1)}, f32[16,256]{1,0:T(8,128)S(1)}, u32[]{:S(2)}, u32[]{:S(2)}) %collective-permute-start.6) | collective-permute-done | bytes 16416 | tf_op jit(solution)/shard_map/ppermute | solution.py:832
  27.0 1.8 %collective-permute-start.7 = (f32[16,256]{1,0:T(8,128)S(1)}, f32[16,256]{1,0:T(8,128)S(1)}, u32[]{:S(2)}, u32[]{:S(2)}) collective-permute-start(f32[16,256]{1,0:T(8,128)S(1)} %add.11.order.mine), channel_id=1, source_target_pairs={{0,8},{1,9},{2,10},{3,11},{4,12},{5,13},{6,14},{7,15},{8,0},{9,1},... | collective-permute-start | bytes 49160 | tf_op jit(solution)/shard_map/ppermute | solution.py:832
  28.8 2.8 %shard_map.86 = f32[5,16,8,128]{3,2,1,0:T(8,128)} custom-call(f32[10,16,8,128]{3,2,1,0:T(8,128)S(1)} %bitcast.10, s32[3,16,8,128]{3,2,1,0:T(8,128)S(1)} %copy-done, f32[15,16,128]{2,1,0:T(8,128)S(1)} %collective-permute-done.near_twin, f32[15,16,128]{2,1,0:T(8,128)S(1)} %collective-permute-done.1.near_other, ...), custom_call_target="tpu_custom_call" | custom-call | flops 2529999872 | bytes 8118000 | tf_op jit(solution)/shard_map/pallas_call | solution.py:839
  31.6 0.0 collective-permute-done.7.theirs
  31.6 0.7 %shard_map.87 = (f32[16,135]{1,0:T(8,128)}, f32[5,16]{1,0:T(8,128)}) custom-call(f32[16,256]{1,0:T(8,128)S(1)} %add.11.order.mine, f32[16,256]{1,0:T(8,128)S(1)} %collective-permute-done.7.theirs), custom_call_target="tpu_custom_call" | custom-call | flops 575000000 | bytes 1845000 | tf_op jit(solution)/shard_map/pallas_call | solution.py:861
  (6 shorter events, 0.1 us)
Async XLA Ops:
  0.6 1.2 %copy-start = (s32[3,16,8,128]{3,2,1,0:T(8,128)S(1)}, s32[3,16,8,128]{3,2,1,0:T(8,128)}, u32[]{:S(2)}) copy-start(s32[3,16,8,128]{3,2,1,0:T(8,128)} %flags.9) | copy-start | bytes 589828
  4.6 3.5 %copy-start.1 = (f32[16,135]{1,0:T(8,128)S(1)}, f32[16,135]{1,0:T(8,128)}, u32[]{:S(2)}) copy-start(f32[16,135]{1,0:T(8,128)} %kernel.3) | copy-start | bytes 25924
  4.6 3.5 %copy-start.2 = (f32[5,16]{1,0:T(8,128)S(1)}, f32[5,16]{1,0:T(8,128)}, u32[]{:S(2)}) copy-start(f32[5,16]{1,0:T(8,128)} %heads.1) | copy-start | bytes 964
  4.7 8.8 %collective-permute-start = (f32[15,16,128]{2,1,0:T(8,128)S(1)}, f32[15,16,128]{2,1,0:T(8,128)S(1)}, u32[]{:S(2)}, u32[]{:S(2)}) collective-permute-start(f32[15,16,128]{2,1,0:T(8,128)S(1)} %get-tuple-element.30.order), channel_id=1, source_target_pairs={{0,1},{1,0},{2,3},{3,2},{4,5},{5,4},{6,7},{7,6},{8,9},{9,8},{10,11... | collective-permute-start | bytes 368648 | tf_op jit(solution)/shard_map/ppermute | solution.py:787
  4.8 8.7 %collective-permute-start.1 = (f32[15,16,128]{2,1,0:T(8,128)S(1)}, f32[15,16,128]{2,1,0:T(8,128)S(1)}, u32[]{:S(2)}, u32[]{:S(2)}) collective-permute-start(f32[15,16,128]{2,1,0:T(8,128)S(1)} %get-tuple-element.31.order2), channel_id=1, source_target_pairs={{0,15},{1,2},{2,1},{3,4},{4,3},{5,6},{6,5},{7,8},{8,7},{9,10},{10,... | collective-permute-start | bytes 368648 | tf_op jit(solution)/shard_map/ppermute | solution.py:788
  9.4 8.9 %collective-permute-start.3 = (f32[28,16,128]{2,1,0:T(8,128)S(1)}, f32[28,16,128]{2,1,0:T(8,128)S(1)}, u32[]{:S(2)}, u32[]{:S(2)}) collective-permute-start(f32[28,16,128]{2,1,0:T(8,128)S(1)} %get-tuple-element.41), channel_id=1, source_target_pairs={{0,1},{1,0},{2,3},{3,2},{4,5},{5,4},{6,7},{7,6},{8,9},{9,8},{10,11... | collective-permute-start | bytes 688136 | tf_op jit(solution)/shard_map/ppermute | solution.py:810
  9.5 8.8 %collective-permute-start.4 = (f32[28,16,128]{2,1,0:T(8,128)S(1)}, f32[28,16,128]{2,1,0:T(8,128)S(1)}, u32[]{:S(2)}, u32[]{:S(2)}) collective-permute-start(f32[28,16,128]{2,1,0:T(8,128)S(1)} %get-tuple-element.42), channel_id=1, source_target_pairs={{0,15},{1,2},{2,1},{3,4},{4,3},{5,6},{6,5},{7,8},{8,7},{9,10},{10,... | collective-permute-start | bytes 688136 | tf_op jit(solution)/shard_map/ppermute | solution.py:811
  18.2 1.2 %collective-permute-start.2 = (f32[16,256]{1,0:T(8,128)S(1)}, f32[16,256]{1,0:T(8,128)S(1)}, u32[]{:S(2)}, u32[]{:S(2)}) collective-permute-start(f32[16,256]{1,0:T(8,128)S(1)} %get-tuple-element.40.order), channel_id=1, source_target_pairs={{0,1},{1,0},{2,3},{3,2},{4,5},{5,4},{6,7},{7,6},{8,9},{9,8},{10,11... | collective-permute-start | bytes 49160 | tf_op jit(solution)/shard_map/ppermute | solution.py:832
  19.5 3.8 %collective-permute-start.5 = (f32[16,256]{1,0:T(8,128)S(1)}, f32[16,256]{1,0:T(8,128)S(1)}, u32[]{:S(2)}, u32[]{:S(2)}) collective-permute-start(f32[16,256]{1,0:T(8,128)S(1)} %add.9.order), channel_id=1, source_target_pairs={{0,2},{1,3},{2,0},{3,1},{4,6},{5,7},{6,4},{7,5},{8,10},{9,11},{10,... | collective-permute-start | bytes 49160 | tf_op jit(solution)/shard_map/ppermute | solution.py:832
  23.2 3.7 %collective-permute-start.6 = (f32[16,256]{1,0:T(8,128)S(1)}, f32[16,256]{1,0:T(8,128)S(1)}, u32[]{:S(2)}, u32[]{:S(2)}) collective-permute-start(f32[16,256]{1,0:T(8,128)S(1)} %add.10.order), channel_id=1, source_target_pairs={{0,4},{1,5},{2,6},{3,7},{4,0},{5,1},{6,2},{7,3},{8,12},{9,13},{10,... | collective-permute-start | bytes 49160 | tf_op jit(solution)/shard_map/ppermute | solution.py:832
  27.0 4.7 %collective-permute-start.7 = (f32[16,256]{1,0:T(8,128)S(1)}, f32[16,256]{1,0:T(8,128)S(1)}, u32[]{:S(2)}, u32[]{:S(2)}) collective-permute-start(f32[16,256]{1,0:T(8,128)S(1)} %add.11.order.mine), channel_id=1, source_target_pairs={{0,8},{1,9},{2,10},{3,11},{4,12},{5,13},{6,14},{7,15},{8,0},{9,1},... | collective-permute-start | bytes 49160 | tf_op jit(solution)/shard_map/ppermute | solution.py:832

commit v14 on v13

--- a/solution.py
+++ b/solution.py
@@ -840,13 +840,13 @@
         functools.partial(yz_kernel, lo, hi), full, [vm((lines, nz), F32)] * 2, 2.2, 9, 1
     )(fields, flags, *near_rims, *far_rims, first, before, rim, order)
     got = exchanged(sums, bits[-4])
-    rim = call(e_kernel, shape(lines, nz), [], 1.1, 5, 1)(flat, *near_rims, *far_rims, sums)
-    got, rim = lax.optimization_barrier((got, rim))
+    own = call(c_back_kernel, full, [vm((nx * 120, nz), F32)], 1.1, 3, 1)(
+        w_cols, d_high, d_low, sums
+    )
+    got, own = lax.optimization_barrier((got, own))
     sums = sums + got
     got = exchanged(sums, bits[-3])
-    own = call(c_back_kernel, full, [vm((nx * 120, nz), F32)], 2.0, 3, 1)(
-        w_cols, d_high, d_low, sums
-    )
+    rim = call(e_kernel, shape(lines, nz), [], 1.1, 5, 1)(flat, *near_rims, *far_rims, sums)
     total = yz(0, third, own, sums)
     got, total = lax.optimization_barrier((got, total))
     sums = sums + got

time: 32.6 us -> 32.6 us (level)
  waiting for transfers between devices: 1.39 us -> 4.42 us
  starting transfers between devices: 10.9 us -> 7.94 us
    ppermute x4, waiting for transfers between devices: 1.38 us -> 4.41 us  [exchanged(): return lax.ppermute(value, 'gy', [(i, i ^ bit) for i in range(count)])]
    ppermute x4, starting transfers between devices: 3.48 us -> 0.47 us  [exchanged(): return lax.ppermute(value, 'gy', [(i, i ^ bit) for i in range(count)])]
  transfers between devices with their start and end apart: 8 -> 8, of which waited for: 3 -> 4; matrix products, arithmetic and copies ran while one was open for 0% -> 0% of each run, Pallas kernels for 45% -> 45%
where the time goes in v14:
time: 32.6 us; the launch traced here: 32.4 us
  Pallas kernels  18.1 us (56%)
  starting transfers between devices  7.94 us (24%)
  waiting for transfers between devices  4.42 us (14%)
  other arithmetic  1.17 us (4%)
  between operations  0.77 us (2%)
    pallas_call x3, Pallas kernels, body(): call(functools.partial(yz_kernel, lo, hi), full, [vm((lines, nz), F32)] *...  6.36 us
    pallas_call x1, Pallas kernels, body(): call(c_kernel, (shape(ch, 256), half_shape(10 * ch, nx * nz), half_shape(...  4.72 us
    ppermute x4, waiting for transfers between devices, exchanged(): return lax.ppermute(value, 'gy', [(i, i ^ bit) for i in range(count)])  4.41 us
    ppermute x1, starting transfers between devices, body(): lax.ppermute(far_other, 'gy', with_other)  4 us
    ppermute x1, starting transfers between devices, body(): lax.ppermute(near_other, 'gy', with_other)  3.33 us
    pallas_call x1, Pallas kernels, body(): early = call(x_early_kernel, full, x_scratch, 0.2, 2)(fields, flags)  2.79 us
    pallas_call x1, Pallas kernels, body(): call(prepare_kernel, (half_shape(20 * ch, COLUMNS), half_shape(384, 512),...  1.19 us
    concatenate x1, other arithmetic, body(): flat = jnp.concatenate([state.reshape(lines, nz), cot.reshape(lines, nz)])  1.15 us
  transfers between devices with their start and end apart: 8, of which 4 were waited for; matrix products, arithmetic and copies ran while one was open for 0% of the time, Pallas kernels for 45%

profile of v14, /device:TPU:0, one launch (start us, length us, event | category | flops | bytes accessed | tf_op | source)
XLA Modules:
  0.0 32.4 jit_solution(11212084745501607854)
XLA Ops:
  0.6 0.0 copy-start
  0.6 1.2 %pad_maximum_fusion.flat = f32[1280,128]{1,0:T(8,128)S(1)} fusion(f32[640,128]{1,0:T(8,128)} %bitcast.12, f32[640,128]{1,0:T(8,128)} %bitcast.13), kind=kLoop, calls=%fused_computation | loop fusion | flops 163840 | bytes 1310720 | tf_op jit(solution)/shard_map/concatenate | solution.py:776
  1.8 0.0 copy-done
  1.8 2.8 %shard_map.76.order.early = f32[5,16,8,128]{3,2,1,0:T(8,128)S(1)} custom-call(f32[10,16,8,128]{3,2,1,0:T(8,128)S(1)} %bitcast.4, s32[3,16,8,128]{3,2,1,0:T(8,128)S(1)} %copy-done), custom_call_target="tpu_custom_call" | custom-call | flops 230000000 | bytes 738000 | tf_op jit(solution)/shard_map/pallas_call | solution.py:784
  4.6 0.0 copy-start.1
  4.6 0.0 copy-start.2
  4.7 0.1 collective-permute-start
  4.8 3.3 %collective-permute-start.1 = (f32[15,16,128]{2,1,0:T(8,128)S(1)}, f32[15,16,128]{2,1,0:T(8,128)S(1)}, u32[]{:S(2)}, u32[]{:S(2)}) collective-permute-start(f32[15,16,128]{2,1,0:T(8,128)S(1)} %get-tuple-element.31.order2), channel_id=1, source_target_pairs={{0,15},{1,2},{2,1},{3,4},{4,3},{5,6},{6,5},{7,8},{8,7},{9,10},{10,... | collective-permute-start | bytes 368648 | tf_op jit(solution)/shard_map/ppermute | solution.py:788
  8.1 0.0 copy-done.1
  8.1 1.2 %shard_map.78 = (bf16[320,720]{1,0:T(8,128)(2,1)S(1)}, bf16[384,512]{1,0:T(8,128)(2,1)S(1)}, bf16[160,192]{1,0:T(8,128)(2,1)S(1)}, f32[160,128]{1,0:T(8,128)S(1)...) custom-call(f32[10,16,8,128]{3,2,1,0:T(8,128)S(1)} %bitcast.5, f32[16,135]{1,0:T(8,128)S(1)} %copy-done.1, ...), custom_call_target="tpu_custom_call" | custom-call | flops 1724999936 | bytes 5535000 | tf_op jit(solution)/shard_map/pallas_call | solution.py:790
  9.3 0.1 shard_map.82
  9.4 0.1 collective-permute-start.4
  9.5 4.0 %collective-permute-start.5 = (f32[28,16,128]{2,1,0:T(8,128)S(1)}, f32[28,16,128]{2,1,0:T(8,128)S(1)}, u32[]{:S(2)}, u32[]{:S(2)}) collective-permute-start(f32[28,16,128]{2,1,0:T(8,128)S(1)} %get-tuple-element.46), channel_id=1, source_target_pairs={{0,15},{1,2},{2,1},{3,4},{4,3},{5,6},{6,5},{7,8},{8,7},{9,10},{10,... | collective-permute-start | bytes 688136 | tf_op jit(solution)/shard_map/ppermute | solution.py:811
  13.5 0.0 collective-permute-done.near_twin
  13.5 0.0 collective-permute-done.1.near_other
  13.5 4.7 %shard_map.80 = (f32[16,256]{1,0:T(8,128)S(1)}, bf16[160,2048]{1,0:T(8,128)(2,1)S(1)}, bf16[160,2048]{1,0:T(8,128)(2,1)S(1)}) custom-call(f32[10,16,8,128]{3,2,1,0:T(8,128)S(1)} %bitcast.7, f32[15,16,128]{2,1,0:T(8,128)S(1)} %collective-permute-done.near_twin, f32[15,16,128]{2,1,0:T(8,128)S(1)} %collective-permute-done.1.near_other, ...), custom_call_target="tpu_custom_call" | custom-call | flops 4830000128 | bytes 15498000 | tf_op jit(solution)/shard_map/pallas_call | solution.py:815
  18.2 0.1 collective-permute-start.2
  18.3 1.1 %shard_map.81.before = f32[5,16,8,128]{3,2,1,0:T(8,128)S(1)} custom-call(bf16[384,512]{1,0:T(8,128)(2,1)S(1)} %get-tuple-element.41.w_cols, bf16[160,2048]{1,0:T(8,128)(2,1)S(1)} %get-tuple-element.42.d_high, bf16[160,2048]{1,0:T(8,128)(2,1)S(1)} %get-tuple-element.43.d_low, f32[16,256]{1,0:T(8,128)S(1)} %get-tuple-element.40.order), custom_call_target="tpu_custom_call" | custom-call | flops 1264999936 | bytes 4059000 | tf_op jit(solution)/shard_map/pallas_call | solution.py:843
  19.4 0.1 collective-permute-done.2
  19.5 0.0 collective-permute-start.3
  19.5 0.0 collective-permute-done.4.far_twin
  19.5 0.0 collective-permute-done.5.far_other
  19.5 1.1 %shard_map.83.rim = f32[640,128]{1,0:T(8,128)S(1)} custom-call(f32[1280,128]{1,0:T(8,128)S(1)} %pad_maximum_fusion.flat, f32[15,16,128]{2,1,0:T(8,128)S(1)} %collective-permute-done.near_twin, f32[15,16,128]{2,1,0:T(8,128)S(1)} %collective-permute-done.1.near_other, f32[28,16,128]{2,1,0:T(8,128)S(1)} %collective-permute-done.4.far_twin, ...), custom_call_target="tpu_custom_call" | custom-call | flops 1264999936 | bytes 4059000 | tf_op jit(solution)/shard_map/pallas_call | solution.py:849
  20.6 1.4 %shard_map.84.before = f32[5,16,8,128]{3,2,1,0:T(8,128)S(1)} custom-call(f32[10,16,8,128]{3,2,1,0:T(8,128)S(1)} %bitcast.8, s32[3,16,8,128]{3,2,1,0:T(8,128)S(1)} %copy-done, f32[15,16,128]{2,1,0:T(8,128)S(1)} %collective-permute-done.near_twin, f32[15,16,128]{2,1,0:T(8,128)S(1)} %collective-permute-done.1.near_other, ...), custom_call_target="tpu_custom_call" | custom-call | flops 2529999872 | bytes 8118000 | tf_op jit(solution)/shard_map/pallas_call | solution.py:839
  22.0 1.2 %collective-permute-done.3 = f32[16,256]{1,0:T(8,128)S(1)} collective-permute-done((f32[16,256]{1,0:T(8,128)S(1)}, f32[16,256]{1,0:T(8,128)S(1)}, u32[]{:S(2)}, u32[]{:S(2)}) %collective-permute-start.3) | collective-permute-done | bytes 16416 | tf_op jit(solution)/shard_map/ppermute | solution.py:832
  23.2 0.0 collective-permute-start.6
  23.2 2.1 %shard_map.85.before = f32[5,16,8,128]{3,2,1,0:T(8,128)S(1)} custom-call(f32[10,16,8,128]{3,2,1,0:T(8,128)S(1)} %bitcast.9, s32[3,16,8,128]{3,2,1,0:T(8,128)S(1)} %copy-done, f32[15,16,128]{2,1,0:T(8,128)S(1)} %collective-permute-done.near_twin, f32[15,16,128]{2,1,0:T(8,128)S(1)} %collective-permute-done.1.near_other, ...), custom_call_target="tpu_custom_call" | custom-call | flops 2529999872 | bytes 8118000 | tf_op jit(solution)/shard_map/pallas_call | solution.py:839
  25.3 1.6 %collective-permute-done.6 = f32[16,256]{1,0:T(8,128)S(1)} collective-permute-done((f32[16,256]{1,0:T(8,128)S(1)}, f32[16,256]{1,0:T(8,128)S(1)}, u32[]{:S(2)}, u32[]{:S(2)}) %collective-permute-start.6) | collective-permute-done | bytes 16416 | tf_op jit(solution)/shard_map/ppermute | solution.py:832
  27.0 0.4 %collective-permute-start.7 = (f32[16,256]{1,0:T(8,128)S(1)}, f32[16,256]{1,0:T(8,128)S(1)}, u32[]{:S(2)}, u32[]{:S(2)}) collective-permute-start(f32[16,256]{1,0:T(8,128)S(1)} %add.11.order.mine), channel_id=1, source_target_pairs={{0,8},{1,9},{2,10},{3,11},{4,12},{5,13},{6,14},{7,15},{8,0},{9,1},... | collective-permute-start | bytes 49160 | tf_op jit(solution)/shard_map/ppermute | solution.py:832
  27.4 2.8 %shard_map.86 = f32[5,16,8,128]{3,2,1,0:T(8,128)} custom-call(f32[10,16,8,128]{3,2,1,0:T(8,128)S(1)} %bitcast.10, s32[3,16,8,128]{3,2,1,0:T(8,128)S(1)} %copy-done, f32[15,16,128]{2,1,0:T(8,128)S(1)} %collective-permute-done.near_twin, f32[15,16,128]{2,1,0:T(8,128)S(1)} %collective-permute-done.1.near_other, ...), custom_call_target="tpu_custom_call" | custom-call | flops 2529999872 | bytes 8118000 | tf_op jit(solution)/shard_map/pallas_call | solution.py:839
  30.2 1.5 %collective-permute-done.7.theirs = f32[16,256]{1,0:T(8,128)S(1)} collective-permute-done((f32[16,256]{1,0:T(8,128)S(1)}, f32[16,256]{1,0:T(8,128)S(1)}, u32[]{:S(2)}, u32[]{:S(2)}) %collective-permute-start.7) | collective-permute-done | bytes 16416 | tf_op jit(solution)/shard_map/ppermute | solution.py:832
  31.7 0.7 %shard_map.87 = (f32[16,135]{1,0:T(8,128)}, f32[5,16]{1,0:T(8,128)}) custom-call(f32[16,256]{1,0:T(8,128)S(1)} %add.11.order.mine, f32[16,256]{1,0:T(8,128)S(1)} %collective-permute-done.7.theirs), custom_call_target="tpu_custom_call" | custom-call | flops 575000000 | bytes 1845000 | tf_op jit(solution)/shard_map/pallas_call | solution.py:861
  (6 shorter events, 0.1 us)
Async XLA Ops:
  0.6 1.2 %copy-start = (s32[3,16,8,128]{3,2,1,0:T(8,128)S(1)}, s32[3,16,8,128]{3,2,1,0:T(8,128)}, u32[]{:S(2)}) copy-start(s32[3,16,8,128]{3,2,1,0:T(8,128)} %flags.9) | copy-start | bytes 589828
  4.6 3.5 %copy-start.1 = (f32[16,135]{1,0:T(8,128)S(1)}, f32[16,135]{1,0:T(8,128)}, u32[]{:S(2)}) copy-start(f32[16,135]{1,0:T(8,128)} %kernel.3) | copy-start | bytes 25924
  4.6 3.5 %copy-start.2 = (f32[5,16]{1,0:T(8,128)S(1)}, f32[5,16]{1,0:T(8,128)}, u32[]{:S(2)}) copy-start(f32[5,16]{1,0:T(8,128)} %heads.1) | copy-start | bytes 964
  4.7 8.8 %collective-permute-start = (f32[15,16,128]{2,1,0:T(8,128)S(1)}, f32[15,16,128]{2,1,0:T(8,128)S(1)}, u32[]{:S(2)}, u32[]{:S(2)}) collective-permute-start(f32[15,16,128]{2,1,0:T(8,128)S(1)} %get-tuple-element.30.order), channel_id=1, source_target_pairs={{0,1},{1,0},{2,3},{3,2},{4,5},{5,4},{6,7},{7,6},{8,9},{9,8},{10,11... | collective-permute-start | bytes 368648 | tf_op jit(solution)/shard_map/ppermute | solution.py:787
  4.8 8.7 %collective-permute-start.1 = (f32[15,16,128]{2,1,0:T(8,128)S(1)}, f32[15,16,128]{2,1,0:T(8,128)S(1)}, u32[]{:S(2)}, u32[]{:S(2)}) collective-permute-start(f32[15,16,128]{2,1,0:T(8,128)S(1)} %get-tuple-element.31.order2), channel_id=1, source_target_pairs={{0,15},{1,2},{2,1},{3,4},{4,3},{5,6},{6,5},{7,8},{8,7},{9,10},{10,... | collective-permute-start | bytes 368648 | tf_op jit(solution)/shard_map/ppermute | solution.py:788
  9.4 10.1 %collective-permute-start.4 = (f32[28,16,128]{2,1,0:T(8,128)S(1)}, f32[28,16,128]{2,1,0:T(8,128)S(1)}, u32[]{:S(2)}, u32[]{:S(2)}) collective-permute-start(f32[28,16,128]{2,1,0:T(8,128)S(1)} %get-tuple-element.45), channel_id=1, source_target_pairs={{0,1},{1,0},{2,3},{3,2},{4,5},{5,4},{6,7},{7,6},{8,9},{9,8},{10,11... | collective-permute-start | bytes 688136 | tf_op jit(solution)/shard_map/ppermute | solution.py:810
  9.5 10.0 %collective-permute-start.5 = (f32[28,16,128]{2,1,0:T(8,128)S(1)}, f32[28,16,128]{2,1,0:T(8,128)S(1)}, u32[]{:S(2)}, u32[]{:S(2)}) collective-permute-start(f32[28,16,128]{2,1,0:T(8,128)S(1)} %get-tuple-element.46), channel_id=1, source_target_pairs={{0,15},{1,2},{2,1},{3,4},{4,3},{5,6},{6,5},{7,8},{8,7},{9,10},{10,... | collective-permute-start | bytes 688136 | tf_op jit(solution)/shard_map/ppermute | solution.py:811
  18.2 1.2 %collective-permute-start.2 = (f32[16,256]{1,0:T(8,128)S(1)}, f32[16,256]{1,0:T(8,128)S(1)}, u32[]{:S(2)}, u32[]{:S(2)}) collective-permute-start(f32[16,256]{1,0:T(8,128)S(1)} %get-tuple-element.40.order), channel_id=1, source_target_pairs={{0,1},{1,0},{2,3},{3,2},{4,5},{5,4},{6,7},{7,6},{8,9},{9,8},{10,11... | collective-permute-start | bytes 49160 | tf_op jit(solution)/shard_map/ppermute | solution.py:832
  19.5 3.7 %collective-permute-start.3 = (f32[16,256]{1,0:T(8,128)S(1)}, f32[16,256]{1,0:T(8,128)S(1)}, u32[]{:S(2)}, u32[]{:S(2)}) collective-permute-start(f32[16,256]{1,0:T(8,128)S(1)} %add.9.order), channel_id=1, source_target_pairs={{0,2},{1,3},{2,0},{3,1},{4,6},{5,7},{6,4},{7,5},{8,10},{9,11},{10,... | collective-permute-start | bytes 49160 | tf_op jit(solution)/shard_map/ppermute | solution.py:832
  23.2 3.7 %collective-permute-start.6 = (f32[16,256]{1,0:T(8,128)S(1)}, f32[16,256]{1,0:T(8,128)S(1)}, u32[]{:S(2)}, u32[]{:S(2)}) collective-permute-start(f32[16,256]{1,0:T(8,128)S(1)} %add.10.order), channel_id=1, source_target_pairs={{0,4},{1,5},{2,6},{3,7},{4,0},{5,1},{6,2},{7,3},{8,12},{9,13},{10,... | collective-permute-start | bytes 49160 | tf_op jit(solution)/shard_map/ppermute | solution.py:832
  27.0 4.7 %collective-permute-start.7 = (f32[16,256]{1,0:T(8,128)S(1)}, f32[16,256]{1,0:T(8,128)S(1)}, u32[]{:S(2)}, u32[]{:S(2)}) collective-permute-start(f32[16,256]{1,0:T(8,128)S(1)} %add.11.order.mine), channel_id=1, source_target_pairs={{0,8},{1,9},{2,10},{3,11},{4,12},{5,13},{6,14},{7,15},{8,0},{9,1},... | collective-permute-start | bytes 49160 | tf_op jit(solution)/shard_map/ppermute | solution.py:832

commit v15 on v14

--- a/solution.py
+++ b/solution.py
@@ -249,7 +249,7 @@
     return state, cot, flags
 
 
-def x_faces(fields, flags, out, pad, gpad, acc):
+def x_faces(lo, hi, fields, flags, acc, pad, gpad):
     state, cot = views(fields)
     nx = state.shape[1]
     for v in range(5):
@@ -258,10 +258,9 @@
         pad[v, pl.ds(nx + 2, 3)] = state[v, pl.ds(0, 3)]
         gpad[v, pl.ds(0, nx)] = cot[v]
         gpad[v, pl.ds(nx, 1)] = cot[v, pl.ds(0, 1)]
-    acc[...] = jnp.zeros_like(acc)
 
     def step(i, carry):
-        x = i * SLABS
+        x = lo + i * SLABS
         cells = [[pad[v, pl.ds(x + k, SLABS)] for k in range(6)] for v in range(5)]
         g = [gpad[v, pl.ds(x, SLABS)] for v in range(5)]
         face = [STEP * (gpad[v, pl.ds(x + 1, SLABS)] - g[v]) for v in range(5)]
@@ -278,23 +277,37 @@
                 acc[v, x + s] = acc[v, x + s] + total
         return carry
 
-    lax.fori_loop(0, nx // SLABS, step, 0)
+    lax.fori_loop(0, (hi - lo) // SLABS, step, 0)
+
+
+def fold_rim(acc, out):
+    nx = out.shape[1]
     for v in range(5):
         acc[v, pl.ds(nx, 2)] = acc[v, pl.ds(nx, 2)] + acc[v, pl.ds(0, 2)]
         acc[v, pl.ds(2, 3)] = acc[v, pl.ds(2, 3)] + acc[v, pl.ds(nx + 2, 3)]
-
-    for v in range(5):
         out[v] = acc[v, pl.ds(2, nx)]
 
 
-def x_early_kernel(fields, flags, out, *scratch):
+def x_early_kernel(fields, flags, out, pad, gpad, acc):
     @pl.when(lax.axis_index("gy") == 0)
     def _():
-        x_faces(fields, flags, out, *scratch)
-
-
-def x_late_kernel(fields, flags, early, order, out, *scratch):
+        acc[...] = jnp.zeros_like(acc)
+        x_faces(0, out.shape[1], fields, flags, acc, pad, gpad)
+        fold_rim(acc, out)
+
+
+def x_late_kernel(fields, flags, order, acc, pad, gpad):
     del order
+
+    @pl.when(lax.axis_index("gy") != 0)
+    def _():
+        acc[...] = jnp.zeros_like(acc)
+        x_faces(0, flags.shape[1] // 2, fields, flags, acc, pad, gpad)
+
+
+def x_last_kernel(fields, flags, early, begun, order, out, pad, gpad, acc):
+    del order
+    nx = out.shape[1]
     first = lax.axis_index("gy") == 0
 
     @pl.when(first)
@@ -303,7 +316,9 @@
 
     @pl.when(jnp.logical_not(first))
     def _():
-        x_faces(fields, flags, out, *scratch)
+        acc[...] = begun[...]
+        x_faces(nx // 2, nx, fields, flags, acc, pad, gpad)
+        fold_rim(acc, out)
 
 
 def z_faces(state, cot, flags, x):
@@ -802,9 +817,14 @@
         3,
         2,
     )(fields, kernel, heads, near_twin, near_other)
-    first = call(x_late_kernel, full, x_scratch, 2.8, 3, 1)(fields, flags, early, patches)
+    begun = call(x_late_kernel, shape(5, nx + 5, ny, nz), x_scratch[:2], 1.5, 2, 1)(
+        fields, flags, patches
+    )
     far_twin, far_other = call(far_kernel, (far, far), [], 0.2, 2, 1)(
-        flat, flags.reshape(3 * nx * ny, nz), first
+        flat, flags.reshape(3 * nx * ny, nz), begun
+    )
+    first = call(x_last_kernel, full, x_scratch, 1.5, 4, 1)(
+        fields, flags, early, begun, far_other
     )
     far_rims = (
         lax.ppermute(far_twin, "gy", with_twin),

time: 32.6 us -> 31.4 us (0.963)
  waiting for transfers between devices: 4.42 us -> 1.29 us
  starting transfers between devices: 7.94 us -> 9.95 us
    ppermute x4, starting transfers between devices: 0.47 us -> 3.82 us  [exchanged(): return lax.ppermute(value, 'gy', [(i, i ^ bit) for i in range(count)])]
    ppermute x4, waiting for transfers between devices: 4.41 us -> 1.28 us  [exchanged(): return lax.ppermute(value, 'gy', [(i, i ^ bit) for i in range(count)])]
    ppermute x1, starting transfers between devices: 4 us -> 2.66 us  [body(): lax.ppermute(far_other, 'gy', with_other)]
  transfers between devices with their start and end apart: 8 -> 8, of which waited for: 4 -> 3; matrix products, arithmetic and copies ran while one was open for 0% -> 0% of each run, Pallas kernels for 45% -> 46%
where the time goes in v15:
time: 31.4 us; the launch traced here: 31.3 us
  Pallas kernels  18.1 us (58%)
  starting transfers between devices  9.95 us (32%)
  waiting for transfers between devices  1.29 us (4%)
  other arithmetic  1.17 us (4%)
  between operations  0.78 us (2%)
    pallas_call x3, Pallas kernels, body(): call(functools.partial(yz_kernel, lo, hi), full, [vm((lines, nz), F32)] *...  6.36 us
    pallas_call x1, Pallas kernels, body(): call(c_kernel, (shape(ch, 256), half_shape(10 * ch, nx * nz), half_shape(...  4.71 us
    ppermute x4, starting transfers between devices, exchanged(): return lax.ppermute(value, 'gy', [(i, i ^ bit) for i in range(count)])  3.82 us
    ppermute x1, starting transfers between devices, body(): lax.ppermute(near_other, 'gy', with_other)  3.33 us
    pallas_call x1, Pallas kernels, body(): early = call(x_early_kernel, full, x_scratch, 0.2, 2)(fields, flags)  2.79 us
    ppermute x1, starting transfers between devices, body(): lax.ppermute(far_other, 'gy', with_other)  2.66 us
    ppermute x4, waiting for transfers between devices, exchanged(): return lax.ppermute(value, 'gy', [(i, i ^ bit) for i in range(count)])  1.28 us
    pallas_call x1, Pallas kernels, body(): call(prepare_kernel, (half_shape(20 * ch, COLUMNS), half_shape(384, 512),...  1.19 us
  transfers between devices with their start and end apart: 8, of which 3 were waited for; matrix products, arithmetic and copies ran while one was open for 0% of the time, Pallas kernels for 46%

profile of v15, /device:TPU:0, one launch (start us, length us, event | category | flops | bytes accessed | tf_op | source)
XLA Modules:
  0.0 31.3 jit_solution(6155110559838457272)
XLA Ops:
  0.6 0.0 copy-start
  0.6 1.2 %pad_maximum_fusion.flat = f32[1280,128]{1,0:T(8,128)S(1)} fusion(f32[640,128]{1,0:T(8,128)} %bitcast.13, f32[640,128]{1,0:T(8,128)} %bitcast.14), kind=kLoop, calls=%fused_computation | loop fusion | flops 163840 | bytes 1310720 | tf_op jit(solution)/shard_map/concatenate | solution.py:791
  1.8 0.0 copy-done
  1.8 2.8 %shard_map.76.order.early = f32[5,16,8,128]{3,2,1,0:T(8,128)S(1)} custom-call(f32[10,16,8,128]{3,2,1,0:T(8,128)S(1)} %bitcast.4, s32[3,16,8,128]{3,2,1,0:T(8,128)S(1)} %copy-done), custom_call_target="tpu_custom_call" | custom-call | flops 230000000 | bytes 738000 | tf_op jit(solution)/shard_map/pallas_call | solution.py:799
  4.6 0.0 copy-start.1
  4.6 0.0 copy-start.2
  4.7 0.1 collective-permute-start
  4.8 3.3 %collective-permute-start.1 = (f32[15,16,128]{2,1,0:T(8,128)S(1)}, f32[15,16,128]{2,1,0:T(8,128)S(1)}, u32[]{:S(2)}, u32[]{:S(2)}) collective-permute-start(f32[15,16,128]{2,1,0:T(8,128)S(1)} %get-tuple-element.31.order2), channel_id=1, source_target_pairs={{0,15},{1,2},{2,1},{3,4},{4,3},{5,6},{6,5},{7,8},{8,7},{9,10},{10,... | collective-permute-start | bytes 368648 | tf_op jit(solution)/shard_map/ppermute | solution.py:803
  8.1 0.0 copy-done.1
  8.1 1.2 %shard_map.78 = (bf16[320,720]{1,0:T(8,128)(2,1)S(1)}, bf16[384,512]{1,0:T(8,128)(2,1)S(1)}, bf16[160,192]{1,0:T(8,128)(2,1)S(1)}, f32[160,128]{1,0:T(8,128)S(1)...) custom-call(f32[10,16,8,128]{3,2,1,0:T(8,128)S(1)} %bitcast.5, f32[16,135]{1,0:T(8,128)S(1)} %copy-done.1, ...), custom_call_target="tpu_custom_call" | custom-call | flops 1724999936 | bytes 5535000 | tf_op jit(solution)/shard_map/pallas_call | solution.py:805
  9.3 0.1 shard_map.80
  9.4 0.1 collective-permute-start.4
  9.5 2.7 %collective-permute-start.5 = (f32[28,16,128]{2,1,0:T(8,128)S(1)}, f32[28,16,128]{2,1,0:T(8,128)S(1)}, u32[]{:S(2)}, u32[]{:S(2)}) collective-permute-start(f32[28,16,128]{2,1,0:T(8,128)S(1)} %get-tuple-element.33.order), channel_id=1, source_target_pairs={{0,15},{1,2},{2,1},{3,4},{4,3},{5,6},{6,5},{7,8},{8,7},{9,10},{10,... | collective-permute-start | bytes 688136 | tf_op jit(solution)/shard_map/ppermute | solution.py:831
  12.2 0.0 collective-permute-done.near_twin
  12.2 0.0 collective-permute-done.1.near_other
  12.2 4.7 %shard_map.82 = (f32[16,256]{1,0:T(8,128)S(1)}, bf16[160,2048]{1,0:T(8,128)(2,1)S(1)}, bf16[160,2048]{1,0:T(8,128)(2,1)S(1)}) custom-call(f32[10,16,8,128]{3,2,1,0:T(8,128)S(1)} %bitcast.8, f32[15,16,128]{2,1,0:T(8,128)S(1)} %collective-permute-done.near_twin, f32[15,16,128]{2,1,0:T(8,128)S(1)} %collective-permute-done.1.near_other, ...), custom_call_target="tpu_custom_call" | custom-call | flops 4830000128 | bytes 15498000 | tf_op jit(solution)/shard_map/pallas_call | solution.py:835
  16.9 0.1 collective-permute-start.2
  17.0 1.1 %shard_map.83.before = f32[5,16,8,128]{3,2,1,0:T(8,128)S(1)} custom-call(bf16[384,512]{1,0:T(8,128)(2,1)S(1)} %get-tuple-element.42.w_cols, bf16[160,2048]{1,0:T(8,128)(2,1)S(1)} %get-tuple-element.43.d_high, bf16[160,2048]{1,0:T(8,128)(2,1)S(1)} %get-tuple-element.44.d_low, f32[16,256]{1,0:T(8,128)S(1)} %get-tuple-element.41.order), custom_call_target="tpu_custom_call" | custom-call | flops 1264999936 | bytes 4059000 | tf_op jit(solution)/shard_map/pallas_call | solution.py:863
  18.0 0.1 collective-permute-done.2
  18.1 0.9 %collective-permute-start.3 = (f32[16,256]{1,0:T(8,128)S(1)}, f32[16,256]{1,0:T(8,128)S(1)}, u32[]{:S(2)}, u32[]{:S(2)}) collective-permute-start(f32[16,256]{1,0:T(8,128)S(1)} %add.9.order), channel_id=1, source_target_pairs={{0,2},{1,3},{2,0},{3,1},{4,6},{5,7},{6,4},{7,5},{8,10},{9,11},{10,... | collective-permute-start | bytes 49160 | tf_op jit(solution)/shard_map/ppermute | solution.py:852
  19.0 0.0 collective-permute-done.4.far_twin
  19.0 0.0 collective-permute-done.5.far_other
  19.0 1.1 %shard_map.84.rim = f32[640,128]{1,0:T(8,128)S(1)} custom-call(f32[1280,128]{1,0:T(8,128)S(1)} %pad_maximum_fusion.flat, f32[15,16,128]{2,1,0:T(8,128)S(1)} %collective-permute-done.near_twin, f32[15,16,128]{2,1,0:T(8,128)S(1)} %collective-permute-done.1.near_other, f32[28,16,128]{2,1,0:T(8,128)S(1)} %collective-permute-done.4.far_twin, ...), custom_call_target="tpu_custom_call" | custom-call | flops 1264999936 | bytes 4059000 | tf_op jit(solution)/shard_map/pallas_call | solution.py:869
  20.1 1.4 %shard_map.85.before = f32[5,16,8,128]{3,2,1,0:T(8,128)S(1)} custom-call(f32[10,16,8,128]{3,2,1,0:T(8,128)S(1)} %bitcast.9, s32[3,16,8,128]{3,2,1,0:T(8,128)S(1)} %copy-done, f32[15,16,128]{2,1,0:T(8,128)S(1)} %collective-permute-done.near_twin, f32[15,16,128]{2,1,0:T(8,128)S(1)} %collective-permute-done.1.near_other, ...), custom_call_target="tpu_custom_call" | custom-call | flops 2529999872 | bytes 8118000 | tf_op jit(solution)/shard_map/pallas_call | solution.py:859
  21.6 0.3 %collective-permute-done.3 = f32[16,256]{1,0:T(8,128)S(1)} collective-permute-done((f32[16,256]{1,0:T(8,128)S(1)}, f32[16,256]{1,0:T(8,128)S(1)}, u32[]{:S(2)}, u32[]{:S(2)}) %collective-permute-start.3) | collective-permute-done | bytes 16416 | tf_op jit(solution)/shard_map/ppermute | solution.py:852
  21.9 0.8 %collective-permute-start.6 = (f32[16,256]{1,0:T(8,128)S(1)}, f32[16,256]{1,0:T(8,128)S(1)}, u32[]{:S(2)}, u32[]{:S(2)}) collective-permute-start(f32[16,256]{1,0:T(8,128)S(1)} %add.10.order), channel_id=1, source_target_pairs={{0,4},{1,5},{2,6},{3,7},{4,0},{5,1},{6,2},{7,3},{8,12},{9,13},{10,... | collective-permute-start | bytes 49160 | tf_op jit(solution)/shard_map/ppermute | solution.py:852
  22.7 2.1 %shard_map.86.before = f32[5,16,8,128]{3,2,1,0:T(8,128)S(1)} custom-call(f32[10,16,8,128]{3,2,1,0:T(8,128)S(1)} %bitcast.10, s32[3,16,8,128]{3,2,1,0:T(8,128)S(1)} %copy-done, f32[15,16,128]{2,1,0:T(8,128)S(1)} %collective-permute-done.near_twin, f32[15,16,128]{2,1,0:T(8,128)S(1)} %collective-permute-done.1.near_other, ...), custom_call_target="tpu_custom_call" | custom-call | flops 2529999872 | bytes 8118000 | tf_op jit(solution)/shard_map/pallas_call | solution.py:859
  24.8 0.9 %collective-permute-done.6 = f32[16,256]{1,0:T(8,128)S(1)} collective-permute-done((f32[16,256]{1,0:T(8,128)S(1)}, f32[16,256]{1,0:T(8,128)S(1)}, u32[]{:S(2)}, u32[]{:S(2)}) %collective-permute-start.6) | collective-permute-done | bytes 16416 | tf_op jit(solution)/shard_map/ppermute | solution.py:852
  25.6 2.1 %collective-permute-start.7 = (f32[16,256]{1,0:T(8,128)S(1)}, f32[16,256]{1,0:T(8,128)S(1)}, u32[]{:S(2)}, u32[]{:S(2)}) collective-permute-start(f32[16,256]{1,0:T(8,128)S(1)} %add.11.order.mine), channel_id=1, source_target_pairs={{0,8},{1,9},{2,10},{3,11},{4,12},{5,13},{6,14},{7,15},{8,0},{9,1},... | collective-permute-start | bytes 49160 | tf_op jit(solution)/shard_map/ppermute | solution.py:852
  27.7 2.8 %shard_map.87 = f32[5,16,8,128]{3,2,1,0:T(8,128)} custom-call(f32[10,16,8,128]{3,2,1,0:T(8,128)S(1)} %bitcast.11, s32[3,16,8,128]{3,2,1,0:T(8,128)S(1)} %copy-done, f32[15,16,128]{2,1,0:T(8,128)S(1)} %collective-permute-done.near_twin, f32[15,16,128]{2,1,0:T(8,128)S(1)} %collective-permute-done.1.near_other, ...), custom_call_target="tpu_custom_call" | custom-call | flops 2529999872 | bytes 8118000 | tf_op jit(solution)/shard_map/pallas_call | solution.py:859
  30.5 0.0 collective-permute-done.7.theirs
  30.5 0.7 %shard_map.88 = (f32[16,135]{1,0:T(8,128)}, f32[5,16]{1,0:T(8,128)}) custom-call(f32[16,256]{1,0:T(8,128)S(1)} %add.11.order.mine, f32[16,256]{1,0:T(8,128)S(1)} %collective-permute-done.7.theirs), custom_call_target="tpu_custom_call" | custom-call | flops 575000000 | bytes 1845000 | tf_op jit(solution)/shard_map/pallas_call | solution.py:881
  (7 shorter events, 0.1 us)
Async XLA Ops:
  0.6 1.2 %copy-start = (s32[3,16,8,128]{3,2,1,0:T(8,128)S(1)}, s32[3,16,8,128]{3,2,1,0:T(8,128)}, u32[]{:S(2)}) copy-start(s32[3,16,8,128]{3,2,1,0:T(8,128)} %flags.11) | copy-start | bytes 589828
  4.6 3.5 %copy-start.1 = (f32[16,135]{1,0:T(8,128)S(1)}, f32[16,135]{1,0:T(8,128)}, u32[]{:S(2)}) copy-start(f32[16,135]{1,0:T(8,128)} %kernel.3) | copy-start | bytes 25924
  4.6 3.5 %copy-start.2 = (f32[5,16]{1,0:T(8,128)S(1)}, f32[5,16]{1,0:T(8,128)}, u32[]{:S(2)}) copy-start(f32[5,16]{1,0:T(8,128)} %heads.1) | copy-start | bytes 964
  4.7 7.5 %collective-permute-start = (f32[15,16,128]{2,1,0:T(8,128)S(1)}, f32[15,16,128]{2,1,0:T(8,128)S(1)}, u32[]{:S(2)}, u32[]{:S(2)}) collective-permute-start(f32[15,16,128]{2,1,0:T(8,128)S(1)} %get-tuple-element.30.order), channel_id=1, source_target_pairs={{0,1},{1,0},{2,3},{3,2},{4,5},{5,4},{6,7},{7,6},{8,9},{9,8},{10,11... | collective-permute-start | bytes 368648 | tf_op jit(solution)/shard_map/ppermute | solution.py:802
  4.8 7.4 %collective-permute-start.1 = (f32[15,16,128]{2,1,0:T(8,128)S(1)}, f32[15,16,128]{2,1,0:T(8,128)S(1)}, u32[]{:S(2)}, u32[]{:S(2)}) collective-permute-start(f32[15,16,128]{2,1,0:T(8,128)S(1)} %get-tuple-element.31.order2), channel_id=1, source_target_pairs={{0,15},{1,2},{2,1},{3,4},{4,3},{5,6},{6,5},{7,8},{8,7},{9,10},{10,... | collective-permute-start | bytes 368648 | tf_op jit(solution)/shard_map/ppermute | solution.py:803
  9.4 9.6 %collective-permute-start.4 = (f32[28,16,128]{2,1,0:T(8,128)S(1)}, f32[28,16,128]{2,1,0:T(8,128)S(1)}, u32[]{:S(2)}, u32[]{:S(2)}) collective-permute-start(f32[28,16,128]{2,1,0:T(8,128)S(1)} %get-tuple-element.46), channel_id=1, source_target_pairs={{0,1},{1,0},{2,3},{3,2},{4,5},{5,4},{6,7},{7,6},{8,9},{9,8},{10,11... | collective-permute-start | bytes 688136 | tf_op jit(solution)/shard_map/ppermute | solution.py:830
  9.5 9.6 %collective-permute-start.5 = (f32[28,16,128]{2,1,0:T(8,128)S(1)}, f32[28,16,128]{2,1,0:T(8,128)S(1)}, u32[]{:S(2)}, u32[]{:S(2)}) collective-permute-start(f32[28,16,128]{2,1,0:T(8,128)S(1)} %get-tuple-element.33.order), channel_id=1, source_target_pairs={{0,15},{1,2},{2,1},{3,4},{4,3},{5,6},{6,5},{7,8},{8,7},{9,10},{10,... | collective-permute-start | bytes 688136 | tf_op jit(solution)/shard_map/ppermute | solution.py:831
  16.9 1.2 %collective-permute-start.2 = (f32[16,256]{1,0:T(8,128)S(1)}, f32[16,256]{1,0:T(8,128)S(1)}, u32[]{:S(2)}, u32[]{:S(2)}) collective-permute-start(f32[16,256]{1,0:T(8,128)S(1)} %get-tuple-element.41.order), channel_id=1, source_target_pairs={{0,1},{1,0},{2,3},{3,2},{4,5},{5,4},{6,7},{7,6},{8,9},{9,8},{10,11... | collective-permute-start | bytes 49160 | tf_op jit(solution)/shard_map/ppermute | solution.py:852
  18.1 3.7 %collective-permute-start.3 = (f32[16,256]{1,0:T(8,128)S(1)}, f32[16,256]{1,0:T(8,128)S(1)}, u32[]{:S(2)}, u32[]{:S(2)}) collective-permute-start(f32[16,256]{1,0:T(8,128)S(1)} %add.9.order), channel_id=1, source_target_pairs={{0,2},{1,3},{2,0},{3,1},{4,6},{5,7},{6,4},{7,5},{8,10},{9,11},{10,... | collective-permute-start | bytes 49160 | tf_op jit(solution)/shard_map/ppermute | solution.py:852
  21.9 3.7 %collective-permute-start.6 = (f32[16,256]{1,0:T(8,128)S(1)}, f32[16,256]{1,0:T(8,128)S(1)}, u32[]{:S(2)}, u32[]{:S(2)}) collective-permute-start(f32[16,256]{1,0:T(8,128)S(1)} %add.10.order), channel_id=1, source_target_pairs={{0,4},{1,5},{2,6},{3,7},{4,0},{5,1},{6,2},{7,3},{8,12},{9,13},{10,... | collective-permute-start | bytes 49160 | tf_op jit(solution)/shard_map/ppermute | solution.py:852
  25.6 4.9 %collective-permute-start.7 = (f32[16,256]{1,0:T(8,128)S(1)}, f32[16,256]{1,0:T(8,128)S(1)}, u32[]{:S(2)}, u32[]{:S(2)}) collective-permute-start(f32[16,256]{1,0:T(8,128)S(1)} %add.11.order.mine), channel_id=1, source_target_pairs={{0,8},{1,9},{2,10},{3,11},{4,12},{5,13},{6,14},{7,15},{8,0},{9,1},... | collective-permute-start | bytes 49160 | tf_op jit(solution)/shard_map/ppermute | solution.py:852

commit v16 on v15

--- a/solution.py
+++ b/solution.py
@@ -871,11 +871,11 @@
     got, total = lax.optimization_barrier((got, total))
     sums = sums + got
     got = exchanged(sums, bits[-2])
-    total = yz(third, nx - nx // 8 * 3, total, sums)
+    total = yz(third, nx - nx // 4, total, sums)
     got, total = lax.optimization_barrier((got, total))
     sums = sums + got
     got = exchanged(sums, bits[-1])
-    flow = yz(nx - nx // 8 * 3, nx, total, sums)
+    flow = yz(nx - nx // 4, nx, total, sums)
     got, flow = lax.optimization_barrier((got, flow))
     scale = float(cells * count) ** (-0.5)
     k_out, h_out = call(

time: 31.4 us -> 31.4 us (level)
  waiting for transfers between devices: 1.29 us -> 0.6 us
  starting transfers between devices: 9.95 us -> 10.6 us
    ppermute x4, starting transfers between devices: 3.82 us -> 4.5 us  [exchanged(): return lax.ppermute(value, 'gy', [(i, i ^ bit) for i in range(count)])]
    ppermute x4, waiting for transfers between devices: 1.28 us -> 0.59 us  [exchanged(): return lax.ppermute(value, 'gy', [(i, i ^ bit) for i in range(count)])]
where the time goes in v16:
time: 31.4 us; the launch traced here: 31.3 us
  Pallas kernels  18.1 us (58%)
  starting transfers between devices  10.6 us (34%)
  other arithmetic  1.17 us (4%)
  between operations  0.78 us (2%)
  waiting for transfers between devices  0.6 us (2%)
    pallas_call x3, Pallas kernels, body(): call(functools.partial(yz_kernel, lo, hi), full, [vm((lines, nz), F32)] *...  6.36 us
    pallas_call x1, Pallas kernels, body(): call(c_kernel, (shape(ch, 256), half_shape(10 * ch, nx * nz), half_shape(...  4.71 us
    ppermute x4, starting transfers between devices, exchanged(): return lax.ppermute(value, 'gy', [(i, i ^ bit) for i in range(count)])  4.5 us
    ppermute x1, starting transfers between devices, body(): lax.ppermute(near_other, 'gy', with_other)  3.33 us
    pallas_call x1, Pallas kernels, body(): early = call(x_early_kernel, full, x_scratch, 0.2, 2)(fields, flags)  2.79 us
    ppermute x1, starting transfers between devices, body(): lax.ppermute(far_other, 'gy', with_other)  2.66 us
    pallas_call x1, Pallas kernels, body(): call(prepare_kernel, (half_shape(20 * ch, COLUMNS), half_shape(384, 512),...  1.19 us
    concatenate x1, other arithmetic, body(): flat = jnp.concatenate([state.reshape(lines, nz), cot.reshape(lines, nz)])  1.15 us
  transfers between devices with their start and end apart: 8, of which 3 were waited for; matrix products, arithmetic and copies ran while one was open for 0% of the time, Pallas kernels for 46%

profile of v16, /device:TPU:0, one launch (start us, length us, event | category | flops | bytes accessed | tf_op | source)
XLA Modules:
  0.0 31.3 jit_solution(2364335998315285512)
XLA Ops:
  0.6 0.0 copy-start
  0.6 1.2 %pad_maximum_fusion.flat = f32[1280,128]{1,0:T(8,128)S(1)} fusion(f32[640,128]{1,0:T(8,128)} %bitcast.13, f32[640,128]{1,0:T(8,128)} %bitcast.14), kind=kLoop, calls=%fused_computation | loop fusion | flops 163840 | bytes 1310720 | tf_op jit(solution)/shard_map/concatenate | solution.py:791
  1.8 0.0 copy-done
  1.8 2.8 %shard_map.76.order.early = f32[5,16,8,128]{3,2,1,0:T(8,128)S(1)} custom-call(f32[10,16,8,128]{3,2,1,0:T(8,128)S(1)} %bitcast.4, s32[3,16,8,128]{3,2,1,0:T(8,128)S(1)} %copy-done), custom_call_target="tpu_custom_call" | custom-call | flops 230000000 | bytes 738000 | tf_op jit(solution)/shard_map/pallas_call | solution.py:799
  4.6 0.0 copy-start.1
  4.6 0.0 copy-start.2
  4.7 0.1 collective-permute-start
  4.8 3.3 %collective-permute-start.1 = (f32[15,16,128]{2,1,0:T(8,128)S(1)}, f32[15,16,128]{2,1,0:T(8,128)S(1)}, u32[]{:S(2)}, u32[]{:S(2)}) collective-permute-start(f32[15,16,128]{2,1,0:T(8,128)S(1)} %get-tuple-element.31.order2), channel_id=1, source_target_pairs={{0,15},{1,2},{2,1},{3,4},{4,3},{5,6},{6,5},{7,8},{8,7},{9,10},{10,... | collective-permute-start | bytes 368648 | tf_op jit(solution)/shard_map/ppermute | solution.py:803
  8.1 0.0 copy-done.1
  8.1 1.2 %shard_map.78 = (bf16[320,720]{1,0:T(8,128)(2,1)S(1)}, bf16[384,512]{1,0:T(8,128)(2,1)S(1)}, bf16[160,192]{1,0:T(8,128)(2,1)S(1)}, f32[160,128]{1,0:T(8,128)S(1)...) custom-call(f32[10,16,8,128]{3,2,1,0:T(8,128)S(1)} %bitcast.5, f32[16,135]{1,0:T(8,128)S(1)} %copy-done.1, ...), custom_call_target="tpu_custom_call" | custom-call | flops 1724999936 | bytes 5535000 | tf_op jit(solution)/shard_map/pallas_call | solution.py:805
  9.3 0.1 shard_map.80
  9.4 0.1 collective-permute-start.4
  9.5 2.7 %collective-permute-start.5 = (f32[28,16,128]{2,1,0:T(8,128)S(1)}, f32[28,16,128]{2,1,0:T(8,128)S(1)}, u32[]{:S(2)}, u32[]{:S(2)}) collective-permute-start(f32[28,16,128]{2,1,0:T(8,128)S(1)} %get-tuple-element.33.order), channel_id=1, source_target_pairs={{0,15},{1,2},{2,1},{3,4},{4,3},{5,6},{6,5},{7,8},{8,7},{9,10},{10,... | collective-permute-start | bytes 688136 | tf_op jit(solution)/shard_map/ppermute | solution.py:831
  12.2 0.0 collective-permute-done.near_twin
  12.2 0.0 collective-permute-done.1.near_other
  12.2 4.7 %shard_map.82 = (f32[16,256]{1,0:T(8,128)S(1)}, bf16[160,2048]{1,0:T(8,128)(2,1)S(1)}, bf16[160,2048]{1,0:T(8,128)(2,1)S(1)}) custom-call(f32[10,16,8,128]{3,2,1,0:T(8,128)S(1)} %bitcast.8, f32[15,16,128]{2,1,0:T(8,128)S(1)} %collective-permute-done.near_twin, f32[15,16,128]{2,1,0:T(8,128)S(1)} %collective-permute-done.1.near_other, ...), custom_call_target="tpu_custom_call" | custom-call | flops 4830000128 | bytes 15498000 | tf_op jit(solution)/shard_map/pallas_call | solution.py:835
  16.9 0.1 collective-permute-start.2
  17.0 1.1 %shard_map.83.before = f32[5,16,8,128]{3,2,1,0:T(8,128)S(1)} custom-call(bf16[384,512]{1,0:T(8,128)(2,1)S(1)} %get-tuple-element.42.w_cols, bf16[160,2048]{1,0:T(8,128)(2,1)S(1)} %get-tuple-element.43.d_high, bf16[160,2048]{1,0:T(8,128)(2,1)S(1)} %get-tuple-element.44.d_low, f32[16,256]{1,0:T(8,128)S(1)} %get-tuple-element.41.order), custom_call_target="tpu_custom_call" | custom-call | flops 1264999936 | bytes 4059000 | tf_op jit(solution)/shard_map/pallas_call | solution.py:863
  18.0 0.1 collective-permute-done.2
  18.1 0.9 %collective-permute-start.3 = (f32[16,256]{1,0:T(8,128)S(1)}, f32[16,256]{1,0:T(8,128)S(1)}, u32[]{:S(2)}, u32[]{:S(2)}) collective-permute-start(f32[16,256]{1,0:T(8,128)S(1)} %add.9.order), channel_id=1, source_target_pairs={{0,2},{1,3},{2,0},{3,1},{4,6},{5,7},{6,4},{7,5},{8,10},{9,11},{10,... | collective-permute-start | bytes 49160 | tf_op jit(solution)/shard_map/ppermute | solution.py:852
  19.0 0.0 collective-permute-done.4.far_twin
  19.0 0.0 collective-permute-done.5.far_other
  19.0 1.1 %shard_map.84.rim = f32[640,128]{1,0:T(8,128)S(1)} custom-call(f32[1280,128]{1,0:T(8,128)S(1)} %pad_maximum_fusion.flat, f32[15,16,128]{2,1,0:T(8,128)S(1)} %collective-permute-done.near_twin, f32[15,16,128]{2,1,0:T(8,128)S(1)} %collective-permute-done.1.near_other, f32[28,16,128]{2,1,0:T(8,128)S(1)} %collective-permute-done.4.far_twin, ...), custom_call_target="tpu_custom_call" | custom-call | flops 1264999936 | bytes 4059000 | tf_op jit(solution)/shard_map/pallas_call | solution.py:869
  20.1 1.4 %shard_map.85.before = f32[5,16,8,128]{3,2,1,0:T(8,128)S(1)} custom-call(f32[10,16,8,128]{3,2,1,0:T(8,128)S(1)} %bitcast.9, s32[3,16,8,128]{3,2,1,0:T(8,128)S(1)} %copy-done, f32[15,16,128]{2,1,0:T(8,128)S(1)} %collective-permute-done.near_twin, f32[15,16,128]{2,1,0:T(8,128)S(1)} %collective-permute-done.1.near_other, ...), custom_call_target="tpu_custom_call" | custom-call | flops 2529999872 | bytes 8118000 | tf_op jit(solution)/shard_map/pallas_call | solution.py:859
  21.6 0.3 %collective-permute-done.3 = f32[16,256]{1,0:T(8,128)S(1)} collective-permute-done((f32[16,256]{1,0:T(8,128)S(1)}, f32[16,256]{1,0:T(8,128)S(1)}, u32[]{:S(2)}, u32[]{:S(2)}) %collective-permute-start.3) | collective-permute-done | bytes 16416 | tf_op jit(solution)/shard_map/ppermute | solution.py:852
  21.9 0.8 %collective-permute-start.6 = (f32[16,256]{1,0:T(8,128)S(1)}, f32[16,256]{1,0:T(8,128)S(1)}, u32[]{:S(2)}, u32[]{:S(2)}) collective-permute-start(f32[16,256]{1,0:T(8,128)S(1)} %add.10.order), channel_id=1, source_target_pairs={{0,4},{1,5},{2,6},{3,7},{4,0},{5,1},{6,2},{7,3},{8,12},{9,13},{10,... | collective-permute-start | bytes 49160 | tf_op jit(solution)/shard_map/ppermute | solution.py:852
  22.7 2.8 %shard_map.86.before = f32[5,16,8,128]{3,2,1,0:T(8,128)S(1)} custom-call(f32[10,16,8,128]{3,2,1,0:T(8,128)S(1)} %bitcast.10, s32[3,16,8,128]{3,2,1,0:T(8,128)S(1)} %copy-done, f32[15,16,128]{2,1,0:T(8,128)S(1)} %collective-permute-done.near_twin, f32[15,16,128]{2,1,0:T(8,128)S(1)} %collective-permute-done.1.near_other, ...), custom_call_target="tpu_custom_call" | custom-call | flops 2529999872 | bytes 8118000 | tf_op jit(solution)/shard_map/pallas_call | solution.py:859
  25.5 0.2 collective-permute-done.6
  25.6 2.8 %collective-permute-start.7 = (f32[16,256]{1,0:T(8,128)S(1)}, f32[16,256]{1,0:T(8,128)S(1)}, u32[]{:S(2)}, u32[]{:S(2)}) collective-permute-start(f32[16,256]{1,0:T(8,128)S(1)} %add.11.order.mine), channel_id=1, source_target_pairs={{0,8},{1,9},{2,10},{3,11},{4,12},{5,13},{6,14},{7,15},{8,0},{9,1},... | collective-permute-start | bytes 49160 | tf_op jit(solution)/shard_map/ppermute | solution.py:852
  28.4 2.1 %shard_map.87 = f32[5,16,8,128]{3,2,1,0:T(8,128)} custom-call(f32[10,16,8,128]{3,2,1,0:T(8,128)S(1)} %bitcast.11, s32[3,16,8,128]{3,2,1,0:T(8,128)S(1)} %copy-done, f32[15,16,128]{2,1,0:T(8,128)S(1)} %collective-permute-done.near_twin, f32[15,16,128]{2,1,0:T(8,128)S(1)} %collective-permute-done.1.near_other, ...), custom_call_target="tpu_custom_call" | custom-call | flops 2529999872 | bytes 8118000 | tf_op jit(solution)/shard_map/pallas_call | solution.py:859
  30.6 0.0 collective-permute-done.7.theirs
  30.6 0.7 %shard_map.88 = (f32[16,135]{1,0:T(8,128)}, f32[5,16]{1,0:T(8,128)}) custom-call(f32[16,256]{1,0:T(8,128)S(1)} %add.11.order.mine, f32[16,256]{1,0:T(8,128)S(1)} %collective-permute-done.7.theirs), custom_call_target="tpu_custom_call" | custom-call | flops 575000000 | bytes 1845000 | tf_op jit(solution)/shard_map/pallas_call | solution.py:881
  (7 shorter events, 0.1 us)
Async XLA Ops:
  0.6 1.2 %copy-start = (s32[3,16,8,128]{3,2,1,0:T(8,128)S(1)}, s32[3,16,8,128]{3,2,1,0:T(8,128)}, u32[]{:S(2)}) copy-start(s32[3,16,8,128]{3,2,1,0:T(8,128)} %flags.11) | copy-start | bytes 589828
  4.6 3.5 %copy-start.1 = (f32[16,135]{1,0:T(8,128)S(1)}, f32[16,135]{1,0:T(8,128)}, u32[]{:S(2)}) copy-start(f32[16,135]{1,0:T(8,128)} %kernel.3) | copy-start | bytes 25924
  4.6 3.5 %copy-start.2 = (f32[5,16]{1,0:T(8,128)S(1)}, f32[5,16]{1,0:T(8,128)}, u32[]{:S(2)}) copy-start(f32[5,16]{1,0:T(8,128)} %heads.1) | copy-start | bytes 964
  4.7 7.5 %collective-permute-start = (f32[15,16,128]{2,1,0:T(8,128)S(1)}, f32[15,16,128]{2,1,0:T(8,128)S(1)}, u32[]{:S(2)}, u32[]{:S(2)}) collective-permute-start(f32[15,16,128]{2,1,0:T(8,128)S(1)} %get-tuple-element.30.order), channel_id=1, source_target_pairs={{0,1},{1,0},{2,3},{3,2},{4,5},{5,4},{6,7},{7,6},{8,9},{9,8},{10,11... | collective-permute-start | bytes 368648 | tf_op jit(solution)/shard_map/ppermute | solution.py:802
  4.8 7.4 %collective-permute-start.1 = (f32[15,16,128]{2,1,0:T(8,128)S(1)}, f32[15,16,128]{2,1,0:T(8,128)S(1)}, u32[]{:S(2)}, u32[]{:S(2)}) collective-permute-start(f32[15,16,128]{2,1,0:T(8,128)S(1)} %get-tuple-element.31.order2), channel_id=1, source_target_pairs={{0,15},{1,2},{2,1},{3,4},{4,3},{5,6},{6,5},{7,8},{8,7},{9,10},{10,... | collective-permute-start | bytes 368648 | tf_op jit(solution)/shard_map/ppermute | solution.py:803
  9.4 9.6 %collective-permute-start.4 = (f32[28,16,128]{2,1,0:T(8,128)S(1)}, f32[28,16,128]{2,1,0:T(8,128)S(1)}, u32[]{:S(2)}, u32[]{:S(2)}) collective-permute-start(f32[28,16,128]{2,1,0:T(8,128)S(1)} %get-tuple-element.46), channel_id=1, source_target_pairs={{0,1},{1,0},{2,3},{3,2},{4,5},{5,4},{6,7},{7,6},{8,9},{9,8},{10,11... | collective-permute-start | bytes 688136 | tf_op jit(solution)/shard_map/ppermute | solution.py:830
  9.5 9.6 %collective-permute-start.5 = (f32[28,16,128]{2,1,0:T(8,128)S(1)}, f32[28,16,128]{2,1,0:T(8,128)S(1)}, u32[]{:S(2)}, u32[]{:S(2)}) collective-permute-start(f32[28,16,128]{2,1,0:T(8,128)S(1)} %get-tuple-element.33.order), channel_id=1, source_target_pairs={{0,15},{1,2},{2,1},{3,4},{4,3},{5,6},{6,5},{7,8},{8,7},{9,10},{10,... | collective-permute-start | bytes 688136 | tf_op jit(solution)/shard_map/ppermute | solution.py:831
  16.9 1.2 %collective-permute-start.2 = (f32[16,256]{1,0:T(8,128)S(1)}, f32[16,256]{1,0:T(8,128)S(1)}, u32[]{:S(2)}, u32[]{:S(2)}) collective-permute-start(f32[16,256]{1,0:T(8,128)S(1)} %get-tuple-element.41.order), channel_id=1, source_target_pairs={{0,1},{1,0},{2,3},{3,2},{4,5},{5,4},{6,7},{7,6},{8,9},{9,8},{10,11... | collective-permute-start | bytes 49160 | tf_op jit(solution)/shard_map/ppermute | solution.py:852
  18.1 3.7 %collective-permute-start.3 = (f32[16,256]{1,0:T(8,128)S(1)}, f32[16,256]{1,0:T(8,128)S(1)}, u32[]{:S(2)}, u32[]{:S(2)}) collective-permute-start(f32[16,256]{1,0:T(8,128)S(1)} %add.9.order), channel_id=1, source_target_pairs={{0,2},{1,3},{2,0},{3,1},{4,6},{5,7},{6,4},{7,5},{8,10},{9,11},{10,... | collective-permute-start | bytes 49160 | tf_op jit(solution)/shard_map/ppermute | solution.py:852
  21.9 3.7 %collective-permute-start.6 = (f32[16,256]{1,0:T(8,128)S(1)}, f32[16,256]{1,0:T(8,128)S(1)}, u32[]{:S(2)}, u32[]{:S(2)}) collective-permute-start(f32[16,256]{1,0:T(8,128)S(1)} %add.10.order), channel_id=1, source_target_pairs={{0,4},{1,5},{2,6},{3,7},{4,0},{5,1},{6,2},{7,3},{8,12},{9,13},{10,... | collective-permute-start | bytes 49160 | tf_op jit(solution)/shard_map/ppermute | solution.py:852
  25.6 4.9 %collective-permute-start.7 = (f32[16,256]{1,0:T(8,128)S(1)}, f32[16,256]{1,0:T(8,128)S(1)}, u32[]{:S(2)}, u32[]{:S(2)}) collective-permute-start(f32[16,256]{1,0:T(8,128)S(1)} %add.11.order.mine), channel_id=1, source_target_pairs={{0,8},{1,9},{2,10},{3,11},{4,12},{5,13},{6,14},{7,15},{8,0},{9,1},... | collective-permute-start | bytes 49160 | tf_op jit(solution)/shard_map/ppermute | solution.py:852
